TPU v7x, 128 devices: a whole 4x4x4 slice. The times are simulated.
128 devices in a mesh: dp: 4 (over y_lo, core), ctx: 32 (over x, z, y_hi).
Axes of the slice: x: 4, y: 4 (y_hi: 2, y_lo: 2; y = y_hi * 2 + y_lo), z: 4, core: 2. Of those that a mesh axis runs over, the one named last changes fastest.
Arguments:
- hidden_in: bfloat16 [4, 8192, 3584], P('dp', 'ctx'), may hold values from -6 to 6
- norm_gain: float32 [3584], replicated, may hold values from 0.1 to 1.9
- w_query: bfloat16 [3584, 1792], P(('dp', 'ctx')), may hold values from -3 to 3
- w_key: bfloat16 [3584, 256], P(('dp', 'ctx')), may hold values from -3 to 3
- value_weight: bfloat16 [3584, 256], P(('dp', 'ctx')), may hold values from -0.09375 to 0.09375
- marker_key_weight: bfloat16 [3584, 256], P(('dp', 'ctx')), may hold values from -0.09375 to 0.09375
- marker_value_weight: bfloat16 [3584, 256], P(('dp', 'ctx')), may hold values from -0.09375 to 0.09375
- ratio_level: int32 [4, 32], P('dp', 'ctx'), may hold values from 0 to 3, as said below
- hist_len: int32 [4], P('dp'), may hold values from 4097 to 8192, as said below
Outputs:
- attended: bfloat16 [4, 8192, 1792], P('dp', 'ctx')
Inputs may be any that keep to these rules, and one draw needn't show every extreme that they name: `ratio_level`: each history has a span at level 0 and a span at level 3, so some span fills all 64 beacon slots. `hist_len`: one history of every draw is used to its full length 8192.
All inputs are finite; a program needn't handle non-finite values.
Results may differ from a plain program's by a relative error of at most 0.0069.
Values may be sent and summed in bfloat16 or wider, within the bound.
No kernel may reach another device: no remote copies, remote signals or barrier semaphores. Data moves between devices by JAX's collectives and lax.ppermute only.
A program may use at most 128 MiB of HBM per device.

v0:
```python
import math

import jax
import jax.numpy as jnp
from jax import lax
from jax.sharding import PartitionSpec as P

QUERY_HEADS = 14
KEY_VALUE_HEADS = 2
HEAD_SIZE = 128


eps_norm = 1e-06
negative_filler = -1e30


def norm_rows(tokens, norm_gain):
    values = tokens.astype(jnp.float32)
    factor = lax.rsqrt(jnp.mean(values * values, axis=-1, keepdims=True) + eps_norm)
    return (values * factor * norm_gain).astype(jnp.bfloat16)


def window_table(span_level, begin_offset, length, token_rows, marker_slot_count):
    stride = (4 * jnp.power(2, span_level)).astype(jnp.int32)
    live_count = token_rows // stride
    slot_ids = lax.broadcasted_iota(jnp.int32, (marker_slot_count, token_rows), 0)
    pos_ids = lax.broadcasted_iota(jnp.int32, (marker_slot_count, token_rows), 1)
    inside = (
        (pos_ids // stride == slot_ids)
        & (slot_ids < live_count)
        & (begin_offset + pos_ids < length)
    )
    slot_col = jnp.arange(marker_slot_count, dtype=jnp.int32)
    live_slot = (slot_col < live_count) & (begin_offset + slot_col * stride < length)
    return (inside, live_slot)


def pool_rows(inside, normed):
    window_sum = jnp.dot(inside.astype(jnp.bfloat16), normed, preferred_element_type=jnp.float32)
    window_size = jnp.sum(inside.astype(jnp.float32), axis=1)
    return (window_sum / jnp.maximum(window_size, 1.0)[:, None]).astype(jnp.bfloat16)


def raw_attention(query_matrix, key_matrix, value_matrix, begin_offset, length, score_scale):
    token_rows = key_matrix.shape[0]
    scores = (
        jnp.einsum("kgtd,skd->kgts", query_matrix, key_matrix, preferred_element_type=jnp.float32)
        * score_scale
    )
    positions = jnp.arange(token_rows, dtype=jnp.int32)
    visible = (positions[None, :] <= positions[:, None]) & (
        begin_offset + positions[None, :] < length
    )
    scores = jnp.where(visible, scores, negative_filler)
    top_score = jnp.max(scores, axis=-1)
    weights = jnp.where(visible, jnp.exp(scores - top_score[..., None]), 0.0)
    weight_sum = jnp.sum(weights, axis=-1)
    weighted = jnp.einsum(
        "kgts,skd->kgtd",
        weights.astype(jnp.bfloat16),
        value_matrix,
        preferred_element_type=jnp.float32,
    )
    return (top_score, weight_sum, weighted)


def beacon_update(
    carry_state,
    query_matrix,
    limit,
    marker_key_rows,
    marker_value_rows,
    beacon_live,
    marker_slot_count,
    score_scale,
):
    row_total = marker_key_rows.shape[0]
    span_of = jnp.arange(row_total, dtype=jnp.int32) // marker_slot_count
    visible = (beacon_live > 0) & (span_of < limit)

    def compute(state):
        running, weight_sum, weighted = state
        scores = (
            jnp.einsum(
                "kgtd,skd->kgts", query_matrix, marker_key_rows, preferred_element_type=jnp.float32
            )
            * score_scale
        )
        scores = jnp.where(visible, scores, negative_filler)
        new_top = jnp.maximum(running, jnp.max(scores, axis=-1))
        weights = jnp.where(visible, jnp.exp(scores - new_top[..., None]), 0.0)
        added = jnp.einsum(
            "kgts,skd->kgtd",
            weights.astype(jnp.bfloat16),
            marker_value_rows,
            preferred_element_type=jnp.float32,
        )
        return (new_top, jnp.sum(weights, axis=-1), added)

    def unchanged(state):
        return state

    return lax.cond(jnp.any(visible), compute, unchanged, carry_state)


def on_device(
    hidden_in,
    norm_gain,
    w_query,
    w_key,
    value_weight,
    marker_key_weight,
    marker_value_weight,
    ratio_level,
    hist_len,
):
    token_rows = hidden_in.shape[1]
    marker_slot_count = token_rows // 4
    my_span = lax.axis_index("ctx")
    begin_offset = my_span * token_rows
    length = hist_len[0]
    query_group_count = QUERY_HEADS // KEY_VALUE_HEADS
    score_scale = 1.0 / math.sqrt(HEAD_SIZE)
    normed = norm_rows(hidden_in[0], norm_gain)
    inside, live_slot = window_table(
        ratio_level[0, 0], begin_offset, length, token_rows, marker_slot_count
    )
    pooled = pool_rows(inside, normed)
    gathered = (
        lax.all_gather(w_query, ("dp", "ctx"), axis=0, tiled=True),
        lax.all_gather(w_key, ("dp", "ctx"), axis=0, tiled=True),
        lax.all_gather(value_weight, ("dp", "ctx"), axis=0, tiled=True),
        lax.all_gather(marker_key_weight, ("dp", "ctx"), axis=0, tiled=True),
        lax.all_gather(marker_value_weight, ("dp", "ctx"), axis=0, tiled=True),
    )
    flattened_query = jnp.dot(normed, gathered[0], preferred_element_type=jnp.float32).astype(
        jnp.bfloat16
    )
    query_matrix = flattened_query.reshape(
        token_rows, KEY_VALUE_HEADS, query_group_count, HEAD_SIZE
    ).transpose(1, 2, 0, 3)
    key_matrix = (
        jnp.dot(normed, gathered[1], preferred_element_type=jnp.float32)
        .astype(jnp.bfloat16)
        .reshape(token_rows, KEY_VALUE_HEADS, HEAD_SIZE)
    )
    value_matrix = (
        jnp.dot(normed, gathered[2], preferred_element_type=jnp.float32)
        .astype(jnp.bfloat16)
        .reshape(token_rows, KEY_VALUE_HEADS, HEAD_SIZE)
    )
    marker_key_rows = jnp.dot(pooled, gathered[3], preferred_element_type=jnp.float32).astype(
        jnp.bfloat16
    )
    marker_value_rows = jnp.dot(pooled, gathered[4], preferred_element_type=jnp.float32).astype(
        jnp.bfloat16
    )
    raw_top, raw_sum, raw_weighted = raw_attention(
        query_matrix, key_matrix, value_matrix, begin_offset, length, score_scale
    )
    halved_rows = token_rows // 2
    first_q = query_matrix[:, :, :halved_rows]
    second_q = query_matrix[:, :, halved_rows:]
    empty_state = (
        jnp.full((KEY_VALUE_HEADS, query_group_count, halved_rows), negative_filler, jnp.float32),
        jnp.zeros((KEY_VALUE_HEADS, query_group_count, halved_rows), jnp.float32),
        jnp.zeros((KEY_VALUE_HEADS, query_group_count, halved_rows, HEAD_SIZE), jnp.float32),
    )
    segment_list = (
        lax.all_gather(marker_key_rows, "ctx", axis=0, tiled=True),
        lax.all_gather(marker_value_rows, "ctx", axis=0, tiled=True),
        lax.all_gather(live_slot.astype(jnp.bfloat16), "ctx", axis=0, tiled=True),
    )
    segment_keys = segment_list[0].reshape(-1, KEY_VALUE_HEADS, HEAD_SIZE)
    segment_values = segment_list[1].reshape(-1, KEY_VALUE_HEADS, HEAD_SIZE)
    first_state = beacon_update(
        empty_state,
        first_q,
        my_span,
        segment_keys,
        segment_values,
        segment_list[2],
        marker_slot_count,
        score_scale,
    )
    second_state = beacon_update(
        empty_state,
        second_q,
        my_span,
        segment_keys,
        segment_values,
        segment_list[2],
        marker_slot_count,
        score_scale,
    )
    first_state, second_state = (first_state, second_state)
    beacon_top = jnp.concatenate([first_state[0], second_state[0]], axis=2)
    beacon_sum = jnp.concatenate([first_state[1], second_state[1]], axis=2)
    beacon_weighted = jnp.concatenate([first_state[2], second_state[2]], axis=2)
    joint_top = jnp.maximum(raw_top, beacon_top)
    raw_factor = jnp.exp(raw_top - joint_top)
    beacon_factor = jnp.exp(beacon_top - joint_top)
    weight_sum = raw_sum * raw_factor + beacon_sum * beacon_factor
    weighted = raw_weighted * raw_factor[..., None] + beacon_weighted * beacon_factor[..., None]
    result = weighted / jnp.where(weight_sum > 0, weight_sum, 1.0)[..., None]
    result = result.transpose(2, 0, 1, 3).reshape(token_rows, QUERY_HEADS * HEAD_SIZE)
    valid = begin_offset + jnp.arange(token_rows, dtype=jnp.int32) < length
    result = jnp.where(valid[:, None], result, 0.0).astype(jnp.bfloat16)
    return result[None]


def solution(mesh):
    return jax.shard_map(
        on_device,
        mesh=mesh,
        in_specs=(
            P("dp", "ctx", None),
            P(),
            P(("dp", "ctx"), None),
            P(("dp", "ctx"), None),
            P(("dp", "ctx"), None),
            P(("dp", "ctx"), None),
            P(("dp", "ctx"), None),
            P("dp", "ctx"),
            P("dp"),
        ),
        out_specs=P("dp", "ctx", None),
        check_vma=False,
    )
```

profile of v0, /device:TPU:6, one launch (start us, length us, event | category | flops | bytes accessed | tf_op | source)
XLA Modules:
  0.0 1765.7 jit_solution(11728841158564989589)
XLA Ops:
  6.5 0.7 all-gather.23.cloned.1.call-update
  7.3 0.0 all-gather.25.cloned.1.call-start
  7.3 0.7 all-gather.25.cloned.1.call-update
  8.0 0.0 all-gather.19.cloned.1.call-start
  8.1 0.7 all-gather.19.cloned.1.call-update
  8.7 0.0 all-gather.21.cloned.1.call-start
  8.8 0.5 all-gather.21.cloned.1.call-update
  9.3 0.0 all-gather.13.cloned.1.call-start
  10.7 0.1 compare_and_fusion
  10.9 0.1 iota_divide_fusion
  11.0 0.2 convert_reduce_fusion
  11.2 1.9 fusion.27
  13.1 2.2 fusion.26
  15.4 295.9 %all-gather.23.cloned.1.call-done = bf16[128,28,256]{2,1,0:T(8,128)(2,1)} async-done(((bf16[1,28,256]{2,1,0:T(8,128)(2,1)}), bf16[128,28,256]{2,1,0:T(8,128)(2,1)}) %all-gather.23.cloned.1.call-update) | async-done | bytes 1835024 | tf_op jit(solution)/shard_map/all_gather | solution.py:133
  311.2 2.5 reshape.241
  313.7 1.1 convolution_convert_fusion.4
  314.7 0.0 all-gather.13.cloned.1.call-update
  314.8 0.0 all-gather.15.cloned.1.call-start
  314.8 299.8 %all-gather.25.cloned.1.call-done = bf16[128,28,256]{2,1,0:T(8,128)(2,1)} async-done(((bf16[1,28,256]{2,1,0:T(8,128)(2,1)}), bf16[128,28,256]{2,1,0:T(8,128)(2,1)}) %all-gather.25.cloned.1.call-update) | async-done | bytes 1835024 | tf_op jit(solution)/shard_map/all_gather | solution.py:134
  614.6 2.5 reshape.243
  617.0 1.1 convolution_convert_fusion.3
  618.1 0.0 all-gather.15.cloned.1.call-update
  618.1 0.0 all-gather.17.cloned.1.call-start
  618.2 0.7 all-gather.17.cloned.1.call-update
  618.9 0.6 dynamic-slice
  620.1 0.2 dynamic-update-slice
  620.3 84.4 %all-reduce = bf16[2048]{0:T(1024)(128)(2,1)S(1)} all-reduce(bf16[2048]{0:T(1024)(128)(2,1)S(1)} %dynamic-update-slice), channel_id=1, replica_groups=mesh['dp'=4,'ctx'=32] {'ctx'}, use_global_device_ids=true, to_apply=%add | all-reduce | flops 2048 | bytes 8192
  704.7 0.7 fusion.70
  706.0 0.1 fusion.44
  706.1 211.7 %all-gather.19.cloned.1.call-done = bf16[128,28,256]{2,1,0:T(8,128)(2,1)} async-done(((bf16[1,28,256]{2,1,0:T(8,128)(2,1)}), bf16[128,28,256]{2,1,0:T(8,128)(2,1)}) %all-gather.19.cloned.1.call-update) | async-done | bytes 1835024 | tf_op jit(solution)/shard_map/all_gather | solution.py:131
  917.8 3.8 reshape.237
  921.6 298.9 %all-gather.21.cloned.1.call-done = bf16[128,28,256]{2,1,0:T(8,128)(2,1)} async-done(((bf16[1,28,256]{2,1,0:T(8,128)(2,1)}), bf16[128,28,256]{2,1,0:T(8,128)(2,1)}) %all-gather.21.cloned.1.call-update) | async-done | bytes 1835024 | tf_op jit(solution)/shard_map/all_gather | solution.py:132
  1220.5 3.8 reshape.239
  1224.3 2.7 convolution_convert_fusion.2
  1226.9 1.1 convolution_convert_fusion.1
  1228.0 62.0 %all-gather.13.cloned.1.call-done = bf16[2048,256]{1,0:T(8,128)(2,1)} async-done(((bf16[64,256]{1,0:T(8,128)(2,1)}), bf16[2048,256]{1,0:T(8,128)(2,1)}) %all-gather.13.cloned.1.call-update) | async-done | bytes 1048592 | tf_op jit(solution)/shard_map/all_gather | solution.py:170
  1290.0 1.3 reshape.215
  1291.3 65.0 %all-gather.15.cloned.1.call-done = bf16[2048,256]{1,0:T(8,128)(2,1)} async-done(((bf16[64,256]{1,0:T(8,128)(2,1)}), bf16[2048,256]{1,0:T(8,128)(2,1)}) %all-gather.15.cloned.1.call-update) | async-done | bytes 1048592 | tf_op jit(solution)/shard_map/all_gather | solution.py:171
  1356.4 2.1 reshape.216
  1358.5 320.7 %all-gather.17.cloned.1.call-done = bf16[128,28,1792]{2,1,0:T(8,128)(2,1)} async-done(((bf16[1,28,1792]{2,1,0:T(8,128)(2,1)}), bf16[128,28,1792]{2,1,0:T(8,128)(2,1)}) %all-gather.17.cloned.1.call-update) | async-done | bytes 12845072 | tf_op jit(solution)/shard_map/all_gather | solution.py:130
  1679.2 17.6 reshape.235
  1696.9 8.7 convolution_convert_fusion
  1705.6 0.5 copy.46
  1706.2 22.3 %conditional.3 = (f32[2,7,128]{2,1,0:T(8,128)}, f32[2,7,128]{2,1,0:T(8,128)S(1)}, f32[2,7,128,128]{2,3,1,0:T(8,128)S(1)}) conditional(s32[]{:T(128)} %convert_element_type.65, () %tuple.39, (pred[2048]{0:T(1024)(128)(4,1)S(1)}, bf16[2,7,256,128]{2,3,1,0:T(8,128)(2,1)S(1)}, bf16[2048,2,128]{2,1,0:T(2,128)(2,1)S(1)}, ...), branch_computations={%region_8.9_spmd, %region_9.12_spmd} | conditional | flops 1926756608 | bytes 53592116 | solution.py:103
  1706.4 0.6 copy.53
  1707.0 6.4 fusion.13
  1713.4 0.6 broadcast_maximum_fusion.1
  1714.0 7.0 fusion.16
  1721.0 7.4 fusion.14
  1728.5 0.0 copy-start.4
  1728.5 0.9 copy-done.4
  1729.4 22.1 %conditional.2 = (f32[2,7,128]{2,1,0:T(8,128)}, f32[2,7,128]{2,1,0:T(8,128)S(1)}, f32[2,7,128,128]{2,3,1,0:T(8,128)S(1)}) conditional(s32[]{:T(128)} %convert_element_type.65, () %tuple.37, (pred[2048]{0:T(1024)(128)(4,1)S(1)}, bf16[2,7,256,128]{2,3,1,0:T(8,128)(2,1)S(1)}, bf16[2048,2,128]{2,1,0:T(2,128)(2,1)S(1)}, ...), branch_computations={%region_4.5_spmd, %region_5.8_spmd} | conditional | flops 1926756608 | bytes 53592116 | solution.py:103
  1729.4 0.6 copy.50
  1730.0 6.4 fusion
  1736.5 0.6 broadcast_maximum_fusion
  1737.0 7.0 fusion.3
  1744.1 7.4 fusion.1
  1751.5 0.7 constant_dynamic-update-slice_fusion.1
  1752.2 0.7 constant_dynamic-update-slice_fusion
  1752.9 0.7 fusion.30
  1753.7 0.9 fusion.31
  1754.6 2.4 fusion.36
  1757.1 0.6 copy.58
  1757.7 1.1 select_convert_fusion
  (24 shorter events, 0.1 us)
Async XLA Ops:
  6.5 304.7 %all-gather.23.cloned.1.call-start = ((), (), s32[]{:S(2)}) async-start(), calls=%async_computation.5 | async-start | bytes 2113536 | tf_op jit(solution)/shard_map/all_gather | solution.py:133
  7.3 607.3 %all-gather.25.cloned.1.call-start = ((), (), s32[]{:S(2)}) async-start(), calls=%async_computation.6 | async-start | bytes 2113536 | tf_op jit(solution)/shard_map/all_gather | solution.py:134
  8.0 909.8 %all-gather.19.cloned.1.call-start = ((), (), s32[]{:S(2)}) async-start(), calls=%async_computation.3 | async-start | bytes 2113536 | tf_op jit(solution)/shard_map/all_gather | solution.py:131
  8.7 1211.8 %all-gather.21.cloned.1.call-start = ((), (), s32[]{:S(2)}) async-start(), calls=%async_computation.4 | async-start | bytes 2113536 | tf_op jit(solution)/shard_map/all_gather | solution.py:132
  9.3 1280.7 %all-gather.13.cloned.1.call-start = ((), (), s32[]{:S(2)}) async-start(), calls=%async_computation | async-start | bytes 1081344 | tf_op jit(solution)/shard_map/all_gather | solution.py:170
  314.7 304.2 %copy-start.8 = (u32[128]{0:T(128)S(1)}, u32[128]{0:T(128)}, u32[]{:S(2)}) copy-start(u32[128]{0:T(128)} %constant.134) | copy-start | bytes 1540
  314.8 1041.6 %all-gather.15.cloned.1.call-start = ((), (), s32[]{:S(2)}) async-start(), calls=%async_computation.1 | async-start | bytes 1081344 | tf_op jit(solution)/shard_map/all_gather | solution.py:171
  618.1 1061.1 %all-gather.17.cloned.1.call-start = ((), (), s32[]{:S(2)}) async-start(), calls=%async_computation.2 | async-start | bytes 14794752 | tf_op jit(solution)/shard_map/all_gather | solution.py:130
  706.1 518.1 %copy-start = (bf16[1,256,3584]{2,1,0:T(8,128)(2,1)S(1)}, bf16[1,256,3584]{2,1,0:T(8,128)(2,1)}, u32[]{:S(2)}) copy-start(bf16[1,256,3584]{2,1,0:T(8,128)(2,1)} %param.13) | copy-start | bytes 5505028
  706.1 518.1 %copy-start.7 = (f32[3584]{0:T(1024)S(1)}, f32[3584]{0:T(1024)}, u32[]{:S(2)}) copy-start(f32[3584]{0:T(1024)} %param.14) | copy-start | bytes 43012
  1224.3 2.7 copy-start.1
  1707.0 7.0 copy-start.2
  1728.5 0.9 copy-start.4
  1730.0 7.0 copy-start.3
  1751.5 3.1 copy-start.6
  1752.9 1.7 copy-start.5
Sparse Core Ops, SparseCore 0:
  9.0 302.1 all-gather.22
  312.9 301.6 all-gather.24
  616.3 301.5 all-gather.18
  919.4 301.0 all-gather.20
  1223.4 66.4 all-gather.12
  1292.9 63.3 all-gather.14
  1358.1 321.1 all-gather.16
where the time goes:
time: 1770 us
  waiting for transfers between devices  1560 us (88%)
  blocking collectives  84.4 us (5%)
  matrix products  46.9 us (3%)
  local copies, waits for them, and re-layouts  39.1 us (2%)
  other arithmetic  21.3 us (1%)
    all_gather x1, waiting for transfers between devices, on_device(): lax.all_gather(w_query, ('dp', 'ctx'), axis=0, tiled=True)  321 us
    all_gather x1, waiting for transfers between devices, on_device(): lax.all_gather(marker_value_weight, ('dp', 'ctx'), axis=0, tiled=True)  300 us
    all_gather x1, waiting for transfers between devices, on_device(): lax.all_gather(value_weight, ('dp', 'ctx'), axis=0, tiled=True)  299 us
    all_gather x1, waiting for transfers between devices, on_device(): lax.all_gather(marker_key_weight, ('dp', 'ctx'), axis=0, tiled=True)  296 us
    all_gather x1, waiting for transfers between devices, on_device(): lax.all_gather(w_key, ('dp', 'ctx'), axis=0, tiled=True)  212 us
    unnamed x1, blocking collectives  84.4 us
    all_gather x1, waiting for transfers between devices, on_device(): lax.all_gather(marker_value_rows, 'ctx', axis=0, tiled=True)  65 us
    all_gather x1, waiting for transfers between devices, on_device(): lax.all_gather(marker_key_rows, 'ctx', axis=0, tiled=True)  62 us
  transfers between devices with their start and end apart: 7, of which 7 were waited for; matrix products, arithmetic and copies ran while one was open for 2% of the time, Pallas kernels for 0%

commit v1 on v0

v1 whole, which is shorter than its diff:
```python
import functools
import math

import jax
import jax.numpy as jnp
import numpy as np
from jax import lax
from jax.experimental import pallas as pl
from jax.experimental.pallas import tpu as pltpu
from jax.sharding import PartitionSpec as P

HEADS = 7
D = 128
WIDTH = 3584
ROWS = 28
TOK = 256
SLOTS = 64
SPANS = 32
EPS = 1e-6
FILL = -1e30
AXES = ("dp", "ctx")
SCALE = 1.0 / math.sqrt(D)


def device_id(x, y, z, c):
    return ((y % 2) * 2 + c) * 32 + (x * 4 + z) * 2 + y // 2


def make_perm(f):
    pairs = []
    for x in range(4):
        for y in range(4):
            for z in range(4):
                for c in range(2):
                    tx, ty, tz, tc = f(x, y, z, c)
                    pairs.append(
                        (device_id(x, y, z, c), device_id(tx % 4, ty % 4, tz % 4, tc % 2))
                    )
    return pairs


SWAP = make_perm(lambda x, y, z, c: (x, y, z, 1 - c))
RING = {
    "x": make_perm(lambda x, y, z, c: (x + 1 - 2 * c, y, z, c)),
    "y": make_perm(lambda x, y, z, c: (x, y + 1 - 2 * c, z, c)),
    "z": make_perm(lambda x, y, z, c: (x, y, z + 1 - 2 * c, c)),
}
HOP = {
    ("x", 1): make_perm(lambda x, y, z, c: (x + 1, y, z, c)),
    ("x", 2): make_perm(lambda x, y, z, c: (x + 2, y, z, c)),
    ("x", 3): make_perm(lambda x, y, z, c: (x + 3, y, z, c)),
    ("z", 1): make_perm(lambda x, y, z, c: (x, y, z + 1, c)),
    ("z", 2): make_perm(lambda x, y, z, c: (x, y, z + 2, c)),
    ("z", 3): make_perm(lambda x, y, z, c: (x, y, z + 3, c)),
    ("y", 2): make_perm(lambda x, y, z, c: (x, y + 2, z, c)),
}


def send(value, pairs):
    return lax.ppermute(value, AXES, pairs)


def feature_runs():
    order = []
    for x in range(4):
        for z in range(4):
            for y in range(4):
                for c in range(2):
                    order.append(device_id(x, y, z, c) * ROWS)
    source = np.concatenate([np.arange(s, s + ROWS) for s in order])
    tiles = []
    for tile in range(WIDTH // 128):
        part = source[tile * 128 : (tile + 1) * 128]
        runs = []
        lane = 0
        while lane < 128:
            end = lane + 1
            while end < 128 and part[end] == part[end - 1] + 1 and part[end] % 128 != 0:
                end += 1
            runs.append((lane, end, int(part[lane])))
            lane = end
        tiles.append(runs)
    return tiles


def norm_body(tokens_ref, gain_ref, out_ref, plain_ref):
    rows = 64

    @pl.loop(0, TOK // rows)
    def _(step):
        here = pl.ds(pl.multiple_of(step * rows, rows), rows)
        values = tokens_ref[here, :].astype(jnp.float32)
        factor = lax.rsqrt(jnp.mean(values * values, axis=-1, keepdims=True) + EPS)
        plain_ref[...] = values * factor * gain_ref[...]
        lane = lax.broadcasted_iota(jnp.int32, (rows, 128), 1)
        for tile, runs in enumerate(feature_runs()):
            joined = jnp.zeros((rows, 128), jnp.float32)
            for first, end, feature in runs:
                block, offset = divmod(feature, 128)
                piece = plain_ref[:, block * 128 : (block + 1) * 128]
                shift = (first - offset) % 128
                if shift:
                    piece = pltpu.roll(piece, shift, 1)
                joined = jnp.where((lane >= first) & (lane < end), piece, joined)
            out_ref[here, tile * 128 : (tile + 1) * 128] = joined.astype(jnp.bfloat16)


def norm_rows(tokens, gain):
    return pl.pallas_call(
        norm_body,
        out_shape=jax.ShapeDtypeStruct((TOK, WIDTH), jnp.bfloat16),
        in_specs=[pl.BlockSpec(memory_space=pltpu.VMEM)] * 2,
        out_specs=pl.BlockSpec(memory_space=pltpu.VMEM),
        scratch_shapes=[pltpu.VMEM((64, WIDTH), jnp.float32)],
        compiler_params=pltpu.CompilerParams(vmem_limit_bytes=24 * 1024 * 1024),
    )(tokens, gain.reshape(1, WIDTH))


def ring_gather(block, axis):
    got = [block]
    for _ in range(3):
        got.append(send(got[-1], RING[axis]))
    return got


def place(pieces, slots, axis, count=4):
    shape = list(pieces[0].shape)
    shape.insert(axis, count)
    joined = jnp.zeros(shape, pieces[0].dtype)
    for piece, slot in zip(pieces, slots):
        joined = lax.dynamic_update_slice_in_dim(joined, jnp.expand_dims(piece, axis), slot, axis)
    return joined


def on_device(tokens, gain, w_query, w_key, w_value, w_mark_key, w_mark_value, level, hist_len):
    dp = lax.axis_index("dp")
    span = lax.axis_index("ctx")
    core = dp % 2
    pos = {"x": span // 8, "z": (span // 2) % 4, "y": (span % 2) * 2 + dp // 2}
    sign = 1 - 2 * core
    slots = {a: [(p - sign * i) % 4 for i in range(4)] for a, p in pos.items()}

    def half(which):
        def cut(w, size):
            return lax.dynamic_slice_in_dim(w, which * size, size, 1)

        return jnp.concatenate(
            [
                cut(w_mark_key, D),
                cut(w_mark_value, D),
                cut(w_key, D),
                cut(w_value, D),
                cut(w_query, HEADS * D),
            ],
            axis=1,
        )

    mine = half(core)
    other = send(half(1 - core), SWAP)
    rows = jnp.where(
        core == 0, jnp.concatenate([mine, other], 0), jnp.concatenate([other, mine], 0)
    )

    normed = norm_rows(tokens[0], gain)
    begin = span * TOK
    length = hist_len[0]
    stride = jnp.left_shift(jnp.int32(4), level[0, 0])
    live = TOK // stride
    slot_ids = lax.broadcasted_iota(jnp.int32, (SLOTS, TOK), 0)
    pos_ids = lax.broadcasted_iota(jnp.int32, (SLOTS, TOK), 1)
    inside = (
        (jnp.right_shift(pos_ids, level[0, 0] + 2) == slot_ids)
        & (slot_ids < live)
        & (begin + pos_ids < length)
    )
    window = jnp.dot(inside.astype(jnp.bfloat16), normed, preferred_element_type=jnp.float32)
    size = jnp.sum(inside.astype(jnp.float32), axis=1)
    pooled = (window / jnp.maximum(size, 1.0)[:, None]).astype(jnp.bfloat16)
    valid = jnp.clip(length - begin, 0, TOK)
    count = jnp.minimum(live, (valid + stride - 1) // stride)
    facts = jnp.concatenate(
        [
            jnp.full((8, WIDTH), count.astype(jnp.bfloat16)),
            jnp.full((8, WIDTH), valid.astype(jnp.bfloat16)),
        ],
        0,
    )
    packed = jnp.concatenate([normed, pooled, facts], 0)
    mate = send(packed, SWAP)
    both = jnp.stack([normed, mate[:TOK]])
    both_pooled = jnp.stack([pooled, mate[TOK : TOK + SLOTS]])
    mate_count = mate[TOK + SLOTS, 0].astype(jnp.int32)
    mate_valid = mate[TOK + SLOTS + 8, 0].astype(jnp.int32)
    counts = jnp.stack([count, mate_count])
    valids = jnp.stack([valid, mate_valid])

    def part(block, order):
        first, second, last = order
        one = place(ring_gather(block, first), slots[first], 0)
        two = place(ring_gather(one, second), slots[second], 0)
        three = place(ring_gather(two, last), slots[last], 0)
        where = {last: 0, second: 1, first: 2}
        full = three.transpose(where["x"], where["z"], where["y"], 3, 4)
        return full.reshape(WIDTH, block.shape[1])

    cols = (256, 896, 1408)
    w_mark = part(rows[:, : cols[0]], ("x", "y", "z"))
    w_a = part(rows[:, cols[0] : cols[1]], ("y", "z", "x"))
    w_b = part(rows[:, cols[1] :], ("z", "x", "y"))

    def project(x, w):
        out = jnp.dot(x.reshape(-1, WIDTH), w, preferred_element_type=jnp.float32)
        return out.astype(jnp.bfloat16).reshape(x.shape[0], x.shape[1], -1)

    beacon = project(both_pooled, w_mark)
    flags = jnp.broadcast_to(counts.astype(jnp.bfloat16)[:, None, None], (2, 8, 256))
    block = jnp.concatenate([beacon, flags], 1)

    pairs = [block, send(block, HOP["y", 2])]
    pairs = jnp.stack(pairs)
    across = jnp.stack([pairs] + [send(pairs, HOP["x", i]) for i in (1, 2, 3)])
    every = jnp.stack([across] + [send(across, HOP["z", i]) for i in (1, 2, 3)])
    back = jnp.arange(4)
    z_of = (pos["z"] - back) % 4
    x_of = (pos["x"] - back) % 4
    h_of = (span % 2) ^ jnp.arange(2)
    owner = (x_of[None, :, None] * 4 + z_of[:, None, None]) * 2 + h_of[None, None, :]
    owner = owner.reshape(SPANS)
    every = every.reshape(SPANS, 2, SLOTS + 8, 256)
    live_counts = every[:, :, SLOTS, 0].astype(jnp.int32)
    beacon_keys = every[:, :, :SLOTS, :D].transpose(1, 0, 2, 3).reshape(2, SPANS * SLOTS, D)
    beacon_values = every[:, :, :SLOTS, D:].transpose(1, 0, 2, 3).reshape(2, SPANS * SLOTS, D)
    seen = (jnp.arange(SLOTS)[None, None, :] < live_counts.T[:, :, None]) & (owner < span)[
        None, :, None
    ]
    seen = seen.reshape(2, SPANS * SLOTS)

    part_a = project(both, w_a)
    part_b = project(both, w_b)
    keys = part_a[..., :D]
    values = part_a[..., D : 2 * D]
    queries = jnp.concatenate([part_a[..., 2 * D :], part_b], -1).reshape(2, TOK, HEADS, D)

    at = jnp.arange(TOK)
    raw_seen = (at[None, None, :] <= at[None, :, None]) & (
        at[None, None, :] < valids[:, None, None]
    )
    raw = jnp.einsum("htgd,hsd->hgts", queries, keys, preferred_element_type=jnp.float32) * SCALE
    raw = jnp.where(raw_seen[:, None], raw, FILL)
    far = (
        jnp.einsum("htgd,hsd->hgts", queries, beacon_keys, preferred_element_type=jnp.float32)
        * SCALE
    )
    far = jnp.where(seen[:, None, None, :], far, FILL)
    top = jnp.maximum(jnp.max(raw, -1), jnp.max(far, -1))[..., None]
    raw_w = jnp.where(raw_seen[:, None], jnp.exp(raw - top), 0.0)
    far_w = jnp.where(seen[:, None, None, :], jnp.exp(far - top), 0.0)
    total = jnp.sum(raw_w, -1) + jnp.sum(far_w, -1)
    summed = jnp.einsum(
        "hgts,hsd->hgtd", raw_w.astype(jnp.bfloat16), values, preferred_element_type=jnp.float32
    ) + jnp.einsum(
        "hgts,hsd->hgtd",
        far_w.astype(jnp.bfloat16),
        beacon_values,
        preferred_element_type=jnp.float32,
    )
    result = summed / jnp.where(total > 0, total, 1.0)[..., None]
    result = jnp.where((at < valids[:, None])[:, None, :, None], result, 0.0)
    result = result.transpose(0, 2, 1, 3).reshape(2, TOK, HEADS * D).astype(jnp.bfloat16)
    back_home = send(result[1], SWAP)
    full = jnp.where(
        core == 0,
        jnp.concatenate([result[0], back_home], -1),
        jnp.concatenate([back_home, result[0]], -1),
    )
    return full[None]


def solution(mesh):
    return jax.shard_map(
        on_device,
        mesh=mesh,
        in_specs=(
            P("dp", "ctx", None),
            P(),
            P(("dp", "ctx"), None),
            P(("dp", "ctx"), None),
            P(("dp", "ctx"), None),
            P(("dp", "ctx"), None),
            P(("dp", "ctx"), None),
            P("dp", "ctx"),
            P("dp"),
        ),
        out_specs=P("dp", "ctx", None),
        check_vma=False,
    )
```

time: 1770 us -> 210 us (0.12)
  the two profiles are of different devices: /device:TPU:6 before, /device:TPU:1 now
where the time goes in v1:
time: 210 us; the launch traced here: 209 us
  starting transfers between devices  70.1 us (33%)
  waiting for transfers between devices  44.5 us (21%)
  matrix products  40.2 us (19%)
  local copies, waits for them, and re-layouts  24.5 us (12%)
  other arithmetic  22.2 us (11%)
  Pallas kernels  3.91 us (2%)
  between operations  3.44 us (2%)
    ppermute x37, starting transfers between devices, send(): return lax.ppermute(value, AXES, pairs)  70.1 us
    ppermute x37, waiting for transfers between devices, send(): return lax.ppermute(value, AXES, pairs)  44.5 us
    reduce_sum x2, other arithmetic, on_device(): total = jnp.sum(raw_w, -1) + jnp.sum(far_w, -1)  15 us
    dot_general x1, matrix products, on_device(): jnp.einsum('hgts,hsd->hgtd', far_w.astype(jnp.bfloat16), beacon_values, p...  14.6 us
    dot_general x1, matrix products, on_device(): jnp.einsum('htgd,hsd->hgts', queries, beacon_keys, preferred_element_type...  11.2 us
    dot_general x3, matrix products, project(): out = jnp.dot(x.reshape(-1, WIDTH), w, preferred_element_type=jnp.float32)  10.9 us
    dynamic_update_slice x36, local copies, waits for them, and re-layouts, place(): lax.dynamic_update_slice_in_dim(joined, jnp.expand_dims(piece, axis), slo...  9.46 us
    unnamed x17, local copies, waits for them, and re-layouts  4.5 us
  transfers between devices with their start and end apart: 37, of which 14 were waited for; matrix products, arithmetic and copies ran while one was open for 14% of the time, Pallas kernels for 2%

profile of v1, /device:TPU:1, one launch (start us, length us, event | category | flops | bytes accessed | tf_op | source)
XLA Modules:
  0.0 208.9 jit_solution(12010798558319458241)
XLA Ops:
  0.7 0.7 constant_dynamic-update-slice_fusion.2
  1.4 0.7 constant_dynamic-update-slice_fusion.1
  2.9 0.9 dynamic-slice_dynamic-update-slice_fusion.1
  3.8 1.5 collective-permute-start.1
  6.9 0.7 reshape.306.gain_ref
  7.8 1.5 copy-done
  9.3 3.9 %shard_map.91 = bf16[256,3584]{1,0:T(8,128)(2,1)S(1)} custom-call(bf16[256,3584]{1,0:T(8,128)(2,1)S(1)} %bitcast.213, f32[1,3584]{1,0:T(1,128)S(1)} %reshape.306.gain_ref), custom_call_target="tpu_custom_call" | custom-call | tf_op jit(solution)/shard_map/pallas_call | solution.py:109
  13.7 2.5 %maximum_maximum_fusion = bf16[336,3584]{1,0:T(8,128)(2,1)} fusion(bf16[64,3584]{1,0:T(8,128)(2,1)S(1)} %fusion.8, bf16[256,3584]{1,0:T(8,128)(2,1)S(1)} %shard_map.91, bf16[336]{0:T(512)(128)(2,1)S(1)} %pad.33.clone, bf16[336]{0:T(512)(128)(2,1)S(1)} %pad.32.clone), kind=kLoop, calls=%fused_computation.18 | loop fusion | flops 9633792 | bytes 4703552 | tf_op jit(solution)/shard_map/concatenate | solution.py:188
  16.9 2.6 %collective-permute-start.20 = (bf16[56,256]{1,0:T(8,128)(2,1)S(1)}, bf16[56,256]{1,0:T(8,128)(2,1)S(1)}, u32[]{:S(2)}, u32[]{:S(2)}) collective-permute-start(bf16[56,256]{1,0:T(8,128)(2,1)S(1)} %slice.73), channel_id=1, source_target_pairs={{0,8},{32,56},{2,10},{34,58},{4,12},{36,60},{6,14},{38,62},{64,72}... | collective-permute-start | bytes 86024 | tf_op jit(solution)/shard_map/ppermute | solution.py:60
  19.5 2.7 %collective-permute-start.2 = (bf16[56,640]{1,0:T(8,128)(2,1)S(1)}, bf16[56,640]{1,0:T(8,128)(2,1)S(1)}, u32[]{:S(2)}, u32[]{:S(2)}) collective-permute-start(bf16[56,640]{1,0:T(8,128)(2,1)S(1)} %slice.68), channel_id=1, source_target_pairs={{0,64},{32,97},{2,66},{34,99},{4,68},{36,101},{6,70},{38,103},{64,... | collective-permute-start | bytes 215048 | tf_op jit(solution)/shard_map/ppermute | solution.py:60
  22.3 3.8 %collective-permute-start.11 = (bf16[56,512]{1,0:T(8,128)(2,1)S(1)}, bf16[56,512]{1,0:T(8,128)(2,1)S(1)}, u32[]{:S(2)}, u32[]{:S(2)}) collective-permute-start(bf16[56,512]{1,0:T(8,128)(2,1)S(1)} %slice.71), channel_id=1, source_target_pairs={{0,2},{32,38},{2,4},{34,32},{4,6},{36,34},{6,0},{38,36},{64,66},{9... | collective-permute-start | bytes 172040 | tf_op jit(solution)/shard_map/ppermute | solution.py:60
  26.8 2.2 %collective-permute-done.21 = bf16[56,256]{1,0:T(8,128)(2,1)S(1)} collective-permute-done((bf16[56,256]{1,0:T(8,128)(2,1)S(1)}, bf16[56,256]{1,0:T(8,128)(2,1)S(1)}, u32[]{:S(2)}, u32[]{:S(2)}) %collective-permute-start.21) | collective-permute-done | bytes 28704 | tf_op jit(solution)/shard_map/ppermute | solution.py:60
  29.0 1.8 collective-permute-start.22
  31.2 2.8 %collective-permute-start.3 = (bf16[56,640]{1,0:T(8,128)(2,1)S(1)}, bf16[56,640]{1,0:T(8,128)(2,1)S(1)}, u32[]{:S(2)}, u32[]{:S(2)}) collective-permute-start(bf16[56,640]{1,0:T(8,128)(2,1)S(1)} %collective-permute-done.2), channel_id=1, source_target_pairs={{0,64},{32,97},{2,66},{34,99},{4,68},{36,101},{6,70},{38,103},{64,... | collective-permute-start | bytes 215048 | tf_op jit(solution)/shard_map/ppermute | solution.py:60
  34.6 0.8 collective-permute-start.13
  35.4 3.0 %collective-permute-start.4 = (bf16[56,640]{1,0:T(8,128)(2,1)S(1)}, bf16[56,640]{1,0:T(8,128)(2,1)S(1)}, u32[]{:S(2)}, u32[]{:S(2)}) collective-permute-start(bf16[56,640]{1,0:T(8,128)(2,1)S(1)} %collective-permute-done.3), channel_id=1, source_target_pairs={{0,64},{32,97},{2,66},{34,99},{4,68},{36,101},{6,70},{38,103},{64,... | collective-permute-start | bytes 215048 | tf_op jit(solution)/shard_map/ppermute | solution.py:60
  38.4 0.8 collective-permute-start.14
  39.9 3.1 %collective-permute-start.5 = (bf16[4,56,640]{2,1,0:T(8,128)(2,1)S(1)}, bf16[4,56,640]{2,1,0:T(8,128)(2,1)S(1)}, u32[]{:S(2)}, u32[]{:S(2)}) collective-permute-start(bf16[4,56,640]{2,1,0:T(8,128)(2,1)S(1)} %bitcast_dynamic-update-slice_fusion.24), channel_id=1, source_target_pairs={{0,2},{32,38},{2,4},{34,32},{4,6},{36,34},{6,0},{38,36},{64,66},{9... | collective-permute-start | bytes 860168 | tf_op jit(solution)/shard_map/ppermute | solution.py:60
  43.2 1.5 collective-permute-start.25
  45.3 1.9 collective-permute-done.25
  47.2 2.9 %collective-permute-start.26 = (bf16[4,4,56,256]{3,2,0,1:T(8,128)(2,1)S(1)}, bf16[4,4,56,256]{3,2,0,1:T(8,128)(2,1)S(1)}, u32[]{:S(2)}, u32[]{:S(2)}) collective-permute-start(bf16[4,4,56,256]{3,2,0,1:T(8,128)(2,1)S(1)} %bitcast_dynamic-update-slice_fusion.23), channel_id=1, source_target_pairs={{0,2},{32,38},{2,4},{34,32},{4,6},{36,34},{6,0},{38,36},{64,66},{9... | collective-permute-start | bytes 1376264 | tf_op jit(solution)/shard_map/ppermute | solution.py:60
  50.5 1.2 collective-permute-start.16
  51.7 6.9 %collective-permute-done.6 = bf16[4,56,640]{2,1,0:T(8,128)(2,1)S(1)} collective-permute-done((bf16[4,56,640]{2,1,0:T(8,128)(2,1)S(1)}, bf16[4,56,640]{2,1,0:T(8,128)(2,1)S(1)}, u32[]{:S(2)}, u32[]{:S(2)}) %collective-permute-start.6) | collective-permute-done | bytes 286752 | tf_op jit(solution)/shard_map/ppermute | solution.py:60
  58.6 3.4 %collective-permute-start.7 = (bf16[4,56,640]{2,1,0:T(8,128)(2,1)S(1)}, bf16[4,56,640]{2,1,0:T(8,128)(2,1)S(1)}, u32[]{:S(2)}, u32[]{:S(2)}) collective-permute-start(bf16[4,56,640]{2,1,0:T(8,128)(2,1)S(1)} %collective-permute-done.6), channel_id=1, source_target_pairs={{0,2},{32,38},{2,4},{34,32},{4,6},{36,34},{6,0},{38,36},{64,66},{9... | collective-permute-start | bytes 860168 | tf_op jit(solution)/shard_map/ppermute | solution.py:60
  62.1 2.8 %collective-permute-start.17 = (bf16[4,4,56,512]{3,2,1,0:T(8,128)(2,1)S(1)}, bf16[4,4,56,512]{3,2,1,0:T(8,128)(2,1)S(1)}, u32[]{:S(2)}, u32[]{:S(2)}) collective-permute-start(bf16[4,4,56,512]{3,2,1,0:T(8,128)(2,1)S(1)} %bitcast_dynamic-update-slice_fusion.16), channel_id=1, source_target_pairs={{0,64},{32,97},{2,66},{34,99},{4,68},{36,101},{6,70},{38,103},{64,... | collective-permute-start | bytes 2752520 | tf_op jit(solution)/shard_map/ppermute | solution.py:60
  66.4 6.7 %collective-permute-done.27 = bf16[4,4,56,256]{3,2,0,1:T(8,128)(2,1)S(1)} collective-permute-done((bf16[4,4,56,256]{3,2,0,1:T(8,128)(2,1)S(1)}, bf16[4,4,56,256]{3,2,0,1:T(8,128)(2,1)S(1)}, u32[]{:S(2)}, u32[]{:S(2)}) %collective-permute-start.27) | collective-permute-done | bytes 458784 | tf_op jit(solution)/shard_map/ppermute | solution.py:60
  73.2 1.2 collective-permute-start.28
  74.4 0.9 collective-permute-done.17
  75.3 3.5 %collective-permute-start.18 = (bf16[4,4,56,512]{3,2,1,0:T(8,128)(2,1)S(1)}, bf16[4,4,56,512]{3,2,1,0:T(8,128)(2,1)}, u32[]{:S(2)}, u32[]{:S(2)}) collective-permute-start(bf16[4,4,56,512]{3,2,1,0:T(8,128)(2,1)S(1)} %collective-permute-done.17), channel_id=1, source_target_pairs={{0,64},{32,97},{2,66},{34,99},{4,68},{36,101},{6,70},{38,103},{64,... | collective-permute-start | bytes 2752520 | tf_op jit(solution)/shard_map/ppermute | solution.py:60
  78.9 2.0 collective-permute-done.28
  80.9 1.0 collective-permute-start.9
  81.9 1.5 bitcast_dynamic-update-slice_fusion.2
  83.5 1.7 fusion.42
  85.8 1.1 slice_bitcast_fusion.3
  87.6 1.0 collective-permute-start.29
  88.5 1.6 slice_bitcast_fusion
  90.2 3.0 %collective-permute-done.29 = bf16[2,72,256]{2,1,0:T(8,128)(2,1)S(1)} collective-permute-done((bf16[2,72,256]{2,1,0:T(8,128)(2,1)S(1)}, bf16[2,72,256]{2,1,0:T(8,128)(2,1)S(1)}, u32[]{:S(2)}, u32[]{:S(2)}) %collective-permute-start.29) | collective-permute-done | bytes 73760 | tf_op jit(solution)/shard_map/ppermute | solution.py:60
  93.5 1.6 collective-permute-start.31
  95.1 2.0 collective-permute-start.32
  97.1 2.2 %pad_maximum_fusion = bf16[2,256,3584]{2,1,0:T(8,128)(2,1)} fusion(bf16[1,256,3584]{2,1,0:T(8,128)(2,1)S(1)} %slice_bitcast_fusion, bf16[1,256,3584]{2,1,0:T(8,128)(2,1)S(1)} %bitcast.212), kind=kLoop, calls=%fused_computation.12 | loop fusion | flops 1835008 | bytes 7340032 | tf_op jit(solution)/shard_map/stack | solution.py:190
  100.0 1.7 collective-permute-done.30
  102.3 1.4 collective-permute-start.33
  103.8 2.7 %collective-permute-start.34 = (bf16[4,2,2,72,256]{4,3,2,1,0:T(8,128)(2,1)S(1)}, bf16[4,2,2,72,256]{4,3,2,1,0:T(8,128)(2,1)S(1)}, u32[]{:S(2)}, u32[]{:S(2)}) collective-permute-start(bf16[4,2,2,72,256]{4,3,2,1,0:T(8,128)(2,1)S(1)} %get-tuple-element.12), channel_id=1, source_target_pairs={{0,4},{32,36},{2,6},{34,38},{4,0},{36,32},{6,2},{38,34},{64,68},{9... | collective-permute-start | bytes 1769480 | tf_op jit(solution)/shard_map/ppermute | solution.py:60
  106.7 2.0 collective-permute-start.19
  108.7 1.3 bitcast_dynamic-update-slice_fusion.4
  110.0 2.8 %collective-permute-done.33 = bf16[4,2,2,72,256]{4,3,2,1,0:T(8,128)(2,1)S(1)} collective-permute-done((bf16[4,2,2,72,256]{4,3,2,1,0:T(8,128)(2,1)S(1)}, bf16[4,2,2,72,256]{4,3,2,1,0:T(8,128)(2,1)S(1)}, u32[]{:S(2)}, u32[]{:S(2)}) %collective-permute-start.33) | collective-permute-done | bytes 589856 | tf_op jit(solution)/shard_map/ppermute | solution.py:60
  112.9 10.3 %collective-permute-done.34 = bf16[4,2,2,72,256]{4,3,2,1,0:T(8,128)(2,1)S(1)} collective-permute-done((bf16[4,2,2,72,256]{4,3,2,1,0:T(8,128)(2,1)S(1)}, bf16[4,2,2,72,256]{4,3,2,1,0:T(8,128)(2,1)S(1)}, u32[]{:S(2)}, u32[]{:S(2)}) %collective-permute-start.34) | collective-permute-done | bytes 589856 | tf_op jit(solution)/shard_map/ppermute | solution.py:60
  124.3 1.1 copy.82
  125.4 4.0 %collective-permute-start.10 = (bf16[4,4,56,640]{3,2,1,0:T(8,128)(2,1)}, bf16[4,4,56,640]{3,2,1,0:T(8,128)(2,1)S(1)}, u32[]{:S(2)}, u32[]{:S(2)}) collective-permute-start(bf16[4,4,56,640]{3,2,1,0:T(8,128)(2,1)} %collective-permute-done.9), channel_id=1, source_target_pairs={{0,8},{32,56},{2,10},{34,58},{4,12},{36,60},{6,14},{38,62},{64,72}... | collective-permute-start | bytes 3440648 | tf_op jit(solution)/shard_map/ppermute | solution.py:60
  129.4 2.4 %bitcast_dynamic-update-slice_fusion.1 = bf16[4,4,4,56,640]{4,3,2,1,0:T(8,128)(2,1)} fusion(bf16[4,4,4,56,640]{4,3,2,1,0:T(8,128)(2,1)} %copy-done.1, s32[]{:T(128)S(6)} %select_n.269, bf16[4,4,56,640]{3,2,1,0:T(8,128)(2,1)} %collective-permute-done.9), kind=kLoop, calls=%fused_computation.33 | loop fusion | bytes 2293764 | tf_op jit(solution)/shard_map/dynamic_update_slice | solution.py:131
  131.8 2.2 %bitcast_dynamic-update-slice_fusion.7 = bf16[4,4,4,56,512]{4,3,0,2,1:T(8,128)(2,1)} fusion(bf16[4,4,4,56,512]{4,3,0,2,1:T(8,128)(2,1)} %copy-done.3, s32[]{:T(128)S(6)} %select_n.252, bf16[4,4,56,512]{3,2,1,0:T(8,128)(2,1)} %collective-permute-done.19), kind=kLoop, calls=%fused_computation.45 | loop fusion | bytes 1835012 | tf_op jit(solution)/shard_map/dynamic_update_slice | solution.py:131
  134.1 4.1 %convolution_convert_fusion.1 = bf16[512,512]{1,0:T(8,128)(2,1)S(1)} fusion(bf16[512,3584]{1,0:T(8,128)(2,1)S(1)} %bitcast.222, bf16[3584,512]{1,0:T(8,128)(2,1)} %bitcast.224), kind=kOutput, calls=%fused_computation.31 | convolution fusion | flops 1879310336 | bytes 7864320 | tf_op jit(solution)/shard_map/dot_general | solution.py:212
  138.4 4.2 %collective-permute-done.10 = bf16[4,4,56,640]{3,2,1,0:T(8,128)(2,1)S(1)} collective-permute-done((bf16[4,4,56,640]{3,2,1,0:T(8,128)(2,1)}, bf16[4,4,56,640]{3,2,1,0:T(8,128)(2,1)S(1)}, u32[]{:S(2)}, u32[]{:S(2)}) %collective-permute-start.10) | collective-permute-done | bytes 1146912 | tf_op jit(solution)/shard_map/ppermute | solution.py:60
  142.6 1.1 bitcast_dynamic-update-slice_fusion
  143.7 6.4 %convolution_convert_fusion = bf16[512,640]{1,0:T(8,128)(2,1)S(1)} fusion(bf16[512,3584]{1,0:T(8,128)(2,1)} %bitcast.221, bf16[3584,640]{1,0:T(8,128)(2,1)} %bitcast.219), kind=kOutput, calls=%fused_computation.30 | convolution fusion | flops 2349137920 | bytes 8912896 | tf_op jit(solution)/shard_map/dot_general | solution.py:212
  150.4 0.7 fusion.9
  151.1 11.2 %bitcast_reduce_fusion = (f32[2,7,256]{2,1,0:T(8,128)S(1)}, f32[2,2048,256,7]{2,1,3,0:T(8,128)}) fusion(pred[2,2048]{1,0:T(4,128)(4,1)S(1)} %compare_and_fusion, bf16[2,2048,128,1]{2,1,3,0:T(8,128)(2,1)S(1)} %bitcast.220, bf16[2,256,7,128]{1,3,2,0:T(8,128)(2,1)S(1)} %bitcast.215), kind=kOutput, calls=%fused_computation.1 | convolution fusion | flops 1901064704 | bytes 31344640 | tf_op jit(solution)/shard_map/htgd,hsd->hgts/dot_general | solution.py:251
  162.3 0.9 fusion.10
  163.2 2.3 %fusion.12 = f32[2,7,256,128]{2,3,1,0:T(8,128)} fusion(f32[2,256,256,7]{2,1,3,0:T(8,128)S(1)} %get-tuple-element.28, f32[2,7,256]{2,1,0:T(8,128)S(1)} %max.24, pred[2,256,256]{1,2,0:T(8,128)(4,1)S(1)} %broadcast_and_fusion, bf16[2,256,640]{2,1,0:T(8,128)(2,1)S(1)} %bitcast.236), kind=kOutput, calls=%fused_computation.20 | convolution fusion | flops 239468544 | bytes 5783552 | tf_op jit(solution)/shard_map/hgts,hsd->hgtd/dot_general | solution.py:259
  165.5 14.1 %fusion.2 = f32[2,7,256]{2,1,0:T(8,128)S(1)} fusion(f32[2,2048,256,7]{2,1,3,0:T(8,128)} %get-tuple-element.30, f32[2,7,256]{2,1,0:T(8,128)S(1)} %max.24, pred[2,2048]{1,0:T(4,128)(4,1)S(1)} %compare_and_fusion), kind=kLoop, calls=%fused_computation.5 | loop fusion | flops 36696576 | bytes 29392896 | tf_op jit(solution)/shard_map/reduce_sum | solution.py:258
  179.6 14.6 %fusion.15 = bf16[2,256,7,128]{1,3,2,0:T(8,128)(2,1)S(1)} fusion(f32[2,7,256,128]{2,3,1,0:T(8,128)S(1)} %copy-done.5, bf16[2,2048,128,1]{2,1,3,0:T(8,128)(2,1)S(1)} %bitcast.228, f32[2,2048,256,7]{2,1,3,0:T(8,128)} %get-tuple-element.30, f32[2,7,256]{2,1,0:T(8,128)S(1)} %max.24, pred[2,2048]{1,0:T(4,128)(4,1)S(1)} %compare_and_fusion, ...), kind=kOutput, calls=%fused_computation.24 | convolution fusion | flops 1917583360 | bytes 33194496 | tf_op jit(solution)/shard_map/hgts,hsd->hgtd/dot_general | solution.py:261
  194.6 11.8 %collective-permute-start.36 = (bf16[256,896]{1,0:T(8,128)(2,1)S(1)}, bf16[256,896]{1,0:T(8,128)(2,1)S(1)}, u32[]{:S(2)}, u32[]{:S(2)}) collective-permute-start(bf16[256,896]{1,0:T(8,128)(2,1)S(1)} %copy.85), channel_id=1, source_target_pairs={{0,32},{32,0},{2,34},{34,2},{4,36},{36,4},{6,38},{38,6},{64,96},{9... | collective-permute-start | bytes 1376264 | tf_op jit(solution)/shard_map/ppermute | solution.py:60
  206.6 1.2 collective-permute-done.36
  207.8 1.1 maximum_select_fusion
  (141 shorter events, 12.2 us)
Async XLA Ops:
  3.8 13.0 %collective-permute-start.1 = (bf16[28,1408]{1,0:T(8,128)(2,1)S(1)}, bf16[28,1408]{1,0:T(8,128)(2,1)S(1)}, u32[]{:S(2)}, u32[]{:S(2)}) collective-permute-start(bf16[28,1408]{1,0:T(8,128)(2,1)S(1)} %get-tuple-element.16), channel_id=1, source_target_pairs={{0,32},{32,0},{2,34},{34,2},{4,36},{36,4},{6,38},{38,6},{64,96},{9... | collective-permute-start | bytes 236552 | tf_op jit(solution)/shard_map/ppermute | solution.py:60
  7.8 1.5 copy-start
  16.2 67.2 %collective-permute-start = (bf16[336,3584]{1,0:T(8,128)(2,1)}, bf16[336,3584]{1,0:T(8,128)(2,1)}, u32[]{:S(2)}, u32[]{:S(2)}) collective-permute-start(bf16[336,3584]{1,0:T(8,128)(2,1)} %maximum_maximum_fusion), channel_id=1, source_target_pairs={{0,32},{32,0},{2,34},{34,2},{4,36},{36,4},{6,38},{38,6},{64,96},{9... | collective-permute-start | bytes 7225352 | tf_op jit(solution)/shard_map/ppermute | solution.py:60
  16.9 9.3 %collective-permute-start.20 = (bf16[56,256]{1,0:T(8,128)(2,1)S(1)}, bf16[56,256]{1,0:T(8,128)(2,1)S(1)}, u32[]{:S(2)}, u32[]{:S(2)}) collective-permute-start(bf16[56,256]{1,0:T(8,128)(2,1)S(1)} %slice.73), channel_id=1, source_target_pairs={{0,8},{32,56},{2,10},{34,58},{4,12},{36,60},{6,14},{38,62},{64,72}... | collective-permute-start | bytes 86024 | tf_op jit(solution)/shard_map/ppermute | solution.py:60
  19.5 11.6 %collective-permute-start.2 = (bf16[56,640]{1,0:T(8,128)(2,1)S(1)}, bf16[56,640]{1,0:T(8,128)(2,1)S(1)}, u32[]{:S(2)}, u32[]{:S(2)}) collective-permute-start(bf16[56,640]{1,0:T(8,128)(2,1)S(1)} %slice.68), channel_id=1, source_target_pairs={{0,64},{32,97},{2,66},{34,99},{4,68},{36,101},{6,70},{38,103},{64,... | collective-permute-start | bytes 215048 | tf_op jit(solution)/shard_map/ppermute | solution.py:60
  22.3 8.5 %collective-permute-start.11 = (bf16[56,512]{1,0:T(8,128)(2,1)S(1)}, bf16[56,512]{1,0:T(8,128)(2,1)S(1)}, u32[]{:S(2)}, u32[]{:S(2)}) collective-permute-start(bf16[56,512]{1,0:T(8,128)(2,1)S(1)} %slice.71), channel_id=1, source_target_pairs={{0,2},{32,38},{2,4},{34,32},{4,6},{36,34},{6,0},{38,36},{64,66},{9... | collective-permute-start | bytes 172040 | tf_op jit(solution)/shard_map/ppermute | solution.py:60
  26.2 2.8 %collective-permute-start.21 = (bf16[56,256]{1,0:T(8,128)(2,1)S(1)}, bf16[56,256]{1,0:T(8,128)(2,1)S(1)}, u32[]{:S(2)}, u32[]{:S(2)}) collective-permute-start(bf16[56,256]{1,0:T(8,128)(2,1)S(1)} %collective-permute-done.20), channel_id=1, source_target_pairs={{0,8},{32,56},{2,10},{34,58},{4,12},{36,60},{6,14},{38,62},{64,72}... | collective-permute-start | bytes 86024 | tf_op jit(solution)/shard_map/ppermute | solution.py:60
  29.0 5.0 %collective-permute-start.22 = (bf16[56,256]{1,0:T(8,128)(2,1)S(1)}, bf16[56,256]{1,0:T(8,128)(2,1)S(1)}, u32[]{:S(2)}, u32[]{:S(2)}) collective-permute-start(bf16[56,256]{1,0:T(8,128)(2,1)S(1)} %collective-permute-done.21), channel_id=1, source_target_pairs={{0,8},{32,56},{2,10},{34,58},{4,12},{36,60},{6,14},{38,62},{64,72}... | collective-permute-start | bytes 86024 | tf_op jit(solution)/shard_map/ppermute | solution.py:60
  30.7 3.9 %collective-permute-start.12 = (bf16[56,512]{1,0:T(8,128)(2,1)S(1)}, bf16[56,512]{1,0:T(8,128)(2,1)S(1)}, u32[]{:S(2)}, u32[]{:S(2)}) collective-permute-start(bf16[56,512]{1,0:T(8,128)(2,1)S(1)} %collective-permute-done.11), channel_id=1, source_target_pairs={{0,2},{32,38},{2,4},{34,32},{4,6},{36,34},{6,0},{38,36},{64,66},{9... | collective-permute-start | bytes 172040 | tf_op jit(solution)/shard_map/ppermute | solution.py:60
  31.2 4.2 %collective-permute-start.3 = (bf16[56,640]{1,0:T(8,128)(2,1)S(1)}, bf16[56,640]{1,0:T(8,128)(2,1)S(1)}, u32[]{:S(2)}, u32[]{:S(2)}) collective-permute-start(bf16[56,640]{1,0:T(8,128)(2,1)S(1)} %collective-permute-done.2), channel_id=1, source_target_pairs={{0,64},{32,97},{2,66},{34,99},{4,68},{36,101},{6,70},{38,103},{64,... | collective-permute-start | bytes 215048 | tf_op jit(solution)/shard_map/ppermute | solution.py:60
  34.0 5.3 %collective-permute-start.23 = (bf16[4,56,256]{2,1,0:T(8,128)(2,1)S(1)}, bf16[4,56,256]{2,1,0:T(8,128)(2,1)S(1)}, u32[]{:S(2)}, u32[]{:S(2)}) collective-permute-start(bf16[4,56,256]{2,1,0:T(8,128)(2,1)S(1)} %bitcast_dynamic-update-slice_fusion.32), channel_id=1, source_target_pairs={{0,64},{32,97},{2,66},{34,99},{4,68},{36,101},{6,70},{38,103},{64,... | collective-permute-start | bytes 344072 | tf_op jit(solution)/shard_map/ppermute | solution.py:60
  34.6 3.8 %collective-permute-start.13 = (bf16[56,512]{1,0:T(8,128)(2,1)S(1)}, bf16[56,512]{1,0:T(8,128)(2,1)S(1)}, u32[]{:S(2)}, u32[]{:S(2)}) collective-permute-start(bf16[56,512]{1,0:T(8,128)(2,1)S(1)} %collective-permute-done.12), channel_id=1, source_target_pairs={{0,2},{32,38},{2,4},{34,32},{4,6},{36,34},{6,0},{38,36},{64,66},{9... | collective-permute-start | bytes 172040 | tf_op jit(solution)/shard_map/ppermute | solution.py:60
  35.4 4.5 %collective-permute-start.4 = (bf16[56,640]{1,0:T(8,128)(2,1)S(1)}, bf16[56,640]{1,0:T(8,128)(2,1)S(1)}, u32[]{:S(2)}, u32[]{:S(2)}) collective-permute-start(bf16[56,640]{1,0:T(8,128)(2,1)S(1)} %collective-permute-done.3), channel_id=1, source_target_pairs={{0,64},{32,97},{2,66},{34,99},{4,68},{36,101},{6,70},{38,103},{64,... | collective-permute-start | bytes 215048 | tf_op jit(solution)/shard_map/ppermute | solution.py:60
  38.4 6.3 %collective-permute-start.14 = (bf16[4,56,512]{2,1,0:T(8,128)(2,1)S(1)}, bf16[4,56,512]{2,1,0:T(8,128)(2,1)S(1)}, u32[]{:S(2)}, u32[]{:S(2)}) collective-permute-start(bf16[4,56,512]{2,1,0:T(8,128)(2,1)S(1)} %bitcast_dynamic-update-slice_fusion.28), channel_id=1, source_target_pairs={{0,8},{32,56},{2,10},{34,58},{4,12},{36,60},{6,14},{38,62},{64,72}... | collective-permute-start | bytes 688136 | tf_op jit(solution)/shard_map/ppermute | solution.py:60
  39.3 3.8 %collective-permute-start.24 = (bf16[4,56,256]{2,1,0:T(8,128)(2,1)S(1)}, bf16[4,56,256]{2,1,0:T(8,128)(2,1)S(1)}, u32[]{:S(2)}, u32[]{:S(2)}) collective-permute-start(bf16[4,56,256]{2,1,0:T(8,128)(2,1)S(1)} %collective-permute-done.23), channel_id=1, source_target_pairs={{0,64},{32,97},{2,66},{34,99},{4,68},{36,101},{6,70},{38,103},{64,... | collective-permute-start | bytes 344072 | tf_op jit(solution)/shard_map/ppermute | solution.py:60
  39.9 10.4 %collective-permute-start.5 = (bf16[4,56,640]{2,1,0:T(8,128)(2,1)S(1)}, bf16[4,56,640]{2,1,0:T(8,128)(2,1)S(1)}, u32[]{:S(2)}, u32[]{:S(2)}) collective-permute-start(bf16[4,56,640]{2,1,0:T(8,128)(2,1)S(1)} %bitcast_dynamic-update-slice_fusion.24), channel_id=1, source_target_pairs={{0,2},{32,38},{2,4},{34,32},{4,6},{36,34},{6,0},{38,36},{64,66},{9... | collective-permute-start | bytes 860168 | tf_op jit(solution)/shard_map/ppermute | solution.py:60
  43.2 4.0 %collective-permute-start.25 = (bf16[4,56,256]{2,1,0:T(8,128)(2,1)S(1)}, bf16[4,56,256]{2,1,0:T(8,128)(2,1)S(1)}, u32[]{:S(2)}, u32[]{:S(2)}) collective-permute-start(bf16[4,56,256]{2,1,0:T(8,128)(2,1)S(1)} %collective-permute-done.24), channel_id=1, source_target_pairs={{0,64},{32,97},{2,66},{34,99},{4,68},{36,101},{6,70},{38,103},{64,... | collective-permute-start | bytes 344072 | tf_op jit(solution)/shard_map/ppermute | solution.py:60
  44.8 5.8 %collective-permute-start.15 = (bf16[4,56,512]{2,1,0:T(8,128)(2,1)S(1)}, bf16[4,56,512]{2,1,0:T(8,128)(2,1)S(1)}, u32[]{:S(2)}, u32[]{:S(2)}) collective-permute-start(bf16[4,56,512]{2,1,0:T(8,128)(2,1)S(1)} %collective-permute-done.14), channel_id=1, source_target_pairs={{0,8},{32,56},{2,10},{34,58},{4,12},{36,60},{6,14},{38,62},{64,72}... | collective-permute-start | bytes 688136 | tf_op jit(solution)/shard_map/ppermute | solution.py:60
  47.2 18.2 %collective-permute-start.26 = (bf16[4,4,56,256]{3,2,0,1:T(8,128)(2,1)S(1)}, bf16[4,4,56,256]{3,2,0,1:T(8,128)(2,1)S(1)}, u32[]{:S(2)}, u32[]{:S(2)}) collective-permute-start(bf16[4,4,56,256]{3,2,0,1:T(8,128)(2,1)S(1)} %bitcast_dynamic-update-slice_fusion.23), channel_id=1, source_target_pairs={{0,2},{32,38},{2,4},{34,32},{4,6},{36,34},{6,0},{38,36},{64,66},{9... | collective-permute-start | bytes 1376264 | tf_op jit(solution)/shard_map/ppermute | solution.py:60
  50.4 8.2 %collective-permute-start.6 = (bf16[4,56,640]{2,1,0:T(8,128)(2,1)S(1)}, bf16[4,56,640]{2,1,0:T(8,128)(2,1)S(1)}, u32[]{:S(2)}, u32[]{:S(2)}) collective-permute-start(bf16[4,56,640]{2,1,0:T(8,128)(2,1)S(1)} %collective-permute-done.5), channel_id=1, source_target_pairs={{0,2},{32,38},{2,4},{34,32},{4,6},{36,34},{6,0},{38,36},{64,66},{9... | collective-permute-start | bytes 860168 | tf_op jit(solution)/shard_map/ppermute | solution.py:60
  50.5 11.6 %collective-permute-start.16 = (bf16[4,56,512]{2,1,0:T(8,128)(2,1)S(1)}, bf16[4,56,512]{2,1,0:T(8,128)(2,1)S(1)}, u32[]{:S(2)}, u32[]{:S(2)}) collective-permute-start(bf16[4,56,512]{2,1,0:T(8,128)(2,1)S(1)} %collective-permute-done.15), channel_id=1, source_target_pairs={{0,8},{32,56},{2,10},{34,58},{4,12},{36,60},{6,14},{38,62},{64,72}... | collective-permute-start | bytes 688136 | tf_op jit(solution)/shard_map/ppermute | solution.py:60
  58.6 7.0 %collective-permute-start.7 = (bf16[4,56,640]{2,1,0:T(8,128)(2,1)S(1)}, bf16[4,56,640]{2,1,0:T(8,128)(2,1)S(1)}, u32[]{:S(2)}, u32[]{:S(2)}) collective-permute-start(bf16[4,56,640]{2,1,0:T(8,128)(2,1)S(1)} %collective-permute-done.6), channel_id=1, source_target_pairs={{0,2},{32,38},{2,4},{34,32},{4,6},{36,34},{6,0},{38,36},{64,66},{9... | collective-permute-start | bytes 860168 | tf_op jit(solution)/shard_map/ppermute | solution.py:60
  62.1 13.2 %collective-permute-start.17 = (bf16[4,4,56,512]{3,2,1,0:T(8,128)(2,1)S(1)}, bf16[4,4,56,512]{3,2,1,0:T(8,128)(2,1)S(1)}, u32[]{:S(2)}, u32[]{:S(2)}) collective-permute-start(bf16[4,4,56,512]{3,2,1,0:T(8,128)(2,1)S(1)} %bitcast_dynamic-update-slice_fusion.16), channel_id=1, source_target_pairs={{0,64},{32,97},{2,66},{34,99},{4,68},{36,101},{6,70},{38,103},{64,... | collective-permute-start | bytes 2752520 | tf_op jit(solution)/shard_map/ppermute | solution.py:60
  65.5 7.7 %collective-permute-start.27 = (bf16[4,4,56,256]{3,2,0,1:T(8,128)(2,1)S(1)}, bf16[4,4,56,256]{3,2,0,1:T(8,128)(2,1)S(1)}, u32[]{:S(2)}, u32[]{:S(2)}) collective-permute-start(bf16[4,4,56,256]{3,2,0,1:T(8,128)(2,1)S(1)} %collective-permute-done.26), channel_id=1, source_target_pairs={{0,2},{32,38},{2,4},{34,32},{4,6},{36,34},{6,0},{38,36},{64,66},{9... | collective-permute-start | bytes 1376264 | tf_op jit(solution)/shard_map/ppermute | solution.py:60
  65.7 15.3 %collective-permute-start.8 = (bf16[4,4,56,640]{3,2,1,0:T(8,128)(2,1)S(1)}, bf16[4,4,56,640]{3,2,1,0:T(8,128)(2,1)}, u32[]{:S(2)}, u32[]{:S(2)}) collective-permute-start(bf16[4,4,56,640]{3,2,1,0:T(8,128)(2,1)S(1)} %bitcast_dynamic-update-slice_fusion.12), channel_id=1, source_target_pairs={{0,8},{32,56},{2,10},{34,58},{4,12},{36,60},{6,14},{38,62},{64,72}... | collective-permute-start | bytes 3440648 | tf_op jit(solution)/shard_map/ppermute | solution.py:60
  73.2 7.7 %collective-permute-start.28 = (bf16[4,4,56,256]{3,2,0,1:T(8,128)(2,1)S(1)}, bf16[4,4,56,256]{3,2,0,1:T(8,128)(2,1)S(1)}, u32[]{:S(2)}, u32[]{:S(2)}) collective-permute-start(bf16[4,4,56,256]{3,2,0,1:T(8,128)(2,1)S(1)} %collective-permute-done.27), channel_id=1, source_target_pairs={{0,2},{32,38},{2,4},{34,32},{4,6},{36,34},{6,0},{38,36},{64,66},{9... | collective-permute-start | bytes 1376264 | tf_op jit(solution)/shard_map/ppermute | solution.py:60
  75.3 31.4 %collective-permute-start.18 = (bf16[4,4,56,512]{3,2,1,0:T(8,128)(2,1)S(1)}, bf16[4,4,56,512]{3,2,1,0:T(8,128)(2,1)}, u32[]{:S(2)}, u32[]{:S(2)}) collective-permute-start(bf16[4,4,56,512]{3,2,1,0:T(8,128)(2,1)S(1)} %collective-permute-done.17), channel_id=1, source_target_pairs={{0,64},{32,97},{2,66},{34,99},{4,68},{36,101},{6,70},{38,103},{64,... | collective-permute-start | bytes 2752520 | tf_op jit(solution)/shard_map/ppermute | solution.py:60
  80.9 44.5 %collective-permute-start.9 = (bf16[4,4,56,640]{3,2,1,0:T(8,128)(2,1)}, bf16[4,4,56,640]{3,2,1,0:T(8,128)(2,1)}, u32[]{:S(2)}, u32[]{:S(2)}) collective-permute-start(bf16[4,4,56,640]{3,2,1,0:T(8,128)(2,1)} %collective-permute-done.8), channel_id=1, source_target_pairs={{0,8},{32,56},{2,10},{34,58},{4,12},{36,60},{6,14},{38,62},{64,72}... | collective-permute-start | bytes 3440648 | tf_op jit(solution)/shard_map/ppermute | solution.py:60
  83.4 4.1 %copy-start.1 = (bf16[4,4,4,56,640]{4,3,2,1,0:T(8,128)(2,1)}, bf16[4,4,4,56,640]{4,3,2,1,0:T(8,128)(2,1)S(1)}, u32[]{:S(2)}) copy-start(bf16[4,4,4,56,640]{4,3,2,1,0:T(8,128)(2,1)S(1)} %bitcast_dynamic-update-slice_fusion.2) | copy-start | bytes 13762564
  87.6 5.6 %collective-permute-start.29 = (bf16[2,72,256]{2,1,0:T(8,128)(2,1)S(1)}, bf16[2,72,256]{2,1,0:T(8,128)(2,1)S(1)}, u32[]{:S(2)}, u32[]{:S(2)}) collective-permute-start(bf16[2,72,256]{2,1,0:T(8,128)(2,1)S(1)} %get-tuple-element.18), channel_id=1, source_target_pairs={{0,1},{32,33},{2,3},{34,35},{4,5},{36,37},{6,7},{38,39},{64,65},{9... | collective-permute-start | bytes 221192 | tf_op jit(solution)/shard_map/ppermute | solution.py:60
  93.2 8.4 %collective-permute-start.30 = (bf16[2,2,72,256]{3,2,1,0:T(8,128)(2,1)S(1)}, bf16[2,2,72,256]{3,2,1,0:T(8,128)(2,1)S(1)}, u32[]{:S(2)}, u32[]{:S(2)}) collective-permute-start(bf16[2,2,72,256]{3,2,1,0:T(8,128)(2,1)S(1)} %get-tuple-element.14), channel_id=1, source_target_pairs={{0,8},{32,40},{2,10},{34,42},{4,12},{36,44},{6,14},{38,46},{64,72}... | collective-permute-start | bytes 442376 | tf_op jit(solution)/shard_map/ppermute | solution.py:60
  93.5 8.7 %collective-permute-start.31 = (bf16[2,2,72,256]{3,2,1,0:T(8,128)(2,1)S(1)}, bf16[2,2,72,256]{3,2,1,0:T(8,128)(2,1)S(1)}, u32[]{:S(2)}, u32[]{:S(2)}) collective-permute-start(bf16[2,2,72,256]{3,2,1,0:T(8,128)(2,1)S(1)} %get-tuple-element.14), channel_id=1, source_target_pairs={{0,16},{32,48},{2,18},{34,50},{4,20},{36,52},{6,22},{38,54},{64,80... | collective-permute-start | bytes 442376 | tf_op jit(solution)/shard_map/ppermute | solution.py:60
  95.1 7.1 %collective-permute-start.32 = (bf16[2,2,72,256]{3,2,1,0:T(8,128)(2,1)S(1)}, bf16[2,2,72,256]{3,2,1,0:T(8,128)(2,1)S(1)}, u32[]{:S(2)}, u32[]{:S(2)}) collective-permute-start(bf16[2,2,72,256]{3,2,1,0:T(8,128)(2,1)S(1)} %get-tuple-element.14), channel_id=1, source_target_pairs={{0,24},{32,56},{2,26},{34,58},{4,28},{36,60},{6,30},{38,62},{64,88... | collective-permute-start | bytes 442376 | tf_op jit(solution)/shard_map/ppermute | solution.py:60
  102.3 10.5 %collective-permute-start.33 = (bf16[4,2,2,72,256]{4,3,2,1,0:T(8,128)(2,1)S(1)}, bf16[4,2,2,72,256]{4,3,2,1,0:T(8,128)(2,1)S(1)}, u32[]{:S(2)}, u32[]{:S(2)}) collective-permute-start(bf16[4,2,2,72,256]{4,3,2,1,0:T(8,128)(2,1)S(1)} %get-tuple-element.12), channel_id=1, source_target_pairs={{0,2},{32,34},{2,4},{34,36},{4,6},{36,38},{6,0},{38,32},{64,66},{9... | collective-permute-start | bytes 1769480 | tf_op jit(solution)/shard_map/ppermute | solution.py:60
  103.8 19.4 %collective-permute-start.34 = (bf16[4,2,2,72,256]{4,3,2,1,0:T(8,128)(2,1)S(1)}, bf16[4,2,2,72,256]{4,3,2,1,0:T(8,128)(2,1)S(1)}, u32[]{:S(2)}, u32[]{:S(2)}) collective-permute-start(bf16[4,2,2,72,256]{4,3,2,1,0:T(8,128)(2,1)S(1)} %get-tuple-element.12), channel_id=1, source_target_pairs={{0,4},{32,36},{2,6},{34,38},{4,0},{36,32},{6,2},{38,34},{64,68},{9... | collective-permute-start | bytes 1769480 | tf_op jit(solution)/shard_map/ppermute | solution.py:60
  106.5 16.7 %collective-permute-start.35 = (bf16[4,2,2,72,256]{4,3,2,1,0:T(8,128)(2,1)S(1)}, bf16[4,2,2,72,256]{4,3,2,1,0:T(8,128)(2,1)S(1)}, u32[]{:S(2)}, u32[]{:S(2)}) collective-permute-start(bf16[4,2,2,72,256]{4,3,2,1,0:T(8,128)(2,1)S(1)} %get-tuple-element.12), channel_id=1, source_target_pairs={{0,6},{32,38},{2,0},{34,32},{4,2},{36,34},{6,4},{38,36},{64,70},{9... | collective-permute-start | bytes 1769480 | tf_op jit(solution)/shard_map/ppermute | solution.py:60
  106.7 25.1 %collective-permute-start.19 = (bf16[4,4,56,512]{3,2,1,0:T(8,128)(2,1)}, bf16[4,4,56,512]{3,2,1,0:T(8,128)(2,1)}, u32[]{:S(2)}, u32[]{:S(2)}) collective-permute-start(bf16[4,4,56,512]{3,2,1,0:T(8,128)(2,1)} %collective-permute-done.18), channel_id=1, source_target_pairs={{0,64},{32,97},{2,66},{34,99},{4,68},{36,101},{6,70},{38,103},{64,... | collective-permute-start | bytes 2752520 | tf_op jit(solution)/shard_map/ppermute | solution.py:60
  110.0 13.9 %copy-start.3 = (bf16[4,4,4,56,512]{4,3,0,2,1:T(8,128)(2,1)}, bf16[4,4,4,56,512]{4,3,0,2,1:T(8,128)(2,1)S(1)}, u32[]{:S(2)}) copy-start(bf16[4,4,4,56,512]{4,3,0,2,1:T(8,128)(2,1)S(1)} %bitcast_dynamic-update-slice_fusion.4) | copy-start | bytes 11010052
  124.3 9.8 %copy-start.2 = (bf16[2,256,3584]{2,1,0:T(8,128)(2,1)S(1)}, bf16[2,256,3584]{2,1,0:T(8,128)(2,1)}, u32[]{:S(2)}) copy-start(bf16[2,256,3584]{2,1,0:T(8,128)(2,1)} %pad_maximum_fusion) | copy-start | bytes 11010052
  125.4 17.2 %collective-permute-start.10 = (bf16[4,4,56,640]{3,2,1,0:T(8,128)(2,1)}, bf16[4,4,56,640]{3,2,1,0:T(8,128)(2,1)S(1)}, u32[]{:S(2)}, u32[]{:S(2)}) collective-permute-start(bf16[4,4,56,640]{3,2,1,0:T(8,128)(2,1)} %collective-permute-done.9), channel_id=1, source_target_pairs={{0,8},{32,56},{2,10},{34,58},{4,12},{36,60},{6,14},{38,62},{64,72}... | collective-permute-start | bytes 3440648 | tf_op jit(solution)/shard_map/ppermute | solution.py:60
  165.5 14.1 %copy-start.4 = (bf16[2,32,64,128]{3,2,1,0:T(8,128)(2,1)S(1)}, bf16[2,32,64,128]{3,2,1,0:T(8,128)(2,1)}, u32[]{:S(2)}) copy-start(bf16[2,32,64,128]{3,2,1,0:T(8,128)(2,1)} %copy.82) | copy-start | bytes 3145732
  165.5 14.1 %copy-start.5 = (f32[2,7,256,128]{2,3,1,0:T(8,128)S(1)}, f32[2,7,256,128]{2,3,1,0:T(8,128)}, u32[]{:S(2)}) copy-start(f32[2,7,256,128]{2,3,1,0:T(8,128)} %fusion.12) | copy-start | bytes 5505028
  194.6 13.2 %collective-permute-start.36 = (bf16[256,896]{1,0:T(8,128)(2,1)S(1)}, bf16[256,896]{1,0:T(8,128)(2,1)S(1)}, u32[]{:S(2)}, u32[]{:S(2)}) collective-permute-start(bf16[256,896]{1,0:T(8,128)(2,1)S(1)} %copy.85), channel_id=1, source_target_pairs={{0,32},{32,0},{2,34},{34,2},{4,36},{36,4},{6,38},{38,6},{64,96},{9... | collective-permute-start | bytes 1376264 | tf_op jit(solution)/shard_map/ppermute | solution.py:60

commit v2 on v1

v2 whole, which is shorter than its diff:
```python
import functools
import math

import jax
import jax.numpy as jnp
import numpy as np
from jax import lax
from jax.experimental import pallas as pl
from jax.experimental.pallas import tpu as pltpu
from jax.sharding import PartitionSpec as P

HEADS = 7
D = 128
WIDTH = 3584
ROWS = 28
TOK = 256
SLOTS = 64
SPANS = 32
EPS = 1e-6
FILL = -1e30
AXES = ("dp", "ctx")
SCALE = 1.0 / math.sqrt(D)


def device_id(x, y, z, c):
    return ((y % 2) * 2 + c) * 32 + (x * 4 + z) * 2 + y // 2


def make_perm(f):
    pairs = []
    for x in range(4):
        for y in range(4):
            for z in range(4):
                for c in range(2):
                    tx, ty, tz, tc = f(x, y, z, c)
                    pairs.append(
                        (device_id(x, y, z, c), device_id(tx % 4, ty % 4, tz % 4, tc % 2))
                    )
    return pairs


SWAP = make_perm(lambda x, y, z, c: (x, y, z, 1 - c))
RING = {
    "x": make_perm(lambda x, y, z, c: (x + 1 - 2 * c, y, z, c)),
    "y": make_perm(lambda x, y, z, c: (x, y + 1 - 2 * c, z, c)),
    "z": make_perm(lambda x, y, z, c: (x, y, z + 1 - 2 * c, c)),
}
ACROSS = make_perm(lambda x, y, z, c: (x, y + 2, z, c))


def flip(axis, turn):
    def partner(x, y, z, c):
        at = {"x": x, "y": y, "z": z}
        at[axis] ^= 1 if (c + turn) % 2 == 0 else 3
        return at["x"], at["y"], at["z"], c

    return make_perm(partner)


FLIP = {(axis, turn): flip(axis, turn) for axis in "xyz" for turn in (0, 1)}

ORDERS = (("z", "x", "y"), ("y", "z", "x"), ("x", "y", "z"))
CUTS = (0, 256, 896, 1408)
KEPT = 3
SLAB = WIDTH // 4
PACK = 2 * TOK + SLOTS + 16


def send(value, pairs):
    return lax.ppermute(value, AXES, pairs)


def feature_runs(order):
    first, second, last = order
    starts = []
    for i in range(4):
        for j in range(4):
            for k in range(4):
                at = {last: i, second: j, first: k}
                for c in range(2):
                    starts.append(device_id(at["x"], at["y"], at["z"], c) * ROWS)
    source = np.concatenate([np.arange(s, s + ROWS) for s in starts])
    tiles = []
    for tile in range(WIDTH // 128):
        part = source[tile * 128 : (tile + 1) * 128]
        runs = []
        lane = 0
        while lane < 128:
            end = lane + 1
            while end < 128 and part[end] == part[end - 1] + 1 and part[end] % 128 != 0:
                end += 1
            runs.append((lane, end, int(part[lane])))
            lane = end
        tiles.append(runs)
    return tiles


def reorder(plain_ref, out_ref, order, count, out_rows):
    lane = lax.broadcasted_iota(jnp.int32, (count, 128), 1)
    for tile, runs in enumerate(feature_runs(order)):
        joined = jnp.zeros((count, 128), jnp.float32)
        for first, end, feature in runs:
            block, offset = divmod(feature, 128)
            piece = plain_ref[:, block * 128 : (block + 1) * 128]
            shift = (first - offset) % 128
            if shift:
                piece = pltpu.roll(piece, shift, 1)
            joined = jnp.where((lane >= first) & (lane < end), piece, joined)
        slab, column = divmod(tile, SLAB // 128)
        out_ref[slab, out_rows, column * 128 : (column + 1) * 128] = joined.astype(jnp.bfloat16)


def norm_body(fact_ref, tokens_ref, gain_ref, out_ref, plain_ref, normed_ref):
    rows = 64
    level, valid, count = fact_ref[0], fact_ref[1], fact_ref[2]

    @pl.loop(0, TOK // rows)
    def _(step):
        here = pl.ds(pl.multiple_of(step * rows, rows), rows)
        below = pl.ds(pl.multiple_of(step * rows + TOK, rows), rows)
        values = tokens_ref[here, :].astype(jnp.float32)
        factor = lax.rsqrt(jnp.mean(values * values, axis=-1, keepdims=True) + EPS)
        plain_ref[...] = values * factor * gain_ref[...]
        normed_ref[here, :] = plain_ref[...].astype(jnp.bfloat16)
        reorder(plain_ref, out_ref, ORDERS[1], rows, here)
        reorder(plain_ref, out_ref, ORDERS[2], rows, below)

    shift = level + 2
    live = jnp.right_shift(TOK, shift)
    slot = lax.broadcasted_iota(jnp.int32, (SLOTS, TOK), 0)
    position = lax.broadcasted_iota(jnp.int32, (SLOTS, TOK), 1)
    inside = (jnp.right_shift(position, shift) == slot) & (slot < live) & (position < valid)
    window = jnp.where(inside, 1.0, 0.0)
    size = jnp.maximum(jnp.sum(window, axis=1, keepdims=True), 1.0)
    sums = jnp.dot(
        window.astype(jnp.bfloat16), normed_ref[...], preferred_element_type=jnp.float32
    )
    plain_ref[...] = sums / size
    reorder(plain_ref, out_ref, ORDERS[0], SLOTS, pl.ds(2 * TOK, SLOTS))
    row = lax.broadcasted_iota(jnp.int32, (16, SLAB), 0)
    facts = jnp.where(row < 8, count, valid).astype(jnp.float32).astype(jnp.bfloat16)
    for slab in range(4):
        out_ref[slab, pl.ds(2 * TOK + SLOTS, 16), :] = facts


def norm_rows(facts, tokens, gain):
    return pl.pallas_call(
        norm_body,
        out_shape=jax.ShapeDtypeStruct((4, PACK, SLAB), jnp.bfloat16),
        in_specs=[pl.BlockSpec(memory_space=pltpu.SMEM)]
        + [pl.BlockSpec(memory_space=pltpu.VMEM)] * 2,
        out_specs=pl.BlockSpec(memory_space=pltpu.VMEM),
        scratch_shapes=[
            pltpu.VMEM((64, WIDTH), jnp.float32),
            pltpu.VMEM((TOK, WIDTH), jnp.bfloat16),
        ],
        compiler_params=pltpu.CompilerParams(vmem_limit_bytes=32 * 1024 * 1024),
    )(facts, tokens, gain.reshape(1, WIDTH))


BLOCK = 512
ROOM = SPANS * SLOTS + BLOCK


def attend_body(which, wide, info_ref, count_ref, part_a_ref, part_b_ref, far_k_ref, far_v_ref, *rest):
    out_ref, near_ref, keys_ref, values_ref, bias_ref, score_ref = rest
    span, valid, column = info_ref[0], info_ref[1], info_ref[2]

    lane = lax.broadcasted_iota(jnp.int32, (1, ROOM), 1)
    bias_ref[...] = jnp.full((1, ROOM), FILL, jnp.float32)

    def pack(i, at):
        place_k, place_v = info_ref[3 + i], info_ref[3 + SPANS + i]
        count = count_ref[place_k]
        here = pl.ds(pl.multiple_of(at, 16), SLOTS)
        keys_ref[here, :] = far_k_ref[place_k, which, :SLOTS, :]
        values_ref[here, :] = far_v_ref[place_v, which]
        bias_ref[...] = jnp.where((lane >= at) & (lane < at + count), 0.0, bias_ref[...])
        return at + ((count + 15) // 16) * 16

    used = lax.fori_loop(0, span, pack, jnp.int32(0))
    rest_rows = pl.ds(pl.multiple_of(used, 16), BLOCK)
    keys_ref[rest_rows, :] = jnp.zeros((BLOCK, D), jnp.bfloat16)
    values_ref[rest_rows, :] = jnp.zeros((BLOCK, D), jnp.bfloat16)
    blocks = (used + BLOCK - 1) // BLOCK

    row = lax.broadcasted_iota(jnp.int32, (TOK, TOK), 0)
    col = lax.broadcasted_iota(jnp.int32, (TOK, TOK), 1)
    near_ref[...] = jnp.where((col <= row) & (col < valid), 0.0, FILL)
    alive = lax.broadcasted_iota(jnp.int32, (TOK, D), 0) < valid
    power = SCALE * math.log2(math.e)
    contract = (((1,), (1,)), ((), ()))

    def fold(op, scores):
        out = scores[:, :D]
        for i in range(1, scores.shape[1] // D):
            out = op(out, scores[:, i * D : (i + 1) * D])
        return out

    for head in range(HEADS):
        if head < KEPT:
            query = part_a_ref[:, (2 + head) * D : (3 + head) * D]
        else:
            query = part_b_ref[:, (head - KEPT) * D : (head - KEPT + 1) * D]
        near = (
            lax.dot_general(
                query, part_a_ref[:, :D], contract, preferred_element_type=jnp.float32
            )
            + near_ref[...]
        )

        def score(i, top, query=query):
            here = pl.ds(pl.multiple_of(i * BLOCK, BLOCK), BLOCK)
            far = lax.dot_general(
                query, keys_ref[here, :], contract, preferred_element_type=jnp.float32
            )
            far = far + bias_ref[:, here]
            score_ref[:, here] = far
            return jnp.maximum(top, fold(jnp.maximum, far))

        top = lax.fori_loop(0, blocks, score, fold(jnp.maximum, near))
        top = jnp.max(top, axis=1, keepdims=True)
        weight = jnp.exp2((near - top) * power)
        total = fold(jnp.add, weight)
        mixed = jnp.dot(
            weight.astype(jnp.bfloat16),
            part_a_ref[:, D : 2 * D],
            preferred_element_type=jnp.float32,
        )

        def mix(i, state, top=top):
            total, mixed = state
            here = pl.ds(pl.multiple_of(i * BLOCK, BLOCK), BLOCK)
            weight = jnp.exp2((score_ref[:, here] - top) * power)
            mixed = mixed + jnp.dot(
                weight.astype(jnp.bfloat16), values_ref[here, :], preferred_element_type=jnp.float32
            )
            return total + fold(jnp.add, weight), mixed

        total, mixed = lax.fori_loop(0, blocks, mix, (total, mixed))
        total = jnp.sum(total, axis=1, keepdims=True)
        result = jnp.where(alive, mixed / total, 0.0).astype(jnp.bfloat16)
        if wide:
            out_ref[:, pl.ds(pl.multiple_of(column + head * D, D), D)] = result
        else:
            out_ref[:, head * D : (head + 1) * D] = result


def attend(which, wide, info, counts, part_a, part_b, far_k, far_v):
    columns = 2 * HEADS * D if wide else HEADS * D
    smem, vmem = pl.BlockSpec(memory_space=pltpu.SMEM), pl.BlockSpec(memory_space=pltpu.VMEM)
    return pl.pallas_call(
        functools.partial(attend_body, which, wide),
        out_shape=jax.ShapeDtypeStruct((TOK, columns), jnp.bfloat16),
        in_specs=[smem, smem, vmem, vmem, vmem, vmem],
        out_specs=vmem,
        scratch_shapes=[
            pltpu.VMEM((TOK, TOK), jnp.float32),
            pltpu.VMEM((ROOM, D), jnp.bfloat16),
            pltpu.VMEM((ROOM, D), jnp.bfloat16),
            pltpu.VMEM((1, ROOM), jnp.float32),
            pltpu.VMEM((TOK, ROOM), jnp.float32),
        ],
        compiler_params=pltpu.CompilerParams(vmem_limit_bytes=32 * 1024 * 1024),
    )(info, counts, part_a, part_b, far_k, far_v)


def double(block, axis):
    pair = jnp.stack([block, send(block, FLIP[axis, 0])])
    return jnp.concatenate([pair, send(pair, FLIP[axis, 1])])


def in_place(pieces, slots, blank):
    joined = blank
    for i, slot in enumerate(slots):
        joined = lax.dynamic_update_slice_in_dim(joined, pieces[i][None], slot, 0)
    return joined


def on_device(tokens, gain, w_query, w_key, w_value, w_mark_key, w_mark_value, level, hist_len):
    dp = lax.axis_index("dp")
    span = lax.axis_index("ctx")
    core = dp % 2
    pos = {"x": span // 8, "z": (span // 2) % 4, "y": (span % 2) * 2 + dp // 2}
    sign = 1 - 2 * core
    near, far = 1 + 2 * core, 3 - 2 * core

    def half(which):
        def cut(w, size):
            return jnp.where(which == 0, w[:, :size], w[:, size:])

        return jnp.concatenate(
            [
                cut(w_mark_key, D),
                cut(w_mark_value, D),
                cut(w_key, D),
                cut(w_value, D),
                cut(w_query, HEADS * D),
            ],
            axis=1,
        )

    mine = half(core)
    other = send(half(1 - core), SWAP)
    rows = jnp.where(
        core == 0, jnp.concatenate([mine, other], 0), jnp.concatenate([other, mine], 0)
    )
    rows, tokens = lax.optimization_barrier((rows, tokens))

    begin = span * TOK
    stride = jnp.left_shift(jnp.int32(4), level[0, 0])
    valid = jnp.clip(hist_len[0] - begin, 0, TOK)
    count = jnp.minimum(TOK // stride, (valid + stride - 1) // stride)
    packed = norm_rows(jnp.stack([level[0, 0], valid, count]), tokens[0], gain)
    mate = send(packed, SWAP)
    facts = mate[0, 2 * TOK + SLOTS :, 0].astype(jnp.int32)
    mate_count, mate_valid = facts[0], facts[8]
    both_a = jnp.concatenate([packed[:, :TOK], mate[:, :TOK]], 1)
    both_b = jnp.concatenate([packed[:, TOK : 2 * TOK], mate[:, TOK : 2 * TOK]], 1)
    pooled = jnp.concatenate(
        [packed[:, 2 * TOK : 2 * TOK + SLOTS], mate[:, 2 * TOK : 2 * TOK + SLOTS]], 1
    )

    def arrive(block, order):
        for axis in order[:2]:
            p = pos[axis]
            blank = jnp.zeros((4,) + block.shape, block.dtype)
            block = in_place(double(block, axis), (p, p ^ near, p ^ far, p ^ 2), blank)
            block = block.reshape(-1, block.shape[-1])
        pieces = [block]
        for _ in range(3):
            pieces.append(send(pieces[-1], RING[order[2]]))
        return pieces

    def project(slabs, pieces, axis):
        out = None
        for i, piece in enumerate(pieces):
            x = lax.dynamic_index_in_dim(slabs, (pos[axis] - sign * i) % 4, 0, keepdims=False)
            term = jnp.dot(x, piece, preferred_element_type=jnp.float32)
            out = term if out is None else out + term
        return out.astype(jnp.bfloat16)

    arrived = [
        arrive(rows[:, CUTS[i] : CUTS[i + 1]], ORDERS[i]) for i in range(3)
    ]
    beacon = project(pooled, arrived[0], ORDERS[0][2]).reshape(2, SLOTS, 2 * D)
    counts = jnp.stack([count, mate_count]).astype(jnp.bfloat16)
    flags = jnp.broadcast_to(counts[:, None, None], (2, 16, D))
    block_k = jnp.concatenate([beacon[..., :D], flags], 1)
    block_v = beacon[..., D:]
    block = jnp.concatenate([block_k, block_v], 1)
    block = jnp.stack([block, send(block, ACROSS)])
    every_k = double(double(block[:, :, : SLOTS + 16], "x"), "z")
    every_v = double(double(block[:, :, SLOTS + 16 :], "z"), "x")
    every_k = every_k.reshape(SPANS, 2, SLOTS + 16, D)
    every_v = every_v.reshape(SPANS, 2, SLOTS, D)

    owner = jnp.arange(SPANS, dtype=jnp.int32)

    def code(axis, at):
        d = at ^ pos[axis]
        return jnp.where(d == 0, 0, jnp.where(d == near, 1, jnp.where(d == far, 2, 3)))

    code_x, code_z = code("x", owner // 8), code("z", (owner // 2) % 4)
    code_h = (owner ^ span) % 2
    at_k = (code_z * 4 + code_x) * 2 + code_h
    at_v = (code_x * 4 + code_z) * 2 + code_h
    live = every_k[:, :, SLOTS, 0].astype(jnp.int32)

    part_a = project(both_a, arrived[1], ORDERS[1][2])
    part_b = project(both_b, arrived[2], ORDERS[2][2])

    def attention(which, valid, wide):
        here = slice(which * TOK, (which + 1) * TOK)
        info = jnp.concatenate(
            [jnp.stack([span, valid, core * (HEADS * D)]), at_k, at_v]
        )
        return attend(
            which,
            wide,
            info,
            live[:, which],
            part_a[here],
            part_b[here],
            every_k,
            every_v,
        )

    away = send(attention(1, mate_valid, False), SWAP)
    home = attention(0, valid, True)
    full = lax.dynamic_update_slice(home, away, (0, (1 - core) * (HEADS * D)))
    return full[None]


def solution(mesh):
    return jax.shard_map(
        on_device,
        mesh=mesh,
        in_specs=(
            P("dp", "ctx", None),
            P(),
            P(("dp", "ctx"), None),
            P(("dp", "ctx"), None),
            P(("dp", "ctx"), None),
            P(("dp", "ctx"), None),
            P(("dp", "ctx"), None),
            P("dp", "ctx"),
            P("dp"),
        ),
        out_specs=P("dp", "ctx", None),
        check_vma=False,
    )
```

time: 210 us -> 189 us (0.900)
  the two profiles are of different devices: /device:TPU:1 before, /device:TPU:111 now
where the time goes in v2:
time: 189 us; the launch traced here: 190 us
  waiting for transfers between devices  63.3 us (33%)
  starting transfers between devices  47 us (25%)
  Pallas kernels  38.6 us (20%)
  matrix products  16.6 us (9%)
  local copies, waits for them, and re-layouts  15.3 us (8%)
  other arithmetic  6.03 us (3%)
  between operations  2.82 us (1%)
    ppermute x33, waiting for transfers between devices, send(): return lax.ppermute(value, AXES, pairs)  63.3 us
    ppermute x33, starting transfers between devices, send(): return lax.ppermute(value, AXES, pairs)  47 us
    pallas_call x2, Pallas kernels, attend(): pl.pallas_call(functools.partial(attend_body, which, wide), out_shape=jax...  28.5 us
    dot_general x12, matrix products, project(): term = jnp.dot(x, piece, preferred_element_type=jnp.float32)  16.6 us
    pallas_call x1, Pallas kernels, norm_rows(): pl.pallas_call(norm_body, out_shape=jax.ShapeDtypeStruct((4, PACK, SLAB),...  10.1 us
    slice x2, local copies, waits for them, and re-layouts, on_device(): both_b = jnp.concatenate([packed[:, TOK:2 * TOK], mate[:, TOK:2 * TOK]], 1)  4.74 us
  transfers between devices with their start and end apart: 33, of which 20 were waited for; matrix products, arithmetic and copies ran while one was open for 15% of the time, Pallas kernels for 8%

profile of v2, /device:TPU:111, one launch (start us, length us, event | category | flops | bytes accessed | tf_op | source)
XLA Modules:
  0.0 189.6 jit_solution(9531416533803502056)
XLA Ops:
  0.0 0.7 constant_dynamic-update-slice_fusion.3
  0.7 0.7 constant_dynamic-update-slice_fusion.2
  1.4 0.7 constant_dynamic-update-slice_fusion.1
  2.2 0.7 constant_dynamic-update-slice_fusion
  2.9 0.9 select_dynamic-update-slice_fusion.1
  3.8 0.8 collective-permute-start
  6.0 0.7 reshape.56.gain_ref
  7.0 1.5 copy-done
  8.5 10.1 %shard_map.91 = bf16[4,592,896]{2,1,0:T(8,128)(2,1)} custom-call(s32[3]{0:T(128)S(1)} %pad_add_fusion.fact_ref, bf16[256,3584]{1,0:T(8,128)(2,1)S(1)} %bitcast.127, f32[1,3584]{1,0:T(1,128)S(1)} %reshape.56.gain_ref), custom_call_target="tpu_custom_call" | custom-call | tf_op jit(solution)/shard_map/pallas_call | solution.py:147
  18.9 1.3 collective-permute-start.14
  20.3 2.3 %collective-permute-done.2 = bf16[56,256]{1,0:T(8,128)(2,1)S(1)} collective-permute-done((bf16[56,256]{1,0:T(8,128)(2,1)S(1)}, bf16[56,256]{1,0:T(8,128)(2,1)S(1)}, u32[]{:S(2)}, u32[]{:S(2)}) %collective-permute-start.2) | collective-permute-done | bytes 28704 | tf_op jit(solution)/shard_map/ppermute | solution.py:70
  22.9 0.4 collective-permute-start.22
  23.7 2.0 %collective-permute-done.3 = bf16[2,56,256]{2,1,0:T(8,128)(2,1)S(1)} collective-permute-done((bf16[2,56,256]{2,1,0:T(8,128)(2,1)S(1)}, bf16[2,56,256]{2,1,0:T(8,128)(2,1)S(1)}, u32[]{:S(2)}, u32[]{:S(2)}) %collective-permute-start.3) | collective-permute-done | bytes 57376 | tf_op jit(solution)/shard_map/ppermute | solution.py:70
  25.7 0.5 collective-permute-start.4
  26.7 1.1 collective-permute-done.15
  27.8 2.4 %collective-permute-start.16 = (bf16[224,640]{1,0:T(8,128)(2,1)S(1)}, bf16[224,640]{1,0:T(8,128)(2,1)S(1)}, u32[]{:S(2)}, u32[]{:S(2)}) collective-permute-start(bf16[224,640]{1,0:T(8,128)(2,1)S(1)} %bitcast.132), channel_id=1, source_target_pairs={{0,2},{32,38},{2,0},{34,36},{4,6},{36,34},{6,4},{38,32},{64,66},{9... | collective-permute-start | bytes 860168 | tf_op jit(solution)/shard_map/ppermute | solution.py:70
  30.2 1.3 collective-permute-start.23
  31.8 2.8 %collective-permute-done.16 = bf16[224,640]{1,0:T(8,128)(2,1)S(1)} collective-permute-done((bf16[224,640]{1,0:T(8,128)(2,1)S(1)}, bf16[224,640]{1,0:T(8,128)(2,1)S(1)}, u32[]{:S(2)}, u32[]{:S(2)}) %collective-permute-start.16) | collective-permute-done | bytes 286752 | tf_op jit(solution)/shard_map/ppermute | solution.py:70
  34.7 0.7 collective-permute-done.23
  35.4 1.2 collective-permute-start.24
  36.7 6.8 %collective-permute-done.17 = bf16[2,224,640]{2,1,0:T(8,128)(2,1)S(1)} collective-permute-done((bf16[2,224,640]{2,1,0:T(8,128)(2,1)S(1)}, bf16[2,224,640]{2,1,0:T(8,128)(2,1)S(1)}, u32[]{:S(2)}, u32[]{:S(2)}) %collective-permute-start.17) | collective-permute-done | bytes 573472 | tf_op jit(solution)/shard_map/ppermute | solution.py:70
  43.6 1.2 collective-permute-start.18
  45.8 14.2 %collective-permute-done.5 = bf16[2,224,256]{2,1,0:T(8,128)(2,1)S(1)} collective-permute-done((bf16[2,224,256]{2,1,0:T(8,128)(2,1)S(1)}, bf16[2,224,256]{2,1,0:T(8,128)(2,1)S(1)}, u32[]{:S(2)}, u32[]{:S(2)}) %collective-permute-start.5) | collective-permute-done | bytes 229408 | tf_op jit(solution)/shard_map/ppermute | solution.py:70
  60.1 2.1 %collective-permute-done.18 = bf16[896,640]{1,0:T(8,128)(2,1)} collective-permute-done((bf16[896,640]{1,0:T(8,128)(2,1)S(1)}, bf16[896,640]{1,0:T(8,128)(2,1)}, u32[]{:S(2)}, u32[]{:S(2)}) %collective-permute-start.18) | collective-permute-done | bytes 1146912 | tf_op jit(solution)/shard_map/ppermute | solution.py:70
  62.7 1.4 collective-permute-start.26
  64.1 6.2 %collective-permute-done.6 = bf16[896,256]{1,0:T(8,128)(2,1)} collective-permute-done((bf16[896,256]{1,0:T(8,128)(2,1)S(1)}, bf16[896,256]{1,0:T(8,128)(2,1)}, u32[]{:S(2)}, u32[]{:S(2)}) %collective-permute-start.6) | collective-permute-done | bytes 458784 | tf_op jit(solution)/shard_map/ppermute | solution.py:70
  70.3 0.6 collective-permute-start.7
  70.9 1.1 slice.199
  72.0 2.4 %fusion.75 = (bf16[4,256,896]{2,1,0:T(8,128)(2,1)S(1)}, bf16[4,256,896]{2,1,0:T(8,128)(2,1)S(1)}) fusion(bf16[4,592,896]{2,1,0:T(8,128)(2,1)} %shard_map.91), kind=kLoop, calls=%fused_computation.180 | loop fusion | bytes 7340032 | tf_op jit(solution)/shard_map/slice | solution.py:319
  74.4 3.9 %collective-permute-done.7 = bf16[896,256]{1,0:T(8,128)(2,1)S(1)} collective-permute-done((bf16[896,256]{1,0:T(8,128)(2,1)}, bf16[896,256]{1,0:T(8,128)(2,1)S(1)}, u32[]{:S(2)}, u32[]{:S(2)}) %collective-permute-start.7) | collective-permute-done | bytes 458784 | tf_op jit(solution)/shard_map/ppermute | solution.py:70
  78.2 1.6 collective-permute-start.8
  79.9 1.3 collective-permute-start.27
  81.5 1.1 slice.200
  82.6 1.3 fusion.37
  84.3 1.8 collective-permute-done.8
  86.4 0.7 slice_convert_fusion.1
  87.1 0.6 fusion.79
  88.6 4.4 %collective-permute-start.9 = (bf16[2,144,128]{2,1,0:T(8,128)(2,1)S(1)}, bf16[2,144,128]{2,1,0:T(8,128)(2,1)S(1)}, u32[]{:S(2)}, u32[]{:S(2)}) collective-permute-start(bf16[2,144,128]{2,1,0:T(8,128)(2,1)S(1)} %get-tuple-element.29), channel_id=1, source_target_pairs={{0,1},{32,33},{2,3},{34,35},{4,5},{36,37},{6,7},{38,39},{64,65},{9... | collective-permute-start | bytes 221192 | tf_op jit(solution)/shard_map/ppermute | solution.py:70
  93.0 2.3 %fusion.74 = (bf16[4,256,896]{2,1,0:T(8,128)(2,1)S(1)}, bf16[4,256,896]{2,1,0:T(8,128)(2,1)S(1)}) fusion(bf16[4,592,896]{2,1,0:T(8,128)(2,1)} %collective-permute-done.1), kind=kLoop, calls=%fused_computation.179 | loop fusion | bytes 7340032 | tf_op jit(solution)/shard_map/slice | solution.py:319
  95.4 2.6 %fusion.11 = f32[512,512]{1,0:T(8,128)S(1)} fusion(bf16[896,512]{1,0:T(8,128)(2,1)} %collective-permute-done.25, s32[]{:T(128)S(6)} %select_n.333, bf16[4,256,896]{2,1,0:T(8,128)(2,1)S(1)} %get-tuple-element.11, bf16[4,256,896]{2,1,0:T(8,128)(2,1)S(1)} %get-tuple-element.9), kind=kOutput, calls=%fused_computation.44 | convolution fusion | flops 471597056 | bytes 5636100 | tf_op jit(solution)/shard_map/dot_general | solution.py:339
  98.0 0.7 convolution_add_fusion.5
  98.7 2.2 %fusion.24 = f32[512,640]{1,0:T(8,128)S(1)} fusion(bf16[896,640]{1,0:T(8,128)(2,1)} %collective-permute-done.18, s32[]{:T(128)S(6)} %select_n.325, bf16[4,256,896]{2,1,0:T(8,128)(2,1)S(1)} %get-tuple-element.12, bf16[4,256,896]{2,1,0:T(8,128)(2,1)S(1)} %get-tuple-element.10), kind=kOutput, calls=%fused_computation.53 | convolution fusion | flops 589037568 | bytes 6127620 | tf_op jit(solution)/shard_map/dot_general | solution.py:339
  100.9 1.0 convolution_add_fusion.2
  101.9 3.3 %convolution_add_fusion.1 = f32[512,640]{1,0:T(8,128)} fusion(f32[512,640]{1,0:T(8,128)S(1)} %convolution_add_fusion.2, bf16[896,640]{1,0:T(8,128)(2,1)} %collective-permute-done.19, s32[]{:T(128)S(6)} %select_n.327, bf16[4,256,896]{2,1,0:T(8,128)(2,1)S(1)} %get-tuple-element.12, bf16[4,256,896]{2,1,0:T(8,128)(2,1)S(1)} %get-tuple-element.10), kind=kOutput, calls=%fused_computation.17 | convolution fusion | flops 589365248 | bytes 7438340 | tf_op jit(solution)/shard_map/dot_general | solution.py:339
  105.2 1.9 convolution_add_fusion.4
  107.1 3.2 %collective-permute-start.28 = (bf16[2,2,64,128]{3,2,1,0:T(8,128)(2,1)S(1)}, bf16[2,2,64,128]{3,2,1,0:T(8,128)(2,1)S(1)}, u32[]{:S(2)}, u32[]{:S(2)}) collective-permute-start(bf16[2,2,64,128]{3,2,1,0:T(8,128)(2,1)S(1)} %pad_maximum_fusion.14), channel_id=1, source_target_pairs={{0,2},{32,38},{2,0},{34,36},{4,6},{36,34},{6,4},{38,32},{64,66},{9... | collective-permute-start | bytes 196616 | tf_op jit(solution)/shard_map/ppermute | solution.py:70
  110.3 2.3 %collective-permute-start.10 = (bf16[2,2,80,128]{3,2,1,0:T(8,128)(2,1)S(1)}, bf16[2,2,80,128]{3,2,1,0:T(8,128)(2,1)S(1)}, u32[]{:S(2)}, u32[]{:S(2)}) collective-permute-start(bf16[2,2,80,128]{3,2,1,0:T(8,128)(2,1)S(1)} %fusion.42), channel_id=1, source_target_pairs={{0,8},{32,56},{2,10},{34,58},{4,12},{36,60},{6,14},{38,62},{64,72}... | collective-permute-start | bytes 245768 | tf_op jit(solution)/shard_map/ppermute | solution.py:70
  112.8 2.1 %collective-permute-done.10 = bf16[2,2,80,128]{3,2,1,0:T(8,128)(2,1)S(1)} collective-permute-done((bf16[2,2,80,128]{3,2,1,0:T(8,128)(2,1)S(1)}, bf16[2,2,80,128]{3,2,1,0:T(8,128)(2,1)S(1)}, u32[]{:S(2)}, u32[]{:S(2)}) %collective-permute-start.10) | collective-permute-done | bytes 81952 | tf_op jit(solution)/shard_map/ppermute | solution.py:70
  115.0 0.7 fusion.1
  115.7 0.7 concatenate.64.info_ref
  116.6 2.2 %collective-permute-start.30 = (bf16[4,2,2,64,128]{4,3,2,1,0:T(8,128)(2,1)S(1)}, bf16[4,2,2,64,128]{4,3,2,1,0:T(8,128)(2,1)S(1)}, u32[]{:S(2)}, u32[]{:S(2)}) collective-permute-start(bf16[4,2,2,64,128]{4,3,2,1,0:T(8,128)(2,1)S(1)} %get-tuple-element.20), channel_id=1, source_target_pairs={{0,8},{32,56},{2,10},{34,58},{4,12},{36,60},{6,14},{38,62},{64,72}... | collective-permute-start | bytes 786440 | tf_op jit(solution)/shard_map/ppermute | solution.py:70
  119.2 1.8 collective-permute-start.12
  121.1 2.0 %collective-permute-done.30 = bf16[4,2,2,64,128]{4,3,2,1,0:T(8,128)(2,1)S(1)} collective-permute-done((bf16[4,2,2,64,128]{4,3,2,1,0:T(8,128)(2,1)S(1)}, bf16[4,2,2,64,128]{4,3,2,1,0:T(8,128)(2,1)S(1)}, u32[]{:S(2)}, u32[]{:S(2)}) %collective-permute-start.30) | collective-permute-done | bytes 262176 | tf_op jit(solution)/shard_map/ppermute | solution.py:70
  123.5 3.6 %collective-permute-done.12 = bf16[4,2,2,80,128]{4,3,2,1,0:T(8,128)(2,1)S(1)} collective-permute-done((bf16[4,2,2,80,128]{4,3,2,1,0:T(8,128)(2,1)S(1)}, bf16[4,2,2,80,128]{4,3,2,1,0:T(8,128)(2,1)S(1)}, u32[]{:S(2)}, u32[]{:S(2)}) %collective-permute-start.12) | collective-permute-done | bytes 327712 | tf_op jit(solution)/shard_map/ppermute | solution.py:70
  127.3 2.2 %fusion = bf16[512,640]{1,0:T(8,128)(2,1)S(1)} fusion(f32[512,640]{1,0:T(8,128)S(1)} %copy-done.3, bf16[896,640]{1,0:T(8,128)(2,1)} %collective-permute-done.20, s32[]{:T(128)S(6)} %select_n.329, bf16[4,256,896]{2,1,0:T(8,128)(2,1)S(1)} %get-tuple-element.12, bf16[4,256,896]{2,1,0:T(8,128)(2,1)S(1)} %copy-done.2), kind=kOutput, calls=%fused_computation.22 | convolution fusion | flops 589692928 | bytes 6782980 | tf_op jit(solution)/shard_map/dot_general | solution.py:339
  129.7 1.6 collective-permute-done.31
  131.4 8.8 %collective-permute-done.13 = bf16[2,4,2,2,80,128]{5,4,3,2,1,0:T(8,128)(2,1)S(1)} collective-permute-done((bf16[2,4,2,2,80,128]{5,4,3,2,1,0:T(8,128)(2,1)S(1)}, bf16[2,4,2,2,80,128]{5,4,3,2,1,0:T(8,128)(2,1)S(1)}, u32[]{:S(2)}, u32[]{:S(2)}) %collective-permute-start.13) | collective-permute-done | bytes 655392 | tf_op jit(solution)/shard_map/ppermute | solution.py:70
  140.3 0.6 slice_convert_fusion
  141.0 1.4 copy.11
  142.4 0.7 slice_bitcast_fusion
  143.1 12.5 %shard_map.93 = bf16[256,896]{1,0:T(8,128)(2,1)} custom-call(s32[67]{0:T(128)S(1)} %concatenate.64.info_ref, s32[32]{0:T(128)S(1)} %get-tuple-element.43.count_ref, bf16[256,640]{1,0:T(8,128)(2,1)S(1)} %get-tuple-element.13.part_a_ref, bf16[256,512]{1,0:T(8,128)(2,1)S(1)} %get-tuple-element.15.part_b_ref, bf16[32,2,80,128]{3,2,1,0:T(8,128)(2,1)S(1)} %bitcast.123, ...), custom_call_target="tpu_custom_call" | custom-call | tf_op jit(solution)/shard_map/pallas_call | solution.py:252
  155.6 16.1 %collective-permute-start.32 = (bf16[256,896]{1,0:T(8,128)(2,1)}, bf16[256,896]{1,0:T(8,128)(2,1)}, u32[]{:S(2)}, u32[]{:S(2)}) collective-permute-start(bf16[256,896]{1,0:T(8,128)(2,1)} %shard_map.93), channel_id=1, source_target_pairs={{0,32},{32,0},{2,34},{34,2},{4,36},{36,4},{6,38},{38,6},{64,96},{9... | collective-permute-start | bytes 1376264 | tf_op jit(solution)/shard_map/ppermute | solution.py:70
  171.8 15.9 %shard_map.92 = bf16[256,1792]{1,0:T(8,128)(2,1)} custom-call(s32[67]{0:T(128)S(1)} %concatenate.51.info_ref, s32[32]{0:T(128)S(1)} %get-tuple-element.44.count_ref, bf16[256,640]{1,0:T(8,128)(2,1)S(1)} %get-tuple-element.14.part_a_ref, bf16[256,512]{1,0:T(8,128)(2,1)S(1)} %get-tuple-element.16.part_b_ref, bf16[32,2,80,128]{3,2,1,0:T(8,128)(2,1)S(1)} %bitcast.124, ...), custom_call_target="tpu_custom_call" | custom-call | tf_op jit(solution)/shard_map/pallas_call | solution.py:252
  187.8 1.8 bitcast_dynamic-update-slice_fusion
  (107 shorter events, 6.7 us)
Async XLA Ops:
  3.8 3.1 %collective-permute-start = (bf16[28,1408]{1,0:T(8,128)(2,1)S(1)}, bf16[28,1408]{1,0:T(8,128)(2,1)S(1)}, u32[]{:S(2)}, u32[]{:S(2)}) collective-permute-start(bf16[28,1408]{1,0:T(8,128)(2,1)S(1)} %get-tuple-element.28), channel_id=1, source_target_pairs={{0,32},{32,0},{2,34},{34,2},{4,36},{36,4},{6,38},{38,6},{64,96},{9... | collective-permute-start | bytes 236552 | tf_op jit(solution)/shard_map/ppermute | solution.py:70
  7.0 1.5 copy-start
  18.7 62.9 %collective-permute-start.1 = (bf16[4,592,896]{2,1,0:T(8,128)(2,1)}, bf16[4,592,896]{2,1,0:T(8,128)(2,1)}, u32[]{:S(2)}, u32[]{:S(2)}) collective-permute-start(bf16[4,592,896]{2,1,0:T(8,128)(2,1)} %shard_map.91), channel_id=1, source_target_pairs={{0,32},{32,0},{2,34},{34,2},{4,36},{36,4},{6,38},{38,6},{64,96},{9... | collective-permute-start | bytes 12730376 | tf_op jit(solution)/shard_map/ppermute | solution.py:70
  18.7 3.9 %collective-permute-start.2 = (bf16[56,256]{1,0:T(8,128)(2,1)S(1)}, bf16[56,256]{1,0:T(8,128)(2,1)S(1)}, u32[]{:S(2)}, u32[]{:S(2)}) collective-permute-start(bf16[56,256]{1,0:T(8,128)(2,1)S(1)} %get-tuple-element.26), channel_id=1, source_target_pairs={{0,2},{32,38},{2,0},{34,36},{4,6},{36,34},{6,4},{38,32},{64,66},{9... | collective-permute-start | bytes 86024 | tf_op jit(solution)/shard_map/ppermute | solution.py:70
  18.7 4.2 %collective-permute-start.21 = (bf16[56,512]{1,0:T(8,128)(2,1)S(1)}, bf16[56,512]{1,0:T(8,128)(2,1)S(1)}, u32[]{:S(2)}, u32[]{:S(2)}) collective-permute-start(bf16[56,512]{1,0:T(8,128)(2,1)S(1)} %get-tuple-element.22), channel_id=1, source_target_pairs={{0,8},{32,56},{2,10},{34,58},{4,12},{36,60},{6,14},{38,62},{64,72}... | collective-permute-start | bytes 172040 | tf_op jit(solution)/shard_map/ppermute | solution.py:70
  18.9 4.5 %collective-permute-start.14 = (bf16[56,640]{1,0:T(8,128)(2,1)S(1)}, bf16[56,640]{1,0:T(8,128)(2,1)S(1)}, u32[]{:S(2)}, u32[]{:S(2)}) collective-permute-start(bf16[56,640]{1,0:T(8,128)(2,1)S(1)} %get-tuple-element.24), channel_id=1, source_target_pairs={{0,64},{32,97},{2,66},{34,99},{4,68},{36,101},{6,70},{38,103},{64,... | collective-permute-start | bytes 215048 | tf_op jit(solution)/shard_map/ppermute | solution.py:70
  22.6 3.1 %collective-permute-start.3 = (bf16[2,56,256]{2,1,0:T(8,128)(2,1)S(1)}, bf16[2,56,256]{2,1,0:T(8,128)(2,1)S(1)}, u32[]{:S(2)}, u32[]{:S(2)}) collective-permute-start(bf16[2,56,256]{2,1,0:T(8,128)(2,1)S(1)} %pad_maximum_fusion.15), channel_id=1, source_target_pairs={{0,6},{32,34},{2,4},{34,32},{4,2},{36,38},{6,0},{38,36},{64,70},{9... | collective-permute-start | bytes 172040 | tf_op jit(solution)/shard_map/ppermute | solution.py:70
  22.9 3.7 %collective-permute-start.22 = (bf16[2,56,512]{2,1,0:T(8,128)(2,1)S(1)}, bf16[2,56,512]{2,1,0:T(8,128)(2,1)S(1)}, u32[]{:S(2)}, u32[]{:S(2)}) collective-permute-start(bf16[2,56,512]{2,1,0:T(8,128)(2,1)S(1)} %pad_maximum_fusion.12), channel_id=1, source_target_pairs={{0,24},{32,40},{2,26},{34,42},{4,28},{36,44},{6,30},{38,46},{64,88... | collective-permute-start | bytes 344072 | tf_op jit(solution)/shard_map/ppermute | solution.py:70
  23.4 4.3 %collective-permute-start.15 = (bf16[2,56,640]{2,1,0:T(8,128)(2,1)S(1)}, bf16[2,56,640]{2,1,0:T(8,128)(2,1)S(1)}, u32[]{:S(2)}, u32[]{:S(2)}) collective-permute-start(bf16[2,56,640]{2,1,0:T(8,128)(2,1)S(1)} %pad_maximum_fusion.10), channel_id=1, source_target_pairs={{0,65},{32,96},{2,67},{34,98},{4,69},{36,100},{6,71},{38,102},{64,... | collective-permute-start | bytes 430088 | tf_op jit(solution)/shard_map/ppermute | solution.py:70
  25.7 19.6 %collective-permute-start.4 = (bf16[224,256]{1,0:T(8,128)(2,1)S(1)}, bf16[224,256]{1,0:T(8,128)(2,1)S(1)}, u32[]{:S(2)}, u32[]{:S(2)}) collective-permute-start(bf16[224,256]{1,0:T(8,128)(2,1)S(1)} %bitcast.149), channel_id=1, source_target_pairs={{0,8},{32,56},{2,10},{34,58},{4,12},{36,60},{6,14},{38,62},{64,72}... | collective-permute-start | bytes 344072 | tf_op jit(solution)/shard_map/ppermute | solution.py:70
  27.8 6.8 %collective-permute-start.16 = (bf16[224,640]{1,0:T(8,128)(2,1)S(1)}, bf16[224,640]{1,0:T(8,128)(2,1)S(1)}, u32[]{:S(2)}, u32[]{:S(2)}) collective-permute-start(bf16[224,640]{1,0:T(8,128)(2,1)S(1)} %bitcast.132), channel_id=1, source_target_pairs={{0,2},{32,38},{2,0},{34,36},{4,6},{36,34},{6,4},{38,32},{64,66},{9... | collective-permute-start | bytes 860168 | tf_op jit(solution)/shard_map/ppermute | solution.py:70
  30.2 5.2 %collective-permute-start.23 = (bf16[224,512]{1,0:T(8,128)(2,1)S(1)}, bf16[224,512]{1,0:T(8,128)(2,1)S(1)}, u32[]{:S(2)}, u32[]{:S(2)}) collective-permute-start(bf16[224,512]{1,0:T(8,128)(2,1)S(1)} %bitcast.135), channel_id=1, source_target_pairs={{0,64},{32,97},{2,66},{34,99},{4,68},{36,101},{6,70},{38,103},{64,... | collective-permute-start | bytes 688136 | tf_op jit(solution)/shard_map/ppermute | solution.py:70
  34.6 8.9 %collective-permute-start.17 = (bf16[2,224,640]{2,1,0:T(8,128)(2,1)S(1)}, bf16[2,224,640]{2,1,0:T(8,128)(2,1)S(1)}, u32[]{:S(2)}, u32[]{:S(2)}) collective-permute-start(bf16[2,224,640]{2,1,0:T(8,128)(2,1)S(1)} %pad_maximum_fusion.3), channel_id=1, source_target_pairs={{0,6},{32,34},{2,4},{34,32},{4,2},{36,38},{6,0},{38,36},{64,70},{9... | collective-permute-start | bytes 1720328 | tf_op jit(solution)/shard_map/ppermute | solution.py:70
  35.4 9.4 %collective-permute-start.24 = (bf16[2,224,512]{2,1,0:T(8,128)(2,1)S(1)}, bf16[2,224,512]{2,1,0:T(8,128)(2,1)S(1)}, u32[]{:S(2)}, u32[]{:S(2)}) collective-permute-start(bf16[2,224,512]{2,1,0:T(8,128)(2,1)S(1)} %pad_maximum_fusion.5), channel_id=1, source_target_pairs={{0,65},{32,96},{2,67},{34,98},{4,69},{36,100},{6,71},{38,102},{64,... | collective-permute-start | bytes 1376264 | tf_op jit(solution)/shard_map/ppermute | solution.py:70
  43.6 18.5 %collective-permute-start.18 = (bf16[896,640]{1,0:T(8,128)(2,1)S(1)}, bf16[896,640]{1,0:T(8,128)(2,1)}, u32[]{:S(2)}, u32[]{:S(2)}) collective-permute-start(bf16[896,640]{1,0:T(8,128)(2,1)S(1)} %bitcast.128), channel_id=1, source_target_pairs={{0,8},{32,56},{2,10},{34,58},{4,12},{36,60},{6,14},{38,62},{64,72}... | collective-permute-start | bytes 3440648 | tf_op jit(solution)/shard_map/ppermute | solution.py:70
  44.9 17.3 %copy-start.4 = (bf16[4,224,512]{2,1,0:T(8,128)(2,1)}, bf16[4,224,512]{2,1,0:T(8,128)(2,1)S(1)}, u32[]{:S(2)}) copy-start(bf16[4,224,512]{2,1,0:T(8,128)(2,1)S(1)} %slice_dynamic-update-slice_fusion.2) | copy-start | bytes 2752516
  44.9 17.8 %collective-permute-start.25 = (bf16[896,512]{1,0:T(8,128)(2,1)S(1)}, bf16[896,512]{1,0:T(8,128)(2,1)}, u32[]{:S(2)}, u32[]{:S(2)}) collective-permute-start(bf16[896,512]{1,0:T(8,128)(2,1)S(1)} %bitcast.130), channel_id=1, source_target_pairs={{0,2},{32,38},{2,4},{34,32},{4,6},{36,34},{6,0},{38,36},{64,66},{9... | collective-permute-start | bytes 2752520 | tf_op jit(solution)/shard_map/ppermute | solution.py:70
  45.4 14.7 %collective-permute-start.5 = (bf16[2,224,256]{2,1,0:T(8,128)(2,1)S(1)}, bf16[2,224,256]{2,1,0:T(8,128)(2,1)S(1)}, u32[]{:S(2)}, u32[]{:S(2)}) collective-permute-start(bf16[2,224,256]{2,1,0:T(8,128)(2,1)S(1)} %pad_maximum_fusion.8), channel_id=1, source_target_pairs={{0,24},{32,40},{2,26},{34,42},{4,28},{36,44},{6,30},{38,46},{64,88... | collective-permute-start | bytes 688136 | tf_op jit(solution)/shard_map/ppermute | solution.py:70
  62.2 18.9 %collective-permute-start.19 = (bf16[896,640]{1,0:T(8,128)(2,1)}, bf16[896,640]{1,0:T(8,128)(2,1)}, u32[]{:S(2)}, u32[]{:S(2)}) collective-permute-start(bf16[896,640]{1,0:T(8,128)(2,1)} %collective-permute-done.18), channel_id=1, source_target_pairs={{0,8},{32,56},{2,10},{34,58},{4,12},{36,60},{6,14},{38,62},{64,72}... | collective-permute-start | bytes 3440648 | tf_op jit(solution)/shard_map/ppermute | solution.py:70
  62.5 7.8 %collective-permute-start.6 = (bf16[896,256]{1,0:T(8,128)(2,1)S(1)}, bf16[896,256]{1,0:T(8,128)(2,1)}, u32[]{:S(2)}, u32[]{:S(2)}) collective-permute-start(bf16[896,256]{1,0:T(8,128)(2,1)S(1)} %bitcast.138), channel_id=1, source_target_pairs={{0,64},{32,97},{2,66},{34,99},{4,68},{36,101},{6,70},{38,103},{64,... | collective-permute-start | bytes 1376264 | tf_op jit(solution)/shard_map/ppermute | solution.py:70
  62.7 17.2 %collective-permute-start.26 = (bf16[896,512]{1,0:T(8,128)(2,1)}, bf16[896,512]{1,0:T(8,128)(2,1)}, u32[]{:S(2)}, u32[]{:S(2)}) collective-permute-start(bf16[896,512]{1,0:T(8,128)(2,1)} %collective-permute-done.25), channel_id=1, source_target_pairs={{0,2},{32,38},{2,4},{34,32},{4,6},{36,34},{6,0},{38,36},{64,66},{9... | collective-permute-start | bytes 2752520 | tf_op jit(solution)/shard_map/ppermute | solution.py:70
  70.3 7.9 %collective-permute-start.7 = (bf16[896,256]{1,0:T(8,128)(2,1)}, bf16[896,256]{1,0:T(8,128)(2,1)S(1)}, u32[]{:S(2)}, u32[]{:S(2)}) collective-permute-start(bf16[896,256]{1,0:T(8,128)(2,1)} %collective-permute-done.6), channel_id=1, source_target_pairs={{0,64},{32,97},{2,66},{34,99},{4,68},{36,101},{6,70},{38,103},{64,... | collective-permute-start | bytes 1376264 | tf_op jit(solution)/shard_map/ppermute | solution.py:70
  78.2 7.9 %collective-permute-start.8 = (bf16[896,256]{1,0:T(8,128)(2,1)S(1)}, bf16[896,256]{1,0:T(8,128)(2,1)S(1)}, u32[]{:S(2)}, u32[]{:S(2)}) collective-permute-start(bf16[896,256]{1,0:T(8,128)(2,1)S(1)} %collective-permute-done.7), channel_id=1, source_target_pairs={{0,64},{32,97},{2,66},{34,99},{4,68},{36,101},{6,70},{38,103},{64,... | collective-permute-start | bytes 1376264 | tf_op jit(solution)/shard_map/ppermute | solution.py:70
  79.9 35.1 %collective-permute-start.27 = (bf16[896,512]{1,0:T(8,128)(2,1)}, bf16[896,512]{1,0:T(8,128)(2,1)S(1)}, u32[]{:S(2)}, u32[]{:S(2)}) collective-permute-start(bf16[896,512]{1,0:T(8,128)(2,1)} %collective-permute-done.26), channel_id=1, source_target_pairs={{0,2},{32,38},{2,4},{34,32},{4,6},{36,34},{6,0},{38,36},{64,66},{9... | collective-permute-start | bytes 2752520 | tf_op jit(solution)/shard_map/ppermute | solution.py:70
  81.1 46.2 %collective-permute-start.20 = (bf16[896,640]{1,0:T(8,128)(2,1)}, bf16[896,640]{1,0:T(8,128)(2,1)}, u32[]{:S(2)}, u32[]{:S(2)}) collective-permute-start(bf16[896,640]{1,0:T(8,128)(2,1)} %collective-permute-done.19), channel_id=1, source_target_pairs={{0,8},{32,56},{2,10},{34,58},{4,12},{36,60},{6,14},{38,62},{64,72}... | collective-permute-start | bytes 3440648 | tf_op jit(solution)/shard_map/ppermute | solution.py:70
  88.6 18.5 %collective-permute-start.9 = (bf16[2,144,128]{2,1,0:T(8,128)(2,1)S(1)}, bf16[2,144,128]{2,1,0:T(8,128)(2,1)S(1)}, u32[]{:S(2)}, u32[]{:S(2)}) collective-permute-start(bf16[2,144,128]{2,1,0:T(8,128)(2,1)S(1)} %get-tuple-element.29), channel_id=1, source_target_pairs={{0,1},{32,33},{2,3},{34,35},{4,5},{36,37},{6,7},{38,39},{64,65},{9... | collective-permute-start | bytes 221192 | tf_op jit(solution)/shard_map/ppermute | solution.py:70
  95.4 6.5 %copy-start.1 = (bf16[4,256,896]{2,1,0:T(8,128)(2,1)}, bf16[4,256,896]{2,1,0:T(8,128)(2,1)S(1)}, u32[]{:S(2)}) copy-start(bf16[4,256,896]{2,1,0:T(8,128)(2,1)S(1)} %get-tuple-element.10) | copy-start | bytes 5505028
  95.4 2.6 %copy-start.5 = (bf16[4,224,512]{2,1,0:T(8,128)(2,1)S(1)}, bf16[4,224,512]{2,1,0:T(8,128)(2,1)}, u32[]{:S(2)}) copy-start(bf16[4,224,512]{2,1,0:T(8,128)(2,1)} %copy-done.4) | copy-start | bytes 2752516
  107.1 5.5 %collective-permute-start.28 = (bf16[2,2,64,128]{3,2,1,0:T(8,128)(2,1)S(1)}, bf16[2,2,64,128]{3,2,1,0:T(8,128)(2,1)S(1)}, u32[]{:S(2)}, u32[]{:S(2)}) collective-permute-start(bf16[2,2,64,128]{3,2,1,0:T(8,128)(2,1)S(1)} %pad_maximum_fusion.14), channel_id=1, source_target_pairs={{0,2},{32,38},{2,0},{34,36},{4,6},{36,34},{6,4},{38,32},{64,66},{9... | collective-permute-start | bytes 196616 | tf_op jit(solution)/shard_map/ppermute | solution.py:70
  110.3 4.6 %collective-permute-start.10 = (bf16[2,2,80,128]{3,2,1,0:T(8,128)(2,1)S(1)}, bf16[2,2,80,128]{3,2,1,0:T(8,128)(2,1)S(1)}, u32[]{:S(2)}, u32[]{:S(2)}) collective-permute-start(bf16[2,2,80,128]{3,2,1,0:T(8,128)(2,1)S(1)} %fusion.42), channel_id=1, source_target_pairs={{0,8},{32,56},{2,10},{34,58},{4,12},{36,60},{6,14},{38,62},{64,72}... | collective-permute-start | bytes 245768 | tf_op jit(solution)/shard_map/ppermute | solution.py:70
  112.7 3.9 %collective-permute-start.29 = (bf16[2,2,2,64,128]{4,3,2,1,0:T(8,128)(2,1)S(1)}, bf16[2,2,2,64,128]{4,3,2,1,0:T(8,128)(2,1)S(1)}, u32[]{:S(2)}, u32[]{:S(2)}) collective-permute-start(bf16[2,2,2,64,128]{4,3,2,1,0:T(8,128)(2,1)S(1)} %pad_maximum_fusion.11), channel_id=1, source_target_pairs={{0,6},{32,34},{2,4},{34,32},{4,2},{36,38},{6,0},{38,36},{64,70},{9... | collective-permute-start | bytes 393224 | tf_op jit(solution)/shard_map/ppermute | solution.py:70
  114.9 4.2 %collective-permute-start.11 = (bf16[2,2,2,80,128]{4,3,2,1,0:T(8,128)(2,1)S(1)}, bf16[2,2,2,80,128]{4,3,2,1,0:T(8,128)(2,1)S(1)}, u32[]{:S(2)}, u32[]{:S(2)}) collective-permute-start(bf16[2,2,2,80,128]{4,3,2,1,0:T(8,128)(2,1)S(1)} %pad_maximum_fusion.9), channel_id=1, source_target_pairs={{0,24},{32,40},{2,26},{34,42},{4,28},{36,44},{6,30},{38,46},{64,88... | collective-permute-start | bytes 491528 | tf_op jit(solution)/shard_map/ppermute | solution.py:70
  116.6 6.5 %collective-permute-start.30 = (bf16[4,2,2,64,128]{4,3,2,1,0:T(8,128)(2,1)S(1)}, bf16[4,2,2,64,128]{4,3,2,1,0:T(8,128)(2,1)S(1)}, u32[]{:S(2)}, u32[]{:S(2)}) collective-permute-start(bf16[4,2,2,64,128]{4,3,2,1,0:T(8,128)(2,1)S(1)} %get-tuple-element.20), channel_id=1, source_target_pairs={{0,8},{32,56},{2,10},{34,58},{4,12},{36,60},{6,14},{38,62},{64,72}... | collective-permute-start | bytes 786440 | tf_op jit(solution)/shard_map/ppermute | solution.py:70
  119.2 8.1 %copy-start.2 = (bf16[4,256,896]{2,1,0:T(8,128)(2,1)S(1)}, bf16[4,256,896]{2,1,0:T(8,128)(2,1)}, u32[]{:S(2)}) copy-start(bf16[4,256,896]{2,1,0:T(8,128)(2,1)} %copy-done.1) | copy-start | bytes 5505028
  119.2 8.1 %copy-start.3 = (f32[512,640]{1,0:T(8,128)S(1)}, f32[512,640]{1,0:T(8,128)}, u32[]{:S(2)}) copy-start(f32[512,640]{1,0:T(8,128)} %convolution_add_fusion.1) | copy-start | bytes 3932164
  119.2 8.0 %collective-permute-start.12 = (bf16[4,2,2,80,128]{4,3,2,1,0:T(8,128)(2,1)S(1)}, bf16[4,2,2,80,128]{4,3,2,1,0:T(8,128)(2,1)S(1)}, u32[]{:S(2)}, u32[]{:S(2)}) collective-permute-start(bf16[4,2,2,80,128]{4,3,2,1,0:T(8,128)(2,1)S(1)} %get-tuple-element.18), channel_id=1, source_target_pairs={{0,2},{32,38},{2,0},{34,36},{4,6},{36,34},{6,4},{38,32},{64,66},{9... | collective-permute-start | bytes 983048 | tf_op jit(solution)/shard_map/ppermute | solution.py:70
  123.2 8.1 %collective-permute-start.31 = (bf16[2,4,2,2,64,128]{5,4,3,2,1,0:T(8,128)(2,1)S(1)}, bf16[2,4,2,2,64,128]{5,4,3,2,1,0:T(8,128)(2,1)S(1)}, u32[]{:S(2)}, u32[]{:S(2)}) collective-permute-start(bf16[2,4,2,2,64,128]{5,4,3,2,1,0:T(8,128)(2,1)S(1)} %pad_maximum_fusion.4), channel_id=1, source_target_pairs={{0,24},{32,40},{2,26},{34,42},{4,28},{36,44},{6,30},{38,46},{64,88... | collective-permute-start | bytes 1572872 | tf_op jit(solution)/shard_map/ppermute | solution.py:70
  127.2 13.0 %collective-permute-start.13 = (bf16[2,4,2,2,80,128]{5,4,3,2,1,0:T(8,128)(2,1)S(1)}, bf16[2,4,2,2,80,128]{5,4,3,2,1,0:T(8,128)(2,1)S(1)}, u32[]{:S(2)}, u32[]{:S(2)}) collective-permute-start(bf16[2,4,2,2,80,128]{5,4,3,2,1,0:T(8,128)(2,1)S(1)} %pad_maximum_fusion.2), channel_id=1, source_target_pairs={{0,6},{32,34},{2,4},{34,32},{4,2},{36,38},{6,0},{38,36},{64,70},{9... | collective-permute-start | bytes 1966088 | tf_op jit(solution)/shard_map/ppermute | solution.py:70
  155.6 32.2 %collective-permute-start.32 = (bf16[256,896]{1,0:T(8,128)(2,1)}, bf16[256,896]{1,0:T(8,128)(2,1)}, u32[]{:S(2)}, u32[]{:S(2)}) collective-permute-start(bf16[256,896]{1,0:T(8,128)(2,1)} %shard_map.93), channel_id=1, source_target_pairs={{0,32},{32,0},{2,34},{34,2},{4,36},{36,4},{6,38},{38,6},{64,96},{9... | collective-permute-start | bytes 1376264 | tf_op jit(solution)/shard_map/ppermute | solution.py:70

commit v3 on v2

--- a/solution.py
+++ b/solution.py
@@ -40,12 +40,12 @@
 
 
 SWAP = make_perm(lambda x, y, z, c: (x, y, z, 1 - c))
+MATE = make_perm(lambda x, y, z, c: (x, y ^ 1, z, c))
+ACROSS = make_perm(lambda x, y, z, c: (x, y ^ 3, z, c))
 RING = {
     "x": make_perm(lambda x, y, z, c: (x + 1 - 2 * c, y, z, c)),
-    "y": make_perm(lambda x, y, z, c: (x, y + 1 - 2 * c, z, c)),
     "z": make_perm(lambda x, y, z, c: (x, y, z + 1 - 2 * c, c)),
 }
-ACROSS = make_perm(lambda x, y, z, c: (x, y + 2, z, c))
 
 
 def flip(axis, turn):
@@ -57,28 +57,24 @@
     return make_perm(partner)
 
 
-FLIP = {(axis, turn): flip(axis, turn) for axis in "xyz" for turn in (0, 1)}
-
-ORDERS = (("z", "x", "y"), ("y", "z", "x"), ("x", "y", "z"))
-CUTS = (0, 256, 896, 1408)
-KEPT = 3
-SLAB = WIDTH // 4
-PACK = 2 * TOK + SLOTS + 16
+FLIP = {(axis, turn): flip(axis, turn) for axis in "xz" for turn in (0, 1)}
+
+CUTS = (0, 256, 640, 1408)
+KEPT = 1
+HALF = WIDTH // 2
 
 
 def send(value, pairs):
     return lax.ppermute(value, AXES, pairs)
 
 
-def feature_runs(order):
-    first, second, last = order
+def feature_runs():
     starts = []
-    for i in range(4):
-        for j in range(4):
-            for k in range(4):
-                at = {last: i, second: j, first: k}
-                for c in range(2):
-                    starts.append(device_id(at["x"], at["y"], at["z"], c) * ROWS)
+    for c in range(2):
+        for z in range(4):
+            for x in range(4):
+                for y in (0, 1, 2, 3):
+                    starts.append(device_id(x, y, z, c) * ROWS)
     source = np.concatenate([np.arange(s, s + ROWS) for s in starts])
     tiles = []
     for tile in range(WIDTH // 128):
@@ -95,9 +91,9 @@
     return tiles
 
 
-def reorder(plain_ref, out_ref, order, count, out_rows):
+def reorder(plain_ref, out_ref, count, out_rows):
     lane = lax.broadcasted_iota(jnp.int32, (count, 128), 1)
-    for tile, runs in enumerate(feature_runs(order)):
+    for tile, runs in enumerate(feature_runs()):
         joined = jnp.zeros((count, 128), jnp.float32)
         for first, end, feature in runs:
             block, offset = divmod(feature, 128)
@@ -106,24 +102,22 @@
             if shift:
                 piece = pltpu.roll(piece, shift, 1)
             joined = jnp.where((lane >= first) & (lane < end), piece, joined)
-        slab, column = divmod(tile, SLAB // 128)
-        out_ref[slab, out_rows, column * 128 : (column + 1) * 128] = joined.astype(jnp.bfloat16)
-
-
-def norm_body(fact_ref, tokens_ref, gain_ref, out_ref, plain_ref, normed_ref):
+        side, column = divmod(tile, HALF // 128)
+        out_ref[side, out_rows, column * 128 : (column + 1) * 128] = joined.astype(jnp.bfloat16)
+
+
+def norm_body(fact_ref, tokens_ref, gain_ref, out_ref, pool_ref, plain_ref, normed_ref):
     rows = 64
     level, valid, count = fact_ref[0], fact_ref[1], fact_ref[2]
 
     @pl.loop(0, TOK // rows)
     def _(step):
         here = pl.ds(pl.multiple_of(step * rows, rows), rows)
-        below = pl.ds(pl.multiple_of(step * rows + TOK, rows), rows)
         values = tokens_ref[here, :].astype(jnp.float32)
         factor = lax.rsqrt(jnp.mean(values * values, axis=-1, keepdims=True) + EPS)
         plain_ref[...] = values * factor * gain_ref[...]
         normed_ref[here, :] = plain_ref[...].astype(jnp.bfloat16)
-        reorder(plain_ref, out_ref, ORDERS[1], rows, here)
-        reorder(plain_ref, out_ref, ORDERS[2], rows, below)
+        reorder(plain_ref, out_ref, rows, here)
 
     shift = level + 2
     live = jnp.right_shift(TOK, shift)
@@ -136,20 +130,23 @@
         window.astype(jnp.bfloat16), normed_ref[...], preferred_element_type=jnp.float32
     )
     plain_ref[...] = sums / size
-    reorder(plain_ref, out_ref, ORDERS[0], SLOTS, pl.ds(2 * TOK, SLOTS))
-    row = lax.broadcasted_iota(jnp.int32, (16, SLAB), 0)
+    reorder(plain_ref, pool_ref, SLOTS, pl.ds(0, SLOTS))
+    row = lax.broadcasted_iota(jnp.int32, (16, HALF), 0)
     facts = jnp.where(row < 8, count, valid).astype(jnp.float32).astype(jnp.bfloat16)
-    for slab in range(4):
-        out_ref[slab, pl.ds(2 * TOK + SLOTS, 16), :] = facts
+    for side in range(2):
+        pool_ref[side, pl.ds(SLOTS, 16), :] = facts
 
 
 def norm_rows(facts, tokens, gain):
+    vmem = pl.BlockSpec(memory_space=pltpu.VMEM)
     return pl.pallas_call(
         norm_body,
-        out_shape=jax.ShapeDtypeStruct((4, PACK, SLAB), jnp.bfloat16),
-        in_specs=[pl.BlockSpec(memory_space=pltpu.SMEM)]
-        + [pl.BlockSpec(memory_space=pltpu.VMEM)] * 2,
-        out_specs=pl.BlockSpec(memory_space=pltpu.VMEM),
+        out_shape=[
+            jax.ShapeDtypeStruct((2, TOK, HALF), jnp.bfloat16),
+            jax.ShapeDtypeStruct((2, SLOTS + 16, HALF), jnp.bfloat16),
+        ],
+        in_specs=[pl.BlockSpec(memory_space=pltpu.SMEM), vmem, vmem],
+        out_specs=[vmem, vmem],
         scratch_shapes=[
             pltpu.VMEM((64, WIDTH), jnp.float32),
             pltpu.VMEM((TOK, WIDTH), jnp.bfloat16),
@@ -162,16 +159,16 @@
 ROOM = SPANS * SLOTS + BLOCK
 
 
-def attend_body(which, wide, info_ref, count_ref, part_a_ref, part_b_ref, far_k_ref, far_v_ref, *rest):
+def attend_body(wide, info_ref, count_ref, part_a_ref, part_b_ref, far_k_ref, far_v_ref, *rest):
     out_ref, near_ref, keys_ref, values_ref, bias_ref, score_ref = rest
-    span, valid, column = info_ref[0], info_ref[1], info_ref[2]
+    span, valid, column, which = info_ref[0], info_ref[1], info_ref[2], info_ref[3]
 
     lane = lax.broadcasted_iota(jnp.int32, (1, ROOM), 1)
     bias_ref[...] = jnp.full((1, ROOM), FILL, jnp.float32)
 
     def pack(i, at):
-        place_k, place_v = info_ref[3 + i], info_ref[3 + SPANS + i]
-        count = count_ref[place_k]
+        place_k, place_v = info_ref[4 + i], info_ref[4 + SPANS + i]
+        count = count_ref[place_k * 2 + which]
         here = pl.ds(pl.multiple_of(at, 16), SLOTS)
         keys_ref[here, :] = far_k_ref[place_k, which, :SLOTS, :]
         values_ref[here, :] = far_v_ref[place_v, which]
@@ -246,11 +243,11 @@
             out_ref[:, head * D : (head + 1) * D] = result
 
 
-def attend(which, wide, info, counts, part_a, part_b, far_k, far_v):
+def attend(wide, info, counts, part_a, part_b, far_k, far_v):
     columns = 2 * HEADS * D if wide else HEADS * D
     smem, vmem = pl.BlockSpec(memory_space=pltpu.SMEM), pl.BlockSpec(memory_space=pltpu.VMEM)
     return pl.pallas_call(
-        functools.partial(attend_body, which, wide),
+        functools.partial(attend_body, wide),
         out_shape=jax.ShapeDtypeStruct((TOK, columns), jnp.bfloat16),
         in_specs=[smem, smem, vmem, vmem, vmem, vmem],
         out_specs=vmem,
@@ -280,10 +277,14 @@
 def on_device(tokens, gain, w_query, w_key, w_value, w_mark_key, w_mark_value, level, hist_len):
     dp = lax.axis_index("dp")
     span = lax.axis_index("ctx")
-    core = dp % 2
-    pos = {"x": span // 8, "z": (span // 2) % 4, "y": (span % 2) * 2 + dp // 2}
+    core, low, high = dp % 2, dp // 2, span % 2
+    head = low ^ high
+    pos = {"x": span // 8, "z": (span // 2) % 4}
     sign = 1 - 2 * core
     near, far = 1 + 2 * core, 3 - 2 * core
+
+    def order(first, one, two):
+        return jnp.where(first == 0, jnp.concatenate([one, two], 0), jnp.concatenate([two, one], 0))
 
     def half(which):
         def cut(w, size):
@@ -300,55 +301,73 @@
             axis=1,
         )
 
-    mine = half(core)
-    other = send(half(1 - core), SWAP)
-    rows = jnp.where(
-        core == 0, jnp.concatenate([mine, other], 0), jnp.concatenate([other, mine], 0)
-    )
-    rows, tokens = lax.optimization_barrier((rows, tokens))
+    mine = half(head)
+    rows = order(low, mine, send(half(1 - head), MATE))
 
     begin = span * TOK
     stride = jnp.left_shift(jnp.int32(4), level[0, 0])
     valid = jnp.clip(hist_len[0] - begin, 0, TOK)
     count = jnp.minimum(TOK // stride, (valid + stride - 1) // stride)
-    packed = norm_rows(jnp.stack([level[0, 0], valid, count]), tokens[0], gain)
-    mate = send(packed, SWAP)
-    facts = mate[0, 2 * TOK + SLOTS :, 0].astype(jnp.int32)
+    normed, pooled = norm_rows(jnp.stack([level[0, 0], valid, count]), tokens[0], gain)
+    mate_pooled = send(pooled, MATE)
+    normed, mate_pooled = lax.optimization_barrier((normed, mate_pooled))
+    both = jnp.concatenate([normed, send(normed, MATE)], 1)
+    facts = mate_pooled[0, SLOTS:, 0].astype(jnp.int32)
     mate_count, mate_valid = facts[0], facts[8]
-    both_a = jnp.concatenate([packed[:, :TOK], mate[:, :TOK]], 1)
-    both_b = jnp.concatenate([packed[:, TOK : 2 * TOK], mate[:, TOK : 2 * TOK]], 1)
-    pooled = jnp.concatenate(
-        [packed[:, 2 * TOK : 2 * TOK + SLOTS], mate[:, 2 * TOK : 2 * TOK + SLOTS]], 1
-    )
-
-    def arrive(block, order):
-        for axis in order[:2]:
-            p = pos[axis]
-            blank = jnp.zeros((4,) + block.shape, block.dtype)
-            block = in_place(double(block, axis), (p, p ^ near, p ^ far, p ^ 2), blank)
-            block = block.reshape(-1, block.shape[-1])
+    both_pooled = jnp.concatenate([pooled[:, :SLOTS], mate_pooled[:, :SLOTS]], 1)
+
+    rows = order(high, rows, send(rows, ACROSS))
+
+    def blank(shape, after):
+        return lax.optimization_barrier((jnp.zeros(shape, jnp.bfloat16), after))[0]
+
+    def second(block, axis):
+        p = pos[axis]
+        joined = blank((4,) + block.shape, block)
+        joined = in_place(double(block, axis), (p, p ^ near, p ^ far, p ^ 2), joined)
+        return joined.reshape(-1, block.shape[-1])
+
+    def ring(block, axis):
         pieces = [block]
         for _ in range(3):
-            pieces.append(send(pieces[-1], RING[order[2]]))
-        return pieces
-
-    def project(slabs, pieces, axis):
-        out = None
-        for i, piece in enumerate(pieces):
-            x = lax.dynamic_index_in_dim(slabs, (pos[axis] - sign * i) % 4, 0, keepdims=False)
-            term = jnp.dot(x, piece, preferred_element_type=jnp.float32)
-            out = term if out is None else out + term
-        return out.astype(jnp.bfloat16)
-
-    arrived = [
-        arrive(rows[:, CUTS[i] : CUTS[i + 1]], ORDERS[i]) for i in range(3)
-    ]
-    beacon = project(pooled, arrived[0], ORDERS[0][2]).reshape(2, SLOTS, 2 * D)
+            pieces.append(send(pieces[-1], RING[axis]))
+        return pieces, [(pos[axis] - sign * i) % 4 for i in range(4)]
+
+    early = second(rows[:, : CUTS[2]], "x")
+    late = second(rows[:, CUTS[2] :], "z")
+
+    z = pos["z"]
+    part_m = double(early[:, : CUTS[1]], "z")
+    part_m = in_place(part_m, (z, z ^ near, z ^ far, z ^ 2), blank(part_m.shape, part_m))
+    part_m = part_m.reshape(HALF, -1)
+    early, part_m = lax.optimization_barrier((early, part_m))
+
+    pieces, slots = ring(early[:, CUTS[1] :], "z")
+    part_a = in_place(pieces, slots, blank((4,) + pieces[0].shape, pieces[0])).reshape(HALF, -1)
+
+    pieces, slots = ring(late, "x")
+    part_b = blank((4, 4, 4 * ROWS, late.shape[-1]), late)
+    for piece, slot in zip(pieces, slots):
+        piece = piece.reshape(4, 1, 4 * ROWS, -1)
+        part_b = lax.dynamic_update_slice_in_dim(part_b, piece, slot, 1)
+    part_b = part_b.reshape(HALF, -1)
+
+    def project(x, own):
+        other = send(own, SWAP)
+
+        def term(side, w):
+            part = lax.dynamic_index_in_dim(x, side, 0, keepdims=False)
+            return jnp.dot(part, w, preferred_element_type=jnp.float32)
+
+        return (term(core, own) + term(1 - core, other)).astype(jnp.bfloat16)
+
+    beacon = project(both_pooled, part_m).reshape(2, SLOTS, 2 * D)
     counts = jnp.stack([count, mate_count]).astype(jnp.bfloat16)
     flags = jnp.broadcast_to(counts[:, None, None], (2, 16, D))
     block_k = jnp.concatenate([beacon[..., :D], flags], 1)
     block_v = beacon[..., D:]
     block = jnp.concatenate([block_k, block_v], 1)
+    block = order(low, block[:1], block[1:])
     block = jnp.stack([block, send(block, ACROSS)])
     every_k = double(double(block[:, :, : SLOTS + 16], "x"), "z")
     every_v = double(double(block[:, :, SLOTS + 16 :], "z"), "x")
@@ -365,30 +384,29 @@
     code_h = (owner ^ span) % 2
     at_k = (code_z * 4 + code_x) * 2 + code_h
     at_v = (code_x * 4 + code_z) * 2 + code_h
-    live = every_k[:, :, SLOTS, 0].astype(jnp.int32)
-
-    part_a = project(both_a, arrived[1], ORDERS[1][2])
-    part_b = project(both_b, arrived[2], ORDERS[2][2])
+    live = every_k[:, :, SLOTS, 0].astype(jnp.int32).reshape(2 * SPANS)
+
+    part_a = project(both, part_a)
+    part_b = project(both, part_b)
 
     def attention(which, valid, wide):
         here = slice(which * TOK, (which + 1) * TOK)
         info = jnp.concatenate(
-            [jnp.stack([span, valid, core * (HEADS * D)]), at_k, at_v]
+            [jnp.stack([span, valid, head * (HEADS * D), low ^ which]), at_k, at_v]
         )
         return attend(
-            which,
             wide,
             info,
-            live[:, which],
+            live,
             part_a[here],
             part_b[here],
             every_k,
             every_v,
         )
 
-    away = send(attention(1, mate_valid, False), SWAP)
+    away = send(attention(1, mate_valid, False), MATE)
     home = attention(0, valid, True)
-    full = lax.dynamic_update_slice(home, away, (0, (1 - core) * (HEADS * D)))
+    full = lax.dynamic_update_slice(home, away, (0, (1 - head) * (HEADS * D)))
     return full[None]
 
 

time: 189 us -> 155 us (0.82)
  the two profiles are of different devices: /device:TPU:111 before, /device:TPU:6 now
where the time goes in v3:
time: 155 us; the launch traced here: 154 us
  waiting for transfers between devices  50 us (32%)
  starting transfers between devices  31.9 us (21%)
  Pallas kernels  29.5 us (19%)
  local copies, waits for them, and re-layouts  18.8 us (12%)
  matrix products  13 us (8%)
  other arithmetic  8.07 us (5%)
  between operations  2.7 us (2%)
    ppermute x29, waiting for transfers between devices, send(): return lax.ppermute(value, AXES, pairs)  50 us
    ppermute x29, starting transfers between devices, send(): return lax.ppermute(value, AXES, pairs)  31.9 us
    pallas_call x2, Pallas kernels, attend(): pl.pallas_call(functools.partial(attend_body, wide), out_shape=jax.ShapeD...  24 us
    dot_general x6, matrix products, term(): return jnp.dot(part, w, preferred_element_type=jnp.float32)  13 us
    pallas_call x1, Pallas kernels, norm_rows(): pl.pallas_call(norm_body, out_shape=[jax.ShapeDtypeStruct((2, TOK, HALF),...  5.55 us
    dynamic_update_slice x4, local copies, waits for them, and re-layouts, on_device(): part_b = lax.dynamic_update_slice_in_dim(part_b, piece, slot, 1)  3.66 us
    dynamic_update_slice x16, local copies, waits for them, and re-layouts, in_place(): joined = lax.dynamic_update_slice_in_dim(joined, pieces[i][None], slot, 0)  3.3 us
    broadcast_in_dim x5, local copies, waits for them, and re-layouts, blank(): return lax.optimization_barrier((jnp.zeros(shape, jnp.bfloat16), after))[0]  3.14 us
  transfers between devices with their start and end apart: 29, of which 16 were waited for; matrix products, arithmetic and copies ran while one was open for 17% of the time, Pallas kernels for 12%

profile of v3, /device:TPU:6, one launch (start us, length us, event | category | flops | bytes accessed | tf_op | source)
XLA Modules:
  0.0 154.0 jit_solution(13463898529670799185)
XLA Ops:
  0.0 0.7 constant_dynamic-update-slice_fusion.3
  0.7 0.7 constant_dynamic-update-slice_fusion.2
  1.4 0.7 constant_dynamic-update-slice_fusion.1
  2.2 0.7 constant_dynamic-update-slice_fusion
  2.9 0.9 select_dynamic-update-slice_fusion.1
  3.8 1.7 %collective-permute-start.1 = (bf16[28,1408]{1,0:T(8,128)(2,1)S(1)}, bf16[28,1408]{1,0:T(8,128)(2,1)S(1)}, u32[]{:S(2)}, u32[]{:S(2)}) collective-permute-start(bf16[28,1408]{1,0:T(8,128)(2,1)S(1)} %get-tuple-element.40), channel_id=1, source_target_pairs={{0,64},{32,96},{2,66},{34,98},{4,68},{36,100},{6,70},{38,102},{64,... | collective-permute-start | bytes 236552 | tf_op jit(solution)/shard_map/ppermute | solution.py:68
  5.4 3.0 %collective-permute-done.1 = bf16[28,1408]{1,0:T(8,128)(2,1)S(1)} collective-permute-done((bf16[28,1408]{1,0:T(8,128)(2,1)S(1)}, bf16[28,1408]{1,0:T(8,128)(2,1)S(1)}, u32[]{:S(2)}, u32[]{:S(2)}) %collective-permute-start.1) | collective-permute-done | bytes 78880 | tf_op jit(solution)/shard_map/ppermute | solution.py:68
  8.5 3.1 %collective-permute-start.2 = (bf16[56,1408]{1,0:T(8,128)(2,1)S(1)}, bf16[56,1408]{1,0:T(8,128)(2,1)S(1)}, u32[]{:S(2)}, u32[]{:S(2)}) collective-permute-start(bf16[56,1408]{1,0:T(8,128)(2,1)S(1)} %maximum_select_fusion.1), channel_id=1, source_target_pairs={{0,65},{32,97},{2,67},{34,99},{4,69},{36,101},{6,71},{38,103},{64,... | collective-permute-start | bytes 473096 | tf_op jit(solution)/shard_map/ppermute | solution.py:68
  12.9 0.7 reshape.107.gain_ref
  13.7 1.5 copy-done
  15.2 5.6 %shard_map.91 = (bf16[2,256,1792]{2,1,0:T(8,128)(2,1)S(1)}, bf16[2,80,1792]{2,1,0:T(8,128)(2,1)S(1)}) custom-call(s32[3]{0:T(128)S(1)} %pad_add_fusion.fact_ref, bf16[256,3584]{1,0:T(8,128)(2,1)S(1)} %bitcast.107, f32[1,3584]{1,0:T(1,128)S(1)} %reshape.107.gain_ref), custom_call_target="tpu_custom_call" | custom-call | tf_op jit(solution)/shard_map/pallas_call | solution.py:142
  21.4 0.9 collective-permute-start.3
  22.3 1.9 %collective-permute-start.18 = (bf16[112,768]{1,0:T(8,128)(2,1)S(1)}, bf16[112,768]{1,0:T(8,128)(2,1)S(1)}, u32[]{:S(2)}, u32[]{:S(2)}) collective-permute-start(bf16[112,768]{1,0:T(8,128)(2,1)S(1)} %get-tuple-element.34), channel_id=1, source_target_pairs={{0,2},{32,38},{2,0},{34,36},{4,6},{36,34},{6,4},{38,32},{64,66},{9... | collective-permute-start | bytes 516104 | tf_op jit(solution)/shard_map/ppermute | solution.py:68
  24.4 2.2 %collective-permute-done.3 = bf16[112,640]{1,0:T(8,128)(2,1)S(1)} collective-permute-done((bf16[112,640]{1,0:T(8,128)(2,1)S(1)}, bf16[112,640]{1,0:T(8,128)(2,1)S(1)}, u32[]{:S(2)}, u32[]{:S(2)}) %collective-permute-start.3) | collective-permute-done | bytes 143392 | tf_op jit(solution)/shard_map/ppermute | solution.py:68
  26.6 0.6 collective-permute-start.4
  27.8 4.1 %collective-permute-start.19 = (bf16[2,112,768]{2,1,0:T(8,128)(2,1)S(1)}, bf16[2,112,768]{2,1,0:T(8,128)(2,1)S(1)}, u32[]{:S(2)}, u32[]{:S(2)}) collective-permute-start(bf16[2,112,768]{2,1,0:T(8,128)(2,1)S(1)} %pad_maximum_fusion.5), channel_id=1, source_target_pairs={{0,6},{32,34},{2,4},{34,32},{4,2},{36,38},{6,0},{38,36},{64,70},{9... | collective-permute-start | bytes 1032200 | tf_op jit(solution)/shard_map/ppermute | solution.py:68
  31.9 2.4 %collective-permute-done = bf16[2,80,1792]{2,1,0:T(8,128)(2,1)} collective-permute-done((bf16[2,80,1792]{2,1,0:T(8,128)(2,1)S(1)}, bf16[2,80,1792]{2,1,0:T(8,128)(2,1)}, u32[]{:S(2)}, u32[]{:S(2)}) %collective-permute-start) | collective-permute-done | bytes 573472 | tf_op jit(solution)/shard_map/ppermute | solution.py:68
  34.3 0.7 slice_convert_fusion.1
  35.0 1.0 slice.127
  37.7 2.0 %collective-permute-start.5 = (bf16[448,256]{1,0:T(8,128)(2,1)S(1)}, bf16[448,256]{1,0:T(8,128)(2,1)S(1)}, u32[]{:S(2)}, u32[]{:S(2)}) collective-permute-start(bf16[448,256]{1,0:T(8,128)(2,1)S(1)} %get-tuple-element.28), channel_id=1, source_target_pairs={{0,2},{32,38},{2,0},{34,36},{4,6},{36,34},{6,4},{38,32},{64,66},{9... | collective-permute-start | bytes 688136 | tf_op jit(solution)/shard_map/ppermute | solution.py:68
  39.9 0.5 collective-permute-start.20
  40.4 3.4 %collective-permute-done.5 = bf16[448,256]{1,0:T(8,128)(2,1)S(1)} collective-permute-done((bf16[448,256]{1,0:T(8,128)(2,1)S(1)}, bf16[448,256]{1,0:T(8,128)(2,1)S(1)}, u32[]{:S(2)}, u32[]{:S(2)}) %collective-permute-start.5) | collective-permute-done | bytes 229408 | tf_op jit(solution)/shard_map/ppermute | solution.py:68
  43.9 4.1 %collective-permute-start.6 = (bf16[2,448,256]{2,1,0:T(8,128)(2,1)S(1)}, bf16[2,448,256]{2,1,0:T(8,128)(2,1)S(1)}, u32[]{:S(2)}, u32[]{:S(2)}) collective-permute-start(bf16[2,448,256]{2,1,0:T(8,128)(2,1)S(1)} %pad_maximum_fusion.4), channel_id=1, source_target_pairs={{0,6},{32,34},{2,4},{34,32},{4,2},{36,38},{6,0},{38,36},{64,70},{9... | collective-permute-start | bytes 1376264 | tf_op jit(solution)/shard_map/ppermute | solution.py:68
  48.0 1.8 %broadcast_in_dim.60 = bf16[4,4,112,768]{3,2,1,0:T(8,128)(2,1)} broadcast(bf16[]{:T(256)} %constant.177.clone.1), dimensions={} | broadcast | bytes 2752514 | tf_op jit(solution)/shard_map/broadcast_in_dim | solution.py:322
  49.8 0.9 bitcast_dynamic-update-slice_fusion
  50.7 3.8 %collective-permute-done.6 = bf16[2,448,256]{2,1,0:T(8,128)(2,1)S(1)} collective-permute-done((bf16[2,448,256]{2,1,0:T(8,128)(2,1)S(1)}, bf16[2,448,256]{2,1,0:T(8,128)(2,1)S(1)}, u32[]{:S(2)}, u32[]{:S(2)}) %collective-permute-start.6) | collective-permute-done | bytes 458784 | tf_op jit(solution)/shard_map/ppermute | solution.py:68
  55.5 1.2 broadcast_in_dim.55
  56.7 0.8 bitcast_dynamic-update-slice_fusion.5
  57.8 5.4 %collective-permute-done.14 = bf16[448,384]{1,0:T(8,128)(2,1)S(1)} collective-permute-done((bf16[448,384]{1,0:T(8,128)(2,1)S(1)}, bf16[448,384]{1,0:T(8,128)(2,1)S(1)}, u32[]{:S(2)}, u32[]{:S(2)}) %collective-permute-start.14) | collective-permute-done | bytes 344096 | tf_op jit(solution)/shard_map/ppermute | solution.py:68
  63.2 0.9 constant_dynamic-update-slice_fusion.12
  64.1 0.8 bitcast_dynamic-update-slice_fusion.4
  64.8 6.8 %collective-permute-done.15 = bf16[448,384]{1,0:T(8,128)(2,1)S(1)} collective-permute-done((bf16[448,384]{1,0:T(8,128)(2,1)S(1)}, bf16[448,384]{1,0:T(8,128)(2,1)S(1)}, u32[]{:S(2)}, u32[]{:S(2)}) %collective-permute-start.15) | collective-permute-done | bytes 344096 | tf_op jit(solution)/shard_map/ppermute | solution.py:68
  71.6 0.7 collective-permute-start.22
  72.3 0.9 constant_dynamic-update-slice_fusion.11
  73.7 0.8 collective-permute-start.8
  74.6 5.6 %collective-permute-done.8 = bf16[2,144,128]{2,1,0:T(8,128)(2,1)S(1)} collective-permute-done((bf16[2,144,128]{2,1,0:T(8,128)(2,1)S(1)}, bf16[2,144,128]{2,1,0:T(8,128)(2,1)S(1)}, u32[]{:S(2)}, u32[]{:S(2)}) %collective-permute-start.8) | collective-permute-done | bytes 73760 | tf_op jit(solution)/shard_map/ppermute | solution.py:68
  80.2 0.6 collective-permute-start.9
  80.9 3.6 %collective-permute-done.24 = bf16[2,2,64,128]{3,2,1,0:T(8,128)(2,1)S(1)} collective-permute-done((bf16[2,2,64,128]{3,2,1,0:T(8,128)(2,1)S(1)}, bf16[2,2,64,128]{3,2,1,0:T(8,128)(2,1)S(1)}, u32[]{:S(2)}, u32[]{:S(2)}) %collective-permute-start.24) | collective-permute-done | bytes 65568 | tf_op jit(solution)/shard_map/ppermute | solution.py:68
  84.4 2.5 %collective-permute-start.25 = (bf16[2,2,2,64,128]{4,3,2,1,0:T(8,128)(2,1)S(1)}, bf16[2,2,2,64,128]{4,3,2,1,0:T(8,128)(2,1)S(1)}, u32[]{:S(2)}, u32[]{:S(2)}) collective-permute-start(bf16[2,2,2,64,128]{4,3,2,1,0:T(8,128)(2,1)S(1)} %pad_maximum_fusion.10), channel_id=1, source_target_pairs={{0,6},{32,34},{2,4},{34,32},{4,2},{36,38},{6,0},{38,36},{64,70},{9... | collective-permute-start | bytes 393224 | tf_op jit(solution)/shard_map/ppermute | solution.py:68
  87.0 1.3 collective-permute-start.10
  88.3 0.9 constant_dynamic-update-slice_fusion.10
  89.3 0.8 bitcast_dynamic-update-slice_fusion.3
  90.0 0.7 collective-permute-done.25
  90.7 0.8 fusion.42
  91.5 1.2 collective-permute-start.26
  92.7 0.9 collective-permute-done.10
  93.6 0.8 fusion.43
  94.4 0.8 bitcast_dynamic-update-slice_fusion.2
  95.2 0.6 concatenate.103.info_ref
  95.8 2.2 %collective-permute-done.26 = bf16[4,2,2,64,128]{4,3,2,1,0:T(8,128)(2,1)S(1)} collective-permute-done((bf16[4,2,2,64,128]{4,3,2,1,0:T(8,128)(2,1)}, bf16[4,2,2,64,128]{4,3,2,1,0:T(8,128)(2,1)S(1)}, u32[]{:S(2)}, u32[]{:S(2)}) %collective-permute-start.26) | collective-permute-done | bytes 262176 | tf_op jit(solution)/shard_map/ppermute | solution.py:68
  98.1 1.4 collective-permute-start.27
  99.5 2.2 %collective-permute-done.11 = bf16[4,2,2,80,128]{4,3,2,1,0:T(8,128)(2,1)S(1)} collective-permute-done((bf16[4,2,2,80,128]{4,3,2,1,0:T(8,128)(2,1)}, bf16[4,2,2,80,128]{4,3,2,1,0:T(8,128)(2,1)S(1)}, u32[]{:S(2)}, u32[]{:S(2)}) %collective-permute-start.11) | collective-permute-done | bytes 327712 | tf_op jit(solution)/shard_map/ppermute | solution.py:68
  101.7 2.4 %collective-permute-start.12 = (bf16[2,4,2,2,80,128]{5,4,3,2,1,0:T(8,128)(2,1)S(1)}, bf16[2,4,2,2,80,128]{5,4,3,2,1,0:T(8,128)(2,1)S(1)}, u32[]{:S(2)}, u32[]{:S(2)}) collective-permute-start(bf16[2,4,2,2,80,128]{5,4,3,2,1,0:T(8,128)(2,1)S(1)} %pad_maximum_fusion.2), channel_id=1, source_target_pairs={{0,6},{32,34},{2,4},{34,32},{4,2},{36,38},{6,0},{38,36},{64,70},{9... | collective-permute-start | bytes 1966088 | tf_op jit(solution)/shard_map/ppermute | solution.py:68
  104.3 1.7 %constant_dynamic-update-slice_fusion.8 = bf16[2,512,1792]{2,1,0:T(8,128)(2,1)S(1)} fusion(bf16[2,512,1792]{2,1,0:T(8,128)(2,1)S(1)} %constant_dynamic-update-slice_fusion.9, bf16[2,256,1792]{2,1,0:T(8,128)(2,1)} %collective-permute-done.13), kind=kLoop, calls=%fused_computation.70 | loop fusion | bytes 3670016 | tf_op jit(solution)/shard_map/concatenate | solution.py:314
  106.0 2.6 %collective-permute-done.27 = bf16[2,4,2,2,64,128]{5,4,3,2,1,0:T(8,128)(2,1)S(1)} collective-permute-done((bf16[2,4,2,2,64,128]{5,4,3,2,1,0:T(8,128)(2,1)S(1)}, bf16[2,4,2,2,64,128]{5,4,3,2,1,0:T(8,128)(2,1)S(1)}, u32[]{:S(2)}, u32[]{:S(2)}) %collective-permute-start.27) | collective-permute-done | bytes 524320 | tf_op jit(solution)/shard_map/ppermute | solution.py:68
  108.7 4.9 %collective-permute-done.12 = bf16[2,4,2,2,80,128]{5,4,3,2,1,0:T(8,128)(2,1)S(1)} collective-permute-done((bf16[2,4,2,2,80,128]{5,4,3,2,1,0:T(8,128)(2,1)S(1)}, bf16[2,4,2,2,80,128]{5,4,3,2,1,0:T(8,128)(2,1)S(1)}, u32[]{:S(2)}, u32[]{:S(2)}) %collective-permute-start.12) | collective-permute-done | bytes 655392 | tf_op jit(solution)/shard_map/ppermute | solution.py:68
  113.8 1.2 fusion.29
  115.1 3.2 %fusion.2 = f32[512,384]{1,0:T(8,128)S(1)} fusion(bf16[1792,384]{1,0:T(8,128)(2,1)} %collective-permute-done.17, bf16[2,512,1792]{2,1,0:T(8,128)(2,1)} %copy-done.3, s32[]{:T(128)S(6)} %select_n.301), kind=kOutput, calls=%fused_computation.2 | convolution fusion | flops 704643072 | bytes 3997700 | tf_op jit(solution)/shard_map/dot_general | solution.py:360
  118.3 2.5 %fusion.17 = bf16[512,384]{1,0:T(8,128)(2,1)S(1)} fusion(f32[512,384]{1,0:T(8,128)S(1)} %fusion.2, bf16[1792,384]{1,0:T(8,128)(2,1)} %bitcast.34, bf16[2,512,1792]{2,1,0:T(8,128)(2,1)S(1)} %copy-done.4, s32[]{:T(128)S(6)} %select_n.274), kind=kOutput, calls=%fused_computation.15 | convolution fusion | flops 705036288 | bytes 4390916 | tf_op jit(solution)/shard_map/dot_general | solution.py:360
  120.8 3.4 %fusion = f32[512,768]{1,0:T(8,128)S(1)} fusion(bf16[1792,768]{1,0:T(8,128)(2,1)} %collective-permute-done.23, bf16[2,512,1792]{2,1,0:T(8,128)(2,1)S(1)} %copy-done.4, s32[]{:T(128)S(6)} %select_n.301), kind=kOutput, calls=%fused_computation | convolution fusion | flops 1409286144 | bytes 6160388 | tf_op jit(solution)/shard_map/dot_general | solution.py:360
  124.2 3.4 %add_convert_fusion = bf16[512,768]{1,0:T(8,128)(2,1)S(1)} fusion(f32[512,768]{1,0:T(8,128)S(1)} %fusion, bf16[1792,768]{1,0:T(8,128)(2,1)} %bitcast.43, bf16[2,512,1792]{2,1,0:T(8,128)(2,1)S(1)} %copy-done.4, s32[]{:T(128)S(6)} %select_n.274), kind=kOutput, calls=%fused_computation.12 | convolution fusion | flops 1410072576 | bytes 6946820 | tf_op jit(solution)/shard_map/dot_general | solution.py:360
  127.7 11.4 %shard_map.93 = bf16[256,896]{1,0:T(8,128)(2,1)S(1)} custom-call(s32[68]{0:T(128)S(1)} %concatenate.103.info_ref, s32[64]{0:T(128)S(1)} %reshape.119.count_ref, bf16[256,384]{1,0:T(8,128)(2,1)S(1)} %get-tuple-element.29.part_a_ref, bf16[256,768]{1,0:T(8,128)(2,1)S(1)} %get-tuple-element.25.part_b_ref, bf16[32,2,80,128]{3,2,1,0:T(8,128)(2,1)S(1)} %bitcast.103, ...), custom_call_target="tpu_custom_call" | custom-call | tf_op jit(solution)/shard_map/pallas_call | solution.py:249
  139.6 12.6 %shard_map.92 = bf16[256,1792]{1,0:T(8,128)(2,1)} custom-call(s32[68]{0:T(128)S(1)} %concatenate.82.info_ref, s32[64]{0:T(128)S(1)} %reshape.119.count_ref, bf16[256,384]{1,0:T(8,128)(2,1)S(1)} %get-tuple-element.30.part_a_ref, bf16[256,768]{1,0:T(8,128)(2,1)S(1)} %get-tuple-element.26.part_b_ref, bf16[32,2,80,128]{3,2,1,0:T(8,128)(2,1)S(1)} %bitcast.104, ...), custom_call_target="tpu_custom_call" | custom-call | tf_op jit(solution)/shard_map/pallas_call | solution.py:249
  152.1 1.8 %bitcast_dynamic-update-slice_fusion.1 = bf16[1,256,1792]{2,1,0:T(8,128)(2,1)} fusion(bf16[1,256,1792]{2,1,0:T(8,128)(2,1)} %bitcast.124, s32[]{:T(128)S(6)} %select_n.321, bf16[256,896]{1,0:T(8,128)(2,1)} %collective-permute-done.28), kind=kLoop, calls=%fused_computation.32 | loop fusion | bytes 917508 | tf_op jit(solution)/shard_map/dynamic_update_slice | solution.py:409
  (88 shorter events, 5.6 us)
Async XLA Ops:
  3.8 4.6 %collective-permute-start.1 = (bf16[28,1408]{1,0:T(8,128)(2,1)S(1)}, bf16[28,1408]{1,0:T(8,128)(2,1)S(1)}, u32[]{:S(2)}, u32[]{:S(2)}) collective-permute-start(bf16[28,1408]{1,0:T(8,128)(2,1)S(1)} %get-tuple-element.40), channel_id=1, source_target_pairs={{0,64},{32,96},{2,66},{34,98},{4,68},{36,100},{6,70},{38,102},{64,... | collective-permute-start | bytes 236552 | tf_op jit(solution)/shard_map/ppermute | solution.py:68
  8.5 12.8 %collective-permute-start.2 = (bf16[56,1408]{1,0:T(8,128)(2,1)S(1)}, bf16[56,1408]{1,0:T(8,128)(2,1)S(1)}, u32[]{:S(2)}, u32[]{:S(2)}) collective-permute-start(bf16[56,1408]{1,0:T(8,128)(2,1)S(1)} %maximum_select_fusion.1), channel_id=1, source_target_pairs={{0,65},{32,97},{2,67},{34,99},{4,69},{36,101},{6,71},{38,103},{64,... | collective-permute-start | bytes 473096 | tf_op jit(solution)/shard_map/ppermute | solution.py:68
  13.7 1.5 copy-start
  20.8 13.5 %collective-permute-start = (bf16[2,80,1792]{2,1,0:T(8,128)(2,1)S(1)}, bf16[2,80,1792]{2,1,0:T(8,128)(2,1)}, u32[]{:S(2)}, u32[]{:S(2)}) collective-permute-start(bf16[2,80,1792]{2,1,0:T(8,128)(2,1)S(1)} %get-tuple-element.15), channel_id=1, source_target_pairs={{0,64},{32,96},{2,66},{34,98},{4,68},{36,100},{6,70},{38,102},{64,... | collective-permute-start | bytes 1720328 | tf_op jit(solution)/shard_map/ppermute | solution.py:68
  21.4 5.2 %collective-permute-start.3 = (bf16[112,640]{1,0:T(8,128)(2,1)S(1)}, bf16[112,640]{1,0:T(8,128)(2,1)S(1)}, u32[]{:S(2)}, u32[]{:S(2)}) collective-permute-start(bf16[112,640]{1,0:T(8,128)(2,1)S(1)} %get-tuple-element.36), channel_id=1, source_target_pairs={{0,8},{32,56},{2,10},{34,58},{4,12},{36,60},{6,14},{38,62},{64,72}... | collective-permute-start | bytes 430088 | tf_op jit(solution)/shard_map/ppermute | solution.py:68
  22.3 5.4 %collective-permute-start.18 = (bf16[112,768]{1,0:T(8,128)(2,1)S(1)}, bf16[112,768]{1,0:T(8,128)(2,1)S(1)}, u32[]{:S(2)}, u32[]{:S(2)}) collective-permute-start(bf16[112,768]{1,0:T(8,128)(2,1)S(1)} %get-tuple-element.34), channel_id=1, source_target_pairs={{0,2},{32,38},{2,0},{34,36},{4,6},{36,34},{6,4},{38,32},{64,66},{9... | collective-permute-start | bytes 516104 | tf_op jit(solution)/shard_map/ppermute | solution.py:68
  26.6 11.0 %collective-permute-start.4 = (bf16[2,112,640]{2,1,0:T(8,128)(2,1)S(1)}, bf16[2,112,640]{2,1,0:T(8,128)(2,1)S(1)}, u32[]{:S(2)}, u32[]{:S(2)}) collective-permute-start(bf16[2,112,640]{2,1,0:T(8,128)(2,1)S(1)} %pad_maximum_fusion.7), channel_id=1, source_target_pairs={{0,24},{32,40},{2,26},{34,42},{4,28},{36,44},{6,30},{38,46},{64,88... | collective-permute-start | bytes 860168 | tf_op jit(solution)/shard_map/ppermute | solution.py:68
  27.8 12.0 %collective-permute-start.19 = (bf16[2,112,768]{2,1,0:T(8,128)(2,1)S(1)}, bf16[2,112,768]{2,1,0:T(8,128)(2,1)S(1)}, u32[]{:S(2)}, u32[]{:S(2)}) collective-permute-start(bf16[2,112,768]{2,1,0:T(8,128)(2,1)S(1)} %pad_maximum_fusion.5), channel_id=1, source_target_pairs={{0,6},{32,34},{2,4},{34,32},{4,2},{36,38},{6,0},{38,36},{64,70},{9... | collective-permute-start | bytes 1032200 | tf_op jit(solution)/shard_map/ppermute | solution.py:68
  37.2 67.1 %collective-permute-start.13 = (bf16[2,256,1792]{2,1,0:T(8,128)(2,1)S(1)}, bf16[2,256,1792]{2,1,0:T(8,128)(2,1)}, u32[]{:S(2)}, u32[]{:S(2)}) collective-permute-start(bf16[2,256,1792]{2,1,0:T(8,128)(2,1)S(1)} %get-tuple-element.20), channel_id=1, source_target_pairs={{0,64},{32,96},{2,66},{34,98},{4,68},{36,100},{6,70},{38,102},{64,... | collective-permute-start | bytes 5505032 | tf_op jit(solution)/shard_map/ppermute | solution.py:68
  37.7 6.1 %collective-permute-start.5 = (bf16[448,256]{1,0:T(8,128)(2,1)S(1)}, bf16[448,256]{1,0:T(8,128)(2,1)S(1)}, u32[]{:S(2)}, u32[]{:S(2)}) collective-permute-start(bf16[448,256]{1,0:T(8,128)(2,1)S(1)} %get-tuple-element.28), channel_id=1, source_target_pairs={{0,2},{32,38},{2,0},{34,36},{4,6},{36,34},{6,4},{38,32},{64,66},{9... | collective-permute-start | bytes 688136 | tf_op jit(solution)/shard_map/ppermute | solution.py:68
  39.9 15.1 %collective-permute-start.20 = (bf16[448,768]{1,0:T(8,128)(2,1)S(1)}, bf16[448,768]{1,0:T(8,128)(2,1)S(1)}, u32[]{:S(2)}, u32[]{:S(2)}) collective-permute-start(bf16[448,768]{1,0:T(8,128)(2,1)S(1)} %bitcast.112), channel_id=1, source_target_pairs={{0,8},{32,56},{2,10},{34,58},{4,12},{36,60},{6,14},{38,62},{64,72}... | collective-permute-start | bytes 2064392 | tf_op jit(solution)/shard_map/ppermute | solution.py:68
  43.9 10.6 %collective-permute-start.6 = (bf16[2,448,256]{2,1,0:T(8,128)(2,1)S(1)}, bf16[2,448,256]{2,1,0:T(8,128)(2,1)S(1)}, u32[]{:S(2)}, u32[]{:S(2)}) collective-permute-start(bf16[2,448,256]{2,1,0:T(8,128)(2,1)S(1)} %pad_maximum_fusion.4), channel_id=1, source_target_pairs={{0,6},{32,34},{2,4},{34,32},{4,2},{36,38},{6,0},{38,36},{64,70},{9... | collective-permute-start | bytes 1376264 | tf_op jit(solution)/shard_map/ppermute | solution.py:68
  54.5 18.8 %collective-permute-start.7 = (bf16[1792,256]{1,0:T(8,128)(2,1)S(1)}, bf16[1792,256]{1,0:T(8,128)(2,1)S(1)}, u32[]{:S(2)}, u32[]{:S(2)}) collective-permute-start(bf16[1792,256]{1,0:T(8,128)(2,1)S(1)} %bitcast.122), channel_id=1, source_target_pairs={{0,32},{32,0},{2,34},{34,2},{4,36},{36,4},{6,38},{38,6},{64,96},{9... | collective-permute-start | bytes 2752520 | tf_op jit(solution)/shard_map/ppermute | solution.py:68
  54.6 8.5 %collective-permute-start.14 = (bf16[448,384]{1,0:T(8,128)(2,1)S(1)}, bf16[448,384]{1,0:T(8,128)(2,1)S(1)}, u32[]{:S(2)}, u32[]{:S(2)}) collective-permute-start(bf16[448,384]{1,0:T(8,128)(2,1)S(1)} %slice.153), channel_id=1, source_target_pairs={{0,2},{32,38},{2,4},{34,32},{4,6},{36,34},{6,0},{38,36},{64,66},{9... | collective-permute-start | bytes 1032200 | tf_op jit(solution)/shard_map/ppermute | solution.py:68
  55.0 16.7 %collective-permute-start.21 = (bf16[448,768]{1,0:T(8,128)(2,1)S(1)}, bf16[448,768]{1,0:T(8,128)(2,1)S(1)}, u32[]{:S(2)}, u32[]{:S(2)}) collective-permute-start(bf16[448,768]{1,0:T(8,128)(2,1)S(1)} %collective-permute-done.20), channel_id=1, source_target_pairs={{0,8},{32,56},{2,10},{34,58},{4,12},{36,60},{6,14},{38,62},{64,72}... | collective-permute-start | bytes 2064392 | tf_op jit(solution)/shard_map/ppermute | solution.py:68
  63.2 8.5 %collective-permute-start.15 = (bf16[448,384]{1,0:T(8,128)(2,1)S(1)}, bf16[448,384]{1,0:T(8,128)(2,1)S(1)}, u32[]{:S(2)}, u32[]{:S(2)}) collective-permute-start(bf16[448,384]{1,0:T(8,128)(2,1)S(1)} %collective-permute-done.14), channel_id=1, source_target_pairs={{0,2},{32,38},{2,4},{34,32},{4,6},{36,34},{6,0},{38,36},{64,66},{9... | collective-permute-start | bytes 1032200 | tf_op jit(solution)/shard_map/ppermute | solution.py:68
  71.6 22.8 %collective-permute-start.16 = (bf16[448,384]{1,0:T(8,128)(2,1)S(1)}, bf16[448,384]{1,0:T(8,128)(2,1)S(1)}, u32[]{:S(2)}, u32[]{:S(2)}) collective-permute-start(bf16[448,384]{1,0:T(8,128)(2,1)S(1)} %collective-permute-done.15), channel_id=1, source_target_pairs={{0,2},{32,38},{2,4},{34,32},{4,6},{36,34},{6,0},{38,36},{64,66},{9... | collective-permute-start | bytes 1032200 | tf_op jit(solution)/shard_map/ppermute | solution.py:68
  71.6 16.7 %collective-permute-start.22 = (bf16[448,768]{1,0:T(8,128)(2,1)S(1)}, bf16[448,768]{1,0:T(8,128)(2,1)S(1)}, u32[]{:S(2)}, u32[]{:S(2)}) collective-permute-start(bf16[448,768]{1,0:T(8,128)(2,1)S(1)} %collective-permute-done.21), channel_id=1, source_target_pairs={{0,8},{32,56},{2,10},{34,58},{4,12},{36,60},{6,14},{38,62},{64,72}... | collective-permute-start | bytes 2064392 | tf_op jit(solution)/shard_map/ppermute | solution.py:68
  73.7 6.4 %collective-permute-start.8 = (bf16[2,144,128]{2,1,0:T(8,128)(2,1)S(1)}, bf16[2,144,128]{2,1,0:T(8,128)(2,1)S(1)}, u32[]{:S(2)}, u32[]{:S(2)}) collective-permute-start(bf16[2,144,128]{2,1,0:T(8,128)(2,1)S(1)} %maximum_select_fusion.3), channel_id=1, source_target_pairs={{0,65},{32,97},{2,67},{34,99},{4,69},{36,101},{6,71},{38,103},{64,... | collective-permute-start | bytes 221192 | tf_op jit(solution)/shard_map/ppermute | solution.py:68
  80.2 4.3 %collective-permute-start.24 = (bf16[2,2,64,128]{3,2,1,0:T(8,128)(2,1)S(1)}, bf16[2,2,64,128]{3,2,1,0:T(8,128)(2,1)S(1)}, u32[]{:S(2)}, u32[]{:S(2)}) collective-permute-start(bf16[2,2,64,128]{3,2,1,0:T(8,128)(2,1)S(1)} %pad_maximum_fusion.12), channel_id=1, source_target_pairs={{0,2},{32,38},{2,0},{34,36},{4,6},{36,34},{6,4},{38,32},{64,66},{9... | collective-permute-start | bytes 196616 | tf_op jit(solution)/shard_map/ppermute | solution.py:68
  80.2 6.8 %collective-permute-start.9 = (bf16[2,2,80,128]{3,2,1,0:T(8,128)(2,1)S(1)}, bf16[2,2,80,128]{3,2,1,0:T(8,128)(2,1)S(1)}, u32[]{:S(2)}, u32[]{:S(2)}) collective-permute-start(bf16[2,2,80,128]{3,2,1,0:T(8,128)(2,1)S(1)} %fusion.28), channel_id=1, source_target_pairs={{0,8},{32,56},{2,10},{34,58},{4,12},{36,60},{6,14},{38,62},{64,72}... | collective-permute-start | bytes 245768 | tf_op jit(solution)/shard_map/ppermute | solution.py:68
  84.4 6.3 %collective-permute-start.25 = (bf16[2,2,2,64,128]{4,3,2,1,0:T(8,128)(2,1)S(1)}, bf16[2,2,2,64,128]{4,3,2,1,0:T(8,128)(2,1)S(1)}, u32[]{:S(2)}, u32[]{:S(2)}) collective-permute-start(bf16[2,2,2,64,128]{4,3,2,1,0:T(8,128)(2,1)S(1)} %pad_maximum_fusion.10), channel_id=1, source_target_pairs={{0,6},{32,34},{2,4},{34,32},{4,2},{36,38},{6,0},{38,36},{64,70},{9... | collective-permute-start | bytes 393224 | tf_op jit(solution)/shard_map/ppermute | solution.py:68
  87.0 6.6 %collective-permute-start.10 = (bf16[2,2,2,80,128]{4,3,2,1,0:T(8,128)(2,1)S(1)}, bf16[2,2,2,80,128]{4,3,2,1,0:T(8,128)(2,1)S(1)}, u32[]{:S(2)}, u32[]{:S(2)}) collective-permute-start(bf16[2,2,2,80,128]{4,3,2,1,0:T(8,128)(2,1)S(1)} %pad_maximum_fusion.9), channel_id=1, source_target_pairs={{0,24},{32,40},{2,26},{34,42},{4,28},{36,44},{6,30},{38,46},{64,88... | collective-permute-start | bytes 491528 | tf_op jit(solution)/shard_map/ppermute | solution.py:68
  89.3 31.6 %collective-permute-start.23 = (bf16[1792,768]{1,0:T(8,128)(2,1)}, bf16[1792,768]{1,0:T(8,128)(2,1)}, u32[]{:S(2)}, u32[]{:S(2)}) collective-permute-start(bf16[1792,768]{1,0:T(8,128)(2,1)} %bitcast.43), channel_id=1, source_target_pairs={{0,32},{32,0},{2,34},{34,2},{4,36},{36,4},{6,38},{38,6},{64,96},{9... | collective-permute-start | bytes 8257544 | tf_op jit(solution)/shard_map/ppermute | solution.py:68
  91.5 6.6 %collective-permute-start.26 = (bf16[4,2,2,64,128]{4,3,2,1,0:T(8,128)(2,1)}, bf16[4,2,2,64,128]{4,3,2,1,0:T(8,128)(2,1)S(1)}, u32[]{:S(2)}, u32[]{:S(2)}) collective-permute-start(bf16[4,2,2,64,128]{4,3,2,1,0:T(8,128)(2,1)} %get-tuple-element.38), channel_id=1, source_target_pairs={{0,8},{32,56},{2,10},{34,58},{4,12},{36,60},{6,14},{38,62},{64,72}... | collective-permute-start | bytes 786440 | tf_op jit(solution)/shard_map/ppermute | solution.py:68
  94.4 7.3 %collective-permute-start.11 = (bf16[4,2,2,80,128]{4,3,2,1,0:T(8,128)(2,1)}, bf16[4,2,2,80,128]{4,3,2,1,0:T(8,128)(2,1)S(1)}, u32[]{:S(2)}, u32[]{:S(2)}) collective-permute-start(bf16[4,2,2,80,128]{4,3,2,1,0:T(8,128)(2,1)} %get-tuple-element.32), channel_id=1, source_target_pairs={{0,2},{32,38},{2,0},{34,36},{4,6},{36,34},{6,4},{38,32},{64,66},{9... | collective-permute-start | bytes 983048 | tf_op jit(solution)/shard_map/ppermute | solution.py:68
  95.2 19.9 %collective-permute-start.17 = (bf16[1792,384]{1,0:T(8,128)(2,1)}, bf16[1792,384]{1,0:T(8,128)(2,1)}, u32[]{:S(2)}, u32[]{:S(2)}) collective-permute-start(bf16[1792,384]{1,0:T(8,128)(2,1)} %bitcast.34), channel_id=1, source_target_pairs={{0,32},{32,0},{2,34},{34,2},{4,36},{36,4},{6,38},{38,6},{64,96},{9... | collective-permute-start | bytes 4128776 | tf_op jit(solution)/shard_map/ppermute | solution.py:68
  98.0 6.2 %copy-start.1 = (bf16[4,2,2,64,128]{4,3,2,1,0:T(8,128)(2,1)}, bf16[4,2,2,64,128]{4,3,2,1,0:T(8,128)(2,1)S(1)}, u32[]{:S(2)}) copy-start(bf16[4,2,2,64,128]{4,3,2,1,0:T(8,128)(2,1)S(1)} %collective-permute-done.26) | copy-start | bytes 786436
  98.1 10.5 %collective-permute-start.27 = (bf16[2,4,2,2,64,128]{5,4,3,2,1,0:T(8,128)(2,1)S(1)}, bf16[2,4,2,2,64,128]{5,4,3,2,1,0:T(8,128)(2,1)S(1)}, u32[]{:S(2)}, u32[]{:S(2)}) collective-permute-start(bf16[2,4,2,2,64,128]{5,4,3,2,1,0:T(8,128)(2,1)S(1)} %pad_maximum_fusion.3), channel_id=1, source_target_pairs={{0,24},{32,40},{2,26},{34,42},{4,28},{36,44},{6,30},{38,46},{64,88... | collective-permute-start | bytes 1572872 | tf_op jit(solution)/shard_map/ppermute | solution.py:68
  101.7 11.9 %collective-permute-start.12 = (bf16[2,4,2,2,80,128]{5,4,3,2,1,0:T(8,128)(2,1)S(1)}, bf16[2,4,2,2,80,128]{5,4,3,2,1,0:T(8,128)(2,1)S(1)}, u32[]{:S(2)}, u32[]{:S(2)}) collective-permute-start(bf16[2,4,2,2,80,128]{5,4,3,2,1,0:T(8,128)(2,1)S(1)} %pad_maximum_fusion.2), channel_id=1, source_target_pairs={{0,6},{32,34},{2,4},{34,32},{4,2},{36,38},{6,0},{38,36},{64,70},{9... | collective-permute-start | bytes 1966088 | tf_op jit(solution)/shard_map/ppermute | solution.py:68
  104.3 4.3 %copy-start.2 = (bf16[4,2,2,64,128]{4,3,2,1,0:T(8,128)(2,1)S(1)}, bf16[4,2,2,64,128]{4,3,2,1,0:T(8,128)(2,1)}, u32[]{:S(2)}) copy-start(bf16[4,2,2,64,128]{4,3,2,1,0:T(8,128)(2,1)} %copy-done.1) | copy-start | bytes 786436
  106.0 7.8 %copy-start.3 = (bf16[2,512,1792]{2,1,0:T(8,128)(2,1)}, bf16[2,512,1792]{2,1,0:T(8,128)(2,1)S(1)}, u32[]{:S(2)}) copy-start(bf16[2,512,1792]{2,1,0:T(8,128)(2,1)S(1)} %constant_dynamic-update-slice_fusion.8) | copy-start | bytes 11010052
  115.1 3.2 %copy-start.4 = (bf16[2,512,1792]{2,1,0:T(8,128)(2,1)S(1)}, bf16[2,512,1792]{2,1,0:T(8,128)(2,1)}, u32[]{:S(2)}) copy-start(bf16[2,512,1792]{2,1,0:T(8,128)(2,1)} %copy-done.3) | copy-start | bytes 11010052
  139.1 13.1 %collective-permute-start.28 = (bf16[256,896]{1,0:T(8,128)(2,1)S(1)}, bf16[256,896]{1,0:T(8,128)(2,1)}, u32[]{:S(2)}, u32[]{:S(2)}) collective-permute-start(bf16[256,896]{1,0:T(8,128)(2,1)S(1)} %shard_map.93), channel_id=1, source_target_pairs={{0,64},{32,96},{2,66},{34,98},{4,68},{36,100},{6,70},{38,102},{64,... | collective-permute-start | bytes 1376264 | tf_op jit(solution)/shard_map/ppermute | solution.py:68

commit v4 on v3

--- a/solution.py
+++ b/solution.py
@@ -155,12 +155,13 @@
     )(facts, tokens, gain.reshape(1, WIDTH))
 
 
-BLOCK = 512
+BLOCK = 256
 ROOM = SPANS * SLOTS + BLOCK
+LINES = HEADS * TOK
 
 
 def attend_body(wide, info_ref, count_ref, part_a_ref, part_b_ref, far_k_ref, far_v_ref, *rest):
-    out_ref, near_ref, keys_ref, values_ref, bias_ref, score_ref = rest
+    out_ref, query_ref, keys_ref, values_ref, bias_ref, score_ref, top_ref, sum_ref, mix_ref = rest
     span, valid, column, which = info_ref[0], info_ref[1], info_ref[2], info_ref[3]
 
     lane = lax.broadcasted_iota(jnp.int32, (1, ROOM), 1)
@@ -181,10 +182,6 @@
     values_ref[rest_rows, :] = jnp.zeros((BLOCK, D), jnp.bfloat16)
     blocks = (used + BLOCK - 1) // BLOCK
 
-    row = lax.broadcasted_iota(jnp.int32, (TOK, TOK), 0)
-    col = lax.broadcasted_iota(jnp.int32, (TOK, TOK), 1)
-    near_ref[...] = jnp.where((col <= row) & (col < valid), 0.0, FILL)
-    alive = lax.broadcasted_iota(jnp.int32, (TOK, D), 0) < valid
     power = SCALE * math.log2(math.e)
     contract = (((1,), (1,)), ((), ()))
 
@@ -194,49 +191,73 @@
             out = op(out, scores[:, i * D : (i + 1) * D])
         return out
 
+    row = lax.broadcasted_iota(jnp.int32, (TOK, TOK), 0)
+    col = lax.broadcasted_iota(jnp.int32, (TOK, TOK), 1)
+    near_bias = jnp.where((col <= row) & (col < valid), 0.0, FILL)
     for head in range(HEADS):
+        here = slice(head * TOK, (head + 1) * TOK)
         if head < KEPT:
             query = part_a_ref[:, (2 + head) * D : (3 + head) * D]
         else:
             query = part_b_ref[:, (head - KEPT) * D : (head - KEPT + 1) * D]
-        near = (
-            lax.dot_general(
-                query, part_a_ref[:, :D], contract, preferred_element_type=jnp.float32
+        query_ref[here, :] = query
+        near = lax.dot_general(
+            query, part_a_ref[:, :D], contract, preferred_element_type=jnp.float32
+        )
+        near = near + near_bias
+        score_ref[here, ROOM:] = near
+        top_ref[here, :] = fold(jnp.maximum, near)
+
+    def score(i, carry):
+        here = pl.ds(pl.multiple_of(i * BLOCK, BLOCK), BLOCK)
+        bias = bias_ref[:, here]
+        for head in range(HEADS):
+            lines = slice(head * TOK, (head + 1) * TOK)
+            far = lax.dot_general(
+                query_ref[lines, :],
+                keys_ref[here, :],
+                contract,
+                preferred_element_type=jnp.float32,
             )
-            + near_ref[...]
-        )
-
-        def score(i, top, query=query):
-            here = pl.ds(pl.multiple_of(i * BLOCK, BLOCK), BLOCK)
-            far = lax.dot_general(
-                query, keys_ref[here, :], contract, preferred_element_type=jnp.float32
-            )
-            far = far + bias_ref[:, here]
-            score_ref[:, here] = far
-            return jnp.maximum(top, fold(jnp.maximum, far))
-
-        top = lax.fori_loop(0, blocks, score, fold(jnp.maximum, near))
-        top = jnp.max(top, axis=1, keepdims=True)
-        weight = jnp.exp2((near - top) * power)
-        total = fold(jnp.add, weight)
-        mixed = jnp.dot(
+            far = far + bias
+            score_ref[lines, here] = far
+            top_ref[lines, :] = jnp.maximum(top_ref[lines, :], fold(jnp.maximum, far))
+        return carry
+
+    lax.fori_loop(0, blocks, score, jnp.int32(0))
+
+    for head in range(HEADS):
+        lines = slice(head * TOK, (head + 1) * TOK)
+        top = jnp.max(top_ref[lines, :], axis=1, keepdims=True)
+        top_ref[lines, :] = jnp.broadcast_to(top, (TOK, D))
+        weight = jnp.exp2((score_ref[lines, ROOM:] - top) * power)
+        sum_ref[lines, :] = fold(jnp.add, weight)
+        mix_ref[lines, :] = jnp.dot(
             weight.astype(jnp.bfloat16),
             part_a_ref[:, D : 2 * D],
             preferred_element_type=jnp.float32,
         )
 
-        def mix(i, state, top=top):
-            total, mixed = state
-            here = pl.ds(pl.multiple_of(i * BLOCK, BLOCK), BLOCK)
-            weight = jnp.exp2((score_ref[:, here] - top) * power)
-            mixed = mixed + jnp.dot(
+    def mix(i, carry):
+        here = pl.ds(pl.multiple_of(i * BLOCK, BLOCK), BLOCK)
+        for head in range(HEADS):
+            lines = slice(head * TOK, (head + 1) * TOK)
+            top = top_ref[lines, :]
+            top = jnp.concatenate([top] * (BLOCK // D), axis=1)
+            weight = jnp.exp2((score_ref[lines, here] - top) * power)
+            sum_ref[lines, :] = sum_ref[lines, :] + fold(jnp.add, weight)
+            mix_ref[lines, :] = mix_ref[lines, :] + jnp.dot(
                 weight.astype(jnp.bfloat16), values_ref[here, :], preferred_element_type=jnp.float32
             )
-            return total + fold(jnp.add, weight), mixed
-
-        total, mixed = lax.fori_loop(0, blocks, mix, (total, mixed))
-        total = jnp.sum(total, axis=1, keepdims=True)
-        result = jnp.where(alive, mixed / total, 0.0).astype(jnp.bfloat16)
+        return carry
+
+    lax.fori_loop(0, blocks, mix, jnp.int32(0))
+
+    alive = lax.broadcasted_iota(jnp.int32, (TOK, D), 0) < valid
+    for head in range(HEADS):
+        lines = slice(head * TOK, (head + 1) * TOK)
+        total = jnp.sum(sum_ref[lines, :], axis=1, keepdims=True)
+        result = jnp.where(alive, mix_ref[lines, :] / total, 0.0).astype(jnp.bfloat16)
         if wide:
             out_ref[:, pl.ds(pl.multiple_of(column + head * D, D), D)] = result
         else:
@@ -252,14 +273,42 @@
         in_specs=[smem, smem, vmem, vmem, vmem, vmem],
         out_specs=vmem,
         scratch_shapes=[
-            pltpu.VMEM((TOK, TOK), jnp.float32),
+            pltpu.VMEM((LINES, D), jnp.bfloat16),
             pltpu.VMEM((ROOM, D), jnp.bfloat16),
             pltpu.VMEM((ROOM, D), jnp.bfloat16),
             pltpu.VMEM((1, ROOM), jnp.float32),
-            pltpu.VMEM((TOK, ROOM), jnp.float32),
+            pltpu.VMEM((LINES, ROOM + TOK), jnp.float32),
+            pltpu.VMEM((LINES, D), jnp.float32),
+            pltpu.VMEM((LINES, D), jnp.float32),
+            pltpu.VMEM((LINES, D), jnp.float32),
         ],
+        compiler_params=pltpu.CompilerParams(vmem_limit_bytes=44 * 1024 * 1024),
+    )(info, counts, part_a, part_b, far_k, far_v)
+
+
+def project_body(side_ref, x_ref, own_ref, other_ref, out_ref):
+    side = side_ref[0]
+    columns = own_ref.shape[1]
+    for first in range(0, columns, 256):
+        here = slice(first, min(first + 256, columns))
+        out = jnp.dot(x_ref[side], own_ref[:, here], preferred_element_type=jnp.float32)
+        out += jnp.dot(x_ref[1 - side], other_ref[:, here], preferred_element_type=jnp.float32)
+        out_ref[:, here] = out.astype(jnp.bfloat16)
+
+
+def project_kernel(side, x, own, other):
+    smem, vmem = pl.BlockSpec(memory_space=pltpu.SMEM), pl.BlockSpec(memory_space=pltpu.VMEM)
+    return pl.pallas_call(
+        project_body,
+        out_shape=jax.ShapeDtypeStruct((x.shape[1], own.shape[1]), jnp.bfloat16),
+        in_specs=[smem, vmem, vmem, vmem],
+        out_specs=vmem,
         compiler_params=pltpu.CompilerParams(vmem_limit_bytes=32 * 1024 * 1024),
-    )(info, counts, part_a, part_b, far_k, far_v)
+    )(side.reshape(1), x, own, other)
+
+
+def after(value, other):
+    return lax.optimization_barrier((value, other))[0]
 
 
 def double(block, axis):
@@ -310,7 +359,6 @@
     count = jnp.minimum(TOK // stride, (valid + stride - 1) // stride)
     normed, pooled = norm_rows(jnp.stack([level[0, 0], valid, count]), tokens[0], gain)
     mate_pooled = send(pooled, MATE)
-    normed, mate_pooled = lax.optimization_barrier((normed, mate_pooled))
     both = jnp.concatenate([normed, send(normed, MATE)], 1)
     facts = mate_pooled[0, SLOTS:, 0].astype(jnp.int32)
     mate_count, mate_valid = facts[0], facts[8]
@@ -327,39 +375,25 @@
         joined = in_place(double(block, axis), (p, p ^ near, p ^ far, p ^ 2), joined)
         return joined.reshape(-1, block.shape[-1])
 
-    def ring(block, axis):
-        pieces = [block]
-        for _ in range(3):
-            pieces.append(send(pieces[-1], RING[axis]))
-        return pieces, [(pos[axis] - sign * i) % 4 for i in range(4)]
-
     early = second(rows[:, : CUTS[2]], "x")
     late = second(rows[:, CUTS[2] :], "z")
 
-    z = pos["z"]
-    part_m = double(early[:, : CUTS[1]], "z")
-    part_m = in_place(part_m, (z, z ^ near, z ^ far, z ^ 2), blank(part_m.shape, part_m))
-    part_m = part_m.reshape(HALF, -1)
-    early, part_m = lax.optimization_barrier((early, part_m))
-
-    pieces, slots = ring(early[:, CUTS[1] :], "z")
-    part_a = in_place(pieces, slots, blank((4,) + pieces[0].shape, pieces[0])).reshape(HALF, -1)
-
-    pieces, slots = ring(late, "x")
-    part_b = blank((4, 4, 4 * ROWS, late.shape[-1]), late)
-    for piece, slot in zip(pieces, slots):
-        piece = piece.reshape(4, 1, 4 * ROWS, -1)
-        part_b = lax.dynamic_update_slice_in_dim(part_b, piece, slot, 1)
-    part_b = part_b.reshape(HALF, -1)
-
     def project(x, own):
-        other = send(own, SWAP)
-
-        def term(side, w):
-            part = lax.dynamic_index_in_dim(x, side, 0, keepdims=False)
-            return jnp.dot(part, w, preferred_element_type=jnp.float32)
-
-        return (term(core, own) + term(1 - core, other)).astype(jnp.bfloat16)
+        return project_kernel(core, x, own, send(own, SWAP))
+
+    x, z = pos["x"], pos["z"]
+    corner = early[:, : CUTS[1]]
+    b_0, a_0 = late, early[:, CUTS[1] :]
+    pair = jnp.stack([corner, send(corner, FLIP["z", 0])])
+    b_1 = send(b_0, RING["x"])
+    pair_far = send(pair, FLIP["z", 1])
+    part_m = in_place(
+        jnp.concatenate([pair, pair_far]),
+        (z, z ^ near, z ^ far, z ^ 2),
+        blank((4,) + corner.shape, corner),
+    ).reshape(HALF, -1)
+    b_2 = send(after(b_1, pair_far), RING["x"])
+    a_1 = send(after(a_0, pair_far), RING["z"])
 
     beacon = project(both_pooled, part_m).reshape(2, SLOTS, 2 * D)
     counts = jnp.stack([count, mate_count]).astype(jnp.bfloat16)
@@ -368,9 +402,18 @@
     block_v = beacon[..., D:]
     block = jnp.concatenate([block_k, block_v], 1)
     block = order(low, block[:1], block[1:])
-    block = jnp.stack([block, send(block, ACROSS)])
-    every_k = double(double(block[:, :, : SLOTS + 16], "x"), "z")
-    every_v = double(double(block[:, :, SLOTS + 16 :], "z"), "x")
+    a_2 = send(after(a_1, block), RING["z"])
+    across = send(block, ACROSS)
+    b_3 = send(after(b_2, across), RING["x"])
+    block = jnp.stack([block, across])
+    pair_k, pair_v = block[:, :, : SLOTS + 16], block[:, :, SLOTS + 16 :]
+    pair_k = jnp.stack([pair_k, send(pair_k, FLIP["x", 0])])
+    pair_v = jnp.stack([pair_v, send(pair_v, FLIP["z", 0])])
+    a_3 = send(after(a_2, (pair_k, pair_v)), RING["z"])
+    half_k = jnp.concatenate([pair_k, send(pair_k, FLIP["x", 1])])
+    half_v = jnp.concatenate([pair_v, send(pair_v, FLIP["z", 1])])
+    every_k = double(half_k, "z")
+    every_v = double(half_v, "x")
     every_k = every_k.reshape(SPANS, 2, SLOTS + 16, D)
     every_v = every_v.reshape(SPANS, 2, SLOTS, D)
 
@@ -386,8 +429,15 @@
     at_v = (code_x * 4 + code_z) * 2 + code_h
     live = every_k[:, :, SLOTS, 0].astype(jnp.int32).reshape(2 * SPANS)
 
-    part_a = project(both, part_a)
-    part_b = project(both, part_b)
+    pieces = [a_0, a_1, a_2, a_3]
+    part_a = blank((4,) + a_0.shape, a_0)
+    part_a = in_place(pieces, [(z - sign * i) % 4 for i in range(4)], part_a)
+    part_b = blank((4, 4, 4 * ROWS, late.shape[-1]), b_0)
+    for i, piece in enumerate([b_0, b_1, b_2, b_3]):
+        piece = piece.reshape(4, 1, 4 * ROWS, -1)
+        part_b = lax.dynamic_update_slice_in_dim(part_b, piece, (x - sign * i) % 4, 1)
+    part_a = project(both, part_a.reshape(HALF, -1))
+    part_b = project(both, part_b.reshape(HALF, -1))
 
     def attention(which, valid, wide):
         here = slice(which * TOK, (which + 1) * TOK)

time: 155 us -> 159 us (1.026)
  matrix products: 13 us -> 0 us
  starting transfers between devices: 31.9 us -> 39.2 us
  waiting for transfers between devices: 50 us -> 55.3 us
  other arithmetic: 8.07 us -> 12.4 us
  local copies, waits for them, and re-layouts: 18.8 us -> 22.4 us
  Pallas kernels: 29.5 us -> 26.5 us
    dot_general x6 -> x0, matrix products: 13 us -> none  [term(): return jnp.dot(part, w, preferred_element_type=jnp.float32)]
    pallas_call x2, Pallas kernels: 24 us -> 11.1 us  [attend(): pl.pallas_call(functools.partial(attend_body, wide), out_shape=jax.ShapeD...]
    pallas_call x0 -> x3, Pallas kernels: none -> 9.83 us  [project_kernel(): pl.pallas_call(project_body, out_shape=jax.ShapeDtypeStruct((x.shape[1],...]
    ppermute x29, starting transfers between devices: 31.9 us -> 39.2 us  [send(): return lax.ppermute(value, AXES, pairs)]
    ppermute x29, waiting for transfers between devices: 50 us -> 55.3 us  [send(): return lax.ppermute(value, AXES, pairs)]
    unnamed x11, local copies, waits for them, and re-layouts: 1.64 us -> 4.9 us
    concatenate x2, other arithmetic: 0.23 us -> 2.36 us  [double(): return jnp.concatenate([pair, send(pair, FLIP[axis, 1])])]
    select_n x4, other arithmetic: 0.18 us -> 2 us  [order(): jnp.where(first == 0, jnp.concatenate([one, two], 0), jnp.concatenate([tw...]
  transfers between devices with their start and end apart: 29 -> 29, of which waited for: 16 -> 14; matrix products, arithmetic and copies ran while one was open for 17% -> 16% of each run, Pallas kernels for 12% -> 10%
where the time goes in v4:
time: 159 us; the launch traced here: 158 us
  waiting for transfers between devices  55.3 us (35%)
  starting transfers between devices  39.2 us (25%)
  Pallas kernels  26.5 us (17%)
  local copies, waits for them, and re-layouts  22.4 us (14%)
  other arithmetic  12.4 us (8%)
  between operations  2.61 us (2%)
    ppermute x29, waiting for transfers between devices, send(): return lax.ppermute(value, AXES, pairs)  55.3 us
    ppermute x29, starting transfers between devices, send(): return lax.ppermute(value, AXES, pairs)  39.2 us
    pallas_call x2, Pallas kernels, attend(): pl.pallas_call(functools.partial(attend_body, wide), out_shape=jax.ShapeD...  11.1 us
    pallas_call x3, Pallas kernels, project_kernel(): pl.pallas_call(project_body, out_shape=jax.ShapeDtypeStruct((x.shape[1],...  9.83 us
    pallas_call x1, Pallas kernels, norm_rows(): pl.pallas_call(norm_body, out_shape=[jax.ShapeDtypeStruct((2, TOK, HALF),...  5.55 us
    unnamed x11, local copies, waits for them, and re-layouts  4.9 us
    dynamic_update_slice x4, local copies, waits for them, and re-layouts, on_device(): lax.dynamic_update_slice_in_dim(part_b, piece, (x - sign * i) % 4, 1)  3.69 us
    dynamic_update_slice x16, local copies, waits for them, and re-layouts, in_place(): joined = lax.dynamic_update_slice_in_dim(joined, pieces[i][None], slot, 0)  3.31 us
  transfers between devices with their start and end apart: 29, of which 14 were waited for; matrix products, arithmetic and copies ran while one was open for 16% of the time, Pallas kernels for 10%

profile of v4, /device:TPU:6, one launch (start us, length us, event | category | flops | bytes accessed | tf_op | source)
XLA Modules:
  0.0 158.4 jit_solution(11912117863272910572)
XLA Ops:
  0.0 0.7 constant_dynamic-update-slice_fusion.3
  0.7 0.7 constant_dynamic-update-slice_fusion.2
  1.4 0.7 constant_dynamic-update-slice_fusion.1
  2.2 0.7 constant_dynamic-update-slice_fusion
  2.9 0.9 select_dynamic-update-slice_fusion.1
  3.8 1.7 %collective-permute-start.1 = (bf16[28,1408]{1,0:T(8,128)(2,1)S(1)}, bf16[28,1408]{1,0:T(8,128)(2,1)S(1)}, u32[]{:S(2)}, u32[]{:S(2)}) collective-permute-start(bf16[28,1408]{1,0:T(8,128)(2,1)S(1)} %get-tuple-element.44), channel_id=1, source_target_pairs={{0,64},{32,96},{2,66},{34,98},{4,68},{36,100},{6,70},{38,102},{64,... | collective-permute-start | bytes 236552 | tf_op jit(solution)/shard_map/ppermute | solution.py:68
  5.4 3.0 %collective-permute-done.1 = bf16[28,1408]{1,0:T(8,128)(2,1)S(1)} collective-permute-done((bf16[28,1408]{1,0:T(8,128)(2,1)S(1)}, bf16[28,1408]{1,0:T(8,128)(2,1)S(1)}, u32[]{:S(2)}, u32[]{:S(2)}) %collective-permute-start.1) | collective-permute-done | bytes 78880 | tf_op jit(solution)/shard_map/ppermute | solution.py:68
  8.4 0.7 maximum_select_fusion.1
  9.1 3.0 %collective-permute-start.2 = (bf16[56,1408]{1,0:T(8,128)(2,1)}, bf16[56,1408]{1,0:T(8,128)(2,1)}, u32[]{:S(2)}, u32[]{:S(2)}) collective-permute-start(bf16[56,1408]{1,0:T(8,128)(2,1)} %maximum_select_fusion.1), channel_id=1, source_target_pairs={{0,65},{32,97},{2,67},{34,99},{4,69},{36,101},{6,71},{38,103},{64,... | collective-permute-start | bytes 473096 | tf_op jit(solution)/shard_map/ppermute | solution.py:68
  13.5 0.7 reshape.113.gain_ref
  14.3 1.5 copy-done.1
  15.8 5.6 %shard_map.91 = (bf16[2,256,1792]{2,1,0:T(8,128)(2,1)S(1)}, bf16[2,80,1792]{2,1,0:T(8,128)(2,1)S(1)}) custom-call(s32[3]{0:T(128)S(1)} %pad_add_fusion.fact_ref, bf16[256,3584]{1,0:T(8,128)(2,1)S(1)} %bitcast.82, f32[1,3584]{1,0:T(1,128)S(1)} %reshape.113.gain_ref), custom_call_target="tpu_custom_call" | custom-call | tf_op jit(solution)/shard_map/pallas_call | solution.py:142
  21.6 1.9 %collective-permute-start.13 = (bf16[2,256,1792]{2,1,0:T(8,128)(2,1)S(1)}, bf16[2,256,1792]{2,1,0:T(8,128)(2,1)}, u32[]{:S(2)}, u32[]{:S(2)}) collective-permute-start(bf16[2,256,1792]{2,1,0:T(8,128)(2,1)S(1)} %get-tuple-element.20), channel_id=1, source_target_pairs={{0,64},{32,96},{2,66},{34,98},{4,68},{36,100},{6,70},{38,102},{64,... | collective-permute-start | bytes 5505032 | tf_op jit(solution)/shard_map/ppermute | solution.py:68
  23.8 1.2 maximum_select_fusion
  25.1 0.9 collective-permute-start.3
  26.0 1.9 %collective-permute-start.19 = (bf16[112,768]{1,0:T(8,128)(2,1)S(1)}, bf16[112,768]{1,0:T(8,128)(2,1)S(1)}, u32[]{:S(2)}, u32[]{:S(2)}) collective-permute-start(bf16[112,768]{1,0:T(8,128)(2,1)S(1)} %get-tuple-element.38), channel_id=1, source_target_pairs={{0,2},{32,38},{2,0},{34,36},{4,6},{36,34},{6,4},{38,32},{64,66},{9... | collective-permute-start | bytes 516104 | tf_op jit(solution)/shard_map/ppermute | solution.py:68
  28.1 2.2 %collective-permute-done.3 = bf16[112,640]{1,0:T(8,128)(2,1)S(1)} collective-permute-done((bf16[112,640]{1,0:T(8,128)(2,1)S(1)}, bf16[112,640]{1,0:T(8,128)(2,1)S(1)}, u32[]{:S(2)}, u32[]{:S(2)}) %collective-permute-start.3) | collective-permute-done | bytes 143392 | tf_op jit(solution)/shard_map/ppermute | solution.py:68
  30.3 0.6 collective-permute-start.4
  31.4 4.1 %collective-permute-start.20 = (bf16[2,112,768]{2,1,0:T(8,128)(2,1)S(1)}, bf16[2,112,768]{2,1,0:T(8,128)(2,1)S(1)}, u32[]{:S(2)}, u32[]{:S(2)}) collective-permute-start(bf16[2,112,768]{2,1,0:T(8,128)(2,1)S(1)} %pad_maximum_fusion.6), channel_id=1, source_target_pairs={{0,6},{32,34},{2,4},{34,32},{4,2},{36,38},{6,0},{38,36},{64,70},{9... | collective-permute-start | bytes 1032200 | tf_op jit(solution)/shard_map/ppermute | solution.py:68
  35.6 1.8 %collective-permute-done = bf16[2,80,1792]{2,1,0:T(8,128)(2,1)S(1)} collective-permute-done((bf16[2,80,1792]{2,1,0:T(8,128)(2,1)S(1)}, bf16[2,80,1792]{2,1,0:T(8,128)(2,1)S(1)}, u32[]{:S(2)}, u32[]{:S(2)}) %collective-permute-start) | collective-permute-done | bytes 573472 | tf_op jit(solution)/shard_map/ppermute | solution.py:68
  37.4 0.6 fusion.12
  38.7 2.0 %collective-permute-start.5 = (bf16[448,256]{1,0:T(8,128)(2,1)S(1)}, bf16[448,256]{1,0:T(8,128)(2,1)S(1)}, u32[]{:S(2)}, u32[]{:S(2)}) collective-permute-start(bf16[448,256]{1,0:T(8,128)(2,1)S(1)} %get-tuple-element.32), channel_id=1, source_target_pairs={{0,2},{32,38},{2,0},{34,36},{4,6},{36,34},{6,4},{38,32},{64,66},{9... | collective-permute-start | bytes 688136 | tf_op jit(solution)/shard_map/ppermute | solution.py:68
  40.8 4.0 %collective-permute-done.5 = bf16[448,256]{1,0:T(8,128)(2,1)S(1)} collective-permute-done((bf16[448,256]{1,0:T(8,128)(2,1)S(1)}, bf16[448,256]{1,0:T(8,128)(2,1)S(1)}, u32[]{:S(2)}, u32[]{:S(2)}) %collective-permute-start.5) | collective-permute-done | bytes 229408 | tf_op jit(solution)/shard_map/ppermute | solution.py:68
  44.9 4.1 %collective-permute-start.6 = (bf16[2,448,256]{2,1,0:T(8,128)(2,1)S(1)}, bf16[2,448,256]{2,1,0:T(8,128)(2,1)S(1)}, u32[]{:S(2)}, u32[]{:S(2)}) collective-permute-start(bf16[2,448,256]{2,1,0:T(8,128)(2,1)S(1)} %pad_maximum_fusion.5), channel_id=1, source_target_pairs={{0,6},{32,34},{2,4},{34,32},{4,2},{36,38},{6,0},{38,36},{64,70},{9... | collective-permute-start | bytes 1376264 | tf_op jit(solution)/shard_map/ppermute | solution.py:68
  49.1 6.4 %collective-permute-done.6 = bf16[2,448,256]{2,1,0:T(8,128)(2,1)S(1)} collective-permute-done((bf16[2,448,256]{2,1,0:T(8,128)(2,1)S(1)}, bf16[2,448,256]{2,1,0:T(8,128)(2,1)S(1)}, u32[]{:S(2)}, u32[]{:S(2)}) %collective-permute-start.6) | collective-permute-done | bytes 458784 | tf_op jit(solution)/shard_map/ppermute | solution.py:68
  56.3 1.2 broadcast_in_dim.55
  57.5 0.8 bitcast_dynamic-update-slice_fusion.5
  58.3 1.8 %broadcast_in_dim.60 = bf16[4,4,112,768]{3,2,1,0:T(8,128)(2,1)} broadcast(bf16[]{:T(256)} %constant.160.clone.1), dimensions={} | broadcast | bytes 2752514 | tf_op jit(solution)/shard_map/broadcast_in_dim | solution.py:370
  60.1 0.9 bitcast_dynamic-update-slice_fusion
  61.0 5.6 %collective-permute-done.21 = bf16[448,768]{1,0:T(8,128)(2,1)S(1)} collective-permute-done((bf16[448,768]{1,0:T(8,128)(2,1)S(1)}, bf16[448,768]{1,0:T(8,128)(2,1)S(1)}, u32[]{:S(2)}, u32[]{:S(2)}) %collective-permute-start.21) | collective-permute-done | bytes 688160 | tf_op jit(solution)/shard_map/ppermute | solution.py:68
  66.7 1.7 %collective-permute-start.22 = (bf16[448,768]{1,0:T(8,128)(2,1)S(1)}, bf16[448,768]{1,0:T(8,128)(2,1)S(1)}, u32[]{:S(2)}, u32[]{:S(2)}) collective-permute-start(bf16[448,768]{1,0:T(8,128)(2,1)S(1)} %collective-permute-done.21), channel_id=1, source_target_pairs={{0,8},{32,56},{2,10},{34,58},{4,12},{36,60},{6,14},{38,62},{64,72}... | collective-permute-start | bytes 2064392 | tf_op jit(solution)/shard_map/ppermute | solution.py:68
  69.2 0.9 constant_dynamic-update-slice_fusion.12
  70.2 7.4 %collective-permute-done.22 = bf16[448,768]{1,0:T(8,128)(2,1)S(1)} collective-permute-done((bf16[448,768]{1,0:T(8,128)(2,1)S(1)}, bf16[448,768]{1,0:T(8,128)(2,1)S(1)}, u32[]{:S(2)}, u32[]{:S(2)}) %collective-permute-start.22) | collective-permute-done | bytes 688160 | tf_op jit(solution)/shard_map/ppermute | solution.py:68
  77.6 2.9 %collective-permute-start.23 = (bf16[448,768]{1,0:T(8,128)(2,1)S(1)}, bf16[448,768]{1,0:T(8,128)(2,1)S(1)}, u32[]{:S(2)}, u32[]{:S(2)}) collective-permute-start(bf16[448,768]{1,0:T(8,128)(2,1)S(1)} %collective-permute-done.22), channel_id=1, source_target_pairs={{0,8},{32,56},{2,10},{34,58},{4,12},{36,60},{6,14},{38,62},{64,72}... | collective-permute-start | bytes 2064392 | tf_op jit(solution)/shard_map/ppermute | solution.py:68
  80.5 0.9 constant_dynamic-update-slice_fusion.11
  81.6 1.9 %collective-permute-start.16 = (bf16[2,2,64,128]{3,2,1,0:T(8,128)(2,1)S(1)}, bf16[2,2,64,128]{3,2,1,0:T(8,128)(2,1)S(1)}, u32[]{:S(2)}, u32[]{:S(2)}) collective-permute-start(bf16[2,2,64,128]{3,2,1,0:T(8,128)(2,1)S(1)} %pad_maximum_fusion.13), channel_id=1, source_target_pairs={{0,2},{32,38},{2,0},{34,36},{4,6},{36,34},{6,4},{38,32},{64,66},{9... | collective-permute-start | bytes 196616 | tf_op jit(solution)/shard_map/ppermute | solution.py:68
  83.6 6.3 %collective-permute-done.23 = bf16[448,768]{1,0:T(8,128)(2,1)S(1)} collective-permute-done((bf16[448,768]{1,0:T(8,128)(2,1)S(1)}, bf16[448,768]{1,0:T(8,128)(2,1)S(1)}, u32[]{:S(2)}, u32[]{:S(2)}) %collective-permute-start.23) | collective-permute-done | bytes 688160 | tf_op jit(solution)/shard_map/ppermute | solution.py:68
  89.8 0.9 constant_dynamic-update-slice_fusion.10
  90.8 3.3 %collective-permute-start.25 = (bf16[2,2,2,64,128]{4,3,2,1,0:T(8,128)(2,1)S(1)}, bf16[2,2,2,64,128]{4,3,2,1,0:T(8,128)(2,1)S(1)}, u32[]{:S(2)}, u32[]{:S(2)}) collective-permute-start(bf16[2,2,2,64,128]{4,3,2,1,0:T(8,128)(2,1)S(1)} %pad_maximum_fusion.11), channel_id=1, source_target_pairs={{0,6},{32,34},{2,4},{34,32},{4,2},{36,38},{6,0},{38,36},{64,70},{9... | collective-permute-start | bytes 393224 | tf_op jit(solution)/shard_map/ppermute | solution.py:68
  94.1 3.8 %collective-permute-start.10 = (bf16[2,2,2,80,128]{4,3,2,1,0:T(8,128)(2,1)S(1)}, bf16[2,2,2,80,128]{4,3,2,1,0:T(8,128)(2,1)S(1)}, u32[]{:S(2)}, u32[]{:S(2)}) collective-permute-start(bf16[2,2,2,80,128]{4,3,2,1,0:T(8,128)(2,1)S(1)} %pad_maximum_fusion.10), channel_id=1, source_target_pairs={{0,24},{32,40},{2,26},{34,42},{4,28},{36,44},{6,30},{38,46},{64,88... | collective-permute-start | bytes 491528 | tf_op jit(solution)/shard_map/ppermute | solution.py:68
  97.9 0.8 bitcast_dynamic-update-slice_fusion.4
  99.0 3.5 %collective-permute-done.10 = bf16[2,2,2,80,128]{4,3,2,1,0:T(8,128)(2,1)S(1)} collective-permute-done((bf16[2,2,2,80,128]{4,3,2,1,0:T(8,128)(2,1)S(1)}, bf16[2,2,2,80,128]{4,3,2,1,0:T(8,128)(2,1)S(1)}, u32[]{:S(2)}, u32[]{:S(2)}) %collective-permute-start.10) | collective-permute-done | bytes 163872 | tf_op jit(solution)/shard_map/ppermute | solution.py:68
  102.6 0.8 fusion.7
  103.3 0.8 bitcast_dynamic-update-slice_fusion.3
  104.1 4.3 %collective-permute-done.17 = bf16[448,384]{1,0:T(8,128)(2,1)S(1)} collective-permute-done((bf16[448,384]{1,0:T(8,128)(2,1)S(1)}, bf16[448,384]{1,0:T(8,128)(2,1)S(1)}, u32[]{:S(2)}, u32[]{:S(2)}) %collective-permute-start.17) | collective-permute-done | bytes 344096 | tf_op jit(solution)/shard_map/ppermute | solution.py:68
  108.5 0.8 bitcast_dynamic-update-slice_fusion.2
  109.3 0.9 pad_maximum_fusion.4
  110.1 3.7 %collective-permute-start.27 = (bf16[2,4,2,2,64,128]{5,4,3,2,1,0:T(8,128)(2,1)}, bf16[2,4,2,2,64,128]{5,4,3,2,1,0:T(8,128)(2,1)}, u32[]{:S(2)}, u32[]{:S(2)}) collective-permute-start(bf16[2,4,2,2,64,128]{5,4,3,2,1,0:T(8,128)(2,1)} %pad_maximum_fusion.4), channel_id=1, source_target_pairs={{0,24},{32,40},{2,26},{34,42},{4,28},{36,44},{6,30},{38,46},{64,88... | collective-permute-start | bytes 1572872 | tf_op jit(solution)/shard_map/ppermute | solution.py:68
  113.8 0.9 pad_maximum_fusion.3
  114.7 1.4 constant_dynamic-update-slice_fusion.9
  116.1 0.7 concatenate.101.info_ref
  116.8 2.9 %constant_dynamic-update-slice_fusion.8.x_ref = bf16[2,512,1792]{2,1,0:T(8,128)(2,1)} fusion(bf16[2,512,1792]{2,1,0:T(8,128)(2,1)} %constant_dynamic-update-slice_fusion.9, bf16[2,256,1792]{2,1,0:T(8,128)(2,1)} %collective-permute-done.13), kind=kLoop, calls=%fused_computation.45 | loop fusion | bytes 3670016 | tf_op jit(solution)/shard_map/concatenate | solution.py:362
  119.7 1.6 %collective-permute-done.27 = bf16[2,4,2,2,64,128]{5,4,3,2,1,0:T(8,128)(2,1)} collective-permute-done((bf16[2,4,2,2,64,128]{5,4,3,2,1,0:T(8,128)(2,1)}, bf16[2,4,2,2,64,128]{5,4,3,2,1,0:T(8,128)(2,1)}, u32[]{:S(2)}, u32[]{:S(2)}) %collective-permute-start.27) | collective-permute-done | bytes 524320 | tf_op jit(solution)/shard_map/ppermute | solution.py:68
  121.3 1.1 pad_maximum_fusion.1
  122.4 4.4 %collective-permute-done.12 = bf16[2,4,2,2,80,128]{5,4,3,2,1,0:T(8,128)(2,1)} collective-permute-done((bf16[2,4,2,2,80,128]{5,4,3,2,1,0:T(8,128)(2,1)}, bf16[2,4,2,2,80,128]{5,4,3,2,1,0:T(8,128)(2,1)}, u32[]{:S(2)}, u32[]{:S(2)}) %collective-permute-start.12) | collective-permute-done | bytes 655392 | tf_op jit(solution)/shard_map/ppermute | solution.py:68
  126.8 1.2 pad_maximum_fusion
  128.0 1.2 fusion.1
  129.4 2.0 %copy-done = bf16[2,512,1792]{2,1,0:T(8,128)(2,1)S(1)} copy-done((bf16[2,512,1792]{2,1,0:T(8,128)(2,1)S(1)}, bf16[2,512,1792]{2,1,0:T(8,128)(2,1)}, u32[]{:S(2)}) %copy-start) | copy-done | bytes 3670040
  131.4 3.8 %shard_map.93 = bf16[512,384]{1,0:T(8,128)(2,1)S(1)} custom-call(s32[1]{0:T(128)} %bitcast.5.side_ref, bf16[2,512,1792]{2,1,0:T(8,128)(2,1)S(1)} %copy-done, bf16[1792,384]{1,0:T(8,128)(2,1)} %bitcast.34.own_ref, bf16[1792,384]{1,0:T(8,128)(2,1)} %collective-permute-done.18.other_ref), custom_call_target="tpu_custom_call" | custom-call | tf_op jit(solution)/shard_map/pallas_call | solution.py:301
  135.3 5.6 %shard_map.94 = bf16[512,768]{1,0:T(8,128)(2,1)S(1)} custom-call(s32[1]{0:T(128)} %bitcast.5.side_ref, bf16[2,512,1792]{2,1,0:T(8,128)(2,1)S(1)} %copy-done, bf16[1792,768]{1,0:T(8,128)(2,1)} %bitcast.42.own_ref, bf16[1792,768]{1,0:T(8,128)(2,1)} %collective-permute-done.24.other_ref), custom_call_target="tpu_custom_call" | custom-call | tf_op jit(solution)/shard_map/pallas_call | solution.py:301
  141.0 5.1 %shard_map.96 = bf16[256,896]{1,0:T(8,128)(2,1)S(1)} custom-call(s32[68]{0:T(128)S(1)} %concatenate.101.info_ref, s32[64]{0:T(128)S(1)} %reshape.125.count_ref, bf16[256,384]{1,0:T(8,128)(2,1)S(1)} %get-tuple-element.33.part_a_ref, bf16[256,768]{1,0:T(8,128)(2,1)S(1)} %get-tuple-element.29.part_b_ref, bf16[32,2,80,128]{3,2,1,0:T(8,128)(2,1)S(1)} %bitcast.76, ...), custom_call_target="tpu_custom_call" | custom-call | tf_op jit(solution)/shard_map/pallas_call | solution.py:270
  146.4 6.0 %shard_map.95 = bf16[256,1792]{1,0:T(8,128)(2,1)} custom-call(s32[68]{0:T(128)S(1)} %concatenate.80.info_ref, s32[64]{0:T(128)S(1)} %reshape.125.count_ref, bf16[256,384]{1,0:T(8,128)(2,1)S(1)} %get-tuple-element.34.part_a_ref, bf16[256,768]{1,0:T(8,128)(2,1)S(1)} %get-tuple-element.30.part_b_ref, bf16[32,2,80,128]{3,2,1,0:T(8,128)(2,1)S(1)} %bitcast.77, ...), custom_call_target="tpu_custom_call" | custom-call | tf_op jit(solution)/shard_map/pallas_call | solution.py:270
  152.4 4.2 %collective-permute-done.28 = bf16[256,896]{1,0:T(8,128)(2,1)} collective-permute-done((bf16[256,896]{1,0:T(8,128)(2,1)S(1)}, bf16[256,896]{1,0:T(8,128)(2,1)}, u32[]{:S(2)}, u32[]{:S(2)}) %collective-permute-start.28) | collective-permute-done | bytes 458784 | tf_op jit(solution)/shard_map/ppermute | solution.py:68
  156.6 1.8 %bitcast_dynamic-update-slice_fusion.1 = bf16[1,256,1792]{2,1,0:T(8,128)(2,1)} fusion(bf16[1,256,1792]{2,1,0:T(8,128)(2,1)} %bitcast.98, s32[]{:T(128)S(6)} %select_n.307, bf16[256,896]{1,0:T(8,128)(2,1)} %collective-permute-done.28), kind=kLoop, calls=%fused_computation.7 | loop fusion | bytes 917508 | tf_op jit(solution)/shard_map/dynamic_update_slice | solution.py:459
  (87 shorter events, 4.3 us)
Async XLA Ops:
  3.8 4.6 %collective-permute-start.1 = (bf16[28,1408]{1,0:T(8,128)(2,1)S(1)}, bf16[28,1408]{1,0:T(8,128)(2,1)S(1)}, u32[]{:S(2)}, u32[]{:S(2)}) collective-permute-start(bf16[28,1408]{1,0:T(8,128)(2,1)S(1)} %get-tuple-element.44), channel_id=1, source_target_pairs={{0,64},{32,96},{2,66},{34,98},{4,68},{36,100},{6,70},{38,102},{64,... | collective-permute-start | bytes 236552 | tf_op jit(solution)/shard_map/ppermute | solution.py:68
  9.1 14.7 %collective-permute-start.2 = (bf16[56,1408]{1,0:T(8,128)(2,1)}, bf16[56,1408]{1,0:T(8,128)(2,1)}, u32[]{:S(2)}, u32[]{:S(2)}) collective-permute-start(bf16[56,1408]{1,0:T(8,128)(2,1)} %maximum_select_fusion.1), channel_id=1, source_target_pairs={{0,65},{32,97},{2,67},{34,99},{4,69},{36,101},{6,71},{38,103},{64,... | collective-permute-start | bytes 473096 | tf_op jit(solution)/shard_map/ppermute | solution.py:68
  14.3 1.5 copy-start.1
  21.4 16.0 %collective-permute-start = (bf16[2,80,1792]{2,1,0:T(8,128)(2,1)S(1)}, bf16[2,80,1792]{2,1,0:T(8,128)(2,1)S(1)}, u32[]{:S(2)}, u32[]{:S(2)}) collective-permute-start(bf16[2,80,1792]{2,1,0:T(8,128)(2,1)S(1)} %get-tuple-element.17), channel_id=1, source_target_pairs={{0,64},{32,96},{2,66},{34,98},{4,68},{36,100},{6,70},{38,102},{64,... | collective-permute-start | bytes 1720328 | tf_op jit(solution)/shard_map/ppermute | solution.py:68
  21.6 95.2 %collective-permute-start.13 = (bf16[2,256,1792]{2,1,0:T(8,128)(2,1)S(1)}, bf16[2,256,1792]{2,1,0:T(8,128)(2,1)}, u32[]{:S(2)}, u32[]{:S(2)}) collective-permute-start(bf16[2,256,1792]{2,1,0:T(8,128)(2,1)S(1)} %get-tuple-element.20), channel_id=1, source_target_pairs={{0,64},{32,96},{2,66},{34,98},{4,68},{36,100},{6,70},{38,102},{64,... | collective-permute-start | bytes 5505032 | tf_op jit(solution)/shard_map/ppermute | solution.py:68
  25.1 5.2 %collective-permute-start.3 = (bf16[112,640]{1,0:T(8,128)(2,1)S(1)}, bf16[112,640]{1,0:T(8,128)(2,1)S(1)}, u32[]{:S(2)}, u32[]{:S(2)}) collective-permute-start(bf16[112,640]{1,0:T(8,128)(2,1)S(1)} %get-tuple-element.40), channel_id=1, source_target_pairs={{0,8},{32,56},{2,10},{34,58},{4,12},{36,60},{6,14},{38,62},{64,72}... | collective-permute-start | bytes 430088 | tf_op jit(solution)/shard_map/ppermute | solution.py:68
  26.0 5.4 %collective-permute-start.19 = (bf16[112,768]{1,0:T(8,128)(2,1)S(1)}, bf16[112,768]{1,0:T(8,128)(2,1)S(1)}, u32[]{:S(2)}, u32[]{:S(2)}) collective-permute-start(bf16[112,768]{1,0:T(8,128)(2,1)S(1)} %get-tuple-element.38), channel_id=1, source_target_pairs={{0,2},{32,38},{2,0},{34,36},{4,6},{36,34},{6,4},{38,32},{64,66},{9... | collective-permute-start | bytes 516104 | tf_op jit(solution)/shard_map/ppermute | solution.py:68
  30.3 8.3 %collective-permute-start.4 = (bf16[2,112,640]{2,1,0:T(8,128)(2,1)S(1)}, bf16[2,112,640]{2,1,0:T(8,128)(2,1)S(1)}, u32[]{:S(2)}, u32[]{:S(2)}) collective-permute-start(bf16[2,112,640]{2,1,0:T(8,128)(2,1)S(1)} %pad_maximum_fusion.8), channel_id=1, source_target_pairs={{0,24},{32,40},{2,26},{34,42},{4,28},{36,44},{6,30},{38,46},{64,88... | collective-permute-start | bytes 860168 | tf_op jit(solution)/shard_map/ppermute | solution.py:68
  31.4 17.6 %collective-permute-start.20 = (bf16[2,112,768]{2,1,0:T(8,128)(2,1)S(1)}, bf16[2,112,768]{2,1,0:T(8,128)(2,1)S(1)}, u32[]{:S(2)}, u32[]{:S(2)}) collective-permute-start(bf16[2,112,768]{2,1,0:T(8,128)(2,1)S(1)} %pad_maximum_fusion.6), channel_id=1, source_target_pairs={{0,6},{32,34},{2,4},{34,32},{4,2},{36,38},{6,0},{38,36},{64,70},{9... | collective-permute-start | bytes 1032200 | tf_op jit(solution)/shard_map/ppermute | solution.py:68
  37.4 7.5 %copy-start.2 = (bf16[2,80,1792]{2,1,0:T(8,128)(2,1)}, bf16[2,80,1792]{2,1,0:T(8,128)(2,1)S(1)}, u32[]{:S(2)}) copy-start(bf16[2,80,1792]{2,1,0:T(8,128)(2,1)S(1)} %collective-permute-done) | copy-start | bytes 1720324
  38.7 6.1 %collective-permute-start.5 = (bf16[448,256]{1,0:T(8,128)(2,1)S(1)}, bf16[448,256]{1,0:T(8,128)(2,1)S(1)}, u32[]{:S(2)}, u32[]{:S(2)}) collective-permute-start(bf16[448,256]{1,0:T(8,128)(2,1)S(1)} %get-tuple-element.32), channel_id=1, source_target_pairs={{0,2},{32,38},{2,0},{34,36},{4,6},{36,34},{6,4},{38,32},{64,66},{9... | collective-permute-start | bytes 688136 | tf_op jit(solution)/shard_map/ppermute | solution.py:68
  44.9 10.6 %collective-permute-start.6 = (bf16[2,448,256]{2,1,0:T(8,128)(2,1)S(1)}, bf16[2,448,256]{2,1,0:T(8,128)(2,1)S(1)}, u32[]{:S(2)}, u32[]{:S(2)}) collective-permute-start(bf16[2,448,256]{2,1,0:T(8,128)(2,1)S(1)} %pad_maximum_fusion.5), channel_id=1, source_target_pairs={{0,6},{32,34},{2,4},{34,32},{4,2},{36,38},{6,0},{38,36},{64,70},{9... | collective-permute-start | bytes 1376264 | tf_op jit(solution)/shard_map/ppermute | solution.py:68
  49.0 7.2 %slice-start = ((bf16[2,80,1792]{2,1,0:T(8,128)(2,1)}), bf16[2,64,1792]{2,1,0:T(8,128)(2,1)S(1)}, s32[]{:S(2)}) async-start(bf16[2,80,1792]{2,1,0:T(8,128)(2,1)} %copy-done.2), calls=%async_computation | async-start | bytes 917504 | tf_op jit(solution)/shard_map/slice | solution.py:365
  55.5 12.8 %collective-permute-start.7 = (bf16[1792,256]{1,0:T(8,128)(2,1)S(1)}, bf16[1792,256]{1,0:T(8,128)(2,1)S(1)}, u32[]{:S(2)}, u32[]{:S(2)}) collective-permute-start(bf16[1792,256]{1,0:T(8,128)(2,1)S(1)} %bitcast.80), channel_id=1, source_target_pairs={{0,32},{32,0},{2,34},{34,2},{4,36},{36,4},{6,38},{38,6},{64,96},{9... | collective-permute-start | bytes 2752520 | tf_op jit(solution)/shard_map/ppermute | solution.py:68
  55.6 11.0 %collective-permute-start.21 = (bf16[448,768]{1,0:T(8,128)(2,1)S(1)}, bf16[448,768]{1,0:T(8,128)(2,1)S(1)}, u32[]{:S(2)}, u32[]{:S(2)}) collective-permute-start(bf16[448,768]{1,0:T(8,128)(2,1)S(1)} %bitcast.88), channel_id=1, source_target_pairs={{0,8},{32,56},{2,10},{34,58},{4,12},{36,60},{6,14},{38,62},{64,72}... | collective-permute-start | bytes 2064392 | tf_op jit(solution)/shard_map/ppermute | solution.py:68
  61.0 20.4 %collective-permute-start.14 = (bf16[448,384]{1,0:T(8,128)(2,1)S(1)}, bf16[448,384]{1,0:T(8,128)(2,1)S(1)}, u32[]{:S(2)}, u32[]{:S(2)}) collective-permute-start(bf16[448,384]{1,0:T(8,128)(2,1)S(1)} %slice.180), channel_id=1, source_target_pairs={{0,2},{32,38},{2,4},{34,32},{4,6},{36,34},{6,0},{38,36},{64,66},{9... | collective-permute-start | bytes 1032200 | tf_op jit(solution)/shard_map/ppermute | solution.py:68
  66.7 10.9 %collective-permute-start.22 = (bf16[448,768]{1,0:T(8,128)(2,1)S(1)}, bf16[448,768]{1,0:T(8,128)(2,1)S(1)}, u32[]{:S(2)}, u32[]{:S(2)}) collective-permute-start(bf16[448,768]{1,0:T(8,128)(2,1)S(1)} %collective-permute-done.21), channel_id=1, source_target_pairs={{0,8},{32,56},{2,10},{34,58},{4,12},{36,60},{6,14},{38,62},{64,72}... | collective-permute-start | bytes 2064392 | tf_op jit(solution)/shard_map/ppermute | solution.py:68
  68.9 8.7 %collective-permute-start.8 = (bf16[2,144,128]{2,1,0:T(8,128)(2,1)S(1)}, bf16[2,144,128]{2,1,0:T(8,128)(2,1)S(1)}, u32[]{:S(2)}, u32[]{:S(2)}) collective-permute-start(bf16[2,144,128]{2,1,0:T(8,128)(2,1)S(1)} %maximum_select_fusion.3), channel_id=1, source_target_pairs={{0,65},{32,97},{2,67},{34,99},{4,69},{36,101},{6,71},{38,103},{64,... | collective-permute-start | bytes 221192 | tf_op jit(solution)/shard_map/ppermute | solution.py:68
  77.6 12.2 %collective-permute-start.23 = (bf16[448,768]{1,0:T(8,128)(2,1)S(1)}, bf16[448,768]{1,0:T(8,128)(2,1)S(1)}, u32[]{:S(2)}, u32[]{:S(2)}) collective-permute-start(bf16[448,768]{1,0:T(8,128)(2,1)S(1)} %collective-permute-done.22), channel_id=1, source_target_pairs={{0,8},{32,56},{2,10},{34,58},{4,12},{36,60},{6,14},{38,62},{64,72}... | collective-permute-start | bytes 2064392 | tf_op jit(solution)/shard_map/ppermute | solution.py:68
  81.4 17.4 %collective-permute-start.15 = (bf16[448,384]{1,0:T(8,128)(2,1)S(1)}, bf16[448,384]{1,0:T(8,128)(2,1)S(1)}, u32[]{:S(2)}, u32[]{:S(2)}) collective-permute-start(bf16[448,384]{1,0:T(8,128)(2,1)S(1)} %collective-permute-done.14), channel_id=1, source_target_pairs={{0,2},{32,38},{2,4},{34,32},{4,6},{36,34},{6,0},{38,36},{64,66},{9... | collective-permute-start | bytes 1032200 | tf_op jit(solution)/shard_map/ppermute | solution.py:68
  81.5 12.6 %collective-permute-start.9 = (bf16[2,2,80,128]{3,2,1,0:T(8,128)(2,1)S(1)}, bf16[2,2,80,128]{3,2,1,0:T(8,128)(2,1)S(1)}, u32[]{:S(2)}, u32[]{:S(2)}) collective-permute-start(bf16[2,2,80,128]{3,2,1,0:T(8,128)(2,1)S(1)} %fusion), channel_id=1, source_target_pairs={{0,8},{32,56},{2,10},{34,58},{4,12},{36,60},{6,14},{38,62},{64,72}... | collective-permute-start | bytes 245768 | tf_op jit(solution)/shard_map/ppermute | solution.py:68
  81.6 9.1 %collective-permute-start.16 = (bf16[2,2,64,128]{3,2,1,0:T(8,128)(2,1)S(1)}, bf16[2,2,64,128]{3,2,1,0:T(8,128)(2,1)S(1)}, u32[]{:S(2)}, u32[]{:S(2)}) collective-permute-start(bf16[2,2,64,128]{3,2,1,0:T(8,128)(2,1)S(1)} %pad_maximum_fusion.13), channel_id=1, source_target_pairs={{0,2},{32,38},{2,0},{34,36},{4,6},{36,34},{6,4},{38,32},{64,66},{9... | collective-permute-start | bytes 196616 | tf_op jit(solution)/shard_map/ppermute | solution.py:68
  90.7 44.5 %collective-permute-start.24 = (bf16[1792,768]{1,0:T(8,128)(2,1)}, bf16[1792,768]{1,0:T(8,128)(2,1)}, u32[]{:S(2)}, u32[]{:S(2)}) collective-permute-start(bf16[1792,768]{1,0:T(8,128)(2,1)} %bitcast.42.own_ref), channel_id=1, source_target_pairs={{0,32},{32,0},{2,34},{34,2},{4,36},{36,4},{6,38},{38,6},{64,96},{9... | collective-permute-start | bytes 8257544 | tf_op jit(solution)/shard_map/ppermute | solution.py:68
  90.8 7.9 %collective-permute-start.25 = (bf16[2,2,2,64,128]{4,3,2,1,0:T(8,128)(2,1)S(1)}, bf16[2,2,2,64,128]{4,3,2,1,0:T(8,128)(2,1)S(1)}, u32[]{:S(2)}, u32[]{:S(2)}) collective-permute-start(bf16[2,2,2,64,128]{4,3,2,1,0:T(8,128)(2,1)S(1)} %pad_maximum_fusion.11), channel_id=1, source_target_pairs={{0,6},{32,34},{2,4},{34,32},{4,2},{36,38},{6,0},{38,36},{64,70},{9... | collective-permute-start | bytes 393224 | tf_op jit(solution)/shard_map/ppermute | solution.py:68
  94.1 8.5 %collective-permute-start.10 = (bf16[2,2,2,80,128]{4,3,2,1,0:T(8,128)(2,1)S(1)}, bf16[2,2,2,80,128]{4,3,2,1,0:T(8,128)(2,1)S(1)}, u32[]{:S(2)}, u32[]{:S(2)}) collective-permute-start(bf16[2,2,2,80,128]{4,3,2,1,0:T(8,128)(2,1)S(1)} %pad_maximum_fusion.10), channel_id=1, source_target_pairs={{0,24},{32,40},{2,26},{34,42},{4,28},{36,44},{6,30},{38,46},{64,88... | collective-permute-start | bytes 491528 | tf_op jit(solution)/shard_map/ppermute | solution.py:68
  98.7 10.6 %collective-permute-start.26 = (bf16[4,2,2,64,128]{4,3,2,1,0:T(8,128)(2,1)S(1)}, bf16[4,2,2,64,128]{4,3,2,1,0:T(8,128)(2,1)S(1)}, u32[]{:S(2)}, u32[]{:S(2)}) collective-permute-start(bf16[4,2,2,64,128]{4,3,2,1,0:T(8,128)(2,1)S(1)} %get-tuple-element.42), channel_id=1, source_target_pairs={{0,8},{32,56},{2,10},{34,58},{4,12},{36,60},{6,14},{38,62},{64,72}... | collective-permute-start | bytes 786440 | tf_op jit(solution)/shard_map/ppermute | solution.py:68
  98.8 9.7 %collective-permute-start.17 = (bf16[448,384]{1,0:T(8,128)(2,1)S(1)}, bf16[448,384]{1,0:T(8,128)(2,1)S(1)}, u32[]{:S(2)}, u32[]{:S(2)}) collective-permute-start(bf16[448,384]{1,0:T(8,128)(2,1)S(1)} %collective-permute-done.15), channel_id=1, source_target_pairs={{0,2},{32,38},{2,4},{34,32},{4,6},{36,34},{6,0},{38,36},{64,66},{9... | collective-permute-start | bytes 1032200 | tf_op jit(solution)/shard_map/ppermute | solution.py:68
  103.3 10.5 %collective-permute-start.11 = (bf16[4,2,2,80,128]{4,3,2,1,0:T(8,128)(2,1)}, bf16[4,2,2,80,128]{4,3,2,1,0:T(8,128)(2,1)S(1)}, u32[]{:S(2)}, u32[]{:S(2)}) collective-permute-start(bf16[4,2,2,80,128]{4,3,2,1,0:T(8,128)(2,1)} %get-tuple-element.36), channel_id=1, source_target_pairs={{0,2},{32,38},{2,0},{34,36},{4,6},{36,34},{6,4},{38,32},{64,66},{9... | collective-permute-start | bytes 983048 | tf_op jit(solution)/shard_map/ppermute | solution.py:68
  109.2 20.1 %collective-permute-start.18 = (bf16[1792,384]{1,0:T(8,128)(2,1)}, bf16[1792,384]{1,0:T(8,128)(2,1)}, u32[]{:S(2)}, u32[]{:S(2)}) collective-permute-start(bf16[1792,384]{1,0:T(8,128)(2,1)} %bitcast.34.own_ref), channel_id=1, source_target_pairs={{0,32},{32,0},{2,34},{34,2},{4,36},{36,4},{6,38},{38,6},{64,96},{9... | collective-permute-start | bytes 4128776 | tf_op jit(solution)/shard_map/ppermute | solution.py:68
  109.2 6.8 %copy-start.3 = (bf16[4,2,2,64,128]{4,3,2,1,0:T(8,128)(2,1)}, bf16[4,2,2,64,128]{4,3,2,1,0:T(8,128)(2,1)S(1)}, u32[]{:S(2)}) copy-start(bf16[4,2,2,64,128]{4,3,2,1,0:T(8,128)(2,1)S(1)} %collective-permute-done.26) | copy-start | bytes 786436
  110.1 11.1 %collective-permute-start.27 = (bf16[2,4,2,2,64,128]{5,4,3,2,1,0:T(8,128)(2,1)}, bf16[2,4,2,2,64,128]{5,4,3,2,1,0:T(8,128)(2,1)}, u32[]{:S(2)}, u32[]{:S(2)}) collective-permute-start(bf16[2,4,2,2,64,128]{5,4,3,2,1,0:T(8,128)(2,1)} %pad_maximum_fusion.4), channel_id=1, source_target_pairs={{0,24},{32,40},{2,26},{34,42},{4,28},{36,44},{6,30},{38,46},{64,88... | collective-permute-start | bytes 1572872 | tf_op jit(solution)/shard_map/ppermute | solution.py:68
  114.7 12.1 %collective-permute-start.12 = (bf16[2,4,2,2,80,128]{5,4,3,2,1,0:T(8,128)(2,1)}, bf16[2,4,2,2,80,128]{5,4,3,2,1,0:T(8,128)(2,1)}, u32[]{:S(2)}, u32[]{:S(2)}) collective-permute-start(bf16[2,4,2,2,80,128]{5,4,3,2,1,0:T(8,128)(2,1)} %pad_maximum_fusion.3), channel_id=1, source_target_pairs={{0,6},{32,34},{2,4},{34,32},{4,2},{36,38},{6,0},{38,36},{64,70},{9... | collective-permute-start | bytes 1966088 | tf_op jit(solution)/shard_map/ppermute | solution.py:68
  116.8 4.5 %copy-start.4 = (bf16[4,2,2,64,128]{4,3,2,1,0:T(8,128)(2,1)S(1)}, bf16[4,2,2,64,128]{4,3,2,1,0:T(8,128)(2,1)}, u32[]{:S(2)}) copy-start(bf16[4,2,2,64,128]{4,3,2,1,0:T(8,128)(2,1)} %copy-done.3) | copy-start | bytes 786436
  129.4 2.0 %copy-start = (bf16[2,512,1792]{2,1,0:T(8,128)(2,1)S(1)}, bf16[2,512,1792]{2,1,0:T(8,128)(2,1)}, u32[]{:S(2)}) copy-start(bf16[2,512,1792]{2,1,0:T(8,128)(2,1)} %constant_dynamic-update-slice_fusion.8.x_ref) | copy-start | bytes 11010052
  146.1 10.5 %collective-permute-start.28 = (bf16[256,896]{1,0:T(8,128)(2,1)S(1)}, bf16[256,896]{1,0:T(8,128)(2,1)}, u32[]{:S(2)}, u32[]{:S(2)}) collective-permute-start(bf16[256,896]{1,0:T(8,128)(2,1)S(1)} %shard_map.96), channel_id=1, source_target_pairs={{0,64},{32,96},{2,66},{34,98},{4,68},{36,100},{6,70},{38,102},{64,... | collective-permute-start | bytes 1376264 | tf_op jit(solution)/shard_map/ppermute | solution.py:68

commit v5 on v4

--- a/solution.py
+++ b/solution.py
@@ -42,11 +42,6 @@
 SWAP = make_perm(lambda x, y, z, c: (x, y, z, 1 - c))
 MATE = make_perm(lambda x, y, z, c: (x, y ^ 1, z, c))
 ACROSS = make_perm(lambda x, y, z, c: (x, y ^ 3, z, c))
-RING = {
-    "x": make_perm(lambda x, y, z, c: (x + 1 - 2 * c, y, z, c)),
-    "z": make_perm(lambda x, y, z, c: (x, y, z + 1 - 2 * c, c)),
-}
-
 
 def flip(axis, turn):
     def partner(x, y, z, c):
@@ -59,21 +54,23 @@
 
 FLIP = {(axis, turn): flip(axis, turn) for axis in "xz" for turn in (0, 1)}
 
-CUTS = (0, 256, 640, 1408)
-KEPT = 1
-HALF = WIDTH // 2
+EARLY = 2 * D
+LATE = (2 + HEADS) * D
+SLAB = WIDTH // 4
+PAIRED = ((0, 1, 2, 3), (0, 3, 1, 2))
 
 
 def send(value, pairs):
     return lax.ppermute(value, AXES, pairs)
 
 
-def feature_runs():
+def feature_runs(last):
     starts = []
     for c in range(2):
-        for z in range(4):
-            for x in range(4):
-                for y in (0, 1, 2, 3):
+        for i in PAIRED[c]:
+            for j in range(4):
+                for y in range(4):
+                    x, z = (i, j) if last == "x" else (j, i)
                     starts.append(device_id(x, y, z, c) * ROWS)
     source = np.concatenate([np.arange(s, s + ROWS) for s in starts])
     tiles = []
@@ -91,9 +88,9 @@
     return tiles
 
 
-def reorder(plain_ref, out_ref, count, out_rows):
+def reorder(plain_ref, out_ref, last, count, out_rows):
     lane = lax.broadcasted_iota(jnp.int32, (count, 128), 1)
-    for tile, runs in enumerate(feature_runs()):
+    for tile, runs in enumerate(feature_runs(last)):
         joined = jnp.zeros((count, 128), jnp.float32)
         for first, end, feature in runs:
             block, offset = divmod(feature, 128)
@@ -102,11 +99,12 @@
             if shift:
                 piece = pltpu.roll(piece, shift, 1)
             joined = jnp.where((lane >= first) & (lane < end), piece, joined)
-        side, column = divmod(tile, HALF // 128)
-        out_ref[side, out_rows, column * 128 : (column + 1) * 128] = joined.astype(jnp.bfloat16)
-
-
-def norm_body(fact_ref, tokens_ref, gain_ref, out_ref, pool_ref, plain_ref, normed_ref):
+        slab, column = divmod(tile, SLAB // 128)
+        out_ref[slab, out_rows, column * 128 : (column + 1) * 128] = joined.astype(jnp.bfloat16)
+
+
+def norm_body(fact_ref, tokens_ref, gain_ref, near_ref, far_ref, *scratch):
+    out_ref, pool_ref, plain_ref, normed_ref = scratch
     rows = 64
     level, valid, count = fact_ref[0], fact_ref[1], fact_ref[2]
 
@@ -117,7 +115,7 @@
         factor = lax.rsqrt(jnp.mean(values * values, axis=-1, keepdims=True) + EPS)
         plain_ref[...] = values * factor * gain_ref[...]
         normed_ref[here, :] = plain_ref[...].astype(jnp.bfloat16)
-        reorder(plain_ref, out_ref, rows, here)
+        reorder(plain_ref, out_ref, "x", rows, here)
 
     shift = level + 2
     live = jnp.right_shift(TOK, shift)
@@ -130,11 +128,16 @@
         window.astype(jnp.bfloat16), normed_ref[...], preferred_element_type=jnp.float32
     )
     plain_ref[...] = sums / size
-    reorder(plain_ref, pool_ref, SLOTS, pl.ds(0, SLOTS))
-    row = lax.broadcasted_iota(jnp.int32, (16, HALF), 0)
+    reorder(plain_ref, pool_ref, "z", SLOTS, pl.ds(0, SLOTS))
+    row = lax.broadcasted_iota(jnp.int32, (16, SLAB), 0)
     facts = jnp.where(row < 8, count, valid).astype(jnp.float32).astype(jnp.bfloat16)
-    for side in range(2):
-        pool_ref[side, pl.ds(SLOTS, 16), :] = facts
+    for i in range(2):
+        near_ref[i, :TOK, :] = out_ref[fact_ref[3 + i]]
+        far_ref[i] = out_ref[fact_ref[5 + i]]
+        for j in range(2):
+            lines = slice(TOK + j * (SLOTS + 16), TOK + j * (SLOTS + 16) + SLOTS)
+            near_ref[i, lines, :] = pool_ref[2 * i + j]
+            near_ref[i, lines.stop : lines.stop + 16, :] = facts
 
 
 def norm_rows(facts, tokens, gain):
@@ -142,16 +145,18 @@
     return pl.pallas_call(
         norm_body,
         out_shape=[
-            jax.ShapeDtypeStruct((2, TOK, HALF), jnp.bfloat16),
-            jax.ShapeDtypeStruct((2, SLOTS + 16, HALF), jnp.bfloat16),
+            jax.ShapeDtypeStruct((2, TOK + 2 * (SLOTS + 16), SLAB), jnp.bfloat16),
+            jax.ShapeDtypeStruct((2, TOK, SLAB), jnp.bfloat16),
         ],
         in_specs=[pl.BlockSpec(memory_space=pltpu.SMEM), vmem, vmem],
         out_specs=[vmem, vmem],
         scratch_shapes=[
+            pltpu.VMEM((4, TOK, SLAB), jnp.bfloat16),
+            pltpu.VMEM((4, SLOTS, SLAB), jnp.bfloat16),
             pltpu.VMEM((64, WIDTH), jnp.float32),
             pltpu.VMEM((TOK, WIDTH), jnp.bfloat16),
         ],
-        compiler_params=pltpu.CompilerParams(vmem_limit_bytes=32 * 1024 * 1024),
+        compiler_params=pltpu.CompilerParams(vmem_limit_bytes=16 * 1024 * 1024),
     )(facts, tokens, gain.reshape(1, WIDTH))
 
 
@@ -160,7 +165,7 @@
 LINES = HEADS * TOK
 
 
-def attend_body(wide, info_ref, count_ref, part_a_ref, part_b_ref, far_k_ref, far_v_ref, *rest):
+def attend_body(wide, info_ref, count_ref, part_ref, far_k_ref, far_v_ref, *rest):
     out_ref, query_ref, keys_ref, values_ref, bias_ref, score_ref, top_ref, sum_ref, mix_ref = rest
     span, valid, column, which = info_ref[0], info_ref[1], info_ref[2], info_ref[3]
 
@@ -196,13 +201,10 @@
     near_bias = jnp.where((col <= row) & (col < valid), 0.0, FILL)
     for head in range(HEADS):
         here = slice(head * TOK, (head + 1) * TOK)
-        if head < KEPT:
-            query = part_a_ref[:, (2 + head) * D : (3 + head) * D]
-        else:
-            query = part_b_ref[:, (head - KEPT) * D : (head - KEPT + 1) * D]
+        query = part_ref[:, (2 + head) * D : (3 + head) * D]
         query_ref[here, :] = query
         near = lax.dot_general(
-            query, part_a_ref[:, :D], contract, preferred_element_type=jnp.float32
+            query, part_ref[:, :D], contract, preferred_element_type=jnp.float32
         )
         near = near + near_bias
         score_ref[here, ROOM:] = near
@@ -234,7 +236,7 @@
         sum_ref[lines, :] = fold(jnp.add, weight)
         mix_ref[lines, :] = jnp.dot(
             weight.astype(jnp.bfloat16),
-            part_a_ref[:, D : 2 * D],
+            part_ref[:, D : 2 * D],
             preferred_element_type=jnp.float32,
         )
 
@@ -264,13 +266,13 @@
             out_ref[:, head * D : (head + 1) * D] = result
 
 
-def attend(wide, info, counts, part_a, part_b, far_k, far_v):
+def attend(wide, info, counts, part, far_k, far_v):
     columns = 2 * HEADS * D if wide else HEADS * D
     smem, vmem = pl.BlockSpec(memory_space=pltpu.SMEM), pl.BlockSpec(memory_space=pltpu.VMEM)
     return pl.pallas_call(
         functools.partial(attend_body, wide),
         out_shape=jax.ShapeDtypeStruct((TOK, columns), jnp.bfloat16),
-        in_specs=[smem, smem, vmem, vmem, vmem, vmem],
+        in_specs=[smem, smem, vmem, vmem, vmem],
         out_specs=vmem,
         scratch_shapes=[
             pltpu.VMEM((LINES, D), jnp.bfloat16),
@@ -282,33 +284,64 @@
             pltpu.VMEM((LINES, D), jnp.float32),
             pltpu.VMEM((LINES, D), jnp.float32),
         ],
-        compiler_params=pltpu.CompilerParams(vmem_limit_bytes=44 * 1024 * 1024),
-    )(info, counts, part_a, part_b, far_k, far_v)
-
-
-def project_body(side_ref, x_ref, own_ref, other_ref, out_ref):
-    side = side_ref[0]
-    columns = own_ref.shape[1]
+        compiler_params=pltpu.CompilerParams(vmem_limit_bytes=28 * 1024 * 1024),
+    )(info, counts, part, far_k, far_v)
+
+
+def project_body(count, slab_ref, x_ref, *refs):
+    weights, total_refs, out_ref = refs[:count], refs[count:-1], refs[-1]
+    rows, columns = out_ref.shape
     for first in range(0, columns, 256):
         here = slice(first, min(first + 256, columns))
-        out = jnp.dot(x_ref[side], own_ref[:, here], preferred_element_type=jnp.float32)
-        out += jnp.dot(x_ref[1 - side], other_ref[:, here], preferred_element_type=jnp.float32)
-        out_ref[:, here] = out.astype(jnp.bfloat16)
-
-
-def project_kernel(side, x, own, other):
+        out = total_refs[0][:, here] if total_refs else None
+        for i in range(count):
+            x = x_ref[slab_ref[i], :rows, :]
+            term = jnp.dot(x, weights[i][:, here], preferred_element_type=jnp.float32)
+            out = term if out is None else out + term
+        out_ref[:, here] = out.astype(out_ref.dtype)
+
+
+def project(slabs, x, weights, total=None, last=False, rows=TOK):
+    smem, vmem = pl.BlockSpec(memory_space=pltpu.SMEM), pl.BlockSpec(memory_space=pltpu.VMEM)
+    totals = () if total is None else (total,)
+    dtype = jnp.bfloat16 if last else jnp.float32
+    return pl.pallas_call(
+        functools.partial(project_body, len(weights)),
+        out_shape=jax.ShapeDtypeStruct((rows, weights[0].shape[1]), dtype),
+        in_specs=[smem] + [vmem] * (1 + len(weights) + len(totals)),
+        out_specs=vmem,
+        compiler_params=pltpu.CompilerParams(vmem_limit_bytes=16 * 1024 * 1024),
+    )(jnp.stack(slabs).astype(jnp.int32), x, *weights, *totals)
+
+
+def after(value, other):
+    return lax.optimization_barrier((value, other))[0]
+
+
+def halves_body(head_ref, *refs):
+    mine_ref, other_ref = refs[-2:]
+
+    def copy(mine):
+        at = 0
+        for ref in refs[:-2]:
+            size = ref.shape[1] // 2
+            mine_ref[:, at : at + size] = ref[:, mine * size : (mine + 1) * size]
+            other_ref[:, at : at + size] = ref[:, (1 - mine) * size : (2 - mine) * size]
+            at += size
+
+    for mine in range(2):
+        pl.when(head_ref[0] == mine)(functools.partial(copy, mine))
+
+
+def halves(head, *weights):
     smem, vmem = pl.BlockSpec(memory_space=pltpu.SMEM), pl.BlockSpec(memory_space=pltpu.VMEM)
     return pl.pallas_call(
-        project_body,
-        out_shape=jax.ShapeDtypeStruct((x.shape[1], own.shape[1]), jnp.bfloat16),
-        in_specs=[smem, vmem, vmem, vmem],
-        out_specs=vmem,
-        compiler_params=pltpu.CompilerParams(vmem_limit_bytes=32 * 1024 * 1024),
-    )(side.reshape(1), x, own, other)
-
-
-def after(value, other):
-    return lax.optimization_barrier((value, other))[0]
+        halves_body,
+        out_shape=[jax.ShapeDtypeStruct((ROWS, EARLY + LATE), jnp.bfloat16)] * 2,
+        in_specs=[smem] + [vmem] * len(weights),
+        out_specs=[vmem, vmem],
+        compiler_params=pltpu.CompilerParams(vmem_limit_bytes=4 * 1024 * 1024),
+    )(head.reshape(1), *weights)
 
 
 def double(block, axis):
@@ -329,40 +362,41 @@
     core, low, high = dp % 2, dp // 2, span % 2
     head = low ^ high
     pos = {"x": span // 8, "z": (span // 2) % 4}
-    sign = 1 - 2 * core
     near, far = 1 + 2 * core, 3 - 2 * core
 
     def order(first, one, two):
         return jnp.where(first == 0, jnp.concatenate([one, two], 0), jnp.concatenate([two, one], 0))
 
-    def half(which):
-        def cut(w, size):
-            return jnp.where(which == 0, w[:, :size], w[:, size:])
-
-        return jnp.concatenate(
-            [
-                cut(w_mark_key, D),
-                cut(w_mark_value, D),
-                cut(w_key, D),
-                cut(w_value, D),
-                cut(w_query, HEADS * D),
-            ],
-            axis=1,
+    mine, other = halves(head, w_mark_key, w_mark_value, w_key, w_value, w_query)
+    rows = order(low, mine, send(other, MATE))
+
+    def pair_of(axis, side):
+        p = pos[axis]
+        inner = jnp.logical_or(p == 1, p == 2).astype(jnp.int32)
+        index = jnp.where(side == 0, p // 2, inner)
+        return index, jnp.where(side == 0, p % 2, p // 2)
+
+    def slabs(axis):
+        mine, theirs = pair_of(axis, core)[0], pair_of(axis, 1 - core)[0]
+        return (
+            (core * 2 + mine, 2 * (1 - core) + theirs),
+            (core * 2 + 1 - mine, 2 * (1 - core) + 1 - theirs),
         )
-
-    mine = half(head)
-    rows = order(low, mine, send(half(1 - head), MATE))
 
     begin = span * TOK
     stride = jnp.left_shift(jnp.int32(4), level[0, 0])
     valid = jnp.clip(hist_len[0] - begin, 0, TOK)
     count = jnp.minimum(TOK // stride, (valid + stride - 1) // stride)
-    normed, pooled = norm_rows(jnp.stack([level[0, 0], valid, count]), tokens[0], gain)
-    mate_pooled = send(pooled, MATE)
-    both = jnp.concatenate([normed, send(normed, MATE)], 1)
-    facts = mate_pooled[0, SLOTS:, 0].astype(jnp.int32)
+    near_slots, far_slots = slabs("x")
+    facts = jnp.stack([level[0, 0], valid, count, *near_slots, *far_slots]).astype(jnp.int32)
+    own_near, own_far = norm_rows(facts, tokens[0], gain)
+    mate_near = send(own_near, MATE)
+    mate_far = send(after(own_far, mate_near), MATE)
+    facts = mate_near[0, TOK + SLOTS : TOK + SLOTS + 16, 0].astype(jnp.int32)
     mate_count, mate_valid = facts[0], facts[8]
-    both_pooled = jnp.concatenate([pooled[:, :SLOTS], mate_pooled[:, :SLOTS]], 1)
+
+    def pooled_of(packed):
+        return packed[:, TOK:].reshape(4, SLOTS + 16, SLAB)[:, :SLOTS]
 
     rows = order(high, rows, send(rows, ACROSS))
 
@@ -375,45 +409,40 @@
         joined = in_place(double(block, axis), (p, p ^ near, p ^ far, p ^ 2), joined)
         return joined.reshape(-1, block.shape[-1])
 
-    early = second(rows[:, : CUTS[2]], "x")
-    late = second(rows[:, CUTS[2] :], "z")
-
-    def project(x, own):
-        return project_kernel(core, x, own, send(own, SWAP))
-
-    x, z = pos["x"], pos["z"]
-    corner = early[:, : CUTS[1]]
-    b_0, a_0 = late, early[:, CUTS[1] :]
-    pair = jnp.stack([corner, send(corner, FLIP["z", 0])])
-    b_1 = send(b_0, RING["x"])
-    pair_far = send(pair, FLIP["z", 1])
-    part_m = in_place(
-        jnp.concatenate([pair, pair_far]),
-        (z, z ^ near, z ^ far, z ^ 2),
-        blank((4,) + corner.shape, corner),
-    ).reshape(HALF, -1)
-    b_2 = send(after(b_1, pair_far), RING["x"])
-    a_1 = send(after(a_0, pair_far), RING["z"])
-
-    beacon = project(both_pooled, part_m).reshape(2, SLOTS, 2 * D)
+    early = second(rows[:, :EARLY], "x")
+    late = second(rows[:, EARLY:], "z")
+
+    early = order(pair_of("z", core)[1], early, send(early, FLIP["z", 0]))
+    late = order(pair_of("x", core)[1], late, send(late, FLIP["x", 0]))
+    early_far = send(early, FLIP["z", 1])
+    gathered = jnp.concatenate([early, early_far], 0)
+    swapped = send(gathered, SWAP)
+    slab_near, slab_far = slabs("z")
+    where_m = (slab_near[0], slab_far[0], slab_near[1], slab_far[1])
+    pieces_m = (early, early_far, swapped[:SLAB], swapped[SLAB:])
+    both_pooled = jnp.concatenate([pooled_of(own_near), pooled_of(mate_near)], 1)
+    beacon = project(where_m, both_pooled, pieces_m, last=True, rows=2 * SLOTS)
+    beacon = beacon.reshape(2, SLOTS, 2 * D)
     counts = jnp.stack([count, mate_count]).astype(jnp.bfloat16)
     flags = jnp.broadcast_to(counts[:, None, None], (2, 16, D))
     block_k = jnp.concatenate([beacon[..., :D], flags], 1)
     block_v = beacon[..., D:]
     block = jnp.concatenate([block_k, block_v], 1)
     block = order(low, block[:1], block[1:])
-    a_2 = send(after(a_1, block), RING["z"])
-    across = send(block, ACROSS)
-    b_3 = send(after(b_2, across), RING["x"])
-    block = jnp.stack([block, across])
-    pair_k, pair_v = block[:, :, : SLOTS + 16], block[:, :, SLOTS + 16 :]
-    pair_k = jnp.stack([pair_k, send(pair_k, FLIP["x", 0])])
-    pair_v = jnp.stack([pair_v, send(pair_v, FLIP["z", 0])])
-    a_3 = send(after(a_2, (pair_k, pair_v)), RING["z"])
-    half_k = jnp.concatenate([pair_k, send(pair_k, FLIP["x", 1])])
-    half_v = jnp.concatenate([pair_v, send(pair_v, FLIP["z", 1])])
-    every_k = double(half_k, "z")
-    every_v = double(half_v, "x")
+    late_far = send(after(late, block), FLIP["x", 1])
+    block = jnp.stack([block, send(block, ACROSS)])
+    half_k = double(block[:, :, : SLOTS + 16], "x")
+    half_v = double(block[:, :, SLOTS + 16 :], "z")
+    zero, one = jnp.int32(0), jnp.int32(1)
+    near_w = (late, send(late, SWAP))
+    own = project((zero, one), own_near, near_w)
+    half_k, half_v = after((half_k, half_v), own)
+    pair_k = jnp.stack([half_k, send(half_k, FLIP["z", 0])])
+    pair_v = jnp.stack([half_v, send(half_v, FLIP["x", 0])])
+    mate = project((zero, one), mate_near, near_w)
+    pair_k, pair_v = after((pair_k, pair_v), (mate, mate_far))
+    every_k = jnp.concatenate([pair_k, send(pair_k, FLIP["z", 1])])
+    every_v = jnp.concatenate([pair_v, send(pair_v, FLIP["x", 1])])
     every_k = every_k.reshape(SPANS, 2, SLOTS + 16, D)
     every_v = every_v.reshape(SPANS, 2, SLOTS, D)
 
@@ -429,18 +458,14 @@
     at_v = (code_x * 4 + code_z) * 2 + code_h
     live = every_k[:, :, SLOTS, 0].astype(jnp.int32).reshape(2 * SPANS)
 
-    pieces = [a_0, a_1, a_2, a_3]
-    part_a = blank((4,) + a_0.shape, a_0)
-    part_a = in_place(pieces, [(z - sign * i) % 4 for i in range(4)], part_a)
-    part_b = blank((4, 4, 4 * ROWS, late.shape[-1]), b_0)
-    for i, piece in enumerate([b_0, b_1, b_2, b_3]):
-        piece = piece.reshape(4, 1, 4 * ROWS, -1)
-        part_b = lax.dynamic_update_slice_in_dim(part_b, piece, (x - sign * i) % 4, 1)
-    part_a = project(both, part_a.reshape(HALF, -1))
-    part_b = project(both, part_b.reshape(HALF, -1))
+    own = project((zero,), own_far, (late_far,), own)
+    mate = project((zero,), mate_far, (late_far,), mate)
+    own, mate = lax.optimization_barrier((own, mate))
+    last_w = (send(late_far, SWAP),)
+    mate = project((one,), mate_far, last_w, mate, last=True)
+    own = project((one,), own_far, last_w, own, last=True)
 
     def attention(which, valid, wide):
-        here = slice(which * TOK, (which + 1) * TOK)
         info = jnp.concatenate(
             [jnp.stack([span, valid, head * (HEADS * D), low ^ which]), at_k, at_v]
         )
@@ -448,8 +473,7 @@
             wide,
             info,
             live,
-            part_a[here],
-            part_b[here],
+            mate if which else own,
             every_k,
             every_v,
         )

time: 159 us -> 163 us (1.025)
  waiting for transfers between devices: 55.3 us -> 69.2 us
  starting transfers between devices: 39.2 us -> 27.2 us
  Pallas kernels: 26.5 us -> 35.5 us
  other arithmetic: 12.4 us -> 8.03 us
  local copies, waits for them, and re-layouts: 22.4 us -> 18.8 us
    ppermute x29 -> x25, waiting for transfers between devices: 55.3 us -> 69.2 us  [send(): return lax.ppermute(value, AXES, pairs)]
    ppermute x29 -> x25, starting transfers between devices: 39.2 us -> 27.2 us  [send(): return lax.ppermute(value, AXES, pairs)]
    pallas_call x4 -> x9, Pallas kernels: 15.4 us -> 22.7 us  [the longest x7 15.8 us: project(): pl.pallas_call(functools.partial(project_body, len(weights)), out_shape=j...]
    unnamed x11 -> x34, local copies, waits for them, and re-layouts: 4.9 us -> 11 us
    dynamic_update_slice x4 -> x0, local copies, waits for them, and re-layouts: 3.69 us -> none  [on_device(): lax.dynamic_update_slice_in_dim(part_b, piece, (x - sign * i) % 4, 1)]
    dynamic_update_slice x16 -> x8, local copies, waits for them, and re-layouts: 3.31 us -> 0.15 us  [in_place(): joined = lax.dynamic_update_slice_in_dim(joined, pieces[i][None], slot, 0)]
    broadcast_in_dim x5 -> x2, local copies, waits for them, and re-layouts: 3.14 us -> 0.1 us  [blank(): return lax.optimization_barrier((jnp.zeros(shape, jnp.bfloat16), after))[0]]
    concatenate x1 -> x0, local copies, waits for them, and re-layouts: 2.93 us -> none  [on_device(): both = jnp.concatenate([normed, send(normed, MATE)], 1)]
  transfers between devices with their start and end apart: 29 -> 25, of which waited for: 14 -> 15; matrix products, arithmetic and copies ran while one was open for 16% -> 8% of each run, Pallas kernels for 10% -> 16%
where the time goes in v5:
time: 163 us; the launch traced here: 161 us
  waiting for transfers between devices  69.2 us (42%)
  Pallas kernels  35.5 us (22%)
  starting transfers between devices  27.2 us (17%)
  local copies, waits for them, and re-layouts  18.8 us (12%)
  other arithmetic  8.03 us (5%)
  between operations  2.61 us (2%)
    ppermute x25, waiting for transfers between devices, send(): return lax.ppermute(value, AXES, pairs)  69.2 us
    ppermute x25, starting transfers between devices, send(): return lax.ppermute(value, AXES, pairs)  27.2 us
    pallas_call x7, Pallas kernels, project(): pl.pallas_call(functools.partial(project_body, len(weights)), out_shape=j...  15.8 us
    pallas_call x2, Pallas kernels, attend(): pl.pallas_call(functools.partial(attend_body, wide), out_shape=jax.ShapeD...  12.8 us
    unnamed x34, local copies, waits for them, and re-layouts  11 us
    pallas_call x1, Pallas kernels, norm_rows(): pl.pallas_call(norm_body, out_shape=[jax.ShapeDtypeStruct((2, TOK + 2 * (...  6.86 us
  transfers between devices with their start and end apart: 25, of which 15 were waited for; matrix products, arithmetic and copies ran while one was open for 8% of the time, Pallas kernels for 16%

profile of v5, /device:TPU:6, one launch (start us, length us, event | category | flops | bytes accessed | tf_op | source)
XLA Modules:
  0.0 161.4 jit_solution(4997274647351563938)
XLA Ops:
  0.0 0.9 copy-done.11
  0.9 0.7 copy-done.12
  1.6 0.7 copy-done.13
  2.3 0.7 copy-done.14
  3.1 0.7 copy-done.15
  3.8 1.6 %collective-permute-start.1 = (bf16[28,1408]{1,0:T(8,128)(2,1)S(1)}, bf16[28,1408]{1,0:T(8,128)(2,1)S(1)}, u32[]{:S(2)}, u32[]{:S(2)}) collective-permute-start(bf16[28,1408]{1,0:T(8,128)(2,1)S(1)} %get-tuple-element.21), channel_id=1, source_target_pairs={{0,64},{32,96},{2,66},{34,98},{4,68},{36,100},{6,70},{38,102},{64,... | collective-permute-start | bytes 236552 | tf_op jit(solution)/shard_map/ppermute | solution.py:64
  5.5 3.0 %collective-permute-done.1 = bf16[28,1408]{1,0:T(8,128)(2,1)S(1)} collective-permute-done((bf16[28,1408]{1,0:T(8,128)(2,1)S(1)}, bf16[28,1408]{1,0:T(8,128)(2,1)S(1)}, u32[]{:S(2)}, u32[]{:S(2)}) %collective-permute-start.1) | collective-permute-done | bytes 78880 | tf_op jit(solution)/shard_map/ppermute | solution.py:64
  8.5 3.1 %collective-permute-start.2 = (bf16[56,1408]{1,0:T(8,128)(2,1)S(1)}, bf16[56,1408]{1,0:T(8,128)(2,1)S(1)}, u32[]{:S(2)}, u32[]{:S(2)}) collective-permute-start(bf16[56,1408]{1,0:T(8,128)(2,1)S(1)} %maximum_select_fusion.3), channel_id=1, source_target_pairs={{0,65},{32,97},{2,67},{34,99},{4,69},{36,101},{6,71},{38,103},{64,... | collective-permute-start | bytes 473096 | tf_op jit(solution)/shard_map/ppermute | solution.py:64
  13.0 0.7 reshape.98.gain_ref
  13.8 1.5 copy-done.10
  15.3 6.9 %shard_map.91 = (bf16[2,416,896]{2,1,0:T(8,128)(2,1)}, bf16[2,256,896]{2,1,0:T(8,128)(2,1)S(1)}) custom-call(s32[7]{0:T(128)S(1)} %stack.130.fact_ref, bf16[256,3584]{1,0:T(8,128)(2,1)S(1)} %bitcast.67, f32[1,3584]{1,0:T(1,128)S(1)} %reshape.98.gain_ref), custom_call_target="tpu_custom_call" | custom-call | tf_op jit(solution)/shard_map/pallas_call | solution.py:145
  22.3 1.3 slice.74
  23.7 0.8 slice.98
  24.7 0.9 collective-permute-start.3
  25.6 1.9 %collective-permute-start.13 = (bf16[112,1152]{1,0:T(8,128)(2,1)S(1)}, bf16[112,1152]{1,0:T(8,128)(2,1)S(1)}, u32[]{:S(2)}, u32[]{:S(2)}) collective-permute-start(bf16[112,1152]{1,0:T(8,128)(2,1)S(1)} %get-tuple-element.36), channel_id=1, source_target_pairs={{0,2},{32,38},{2,0},{34,36},{4,6},{36,34},{6,4},{38,32},{64,66},{9... | collective-permute-start | bytes 774152 | tf_op jit(solution)/shard_map/ppermute | solution.py:64
  27.7 1.3 collective-permute-done.3
  29.0 0.6 collective-permute-start.4
  29.6 5.5 %collective-permute-done.4 = bf16[2,112,256]{2,1,0:T(8,128)(2,1)S(1)} collective-permute-done((bf16[2,112,256]{2,1,0:T(8,128)(2,1)S(1)}, bf16[2,112,256]{2,1,0:T(8,128)(2,1)S(1)}, u32[]{:S(2)}, u32[]{:S(2)}) %collective-permute-start.4) | collective-permute-done | bytes 114720 | tf_op jit(solution)/shard_map/ppermute | solution.py:64
  35.1 2.0 %collective-permute-start.5 = (bf16[448,256]{1,0:T(8,128)(2,1)S(1)}, bf16[448,256]{1,0:T(8,128)(2,1)S(1)}, u32[]{:S(2)}, u32[]{:S(2)}) collective-permute-start(bf16[448,256]{1,0:T(8,128)(2,1)S(1)} %bitcast.80), channel_id=1, source_target_pairs={{0,2},{32,38},{2,0},{34,36},{4,6},{36,34},{6,4},{38,32},{64,66},{9... | collective-permute-start | bytes 688136 | tf_op jit(solution)/shard_map/ppermute | solution.py:64
  37.2 2.6 %collective-permute-start.14 = (bf16[2,112,1152]{2,1,0:T(8,128)(2,1)S(1)}, bf16[2,112,1152]{2,1,0:T(8,128)(2,1)S(1)}, u32[]{:S(2)}, u32[]{:S(2)}) collective-permute-start(bf16[2,112,1152]{2,1,0:T(8,128)(2,1)S(1)} %pad_maximum_fusion.6), channel_id=1, source_target_pairs={{0,6},{32,34},{2,4},{34,32},{4,2},{36,38},{6,0},{38,36},{64,70},{9... | collective-permute-start | bytes 1548296 | tf_op jit(solution)/shard_map/ppermute | solution.py:64
  39.8 3.8 %collective-permute-done.5 = bf16[448,256]{1,0:T(8,128)(2,1)S(1)} collective-permute-done((bf16[448,256]{1,0:T(8,128)(2,1)S(1)}, bf16[448,256]{1,0:T(8,128)(2,1)S(1)}, u32[]{:S(2)}, u32[]{:S(2)}) %collective-permute-start.5) | collective-permute-done | bytes 229408 | tf_op jit(solution)/shard_map/ppermute | solution.py:64
  43.8 4.2 %collective-permute-start.6 = (bf16[896,256]{1,0:T(8,128)(2,1)S(1)}, bf16[896,256]{1,0:T(8,128)(2,1)S(1)}, u32[]{:S(2)}, u32[]{:S(2)}) collective-permute-start(bf16[896,256]{1,0:T(8,128)(2,1)S(1)} %maximum_select_fusion.1.refs_0_), channel_id=1, source_target_pairs={{0,6},{32,34},{2,4},{34,32},{4,2},{36,38},{6,0},{38,36},{64,70},{9... | collective-permute-start | bytes 1376264 | tf_op jit(solution)/shard_map/ppermute | solution.py:64
  48.1 6.4 %collective-permute-done.6.refs_1_ = bf16[896,256]{1,0:T(8,128)(2,1)S(1)} collective-permute-done((bf16[896,256]{1,0:T(8,128)(2,1)S(1)}, bf16[896,256]{1,0:T(8,128)(2,1)S(1)}, u32[]{:S(2)}, u32[]{:S(2)}) %collective-permute-start.6) | collective-permute-done | bytes 458784 | tf_op jit(solution)/shard_map/ppermute | solution.py:64
  54.8 0.6 collective-permute-done.x_ref
  55.5 0.7 fusion.9
  57.2 1.0 shard_map.93
  58.3 11.1 %collective-permute-done.15 = bf16[448,1152]{1,0:T(8,128)(2,1)S(1)} collective-permute-done((bf16[448,1152]{1,0:T(8,128)(2,1)S(1)}, bf16[448,1152]{1,0:T(8,128)(2,1)S(1)}, u32[]{:S(2)}, u32[]{:S(2)}) %collective-permute-start.15) | collective-permute-done | bytes 1032224 | tf_op jit(solution)/shard_map/ppermute | solution.py:64
  69.4 0.8 maximum_select_fusion.refs_0_
  70.2 0.6 collective-permute-start.21
  71.0 1.7 %collective-permute-start.19 = (bf16[2,256,896]{2,1,0:T(8,128)(2,1)S(1)}, bf16[2,256,896]{2,1,0:T(8,128)(2,1)S(1)}, u32[]{:S(2)}, u32[]{:S(2)}) collective-permute-start(bf16[2,256,896]{2,1,0:T(8,128)(2,1)S(1)} %get-tuple-element.27.x_ref), channel_id=1, source_target_pairs={{0,64},{32,96},{2,66},{34,98},{4,68},{36,100},{6,70},{38,102},{64,... | collective-permute-start | bytes 2752520 | tf_op jit(solution)/shard_map/ppermute | solution.py:64
  73.0 5.2 %collective-permute-done.8 = bf16[2,144,128]{2,1,0:T(8,128)(2,1)S(1)} collective-permute-done((bf16[2,144,128]{2,1,0:T(8,128)(2,1)S(1)}, bf16[2,144,128]{2,1,0:T(8,128)(2,1)S(1)}, u32[]{:S(2)}, u32[]{:S(2)}) %collective-permute-start.8) | collective-permute-done | bytes 73760 | tf_op jit(solution)/shard_map/ppermute | solution.py:64
  78.3 1.7 %collective-permute-start.9 = (bf16[2,2,80,128]{3,2,1,0:T(8,128)(2,1)S(1)}, bf16[2,2,80,128]{3,2,1,0:T(8,128)(2,1)S(1)}, u32[]{:S(2)}, u32[]{:S(2)}) collective-permute-start(bf16[2,2,80,128]{3,2,1,0:T(8,128)(2,1)S(1)} %fusion), channel_id=1, source_target_pairs={{0,8},{32,56},{2,10},{34,58},{4,12},{36,60},{6,14},{38,62},{64,72}... | collective-permute-start | bytes 245768 | tf_op jit(solution)/shard_map/ppermute | solution.py:64
  80.0 18.2 %collective-permute-done.21.refs_0_ = bf16[896,1152]{1,0:T(8,128)(2,1)} collective-permute-done((bf16[896,1152]{1,0:T(8,128)(2,1)S(1)}, bf16[896,1152]{1,0:T(8,128)(2,1)}, u32[]{:S(2)}, u32[]{:S(2)}) %collective-permute-start.21) | collective-permute-done | bytes 2064416 | tf_op jit(solution)/shard_map/ppermute | solution.py:64
  98.2 3.3 %collective-permute-start.12 = (bf16[2,2,2,64,128]{4,3,2,1,0:T(8,128)(2,1)S(1)}, bf16[2,2,2,64,128]{4,3,2,1,0:T(8,128)(2,1)S(1)}, u32[]{:S(2)}, u32[]{:S(2)}) collective-permute-start(bf16[2,2,2,64,128]{4,3,2,1,0:T(8,128)(2,1)S(1)} %pad_maximum_fusion.10), channel_id=1, source_target_pairs={{0,6},{32,34},{2,4},{34,32},{4,2},{36,38},{6,0},{38,36},{64,70},{9... | collective-permute-start | bytes 393224 | tf_op jit(solution)/shard_map/ppermute | solution.py:64
  101.6 0.6 collective-permute-start.10
  102.1 2.4 %collective-permute-done.12 = bf16[2,2,2,64,128]{4,3,2,1,0:T(8,128)(2,1)S(1)} collective-permute-done((bf16[2,2,2,64,128]{4,3,2,1,0:T(8,128)(2,1)S(1)}, bf16[2,2,2,64,128]{4,3,2,1,0:T(8,128)(2,1)S(1)}, u32[]{:S(2)}, u32[]{:S(2)}) %collective-permute-start.12) | collective-permute-done | bytes 131104 | tf_op jit(solution)/shard_map/ppermute | solution.py:64
  104.5 3.7 %collective-permute-done.10 = bf16[2,2,2,80,128]{4,3,2,1,0:T(8,128)(2,1)S(1)} collective-permute-done((bf16[2,2,2,80,128]{4,3,2,1,0:T(8,128)(2,1)S(1)}, bf16[2,2,2,80,128]{4,3,2,1,0:T(8,128)(2,1)S(1)}, u32[]{:S(2)}, u32[]{:S(2)}) %collective-permute-start.10) | collective-permute-done | bytes 163872 | tf_op jit(solution)/shard_map/ppermute | solution.py:64
  108.3 3.0 %shard_map.94.refs_1_ = f32[256,1152]{1,0:T(8,128)S(1)} custom-call(s32[2]{0:T(128)S(1)} %iota.15.slab_ref, bf16[2,416,896]{2,1,0:T(8,128)(2,1)} %get-tuple-element.19.x_ref, bf16[896,1152]{1,0:T(8,128)(2,1)S(1)} %maximum_select_fusion.refs_0_, bf16[896,1152]{1,0:T(8,128)(2,1)S(1)} %collective-permute-done.16.refs_1_), custom_call_target="tpu_custom_call" | custom-call | tf_op jit(solution)/shard_map/pallas_call | solution.py:308
  111.3 0.3 collective-permute-start.18
  111.7 2.1 %shard_map.95.refs_1_ = f32[256,1152]{1,0:T(8,128)S(1)} custom-call(s32[2]{0:T(128)S(1)} %iota.16.slab_ref, bf16[2,416,896]{2,1,0:T(8,128)(2,1)S(1)} %copy-done.9, bf16[896,1152]{1,0:T(8,128)(2,1)S(1)} %maximum_select_fusion.refs_0_, bf16[896,1152]{1,0:T(8,128)(2,1)S(1)} %collective-permute-done.16.refs_1_), custom_call_target="tpu_custom_call" | custom-call | tf_op jit(solution)/shard_map/pallas_call | solution.py:308
  113.7 4.2 %collective-permute-done.18 = bf16[4,2,2,64,128]{4,3,2,1,0:T(8,128)(2,1)S(1)} collective-permute-done((bf16[4,2,2,64,128]{4,3,2,1,0:T(8,128)(2,1)S(1)}, bf16[4,2,2,64,128]{4,3,2,1,0:T(8,128)(2,1)S(1)}, u32[]{:S(2)}, u32[]{:S(2)}) %collective-permute-start.18) | collective-permute-done | bytes 262176 | tf_op jit(solution)/shard_map/ppermute | solution.py:64
  117.9 0.9 pad_maximum_fusion.5
  118.8 0.9 pad_maximum_fusion.4
  119.7 0.9 copy-done.5
  120.7 0.5 collective-permute-start.23
  121.2 0.7 concatenate.107.info_ref
  121.9 1.2 copy-done.3
  123.1 2.5 %shard_map.96.refs_1_ = f32[256,1152]{1,0:T(8,128)S(1)} custom-call(s32[1]{0:T(128)} %constant.160.clone.1.slab_ref, bf16[2,256,896]{2,1,0:T(8,128)(2,1)S(1)} %copy-done.3, bf16[896,1152]{1,0:T(8,128)(2,1)} %collective-permute-done.21.refs_0_, f32[256,1152]{1,0:T(8,128)S(1)} %shard_map.94.refs_1_), custom_call_target="tpu_custom_call" | custom-call | tf_op jit(solution)/shard_map/pallas_call | solution.py:308
  125.6 2.4 %shard_map.97.refs_1_ = f32[256,1152]{1,0:T(8,128)S(1)} custom-call(s32[1]{0:T(128)} %constant.160.clone.1.slab_ref, bf16[2,256,896]{2,1,0:T(8,128)(2,1)S(1)} %copy-done.6, bf16[896,1152]{1,0:T(8,128)(2,1)} %collective-permute-done.21.refs_0_, f32[256,1152]{1,0:T(8,128)S(1)} %shard_map.95.refs_1_), custom_call_target="tpu_custom_call" | custom-call | tf_op jit(solution)/shard_map/pallas_call | solution.py:308
  128.0 3.4 %collective-permute-done.23 = bf16[2,4,2,2,64,128]{5,4,3,2,1,0:T(8,128)(2,1)} collective-permute-done((bf16[2,4,2,2,64,128]{5,4,3,2,1,0:T(8,128)(2,1)}, bf16[2,4,2,2,64,128]{5,4,3,2,1,0:T(8,128)(2,1)}, u32[]{:S(2)}, u32[]{:S(2)}) %collective-permute-start.23) | collective-permute-done | bytes 524320 | tf_op jit(solution)/shard_map/ppermute | solution.py:64
  131.4 1.3 pad_maximum_fusion.1
  132.7 0.6 collective-permute-done.20
  133.3 1.4 pad_maximum_fusion
  134.7 1.8 %fusion.1 = s32[32,2]{1,0:T(8,128)} fusion(bf16[32,2,80,128]{3,2,1,0:T(8,128)(2,1)S(1)} %bitcast.62), kind=kLoop, calls=%fused_computation.29 | loop fusion | flops 64 | bytes 384 | tf_op jit(solution)/shard_map/convert_element_type | solution.py:459
  136.5 0.8 reshape.107.count_ref
  137.3 1.3 copy-done.1
  138.6 1.2 copy-done.7
  139.8 2.4 %shard_map.100.part_ref = bf16[256,1152]{1,0:T(8,128)(2,1)S(1)} custom-call(s32[1]{0:T(128)} %constant.159.clone.1.slab_ref, bf16[2,256,896]{2,1,0:T(8,128)(2,1)S(1)} %copy-done.7, bf16[896,1152]{1,0:T(8,128)(2,1)} %collective-permute-done.22.refs_0_, f32[256,1152]{1,0:T(8,128)S(1)} %copy-done.1), custom_call_target="tpu_custom_call" | custom-call | tf_op jit(solution)/shard_map/pallas_call | solution.py:308
  142.2 6.8 %shard_map.101 = bf16[256,896]{1,0:T(8,128)(2,1)} custom-call(s32[68]{0:T(128)S(1)} %concatenate.107.info_ref, s32[64]{0:T(128)S(1)} %reshape.107.count_ref, bf16[256,1152]{1,0:T(8,128)(2,1)S(1)} %shard_map.100.part_ref, bf16[32,2,80,128]{3,2,1,0:T(8,128)(2,1)S(1)} %bitcast.63, bf16[32,2,64,128]{3,2,1,0:T(8,128)(2,1)S(1)} %bitcast.65), custom_call_target="tpu_custom_call" | custom-call | tf_op jit(solution)/shard_map/pallas_call | solution.py:272
  149.0 0.8 collective-permute-start.24
  149.9 1.2 copy-done.4
  151.1 2.4 %shard_map.98.part_ref = bf16[256,1152]{1,0:T(8,128)(2,1)S(1)} custom-call(s32[1]{0:T(128)} %constant.159.clone.1.slab_ref, bf16[2,256,896]{2,1,0:T(8,128)(2,1)S(1)} %copy-done.4, bf16[896,1152]{1,0:T(8,128)(2,1)} %collective-permute-done.22.refs_0_, f32[256,1152]{1,0:T(8,128)S(1)} %shard_map.96.refs_1_), custom_call_target="tpu_custom_call" | custom-call | tf_op jit(solution)/shard_map/pallas_call | solution.py:308
  153.5 6.0 %shard_map.99 = bf16[256,1792]{1,0:T(8,128)(2,1)} custom-call(s32[68]{0:T(128)S(1)} %concatenate.84.info_ref, s32[64]{0:T(128)S(1)} %reshape.107.count_ref, bf16[256,1152]{1,0:T(8,128)(2,1)S(1)} %shard_map.98.part_ref, bf16[32,2,80,128]{3,2,1,0:T(8,128)(2,1)S(1)} %bitcast.64, bf16[32,2,64,128]{3,2,1,0:T(8,128)(2,1)S(1)} %bitcast.66), custom_call_target="tpu_custom_call" | custom-call | tf_op jit(solution)/shard_map/pallas_call | solution.py:272
  159.5 1.8 %bitcast_dynamic-update-slice_fusion = bf16[1,256,1792]{2,1,0:T(8,128)(2,1)} fusion(bf16[1,256,1792]{2,1,0:T(8,128)(2,1)} %bitcast.82, s32[]{:T(128)S(6)} %select_n.231, bf16[256,896]{1,0:T(8,128)(2,1)} %collective-permute-done.24), kind=kLoop, calls=%fused_computation.9 | loop fusion | bytes 917508 | tf_op jit(solution)/shard_map/dynamic_update_slice | solution.py:483
  (89 shorter events, 2.6 us)
Async XLA Ops:
  0.0 0.9 copy-start.11
  0.9 0.7 copy-start.12
  1.6 0.7 copy-start.13
  2.3 0.7 copy-start.14
  3.1 0.7 copy-start.15
  3.8 4.6 %collective-permute-start.1 = (bf16[28,1408]{1,0:T(8,128)(2,1)S(1)}, bf16[28,1408]{1,0:T(8,128)(2,1)S(1)}, u32[]{:S(2)}, u32[]{:S(2)}) collective-permute-start(bf16[28,1408]{1,0:T(8,128)(2,1)S(1)} %get-tuple-element.21), channel_id=1, source_target_pairs={{0,64},{32,96},{2,66},{34,98},{4,68},{36,100},{6,70},{38,102},{64,... | collective-permute-start | bytes 236552 | tf_op jit(solution)/shard_map/ppermute | solution.py:64
  8.5 16.1 %collective-permute-start.2 = (bf16[56,1408]{1,0:T(8,128)(2,1)S(1)}, bf16[56,1408]{1,0:T(8,128)(2,1)S(1)}, u32[]{:S(2)}, u32[]{:S(2)}) collective-permute-start(bf16[56,1408]{1,0:T(8,128)(2,1)S(1)} %maximum_select_fusion.3), channel_id=1, source_target_pairs={{0,65},{32,97},{2,67},{34,99},{4,69},{36,101},{6,71},{38,103},{64,... | collective-permute-start | bytes 473096 | tf_op jit(solution)/shard_map/ppermute | solution.py:64
  13.8 1.5 copy-start.10
  22.2 48.8 %copy-start.2 = (bf16[2,256,896]{2,1,0:T(8,128)(2,1)}, bf16[2,256,896]{2,1,0:T(8,128)(2,1)S(1)}, u32[]{:S(2)}) copy-start(bf16[2,256,896]{2,1,0:T(8,128)(2,1)S(1)} %get-tuple-element.27.x_ref) | copy-start | bytes 2752516
  22.2 33.2 %collective-permute-start = (bf16[2,416,896]{2,1,0:T(8,128)(2,1)}, bf16[2,416,896]{2,1,0:T(8,128)(2,1)S(1)}, u32[]{:S(2)}, u32[]{:S(2)}) collective-permute-start(bf16[2,416,896]{2,1,0:T(8,128)(2,1)} %get-tuple-element.19.x_ref), channel_id=1, source_target_pairs={{0,64},{32,96},{2,66},{34,98},{4,68},{36,100},{6,70},{38,102},{64,... | collective-permute-start | bytes 4472840 | tf_op jit(solution)/shard_map/ppermute | solution.py:64
  24.7 4.3 %collective-permute-start.3 = (bf16[112,256]{1,0:T(8,128)(2,1)S(1)}, bf16[112,256]{1,0:T(8,128)(2,1)S(1)}, u32[]{:S(2)}, u32[]{:S(2)}) collective-permute-start(bf16[112,256]{1,0:T(8,128)(2,1)S(1)} %get-tuple-element.38), channel_id=1, source_target_pairs={{0,8},{32,56},{2,10},{34,58},{4,12},{36,60},{6,14},{38,62},{64,72}... | collective-permute-start | bytes 172040 | tf_op jit(solution)/shard_map/ppermute | solution.py:64
  25.6 11.5 %collective-permute-start.13 = (bf16[112,1152]{1,0:T(8,128)(2,1)S(1)}, bf16[112,1152]{1,0:T(8,128)(2,1)S(1)}, u32[]{:S(2)}, u32[]{:S(2)}) collective-permute-start(bf16[112,1152]{1,0:T(8,128)(2,1)S(1)} %get-tuple-element.36), channel_id=1, source_target_pairs={{0,2},{32,38},{2,0},{34,36},{4,6},{36,34},{6,4},{38,32},{64,66},{9... | collective-permute-start | bytes 774152 | tf_op jit(solution)/shard_map/ppermute | solution.py:64
  29.0 6.1 %collective-permute-start.4 = (bf16[2,112,256]{2,1,0:T(8,128)(2,1)S(1)}, bf16[2,112,256]{2,1,0:T(8,128)(2,1)S(1)}, u32[]{:S(2)}, u32[]{:S(2)}) collective-permute-start(bf16[2,112,256]{2,1,0:T(8,128)(2,1)S(1)} %pad_maximum_fusion.11), channel_id=1, source_target_pairs={{0,24},{32,40},{2,26},{34,42},{4,28},{36,44},{6,30},{38,46},{64,88... | collective-permute-start | bytes 344072 | tf_op jit(solution)/shard_map/ppermute | solution.py:64
  35.1 8.5 %collective-permute-start.5 = (bf16[448,256]{1,0:T(8,128)(2,1)S(1)}, bf16[448,256]{1,0:T(8,128)(2,1)S(1)}, u32[]{:S(2)}, u32[]{:S(2)}) collective-permute-start(bf16[448,256]{1,0:T(8,128)(2,1)S(1)} %bitcast.80), channel_id=1, source_target_pairs={{0,2},{32,38},{2,0},{34,36},{4,6},{36,34},{6,4},{38,32},{64,66},{9... | collective-permute-start | bytes 688136 | tf_op jit(solution)/shard_map/ppermute | solution.py:64
  37.2 10.9 %collective-permute-start.14 = (bf16[2,112,1152]{2,1,0:T(8,128)(2,1)S(1)}, bf16[2,112,1152]{2,1,0:T(8,128)(2,1)S(1)}, u32[]{:S(2)}, u32[]{:S(2)}) collective-permute-start(bf16[2,112,1152]{2,1,0:T(8,128)(2,1)S(1)} %pad_maximum_fusion.6), channel_id=1, source_target_pairs={{0,6},{32,34},{2,4},{34,32},{4,2},{36,38},{6,0},{38,36},{64,70},{9... | collective-permute-start | bytes 1548296 | tf_op jit(solution)/shard_map/ppermute | solution.py:64
  43.8 10.7 %collective-permute-start.6 = (bf16[896,256]{1,0:T(8,128)(2,1)S(1)}, bf16[896,256]{1,0:T(8,128)(2,1)S(1)}, u32[]{:S(2)}, u32[]{:S(2)}) collective-permute-start(bf16[896,256]{1,0:T(8,128)(2,1)S(1)} %maximum_select_fusion.1.refs_0_), channel_id=1, source_target_pairs={{0,6},{32,34},{2,4},{34,32},{4,2},{36,38},{6,0},{38,36},{64,70},{9... | collective-permute-start | bytes 1376264 | tf_op jit(solution)/shard_map/ppermute | solution.py:64
  48.1 8.8 %copy-start.16 = (bf16[4,64,896]{2,1,0:T(8,128)(2,1)S(1)}, bf16[4,64,896]{2,1,0:T(8,128)(2,1)}, u32[]{:S(2)}) copy-start(bf16[4,64,896]{2,1,0:T(8,128)(2,1)} %slice.98) | copy-start | bytes 1376260
  54.6 2.6 %collective-permute-start.7 = (bf16[1792,256]{1,0:T(8,128)(2,1)S(1)}, bf16[1792,256]{1,0:T(8,128)(2,1)S(1)}, u32[]{:S(2)}, u32[]{:S(2)}) collective-permute-start(bf16[1792,256]{1,0:T(8,128)(2,1)S(1)} %pad_maximum_fusion.3), channel_id=1, source_target_pairs={{0,32},{32,0},{2,34},{34,2},{4,36},{36,4},{6,38},{38,6},{64,96},{9... | collective-permute-start | bytes 2752520 | tf_op jit(solution)/shard_map/ppermute | solution.py:64
  54.7 14.7 %collective-permute-start.15 = (bf16[448,1152]{1,0:T(8,128)(2,1)S(1)}, bf16[448,1152]{1,0:T(8,128)(2,1)S(1)}, u32[]{:S(2)}, u32[]{:S(2)}) collective-permute-start(bf16[448,1152]{1,0:T(8,128)(2,1)S(1)} %bitcast.69), channel_id=1, source_target_pairs={{0,8},{32,56},{2,10},{34,58},{4,12},{36,60},{6,14},{38,62},{64,72}... | collective-permute-start | bytes 3096584 | tf_op jit(solution)/shard_map/ppermute | solution.py:64
  55.4 1.6 %copy-start.8 = (bf16[2,416,896]{2,1,0:T(8,128)(2,1)}, bf16[2,416,896]{2,1,0:T(8,128)(2,1)S(1)}, u32[]{:S(2)}) copy-start(bf16[2,416,896]{2,1,0:T(8,128)(2,1)S(1)} %collective-permute-done.x_ref) | copy-start | bytes 4472836
  70.2 28.0 %collective-permute-start.21 = (bf16[896,1152]{1,0:T(8,128)(2,1)S(1)}, bf16[896,1152]{1,0:T(8,128)(2,1)}, u32[]{:S(2)}, u32[]{:S(2)}) collective-permute-start(bf16[896,1152]{1,0:T(8,128)(2,1)S(1)} %maximum_select_fusion.refs_0_), channel_id=1, source_target_pairs={{0,24},{32,40},{2,26},{34,42},{4,28},{36,44},{6,30},{38,46},{64,88... | collective-permute-start | bytes 6193160 | tf_op jit(solution)/shard_map/ppermute | solution.py:64
  70.8 37.4 %collective-permute-start.16 = (bf16[896,1152]{1,0:T(8,128)(2,1)S(1)}, bf16[896,1152]{1,0:T(8,128)(2,1)S(1)}, u32[]{:S(2)}, u32[]{:S(2)}) collective-permute-start(bf16[896,1152]{1,0:T(8,128)(2,1)S(1)} %maximum_select_fusion.refs_0_), channel_id=1, source_target_pairs={{0,32},{32,0},{2,34},{34,2},{4,36},{36,4},{6,38},{38,6},{64,96},{9... | collective-permute-start | bytes 6193160 | tf_op jit(solution)/shard_map/ppermute | solution.py:64
  71.0 48.8 %collective-permute-start.19 = (bf16[2,256,896]{2,1,0:T(8,128)(2,1)S(1)}, bf16[2,256,896]{2,1,0:T(8,128)(2,1)S(1)}, u32[]{:S(2)}, u32[]{:S(2)}) collective-permute-start(bf16[2,256,896]{2,1,0:T(8,128)(2,1)S(1)} %get-tuple-element.27.x_ref), channel_id=1, source_target_pairs={{0,64},{32,96},{2,66},{34,98},{4,68},{36,100},{6,70},{38,102},{64,... | collective-permute-start | bytes 2752520 | tf_op jit(solution)/shard_map/ppermute | solution.py:64
  72.7 5.6 %collective-permute-start.8 = (bf16[2,144,128]{2,1,0:T(8,128)(2,1)S(1)}, bf16[2,144,128]{2,1,0:T(8,128)(2,1)S(1)}, u32[]{:S(2)}, u32[]{:S(2)}) collective-permute-start(bf16[2,144,128]{2,1,0:T(8,128)(2,1)S(1)} %maximum_select_fusion.5), channel_id=1, source_target_pairs={{0,65},{32,97},{2,67},{34,99},{4,69},{36,101},{6,71},{38,103},{64,... | collective-permute-start | bytes 221192 | tf_op jit(solution)/shard_map/ppermute | solution.py:64
  78.3 23.3 %collective-permute-start.9 = (bf16[2,2,80,128]{3,2,1,0:T(8,128)(2,1)S(1)}, bf16[2,2,80,128]{3,2,1,0:T(8,128)(2,1)S(1)}, u32[]{:S(2)}, u32[]{:S(2)}) collective-permute-start(bf16[2,2,80,128]{3,2,1,0:T(8,128)(2,1)S(1)} %fusion), channel_id=1, source_target_pairs={{0,8},{32,56},{2,10},{34,58},{4,12},{36,60},{6,14},{38,62},{64,72}... | collective-permute-start | bytes 245768 | tf_op jit(solution)/shard_map/ppermute | solution.py:64
  80.0 18.2 %collective-permute-start.11 = (bf16[2,2,64,128]{3,2,1,0:T(8,128)(2,1)S(1)}, bf16[2,2,64,128]{3,2,1,0:T(8,128)(2,1)S(1)}, u32[]{:S(2)}, u32[]{:S(2)}) collective-permute-start(bf16[2,2,64,128]{3,2,1,0:T(8,128)(2,1)S(1)} %pad_maximum_fusion.13), channel_id=1, source_target_pairs={{0,2},{32,38},{2,0},{34,36},{4,6},{36,34},{6,4},{38,32},{64,66},{9... | collective-permute-start | bytes 196616 | tf_op jit(solution)/shard_map/ppermute | solution.py:64
  98.2 39.1 %collective-permute-start.22 = (bf16[896,1152]{1,0:T(8,128)(2,1)}, bf16[896,1152]{1,0:T(8,128)(2,1)}, u32[]{:S(2)}, u32[]{:S(2)}) collective-permute-start(bf16[896,1152]{1,0:T(8,128)(2,1)} %collective-permute-done.21.refs_0_), channel_id=1, source_target_pairs={{0,32},{32,0},{2,34},{34,2},{4,36},{36,4},{6,38},{38,6},{64,96},{9... | collective-permute-start | bytes 6193160 | tf_op jit(solution)/shard_map/ppermute | solution.py:64
  98.2 6.3 %collective-permute-start.12 = (bf16[2,2,2,64,128]{4,3,2,1,0:T(8,128)(2,1)S(1)}, bf16[2,2,2,64,128]{4,3,2,1,0:T(8,128)(2,1)S(1)}, u32[]{:S(2)}, u32[]{:S(2)}) collective-permute-start(bf16[2,2,2,64,128]{4,3,2,1,0:T(8,128)(2,1)S(1)} %pad_maximum_fusion.10), channel_id=1, source_target_pairs={{0,6},{32,34},{2,4},{34,32},{4,2},{36,38},{6,0},{38,36},{64,70},{9... | collective-permute-start | bytes 393224 | tf_op jit(solution)/shard_map/ppermute | solution.py:64
  101.6 6.6 %collective-permute-start.10 = (bf16[2,2,2,80,128]{4,3,2,1,0:T(8,128)(2,1)S(1)}, bf16[2,2,2,80,128]{4,3,2,1,0:T(8,128)(2,1)S(1)}, u32[]{:S(2)}, u32[]{:S(2)}) collective-permute-start(bf16[2,2,2,80,128]{4,3,2,1,0:T(8,128)(2,1)S(1)} %pad_maximum_fusion.9), channel_id=1, source_target_pairs={{0,24},{32,40},{2,26},{34,42},{4,28},{36,44},{6,30},{38,46},{64,88... | collective-permute-start | bytes 491528 | tf_op jit(solution)/shard_map/ppermute | solution.py:64
  108.3 3.4 %copy-start.9 = (bf16[2,416,896]{2,1,0:T(8,128)(2,1)S(1)}, bf16[2,416,896]{2,1,0:T(8,128)(2,1)}, u32[]{:S(2)}) copy-start(bf16[2,416,896]{2,1,0:T(8,128)(2,1)} %copy-done.8) | copy-start | bytes 4472836
  111.3 6.6 %collective-permute-start.18 = (bf16[4,2,2,64,128]{4,3,2,1,0:T(8,128)(2,1)S(1)}, bf16[4,2,2,64,128]{4,3,2,1,0:T(8,128)(2,1)S(1)}, u32[]{:S(2)}, u32[]{:S(2)}) collective-permute-start(bf16[4,2,2,64,128]{4,3,2,1,0:T(8,128)(2,1)S(1)} %pad_maximum_fusion.8), channel_id=1, source_target_pairs={{0,8},{32,56},{2,10},{34,58},{4,12},{36,60},{6,14},{38,62},{64,72}... | collective-permute-start | bytes 786440 | tf_op jit(solution)/shard_map/ppermute | solution.py:64
  111.6 7.3 %collective-permute-start.17 = (bf16[4,2,2,80,128]{4,3,2,1,0:T(8,128)(2,1)S(1)}, bf16[4,2,2,80,128]{4,3,2,1,0:T(8,128)(2,1)S(1)}, u32[]{:S(2)}, u32[]{:S(2)}) collective-permute-start(bf16[4,2,2,80,128]{4,3,2,1,0:T(8,128)(2,1)S(1)} %pad_maximum_fusion.7), channel_id=1, source_target_pairs={{0,2},{32,38},{2,0},{34,36},{4,6},{36,34},{6,4},{38,32},{64,66},{9... | collective-permute-start | bytes 983048 | tf_op jit(solution)/shard_map/ppermute | solution.py:64
  119.7 0.9 copy-start.5
  120.7 10.7 %collective-permute-start.23 = (bf16[2,4,2,2,64,128]{5,4,3,2,1,0:T(8,128)(2,1)}, bf16[2,4,2,2,64,128]{5,4,3,2,1,0:T(8,128)(2,1)}, u32[]{:S(2)}, u32[]{:S(2)}) collective-permute-start(bf16[2,4,2,2,64,128]{5,4,3,2,1,0:T(8,128)(2,1)} %pad_maximum_fusion.5), channel_id=1, source_target_pairs={{0,24},{32,40},{2,26},{34,42},{4,28},{36,44},{6,30},{38,46},{64,88... | collective-permute-start | bytes 1572872 | tf_op jit(solution)/shard_map/ppermute | solution.py:64
  121.2 12.1 %collective-permute-start.20 = (bf16[2,4,2,2,80,128]{5,4,3,2,1,0:T(8,128)(2,1)}, bf16[2,4,2,2,80,128]{5,4,3,2,1,0:T(8,128)(2,1)}, u32[]{:S(2)}, u32[]{:S(2)}) collective-permute-start(bf16[2,4,2,2,80,128]{5,4,3,2,1,0:T(8,128)(2,1)} %pad_maximum_fusion.4), channel_id=1, source_target_pairs={{0,6},{32,34},{2,4},{34,32},{4,2},{36,38},{6,0},{38,36},{64,70},{9... | collective-permute-start | bytes 1966088 | tf_op jit(solution)/shard_map/ppermute | solution.py:64
  121.9 1.2 copy-start.3
  123.1 2.5 %copy-start.6 = (bf16[2,256,896]{2,1,0:T(8,128)(2,1)S(1)}, bf16[2,256,896]{2,1,0:T(8,128)(2,1)}, u32[]{:S(2)}) copy-start(bf16[2,256,896]{2,1,0:T(8,128)(2,1)} %copy-done.5) | copy-start | bytes 2752516
  128.0 6.7 %copy-start = (f32[256,1152]{1,0:T(8,128)}, f32[256,1152]{1,0:T(8,128)S(1)}, u32[]{:S(2)}) copy-start(f32[256,1152]{1,0:T(8,128)S(1)} %shard_map.97.refs_1_) | copy-start | bytes 3538948
  137.3 1.3 copy-start.1
  138.6 1.2 copy-start.7
  149.0 10.5 %collective-permute-start.24 = (bf16[256,896]{1,0:T(8,128)(2,1)}, bf16[256,896]{1,0:T(8,128)(2,1)}, u32[]{:S(2)}, u32[]{:S(2)}) collective-permute-start(bf16[256,896]{1,0:T(8,128)(2,1)} %shard_map.101), channel_id=1, source_target_pairs={{0,64},{32,96},{2,66},{34,98},{4,68},{36,100},{6,70},{38,102},{64,... | collective-permute-start | bytes 1376264 | tf_op jit(solution)/shard_map/ppermute | solution.py:64
  149.9 1.2 copy-start.4

commit v6 on v5

--- a/solution.py
+++ b/solution.py
@@ -54,8 +54,8 @@
 
 FLIP = {(axis, turn): flip(axis, turn) for axis in "xz" for turn in (0, 1)}
 
-EARLY = 2 * D
-LATE = (2 + HEADS) * D
+KEPT = 2
+CUTS = (0, 2 * D, (4 + KEPT) * D, (4 + HEADS) * D)
 SLAB = WIDTH // 4
 PAIRED = ((0, 1, 2, 3), (0, 3, 1, 2))
 
@@ -165,9 +165,10 @@
 LINES = HEADS * TOK
 
 
-def attend_body(wide, info_ref, count_ref, part_ref, far_k_ref, far_v_ref, *rest):
+def attend_body(wide, info_ref, count_ref, part_ref, more_ref, far_k_ref, far_v_ref, *rest):
     out_ref, query_ref, keys_ref, values_ref, bias_ref, score_ref, top_ref, sum_ref, mix_ref = rest
     span, valid, column, which = info_ref[0], info_ref[1], info_ref[2], info_ref[3]
+    own = slice(0, TOK) if wide else slice(TOK, 2 * TOK)
 
     lane = lax.broadcasted_iota(jnp.int32, (1, ROOM), 1)
     bias_ref[...] = jnp.full((1, ROOM), FILL, jnp.float32)
@@ -201,10 +202,13 @@
     near_bias = jnp.where((col <= row) & (col < valid), 0.0, FILL)
     for head in range(HEADS):
         here = slice(head * TOK, (head + 1) * TOK)
-        query = part_ref[:, (2 + head) * D : (3 + head) * D]
+        if head < KEPT:
+            query = part_ref[own, (2 + head) * D : (3 + head) * D]
+        else:
+            query = more_ref[:, (head - KEPT) * D : (head - KEPT + 1) * D]
         query_ref[here, :] = query
         near = lax.dot_general(
-            query, part_ref[:, :D], contract, preferred_element_type=jnp.float32
+            query, part_ref[own, :D], contract, preferred_element_type=jnp.float32
         )
         near = near + near_bias
         score_ref[here, ROOM:] = near
@@ -236,7 +240,7 @@
         sum_ref[lines, :] = fold(jnp.add, weight)
         mix_ref[lines, :] = jnp.dot(
             weight.astype(jnp.bfloat16),
-            part_ref[:, D : 2 * D],
+            part_ref[own, D : 2 * D],
             preferred_element_type=jnp.float32,
         )
 
@@ -266,13 +270,13 @@
             out_ref[:, head * D : (head + 1) * D] = result
 
 
-def attend(wide, info, counts, part, far_k, far_v):
+def attend(wide, info, counts, part, more, far_k, far_v):
     columns = 2 * HEADS * D if wide else HEADS * D
     smem, vmem = pl.BlockSpec(memory_space=pltpu.SMEM), pl.BlockSpec(memory_space=pltpu.VMEM)
     return pl.pallas_call(
         functools.partial(attend_body, wide),
         out_shape=jax.ShapeDtypeStruct((TOK, columns), jnp.bfloat16),
-        in_specs=[smem, smem, vmem, vmem, vmem],
+        in_specs=[smem, smem, vmem, vmem, vmem, vmem],
         out_specs=vmem,
         scratch_shapes=[
             pltpu.VMEM((LINES, D), jnp.bfloat16),
@@ -285,7 +289,7 @@
             pltpu.VMEM((LINES, D), jnp.float32),
         ],
         compiler_params=pltpu.CompilerParams(vmem_limit_bytes=28 * 1024 * 1024),
-    )(info, counts, part, far_k, far_v)
+    )(info, counts, part, more, far_k, far_v)
 
 
 def project_body(count, slab_ref, x_ref, *refs):
@@ -314,6 +318,51 @@
     )(jnp.stack(slabs).astype(jnp.int32), x, *weights, *totals)
 
 
+def crossed_body(info_ref, own_near, own_far, mate_near, mate_far, *refs):
+    pieces, out_ref, full_ref = refs[:4], refs[4], refs[5]
+    core = info_ref[0]
+    block = 4 * ROWS
+    for i, piece in enumerate(pieces):
+        theirs, is_far = divmod(i, 2)
+        side = core if theirs == 0 else 1 - core
+        pair_x, pair_z = info_ref[1 + theirs], info_ref[3 + theirs]
+        if is_far:
+            pair_z = 1 - pair_z
+        for t in range(2):
+            split = jnp.where(pair_z == 0, PAIRED[1][t], PAIRED[1][2 + t])
+            z = jnp.where(side == 0, 2 * pair_z + t, split)
+            for x in range(4):
+                at = jnp.where(side == 0, x, PAIRED[1].index(x))
+                slab = jnp.where(at // 2 == pair_x, 0, 2) + theirs
+                line = slab * SLAB + ((at % 2) * 4 + z) * block
+                source = slice((t * 4 + x) * block, (t * 4 + x + 1) * block)
+                full_ref[pl.ds(pl.multiple_of(line, 16), block), :] = piece[source, :]
+    columns = out_ref.shape[1]
+    for first in range(0, columns, 256):
+        here = slice(first, first + 256)
+        for j, (near_ref, far_ref) in enumerate(((own_near, own_far), (mate_near, mate_far))):
+            out = None
+            for slab in range(4):
+                x_ref = near_ref if slab < 2 else far_ref
+                w = full_ref[slab * SLAB : (slab + 1) * SLAB, here]
+                term = jnp.dot(x_ref[slab % 2, :TOK, :], w, preferred_element_type=jnp.float32)
+                out = term if out is None else out + term
+            out_ref[j * TOK : (j + 1) * TOK, here] = out.astype(jnp.bfloat16)
+
+
+def project_crossed(info, tokens, pieces):
+    smem, vmem = pl.BlockSpec(memory_space=pltpu.SMEM), pl.BlockSpec(memory_space=pltpu.VMEM)
+    columns = pieces[0].shape[1]
+    return pl.pallas_call(
+        crossed_body,
+        out_shape=jax.ShapeDtypeStruct((2 * TOK, columns), jnp.bfloat16),
+        in_specs=[smem] + [vmem] * 8,
+        out_specs=vmem,
+        scratch_shapes=[pltpu.VMEM((WIDTH, columns), jnp.bfloat16)],
+        compiler_params=pltpu.CompilerParams(vmem_limit_bytes=16 * 1024 * 1024),
+    )(info, *tokens, *pieces)
+
+
 def after(value, other):
     return lax.optimization_barrier((value, other))[0]
 
@@ -337,7 +386,7 @@
     smem, vmem = pl.BlockSpec(memory_space=pltpu.SMEM), pl.BlockSpec(memory_space=pltpu.VMEM)
     return pl.pallas_call(
         halves_body,
-        out_shape=[jax.ShapeDtypeStruct((ROWS, EARLY + LATE), jnp.bfloat16)] * 2,
+        out_shape=[jax.ShapeDtypeStruct((ROWS, CUTS[-1]), jnp.bfloat16)] * 2,
         in_specs=[smem] + [vmem] * len(weights),
         out_specs=[vmem, vmem],
         compiler_params=pltpu.CompilerParams(vmem_limit_bytes=4 * 1024 * 1024),
@@ -409,12 +458,17 @@
         joined = in_place(double(block, axis), (p, p ^ near, p ^ far, p ^ 2), joined)
         return joined.reshape(-1, block.shape[-1])
 
-    early = second(rows[:, :EARLY], "x")
-    late = second(rows[:, EARLY:], "z")
-
-    early = order(pair_of("z", core)[1], early, send(early, FLIP["z", 0]))
-    late = order(pair_of("x", core)[1], late, send(late, FLIP["x", 0]))
+    early = second(rows[:, : CUTS[2]], "x")
+    late = second(rows[:, CUTS[2] :], "z")
+
+    early, cross = early[:, : CUTS[1]], early[:, CUTS[1] :]
+    z_second, x_second = pair_of("z", core)[1], pair_of("x", core)[1]
+    early = order(z_second, early, send(early, FLIP["z", 0]))
+    cross = order(z_second, cross, send(cross, FLIP["z", 0]))
+    late = order(x_second, late, send(late, FLIP["x", 0]))
     early_far = send(early, FLIP["z", 1])
+    cross_far = send(after(cross, early_far), FLIP["z", 1])
+    late_far = send(late, FLIP["x", 1])
     gathered = jnp.concatenate([early, early_far], 0)
     swapped = send(gathered, SWAP)
     slab_near, slab_far = slabs("z")
@@ -429,7 +483,6 @@
     block_v = beacon[..., D:]
     block = jnp.concatenate([block_k, block_v], 1)
     block = order(low, block[:1], block[1:])
-    late_far = send(after(late, block), FLIP["x", 1])
     block = jnp.stack([block, send(block, ACROSS)])
     half_k = double(block[:, :, : SLOTS + 16], "x")
     half_v = double(block[:, :, SLOTS + 16 :], "z")
@@ -437,6 +490,10 @@
     near_w = (late, send(late, SWAP))
     own = project((zero, one), own_near, near_w)
     half_k, half_v = after((half_k, half_v), own)
+    crossed = jnp.concatenate([cross, cross_far], 0)
+    crossed, far_w = after((crossed, late_far), (half_k, half_v))
+    crossed = send(crossed, SWAP)
+    far_w = (far_w, send(far_w, SWAP))
     pair_k = jnp.stack([half_k, send(half_k, FLIP["z", 0])])
     pair_v = jnp.stack([half_v, send(half_v, FLIP["x", 0])])
     mate = project((zero, one), mate_near, near_w)
@@ -458,12 +515,14 @@
     at_v = (code_x * 4 + code_z) * 2 + code_h
     live = every_k[:, :, SLOTS, 0].astype(jnp.int32).reshape(2 * SPANS)
 
-    own = project((zero,), own_far, (late_far,), own)
-    mate = project((zero,), mate_far, (late_far,), mate)
-    own, mate = lax.optimization_barrier((own, mate))
-    last_w = (send(late_far, SWAP),)
-    mate = project((one,), mate_far, last_w, mate, last=True)
-    own = project((one,), own_far, last_w, own, last=True)
+    pairs = [pair_of(axis, side)[0] for axis in "xz" for side in (core, 1 - core)]
+    part = project_crossed(
+        jnp.stack([core, *pairs]).astype(jnp.int32),
+        (own_near, own_far, mate_near, mate_far),
+        (cross, cross_far, crossed[:SLAB], crossed[SLAB:]),
+    )
+    own = project((zero, one), own_far, far_w, own, last=True)
+    mate = project((zero, one), mate_far, far_w, mate, last=True)
 
     def attention(which, valid, wide):
         info = jnp.concatenate(
@@ -473,6 +532,7 @@
             wide,
             info,
             live,
+            part,
             mate if which else own,
             every_k,
             every_v,

time: 163 us -> 150 us (0.920)
  waiting for transfers between devices: 69.2 us -> 44.6 us
  local copies, waits for them, and re-layouts: 18.8 us -> 26.5 us
  starting transfers between devices: 27.2 us -> 34.9 us
  Pallas kernels: 35.5 us -> 29 us
  other arithmetic: 8.03 us -> 11 us
    ppermute x25 -> x28, waiting for transfers between devices: 69.2 us -> 44.6 us  [send(): return lax.ppermute(value, AXES, pairs)]
    ppermute x25 -> x28, starting transfers between devices: 27.2 us -> 34.9 us  [send(): return lax.ppermute(value, AXES, pairs)]
    pallas_call x7 -> x5, Pallas kernels: 15.8 us -> 9.12 us  [project(): pl.pallas_call(functools.partial(project_body, len(weights)), out_shape=j...]
    pallas_call x1 -> x2, Pallas kernels: 0.02 us -> 3.16 us  [the longest x1 3.13 us: project_crossed(): pl.pallas_call(crossed_body, out_shape=jax.ShapeDtypeStruct((2 * TOK, col...]
    select_n x6 -> x7, other arithmetic: 1.21 us -> 4.33 us  [order(): jnp.where(first == 0, jnp.concatenate([one, two], 0), jnp.concatenate([tw...]
    dynamic_update_slice x8, local copies, waits for them, and re-layouts: 0.15 us -> 2.73 us  [in_place(): joined = lax.dynamic_update_slice_in_dim(joined, pieces[i][None], slot, 0)]
    slice x0 -> x3, local copies, waits for them, and re-layouts: none -> 2.56 us  [the longest x1 1.73 us: on_device(): crossed[SLAB:]]
    unnamed x34 -> x56, local copies, waits for them, and re-layouts: 11 us -> 12.9 us
  transfers between devices with their start and end apart: 25 -> 28, of which waited for: 15 -> 17; matrix products, arithmetic and copies ran while one was open for 8% -> 14% of each run, Pallas kernels for 16% -> 14%
where the time goes in v6:
time: 150 us; the launch traced here: 149 us
  waiting for transfers between devices  44.6 us (30%)
  starting transfers between devices  34.9 us (23%)
  Pallas kernels  29 us (19%)
  local copies, waits for them, and re-layouts  26.5 us (18%)
  other arithmetic  11 us (7%)
  between operations  2.65 us (2%)
    ppermute x28, waiting for transfers between devices, send(): return lax.ppermute(value, AXES, pairs)  44.6 us
    ppermute x28, starting transfers between devices, send(): return lax.ppermute(value, AXES, pairs)  34.9 us
    unnamed x56, local copies, waits for them, and re-layouts  12.9 us
    pallas_call x2, Pallas kernels, attend(): pl.pallas_call(functools.partial(attend_body, wide), out_shape=jax.ShapeD...  11 us
    pallas_call x5, Pallas kernels, project(): pl.pallas_call(functools.partial(project_body, len(weights)), out_shape=j...  9.12 us
    pallas_call x1, Pallas kernels, norm_rows(): pl.pallas_call(norm_body, out_shape=[jax.ShapeDtypeStruct((2, TOK + 2 * (...  5.71 us
    select_n x7, other arithmetic, order(): jnp.where(first == 0, jnp.concatenate([one, two], 0), jnp.concatenate([tw...  4.33 us
    pallas_call x1, Pallas kernels, project_crossed(): pl.pallas_call(crossed_body, out_shape=jax.ShapeDtypeStruct((2 * TOK, col...  3.13 us
  transfers between devices with their start and end apart: 28, of which 17 were waited for; matrix products, arithmetic and copies ran while one was open for 14% of the time, Pallas kernels for 14%

profile of v6, /device:TPU:6, one launch (start us, length us, event | category | flops | bytes accessed | tf_op | source)
XLA Modules:
  0.0 148.6 jit_solution(3045892918883323671)
XLA Ops:
  0.0 0.9 copy-done.22
  0.9 0.7 copy-done.23
  1.6 0.7 copy-done.24
  3.8 1.6 %collective-permute-start.1 = (bf16[28,1408]{1,0:T(8,128)(2,1)S(1)}, bf16[28,1408]{1,0:T(8,128)(2,1)S(1)}, u32[]{:S(2)}, u32[]{:S(2)}) collective-permute-start(bf16[28,1408]{1,0:T(8,128)(2,1)S(1)} %get-tuple-element.21), channel_id=1, source_target_pairs={{0,64},{32,96},{2,66},{34,98},{4,68},{36,100},{6,70},{38,102},{64,... | collective-permute-start | bytes 236552 | tf_op jit(solution)/shard_map/ppermute | solution.py:64
  5.5 3.0 %collective-permute-done.1 = bf16[28,1408]{1,0:T(8,128)(2,1)S(1)} collective-permute-done((bf16[28,1408]{1,0:T(8,128)(2,1)S(1)}, bf16[28,1408]{1,0:T(8,128)(2,1)S(1)}, u32[]{:S(2)}, u32[]{:S(2)}) %collective-permute-start.1) | collective-permute-done | bytes 78880 | tf_op jit(solution)/shard_map/ppermute | solution.py:64
  8.5 3.1 %collective-permute-start.2 = (bf16[56,1408]{1,0:T(8,128)(2,1)S(1)}, bf16[56,1408]{1,0:T(8,128)(2,1)S(1)}, u32[]{:S(2)}, u32[]{:S(2)}) collective-permute-start(bf16[56,1408]{1,0:T(8,128)(2,1)S(1)} %maximum_select_fusion.4), channel_id=1, source_target_pairs={{0,65},{32,97},{2,67},{34,99},{4,69},{36,101},{6,71},{38,103},{64,... | collective-permute-start | bytes 473096 | tf_op jit(solution)/shard_map/ppermute | solution.py:64
  13.0 0.7 reshape.98.gain_ref
  13.8 1.5 %copy-done.21 = bf16[1,256,3584]{2,1,0:T(8,128)(2,1)S(1)} copy-done((bf16[1,256,3584]{2,1,0:T(8,128)(2,1)S(1)}, bf16[1,256,3584]{2,1,0:T(8,128)(2,1)}, u32[]{:S(2)}) %copy-start.21) | copy-done | bytes 1835032
  15.3 5.7 %shard_map.91 = (bf16[2,416,896]{2,1,0:T(8,128)(2,1)S(1)}, bf16[2,256,896]{2,1,0:T(8,128)(2,1)S(1)}) custom-call(s32[7]{0:T(128)S(1)} %stack.148.fact_ref, bf16[256,3584]{1,0:T(8,128)(2,1)S(1)} %bitcast.72, f32[1,3584]{1,0:T(1,128)S(1)} %reshape.98.gain_ref), custom_call_target="tpu_custom_call" | custom-call | tf_op jit(solution)/shard_map/pallas_call | solution.py:145
  21.1 0.9 copy-done.8
  22.2 0.9 collective-permute-start.3
  23.1 1.9 %collective-permute-start.13 = (bf16[112,640]{1,0:T(8,128)(2,1)S(1)}, bf16[112,640]{1,0:T(8,128)(2,1)S(1)}, u32[]{:S(2)}, u32[]{:S(2)}) collective-permute-start(bf16[112,640]{1,0:T(8,128)(2,1)S(1)} %get-tuple-element.38), channel_id=1, source_target_pairs={{0,2},{32,38},{2,0},{34,36},{4,6},{36,34},{6,4},{38,32},{64,66},{9... | collective-permute-start | bytes 430088 | tf_op jit(solution)/shard_map/ppermute | solution.py:64
  25.1 0.9 broadcast_in_dim.33
  26.7 1.0 collective-permute-done.3
  28.4 4.1 %collective-permute-start.14 = (bf16[2,112,640]{2,1,0:T(8,128)(2,1)S(1)}, bf16[2,112,640]{2,1,0:T(8,128)(2,1)S(1)}, u32[]{:S(2)}, u32[]{:S(2)}) collective-permute-start(bf16[2,112,640]{2,1,0:T(8,128)(2,1)S(1)} %pad_maximum_fusion.9), channel_id=1, source_target_pairs={{0,6},{32,34},{2,4},{34,32},{4,2},{36,38},{6,0},{38,36},{64,70},{9... | collective-permute-start | bytes 860168 | tf_op jit(solution)/shard_map/ppermute | solution.py:64
  32.5 3.8 %collective-permute-done.4 = bf16[2,112,768]{2,1,0:T(8,128)(2,1)S(1)} collective-permute-done((bf16[2,112,768]{2,1,0:T(8,128)(2,1)S(1)}, bf16[2,112,768]{2,1,0:T(8,128)(2,1)S(1)}, u32[]{:S(2)}, u32[]{:S(2)}) %collective-permute-start.4) | collective-permute-done | bytes 344096 | tf_op jit(solution)/shard_map/ppermute | solution.py:64
  36.4 2.0 %collective-permute-start.5 = (bf16[448,256]{1,0:T(8,128)(2,1)S(1)}, bf16[448,256]{1,0:T(8,128)(2,1)S(1)}, u32[]{:S(2)}, u32[]{:S(2)}) collective-permute-start(bf16[448,256]{1,0:T(8,128)(2,1)S(1)} %slice.120), channel_id=1, source_target_pairs={{0,2},{32,38},{2,0},{34,36},{4,6},{36,34},{6,4},{38,32},{64,66},{9... | collective-permute-start | bytes 688136 | tf_op jit(solution)/shard_map/ppermute | solution.py:64
  39.0 4.2 %collective-permute-done.5 = bf16[448,256]{1,0:T(8,128)(2,1)S(1)} collective-permute-done((bf16[448,256]{1,0:T(8,128)(2,1)S(1)}, bf16[448,256]{1,0:T(8,128)(2,1)S(1)}, u32[]{:S(2)}, u32[]{:S(2)}) %collective-permute-start.5) | collective-permute-done | bytes 229408 | tf_op jit(solution)/shard_map/ppermute | solution.py:64
  43.4 4.1 %collective-permute-start.6 = (bf16[896,256]{1,0:T(8,128)(2,1)S(1)}, bf16[896,256]{1,0:T(8,128)(2,1)}, u32[]{:S(2)}, u32[]{:S(2)}) collective-permute-start(bf16[896,256]{1,0:T(8,128)(2,1)S(1)} %maximum_select_fusion.2.refs_0_), channel_id=1, source_target_pairs={{0,6},{32,34},{2,4},{34,32},{4,2},{36,38},{6,0},{38,36},{64,70},{9... | collective-permute-start | bytes 1376264 | tf_op jit(solution)/shard_map/ppermute | solution.py:64
  48.2 0.8 slice.135
  49.7 0.9 slice.86
  50.5 1.8 %slice.114 = bf16[4,64,896]{2,1,0:T(8,128)(2,1)} slice(bf16[4,80,896]{2,1,0:T(8,128)(2,1)} %bitcast.76), slice={[0:4], [0:64], [0:896]} | slice | bytes 917504 | tf_op jit(solution)/shard_map/slice | solution.py:448
  52.4 3.3 %collective-permute-done.6.refs_1_ = bf16[896,256]{1,0:T(8,128)(2,1)} collective-permute-done((bf16[896,256]{1,0:T(8,128)(2,1)S(1)}, bf16[896,256]{1,0:T(8,128)(2,1)}, u32[]{:S(2)}, u32[]{:S(2)}) %collective-permute-start.6) | collective-permute-done | bytes 458784 | tf_op jit(solution)/shard_map/ppermute | solution.py:64
  55.6 1.1 pad_maximum_fusion.4
  56.9 0.9 collective-permute-done.21
  57.8 1.7 %maximum_select_fusion.1.refs_0_ = bf16[896,512]{1,0:T(8,128)(2,1)S(1)} fusion(bf16[448,512]{1,0:T(8,128)(2,1)} %collective-permute-done.21, bf16[448,512]{1,0:T(8,128)(2,1)} %slice.135, pred[]{:T(512)S(6)} %eq.102), kind=kLoop, calls=%fused_computation.6 | loop fusion | flops 4128768 | bytes 1835009 | tf_op jit(solution)/shard_map/jit(_where)/select_n | solution.py:417
  59.7 2.3 %maximum_select_fusion.refs_0_ = bf16[896,640]{1,0:T(8,128)(2,1)S(1)} fusion(bf16[448,640]{1,0:T(8,128)(2,1)} %collective-permute-done.15, bf16[448,640]{1,0:T(8,128)(2,1)} %bitcast.36, pred[]{:T(512)S(6)} %eq.104), kind=kLoop, calls=%fused_computation.2 | loop fusion | flops 5160960 | bytes 2293761 | tf_op jit(solution)/shard_map/jit(_where)/select_n | solution.py:417
  62.1 1.9 %collective-permute-start.23 = (bf16[896,640]{1,0:T(8,128)(2,1)S(1)}, bf16[896,640]{1,0:T(8,128)(2,1)}, u32[]{:S(2)}, u32[]{:S(2)}) collective-permute-start(bf16[896,640]{1,0:T(8,128)(2,1)S(1)} %maximum_select_fusion.refs_0_), channel_id=1, source_target_pairs={{0,24},{32,40},{2,26},{34,42},{4,28},{36,44},{6,30},{38,46},{64,88... | collective-permute-start | bytes 3440648 | tf_op jit(solution)/shard_map/ppermute | solution.py:64
  63.9 3.0 %collective-permute-start.22 = (bf16[896,512]{1,0:T(8,128)(2,1)S(1)}, bf16[896,512]{1,0:T(8,128)(2,1)S(1)}, u32[]{:S(2)}, u32[]{:S(2)}) collective-permute-start(bf16[896,512]{1,0:T(8,128)(2,1)S(1)} %maximum_select_fusion.1.refs_0_), channel_id=1, source_target_pairs={{0,6},{32,34},{2,4},{34,32},{4,2},{36,38},{6,0},{38,36},{64,70},{9... | collective-permute-start | bytes 2752520 | tf_op jit(solution)/shard_map/ppermute | solution.py:64
  68.3 2.0 %collective-permute-start.19 = (bf16[2,256,896]{2,1,0:T(8,128)(2,1)S(1)}, bf16[2,256,896]{2,1,0:T(8,128)(2,1)S(1)}, u32[]{:S(2)}, u32[]{:S(2)}) collective-permute-start(bf16[2,256,896]{2,1,0:T(8,128)(2,1)S(1)} %copy-done.9), channel_id=1, source_target_pairs={{0,64},{32,96},{2,66},{34,98},{4,68},{36,100},{6,70},{38,102},{64,... | collective-permute-start | bytes 2752520 | tf_op jit(solution)/shard_map/ppermute | solution.py:64
  70.6 1.5 shard_map.93
  72.6 5.3 %collective-permute-done.8 = bf16[2,144,128]{2,1,0:T(8,128)(2,1)S(1)} collective-permute-done((bf16[2,144,128]{2,1,0:T(8,128)(2,1)S(1)}, bf16[2,144,128]{2,1,0:T(8,128)(2,1)S(1)}, u32[]{:S(2)}, u32[]{:S(2)}) %collective-permute-start.8) | collective-permute-done | bytes 73760 | tf_op jit(solution)/shard_map/ppermute | solution.py:64
  77.9 4.2 %collective-permute-done.11 = bf16[2,2,64,128]{3,2,1,0:T(8,128)(2,1)S(1)} collective-permute-done((bf16[2,2,64,128]{3,2,1,0:T(8,128)(2,1)S(1)}, bf16[2,2,64,128]{3,2,1,0:T(8,128)(2,1)S(1)}, u32[]{:S(2)}, u32[]{:S(2)}) %collective-permute-start.11) | collective-permute-done | bytes 65568 | tf_op jit(solution)/shard_map/ppermute | solution.py:64
  82.1 4.4 %collective-permute-done.9 = bf16[2,2,80,128]{3,2,1,0:T(8,128)(2,1)S(1)} collective-permute-done((bf16[2,2,80,128]{3,2,1,0:T(8,128)(2,1)S(1)}, bf16[2,2,80,128]{3,2,1,0:T(8,128)(2,1)S(1)}, u32[]{:S(2)}, u32[]{:S(2)}) %collective-permute-start.9) | collective-permute-done | bytes 81952 | tf_op jit(solution)/shard_map/ppermute | solution.py:64
  86.9 1.7 %collective-permute-start.10 = (bf16[2,2,2,80,128]{4,3,2,1,0:T(8,128)(2,1)S(1)}, bf16[2,2,2,80,128]{4,3,2,1,0:T(8,128)(2,1)S(1)}, u32[]{:S(2)}, u32[]{:S(2)}) collective-permute-start(bf16[2,2,2,80,128]{4,3,2,1,0:T(8,128)(2,1)S(1)} %pad_maximum_fusion.11), channel_id=1, source_target_pairs={{0,24},{32,40},{2,26},{34,42},{4,28},{36,44},{6,30},{38,46},{64,88... | collective-permute-start | bytes 491528 | tf_op jit(solution)/shard_map/ppermute | solution.py:64
  88.5 1.4 pad_maximum_fusion
  89.9 1.5 %shard_map.94.refs_2_ = f32[256,640]{1,0:T(8,128)S(1)} custom-call(s32[2]{0:T(128)S(1)} %iota.19.slab_ref, bf16[2,416,896]{2,1,0:T(8,128)(2,1)S(1)} %get-tuple-element.19.x_ref.own_near, bf16[896,640]{1,0:T(8,128)(2,1)S(1)} %maximum_select_fusion.refs_0_, bf16[896,640]{1,0:T(8,128)(2,1)S(1)} %collective-permute-done.16.refs_1_), custom_call_target="tpu_custom_call" | custom-call | tf_op jit(solution)/shard_map/pallas_call | solution.py:312
  91.5 1.3 collective-permute-done.12
  92.8 0.7 collective-permute-done.10
  94.0 1.5 %shard_map.95.refs_2_ = f32[256,640]{1,0:T(8,128)S(1)} custom-call(s32[2]{0:T(128)S(1)} %iota.20.slab_ref, bf16[2,416,896]{2,1,0:T(8,128)(2,1)S(1)} %collective-permute-done.x_ref.mate_near, bf16[896,640]{1,0:T(8,128)(2,1)S(1)} %maximum_select_fusion.refs_0_, bf16[896,640]{1,0:T(8,128)(2,1)S(1)} %collective-permute-done.16.refs_1_), custom_call_target="tpu_custom_call" | custom-call | tf_op jit(solution)/shard_map/pallas_call | solution.py:312
  95.6 3.3 %collective-permute-start.25 = (bf16[896,640]{1,0:T(8,128)(2,1)}, bf16[896,640]{1,0:T(8,128)(2,1)S(1)}, u32[]{:S(2)}, u32[]{:S(2)}) collective-permute-start(bf16[896,640]{1,0:T(8,128)(2,1)} %collective-permute-done.23.refs_0_), channel_id=1, source_target_pairs={{0,32},{32,0},{2,34},{34,2},{4,36},{36,4},{6,38},{38,6},{64,96},{9... | collective-permute-start | bytes 3440648 | tf_op jit(solution)/shard_map/ppermute | solution.py:64
  98.9 1.4 collective-permute-done.18
  100.3 0.7 collective-permute-done.17
  101.1 1.0 pad_maximum_fusion.5
  102.1 1.0 copy-done.14
  103.0 1.6 %collective-permute-start.26 = (bf16[2,4,2,2,64,128]{5,4,3,2,1,0:T(8,128)(2,1)S(1)}, bf16[2,4,2,2,64,128]{5,4,3,2,1,0:T(8,128)(2,1)S(1)}, u32[]{:S(2)}, u32[]{:S(2)}) collective-permute-start(bf16[2,4,2,2,64,128]{5,4,3,2,1,0:T(8,128)(2,1)S(1)} %pad_maximum_fusion.6), channel_id=1, source_target_pairs={{0,24},{32,40},{2,26},{34,42},{4,28},{36,44},{6,30},{38,46},{64,88... | collective-permute-start | bytes 1572872 | tf_op jit(solution)/shard_map/ppermute | solution.py:64
  104.6 1.9 %collective-permute-start.20 = (bf16[2,4,2,2,80,128]{5,4,3,2,1,0:T(8,128)(2,1)}, bf16[2,4,2,2,80,128]{5,4,3,2,1,0:T(8,128)(2,1)}, u32[]{:S(2)}, u32[]{:S(2)}) collective-permute-start(bf16[2,4,2,2,80,128]{5,4,3,2,1,0:T(8,128)(2,1)} %pad_maximum_fusion.5), channel_id=1, source_target_pairs={{0,6},{32,34},{2,4},{34,32},{4,2},{36,38},{6,0},{38,36},{64,70},{9... | collective-permute-start | bytes 1966088 | tf_op jit(solution)/shard_map/ppermute | solution.py:64
  106.6 0.7 concatenate.119.info_ref
  107.3 6.1 %collective-permute-done.26 = bf16[2,4,2,2,64,128]{5,4,3,2,1,0:T(8,128)(2,1)S(1)} collective-permute-done((bf16[2,4,2,2,64,128]{5,4,3,2,1,0:T(8,128)(2,1)S(1)}, bf16[2,4,2,2,64,128]{5,4,3,2,1,0:T(8,128)(2,1)S(1)}, u32[]{:S(2)}, u32[]{:S(2)}) %collective-permute-start.26) | collective-permute-done | bytes 524320 | tf_op jit(solution)/shard_map/ppermute | solution.py:64
  113.5 3.2 %collective-permute-done.20 = bf16[2,4,2,2,80,128]{5,4,3,2,1,0:T(8,128)(2,1)} collective-permute-done((bf16[2,4,2,2,80,128]{5,4,3,2,1,0:T(8,128)(2,1)}, bf16[2,4,2,2,80,128]{5,4,3,2,1,0:T(8,128)(2,1)}, u32[]{:S(2)}, u32[]{:S(2)}) %collective-permute-start.20) | collective-permute-done | bytes 655392 | tf_op jit(solution)/shard_map/ppermute | solution.py:64
  116.7 1.4 pad_maximum_fusion.1
  118.1 1.2 fusion.1
  119.5 1.6 %copy-done.15 = bf16[2,256,896]{2,1,0:T(8,128)(2,1)S(1)} copy-done((bf16[2,256,896]{2,1,0:T(8,128)(2,1)S(1)}, bf16[2,256,896]{2,1,0:T(8,128)(2,1)}, u32[]{:S(2)}) %copy-start.15) | copy-done | bytes 917528
  121.1 1.1 copy-done.20
  122.2 2.4 %shard_map.99.more_ref = bf16[256,640]{1,0:T(8,128)(2,1)S(1)} custom-call(s32[2]{0:T(128)S(1)} %iota.22.slab_ref, bf16[2,256,896]{2,1,0:T(8,128)(2,1)S(1)} %copy-done.15, bf16[896,640]{1,0:T(8,128)(2,1)} %collective-permute-done.23.refs_0_, bf16[896,640]{1,0:T(8,128)(2,1)S(1)} %collective-permute-done.25.refs_1_, f32[256,640]{1,0:T(8,128)S(1)} %copy-done.20), custom_call_target="tpu_custom_call" | custom-call | tf_op jit(solution)/shard_map/pallas_call | solution.py:312
  124.6 1.7 %fusion.6 = (bf16[896,512]{1,0:T(8,128)(2,1)S(1)}, bf16[896,512]{1,0:T(8,128)(2,1)S(1)}) fusion(bf16[1792,512]{1,0:T(8,128)(2,1)} %collective-permute-done.24), kind=kLoop, calls=%fused_computation.70 | loop fusion | bytes 3670016 | tf_op jit(solution)/shard_map/slice | solution.py:522
  126.9 3.1 %shard_map.96.part_ref = bf16[512,512]{1,0:T(8,128)(2,1)S(1)} custom-call(s32[5]{0:T(128)S(1)} %stack.175.info_ref, bf16[2,416,896]{2,1,0:T(8,128)(2,1)S(1)} %copy-done.3, bf16[2,256,896]{2,1,0:T(8,128)(2,1)S(1)} %copy-done.10, bf16[2,416,896]{2,1,0:T(8,128)(2,1)S(1)} %copy-done.1, bf16[2,256,896]{2,1,0:T(8,128)(2,1)S(1)} %copy-done.16, ...), custom_call_target="tpu_custom_call" | custom-call | tf_op jit(solution)/shard_map/pallas_call | solution.py:356
  130.1 4.9 %shard_map.100 = bf16[256,896]{1,0:T(8,128)(2,1)} custom-call(s32[68]{0:T(128)S(1)} %concatenate.119.info_ref, s32[64]{0:T(128)S(1)} %reshape.107.count_ref, bf16[512,512]{1,0:T(8,128)(2,1)S(1)} %shard_map.96.part_ref, bf16[256,640]{1,0:T(8,128)(2,1)S(1)} %shard_map.99.more_ref, bf16[32,2,80,128]{3,2,1,0:T(8,128)(2,1)S(1)} %bitcast.68, ...), custom_call_target="tpu_custom_call" | custom-call | tf_op jit(solution)/shard_map/pallas_call | solution.py:276
  135.1 1.3 copy-done.7
  136.4 1.2 copy-done.11
  137.6 2.2 %shard_map.97.more_ref = bf16[256,640]{1,0:T(8,128)(2,1)S(1)} custom-call(s32[2]{0:T(128)S(1)} %iota.21.slab_ref, bf16[2,256,896]{2,1,0:T(8,128)(2,1)S(1)} %copy-done.11, bf16[896,640]{1,0:T(8,128)(2,1)} %collective-permute-done.23.refs_0_, bf16[896,640]{1,0:T(8,128)(2,1)S(1)} %copy-done.7, f32[256,640]{1,0:T(8,128)S(1)} %copy-done.18), custom_call_target="tpu_custom_call" | custom-call | tf_op jit(solution)/shard_map/pallas_call | solution.py:312
  139.8 6.0 %shard_map.98 = bf16[256,1792]{1,0:T(8,128)(2,1)} custom-call(s32[68]{0:T(128)S(1)} %concatenate.93.info_ref, s32[64]{0:T(128)S(1)} %reshape.107.count_ref, bf16[512,512]{1,0:T(8,128)(2,1)S(1)} %shard_map.96.part_ref, bf16[256,640]{1,0:T(8,128)(2,1)S(1)} %shard_map.97.more_ref, bf16[32,2,80,128]{3,2,1,0:T(8,128)(2,1)S(1)} %bitcast.69, ...), custom_call_target="tpu_custom_call" | custom-call | tf_op jit(solution)/shard_map/pallas_call | solution.py:276
  145.9 0.9 collective-permute-done.27
  146.8 1.8 %bitcast_dynamic-update-slice_fusion = bf16[1,256,1792]{2,1,0:T(8,128)(2,1)} fusion(bf16[1,256,1792]{2,1,0:T(8,128)(2,1)} %bitcast.84, s32[]{:T(128)S(6)} %select_n.249, bf16[256,896]{1,0:T(8,128)(2,1)} %collective-permute-done.27), kind=kLoop, calls=%fused_computation.10 | loop fusion | bytes 917508 | tf_op jit(solution)/shard_map/dynamic_update_slice | solution.py:543
  (124 shorter events, 9.4 us)
Async XLA Ops:
  0.0 0.9 copy-start.22
  0.9 0.7 copy-start.23
  1.6 0.7 copy-start.24
  2.3 0.7 copy-start.25
  3.1 0.7 copy-start.26
  3.8 4.6 %collective-permute-start.1 = (bf16[28,1408]{1,0:T(8,128)(2,1)S(1)}, bf16[28,1408]{1,0:T(8,128)(2,1)S(1)}, u32[]{:S(2)}, u32[]{:S(2)}) collective-permute-start(bf16[28,1408]{1,0:T(8,128)(2,1)S(1)} %get-tuple-element.21), channel_id=1, source_target_pairs={{0,64},{32,96},{2,66},{34,98},{4,68},{36,100},{6,70},{38,102},{64,... | collective-permute-start | bytes 236552 | tf_op jit(solution)/shard_map/ppermute | solution.py:64
  8.5 13.6 %collective-permute-start.2 = (bf16[56,1408]{1,0:T(8,128)(2,1)S(1)}, bf16[56,1408]{1,0:T(8,128)(2,1)S(1)}, u32[]{:S(2)}, u32[]{:S(2)}) collective-permute-start(bf16[56,1408]{1,0:T(8,128)(2,1)S(1)} %maximum_select_fusion.4), channel_id=1, source_target_pairs={{0,65},{32,97},{2,67},{34,99},{4,69},{36,101},{6,71},{38,103},{64,... | collective-permute-start | bytes 473096 | tf_op jit(solution)/shard_map/ppermute | solution.py:64
  13.8 1.5 %copy-start.21 = (bf16[1,256,3584]{2,1,0:T(8,128)(2,1)S(1)}, bf16[1,256,3584]{2,1,0:T(8,128)(2,1)}, u32[]{:S(2)}) copy-start(bf16[1,256,3584]{2,1,0:T(8,128)(2,1)} %param.9) | copy-start | bytes 5505028
  21.0 0.9 copy-start.8
  22.0 68.0 %copy-start.2 = (bf16[2,416,896]{2,1,0:T(8,128)(2,1)}, bf16[2,416,896]{2,1,0:T(8,128)(2,1)S(1)}, u32[]{:S(2)}) copy-start(bf16[2,416,896]{2,1,0:T(8,128)(2,1)S(1)} %get-tuple-element.19.x_ref.own_near) | copy-start | bytes 4472836
  22.0 44.9 %collective-permute-start = (bf16[2,416,896]{2,1,0:T(8,128)(2,1)S(1)}, bf16[2,416,896]{2,1,0:T(8,128)(2,1)S(1)}, u32[]{:S(2)}, u32[]{:S(2)}) collective-permute-start(bf16[2,416,896]{2,1,0:T(8,128)(2,1)S(1)} %get-tuple-element.19.x_ref.own_near), channel_id=1, source_target_pairs={{0,64},{32,96},{2,66},{34,98},{4,68},{36,100},{6,70},{38,102},{64,... | collective-permute-start | bytes 4472840 | tf_op jit(solution)/shard_map/ppermute | solution.py:64
  22.2 5.5 %collective-permute-start.3 = (bf16[112,768]{1,0:T(8,128)(2,1)S(1)}, bf16[112,768]{1,0:T(8,128)(2,1)S(1)}, u32[]{:S(2)}, u32[]{:S(2)}) collective-permute-start(bf16[112,768]{1,0:T(8,128)(2,1)S(1)} %get-tuple-element.40), channel_id=1, source_target_pairs={{0,8},{32,56},{2,10},{34,58},{4,12},{36,60},{6,14},{38,62},{64,72}... | collective-permute-start | bytes 516104 | tf_op jit(solution)/shard_map/ppermute | solution.py:64
  23.1 5.2 %collective-permute-start.13 = (bf16[112,640]{1,0:T(8,128)(2,1)S(1)}, bf16[112,640]{1,0:T(8,128)(2,1)S(1)}, u32[]{:S(2)}, u32[]{:S(2)}) collective-permute-start(bf16[112,640]{1,0:T(8,128)(2,1)S(1)} %get-tuple-element.38), channel_id=1, source_target_pairs={{0,2},{32,38},{2,0},{34,36},{4,6},{36,34},{6,4},{38,32},{64,66},{9... | collective-permute-start | bytes 430088 | tf_op jit(solution)/shard_map/ppermute | solution.py:64
  27.8 8.5 %collective-permute-start.4 = (bf16[2,112,768]{2,1,0:T(8,128)(2,1)S(1)}, bf16[2,112,768]{2,1,0:T(8,128)(2,1)S(1)}, u32[]{:S(2)}, u32[]{:S(2)}) collective-permute-start(bf16[2,112,768]{2,1,0:T(8,128)(2,1)S(1)} %pad_maximum_fusion.7), channel_id=1, source_target_pairs={{0,24},{32,40},{2,26},{34,42},{4,28},{36,44},{6,30},{38,46},{64,88... | collective-permute-start | bytes 1032200 | tf_op jit(solution)/shard_map/ppermute | solution.py:64
  28.4 19.2 %collective-permute-start.14 = (bf16[2,112,640]{2,1,0:T(8,128)(2,1)S(1)}, bf16[2,112,640]{2,1,0:T(8,128)(2,1)S(1)}, u32[]{:S(2)}, u32[]{:S(2)}) collective-permute-start(bf16[2,112,640]{2,1,0:T(8,128)(2,1)S(1)} %pad_maximum_fusion.9), channel_id=1, source_target_pairs={{0,6},{32,34},{2,4},{34,32},{4,2},{36,38},{6,0},{38,36},{64,70},{9... | collective-permute-start | bytes 860168 | tf_op jit(solution)/shard_map/ppermute | solution.py:64
  36.4 6.8 %collective-permute-start.5 = (bf16[448,256]{1,0:T(8,128)(2,1)S(1)}, bf16[448,256]{1,0:T(8,128)(2,1)S(1)}, u32[]{:S(2)}, u32[]{:S(2)}) collective-permute-start(bf16[448,256]{1,0:T(8,128)(2,1)S(1)} %slice.120), channel_id=1, source_target_pairs={{0,2},{32,38},{2,0},{34,36},{4,6},{36,34},{6,4},{38,32},{64,66},{9... | collective-permute-start | bytes 688136 | tf_op jit(solution)/shard_map/ppermute | solution.py:64
  43.4 12.2 %collective-permute-start.6 = (bf16[896,256]{1,0:T(8,128)(2,1)S(1)}, bf16[896,256]{1,0:T(8,128)(2,1)}, u32[]{:S(2)}, u32[]{:S(2)}) collective-permute-start(bf16[896,256]{1,0:T(8,128)(2,1)S(1)} %maximum_select_fusion.2.refs_0_), channel_id=1, source_target_pairs={{0,6},{32,34},{2,4},{34,32},{4,2},{36,38},{6,0},{38,36},{64,70},{9... | collective-permute-start | bytes 1376264 | tf_op jit(solution)/shard_map/ppermute | solution.py:64
  49.0 8.8 %collective-permute-start.21 = (bf16[448,512]{1,0:T(8,128)(2,1)}, bf16[448,512]{1,0:T(8,128)(2,1)}, u32[]{:S(2)}, u32[]{:S(2)}) collective-permute-start(bf16[448,512]{1,0:T(8,128)(2,1)} %slice.135), channel_id=1, source_target_pairs={{0,2},{32,38},{2,0},{34,36},{4,6},{36,34},{6,4},{38,32},{64,66},{9... | collective-permute-start | bytes 1376264 | tf_op jit(solution)/shard_map/ppermute | solution.py:64
  49.7 10.0 %collective-permute-start.15 = (bf16[448,640]{1,0:T(8,128)(2,1)}, bf16[448,640]{1,0:T(8,128)(2,1)}, u32[]{:S(2)}, u32[]{:S(2)}) collective-permute-start(bf16[448,640]{1,0:T(8,128)(2,1)} %bitcast.36), channel_id=1, source_target_pairs={{0,8},{32,56},{2,10},{34,58},{4,12},{36,60},{6,14},{38,62},{64,72}... | collective-permute-start | bytes 1720328 | tf_op jit(solution)/shard_map/ppermute | solution.py:64
  56.7 13.8 %collective-permute-start.7 = (bf16[1792,256]{1,0:T(8,128)(2,1)S(1)}, bf16[1792,256]{1,0:T(8,128)(2,1)S(1)}, u32[]{:S(2)}, u32[]{:S(2)}) collective-permute-start(bf16[1792,256]{1,0:T(8,128)(2,1)S(1)} %pad_maximum_fusion.4), channel_id=1, source_target_pairs={{0,32},{32,0},{2,34},{34,2},{4,36},{36,4},{6,38},{38,6},{64,96},{9... | collective-permute-start | bytes 2752520 | tf_op jit(solution)/shard_map/ppermute | solution.py:64
  59.5 29.1 %copy-start.4 = (bf16[896,512]{1,0:T(8,128)(2,1)}, bf16[896,512]{1,0:T(8,128)(2,1)S(1)}, u32[]{:S(2)}) copy-start(bf16[896,512]{1,0:T(8,128)(2,1)S(1)} %maximum_select_fusion.1.refs_0_) | copy-start | bytes 2752516
  59.5 8.8 %copy-start.9 = (bf16[2,256,896]{2,1,0:T(8,128)(2,1)S(1)}, bf16[2,256,896]{2,1,0:T(8,128)(2,1)}, u32[]{:S(2)}) copy-start(bf16[2,256,896]{2,1,0:T(8,128)(2,1)} %copy-done.8) | copy-start | bytes 2752516
  59.5 10.9 %copy-start.27 = (bf16[4,64,896]{2,1,0:T(8,128)(2,1)S(1)}, bf16[4,64,896]{2,1,0:T(8,128)(2,1)}, u32[]{:S(2)}) copy-start(bf16[4,64,896]{2,1,0:T(8,128)(2,1)} %slice.114) | copy-start | bytes 1376260
  62.0 27.9 %collective-permute-start.16 = (bf16[896,640]{1,0:T(8,128)(2,1)S(1)}, bf16[896,640]{1,0:T(8,128)(2,1)S(1)}, u32[]{:S(2)}, u32[]{:S(2)}) collective-permute-start(bf16[896,640]{1,0:T(8,128)(2,1)S(1)} %maximum_select_fusion.refs_0_), channel_id=1, source_target_pairs={{0,32},{32,0},{2,34},{34,2},{4,36},{36,4},{6,38},{38,6},{64,96},{9... | collective-permute-start | bytes 3440648 | tf_op jit(solution)/shard_map/ppermute | solution.py:64
  62.1 31.5 %collective-permute-start.23 = (bf16[896,640]{1,0:T(8,128)(2,1)S(1)}, bf16[896,640]{1,0:T(8,128)(2,1)}, u32[]{:S(2)}, u32[]{:S(2)}) collective-permute-start(bf16[896,640]{1,0:T(8,128)(2,1)S(1)} %maximum_select_fusion.refs_0_), channel_id=1, source_target_pairs={{0,24},{32,40},{2,26},{34,42},{4,28},{36,44},{6,30},{38,46},{64,88... | collective-permute-start | bytes 3440648 | tf_op jit(solution)/shard_map/ppermute | solution.py:64
  63.9 22.9 %collective-permute-start.22 = (bf16[896,512]{1,0:T(8,128)(2,1)S(1)}, bf16[896,512]{1,0:T(8,128)(2,1)S(1)}, u32[]{:S(2)}, u32[]{:S(2)}) collective-permute-start(bf16[896,512]{1,0:T(8,128)(2,1)S(1)} %maximum_select_fusion.1.refs_0_), channel_id=1, source_target_pairs={{0,6},{32,34},{2,4},{34,32},{4,2},{36,38},{6,0},{38,36},{64,70},{9... | collective-permute-start | bytes 2752520 | tf_op jit(solution)/shard_map/ppermute | solution.py:64
  66.9 27.1 %copy-start = (bf16[2,416,896]{2,1,0:T(8,128)(2,1)}, bf16[2,416,896]{2,1,0:T(8,128)(2,1)S(1)}, u32[]{:S(2)}) copy-start(bf16[2,416,896]{2,1,0:T(8,128)(2,1)S(1)} %collective-permute-done.x_ref.mate_near) | copy-start | bytes 4472836
  68.3 33.7 %collective-permute-start.19 = (bf16[2,256,896]{2,1,0:T(8,128)(2,1)S(1)}, bf16[2,256,896]{2,1,0:T(8,128)(2,1)S(1)}, u32[]{:S(2)}, u32[]{:S(2)}) collective-permute-start(bf16[2,256,896]{2,1,0:T(8,128)(2,1)S(1)} %copy-done.9), channel_id=1, source_target_pairs={{0,64},{32,96},{2,66},{34,98},{4,68},{36,100},{6,70},{38,102},{64,... | collective-permute-start | bytes 2752520 | tf_op jit(solution)/shard_map/ppermute | solution.py:64
  72.2 5.6 %collective-permute-start.8 = (bf16[2,144,128]{2,1,0:T(8,128)(2,1)S(1)}, bf16[2,144,128]{2,1,0:T(8,128)(2,1)S(1)}, u32[]{:S(2)}, u32[]{:S(2)}) collective-permute-start(bf16[2,144,128]{2,1,0:T(8,128)(2,1)S(1)} %maximum_select_fusion.6), channel_id=1, source_target_pairs={{0,65},{32,97},{2,67},{34,99},{4,69},{36,101},{6,71},{38,103},{64,... | collective-permute-start | bytes 221192 | tf_op jit(solution)/shard_map/ppermute | solution.py:64
  77.9 4.3 %collective-permute-start.11 = (bf16[2,2,64,128]{3,2,1,0:T(8,128)(2,1)S(1)}, bf16[2,2,64,128]{3,2,1,0:T(8,128)(2,1)S(1)}, u32[]{:S(2)}, u32[]{:S(2)}) collective-permute-start(bf16[2,2,64,128]{3,2,1,0:T(8,128)(2,1)S(1)} %pad_maximum_fusion.14), channel_id=1, source_target_pairs={{0,2},{32,38},{2,0},{34,36},{4,6},{36,34},{6,4},{38,32},{64,66},{9... | collective-permute-start | bytes 196616 | tf_op jit(solution)/shard_map/ppermute | solution.py:64
  82.1 4.4 %collective-permute-start.9 = (bf16[2,2,80,128]{3,2,1,0:T(8,128)(2,1)S(1)}, bf16[2,2,80,128]{3,2,1,0:T(8,128)(2,1)S(1)}, u32[]{:S(2)}, u32[]{:S(2)}) collective-permute-start(bf16[2,2,80,128]{3,2,1,0:T(8,128)(2,1)S(1)} %fusion), channel_id=1, source_target_pairs={{0,8},{32,56},{2,10},{34,58},{4,12},{36,60},{6,14},{38,62},{64,72}... | collective-permute-start | bytes 245768 | tf_op jit(solution)/shard_map/ppermute | solution.py:64
  86.6 6.2 %collective-permute-start.12 = (bf16[2,2,2,64,128]{4,3,2,1,0:T(8,128)(2,1)S(1)}, bf16[2,2,2,64,128]{4,3,2,1,0:T(8,128)(2,1)S(1)}, u32[]{:S(2)}, u32[]{:S(2)}) collective-permute-start(bf16[2,2,2,64,128]{4,3,2,1,0:T(8,128)(2,1)S(1)} %pad_maximum_fusion.12), channel_id=1, source_target_pairs={{0,6},{32,34},{2,4},{34,32},{4,2},{36,38},{6,0},{38,36},{64,70},{9... | collective-permute-start | bytes 393224 | tf_op jit(solution)/shard_map/ppermute | solution.py:64
  86.9 3.0 %copy-start.12 = (bf16[896,512]{1,0:T(8,128)(2,1)}, bf16[896,512]{1,0:T(8,128)(2,1)S(1)}, u32[]{:S(2)}) copy-start(bf16[896,512]{1,0:T(8,128)(2,1)S(1)} %collective-permute-done.22.refs_1_) | copy-start | bytes 2752516
  86.9 6.6 %collective-permute-start.10 = (bf16[2,2,2,80,128]{4,3,2,1,0:T(8,128)(2,1)S(1)}, bf16[2,2,2,80,128]{4,3,2,1,0:T(8,128)(2,1)S(1)}, u32[]{:S(2)}, u32[]{:S(2)}) collective-permute-start(bf16[2,2,2,80,128]{4,3,2,1,0:T(8,128)(2,1)S(1)} %pad_maximum_fusion.11), channel_id=1, source_target_pairs={{0,24},{32,40},{2,26},{34,42},{4,28},{36,44},{6,30},{38,46},{64,88... | collective-permute-start | bytes 491528 | tf_op jit(solution)/shard_map/ppermute | solution.py:64
  91.5 4.1 %copy-start.17 = (f32[256,640]{1,0:T(8,128)}, f32[256,640]{1,0:T(8,128)S(1)}, u32[]{:S(2)}) copy-start(f32[256,640]{1,0:T(8,128)S(1)} %shard_map.94.refs_2_) | copy-start | bytes 1966084
  93.5 31.0 %collective-permute-start.24 = (bf16[1792,512]{1,0:T(8,128)(2,1)}, bf16[1792,512]{1,0:T(8,128)(2,1)}, u32[]{:S(2)}, u32[]{:S(2)}) collective-permute-start(bf16[1792,512]{1,0:T(8,128)(2,1)} %pad_maximum_fusion), channel_id=1, source_target_pairs={{0,32},{32,0},{2,34},{34,2},{4,36},{36,4},{6,38},{38,6},{64,96},{9... | collective-permute-start | bytes 5505032 | tf_op jit(solution)/shard_map/ppermute | solution.py:64
  93.8 6.5 %collective-permute-start.18 = (bf16[4,2,2,64,128]{4,3,2,1,0:T(8,128)(2,1)S(1)}, bf16[4,2,2,64,128]{4,3,2,1,0:T(8,128)(2,1)S(1)}, u32[]{:S(2)}, u32[]{:S(2)}) collective-permute-start(bf16[4,2,2,64,128]{4,3,2,1,0:T(8,128)(2,1)S(1)} %pad_maximum_fusion.10), channel_id=1, source_target_pairs={{0,8},{32,56},{2,10},{34,58},{4,12},{36,60},{6,14},{38,62},{64,72}... | collective-permute-start | bytes 786440 | tf_op jit(solution)/shard_map/ppermute | solution.py:64
  93.9 7.2 %collective-permute-start.17 = (bf16[4,2,2,80,128]{4,3,2,1,0:T(8,128)(2,1)S(1)}, bf16[4,2,2,80,128]{4,3,2,1,0:T(8,128)(2,1)S(1)}, u32[]{:S(2)}, u32[]{:S(2)}) collective-permute-start(bf16[4,2,2,80,128]{4,3,2,1,0:T(8,128)(2,1)S(1)} %pad_maximum_fusion.8), channel_id=1, source_target_pairs={{0,2},{32,38},{2,0},{34,36},{4,6},{36,34},{6,4},{38,32},{64,66},{9... | collective-permute-start | bytes 983048 | tf_op jit(solution)/shard_map/ppermute | solution.py:64
  95.6 6.5 %copy-start.19 = (f32[256,640]{1,0:T(8,128)}, f32[256,640]{1,0:T(8,128)S(1)}, u32[]{:S(2)}) copy-start(f32[256,640]{1,0:T(8,128)S(1)} %shard_map.95.refs_2_) | copy-start | bytes 1966084
  95.6 23.9 %collective-permute-start.25 = (bf16[896,640]{1,0:T(8,128)(2,1)}, bf16[896,640]{1,0:T(8,128)(2,1)S(1)}, u32[]{:S(2)}, u32[]{:S(2)}) collective-permute-start(bf16[896,640]{1,0:T(8,128)(2,1)} %collective-permute-done.23.refs_0_), channel_id=1, source_target_pairs={{0,32},{32,0},{2,34},{34,2},{4,36},{36,4},{6,38},{38,6},{64,96},{9... | collective-permute-start | bytes 3440648 | tf_op jit(solution)/shard_map/ppermute | solution.py:64
  102.1 1.0 copy-start.14
  103.0 10.4 %collective-permute-start.26 = (bf16[2,4,2,2,64,128]{5,4,3,2,1,0:T(8,128)(2,1)S(1)}, bf16[2,4,2,2,64,128]{5,4,3,2,1,0:T(8,128)(2,1)S(1)}, u32[]{:S(2)}, u32[]{:S(2)}) collective-permute-start(bf16[2,4,2,2,64,128]{5,4,3,2,1,0:T(8,128)(2,1)S(1)} %pad_maximum_fusion.6), channel_id=1, source_target_pairs={{0,24},{32,40},{2,26},{34,42},{4,28},{36,44},{6,30},{38,46},{64,88... | collective-permute-start | bytes 1572872 | tf_op jit(solution)/shard_map/ppermute | solution.py:64
  104.6 12.1 %collective-permute-start.20 = (bf16[2,4,2,2,80,128]{5,4,3,2,1,0:T(8,128)(2,1)}, bf16[2,4,2,2,80,128]{5,4,3,2,1,0:T(8,128)(2,1)}, u32[]{:S(2)}, u32[]{:S(2)}) collective-permute-start(bf16[2,4,2,2,80,128]{5,4,3,2,1,0:T(8,128)(2,1)} %pad_maximum_fusion.5), channel_id=1, source_target_pairs={{0,6},{32,34},{2,4},{34,32},{4,2},{36,38},{6,0},{38,36},{64,70},{9... | collective-permute-start | bytes 1966088 | tf_op jit(solution)/shard_map/ppermute | solution.py:64
  119.5 5.1 %copy-start.6 = (bf16[896,640]{1,0:T(8,128)(2,1)}, bf16[896,640]{1,0:T(8,128)(2,1)S(1)}, u32[]{:S(2)}) copy-start(bf16[896,640]{1,0:T(8,128)(2,1)S(1)} %collective-permute-done.25.refs_1_) | copy-start | bytes 3440644
  119.5 1.6 %copy-start.15 = (bf16[2,256,896]{2,1,0:T(8,128)(2,1)S(1)}, bf16[2,256,896]{2,1,0:T(8,128)(2,1)}, u32[]{:S(2)}) copy-start(bf16[2,256,896]{2,1,0:T(8,128)(2,1)} %copy-done.14) | copy-start | bytes 2752516
  121.1 1.1 copy-start.20
  122.2 4.2 %copy-start.5 = (bf16[896,512]{1,0:T(8,128)(2,1)S(1)}, bf16[896,512]{1,0:T(8,128)(2,1)}, u32[]{:S(2)}) copy-start(bf16[896,512]{1,0:T(8,128)(2,1)} %copy-done.4) | copy-start | bytes 2752516
  122.2 4.2 %copy-start.10 = (bf16[2,256,896]{2,1,0:T(8,128)(2,1)S(1)}, bf16[2,256,896]{2,1,0:T(8,128)(2,1)}, u32[]{:S(2)}) copy-start(bf16[2,256,896]{2,1,0:T(8,128)(2,1)} %copy-done.8) | copy-start | bytes 2752516
  122.2 4.2 %copy-start.13 = (bf16[896,512]{1,0:T(8,128)(2,1)S(1)}, bf16[896,512]{1,0:T(8,128)(2,1)}, u32[]{:S(2)}) copy-start(bf16[896,512]{1,0:T(8,128)(2,1)} %copy-done.12) | copy-start | bytes 2752516
  122.2 4.2 %copy-start.16 = (bf16[2,256,896]{2,1,0:T(8,128)(2,1)S(1)}, bf16[2,256,896]{2,1,0:T(8,128)(2,1)}, u32[]{:S(2)}) copy-start(bf16[2,256,896]{2,1,0:T(8,128)(2,1)} %copy-done.14) | copy-start | bytes 2752516
  124.6 1.9 %copy-start.1 = (bf16[2,416,896]{2,1,0:T(8,128)(2,1)S(1)}, bf16[2,416,896]{2,1,0:T(8,128)(2,1)}, u32[]{:S(2)}) copy-start(bf16[2,416,896]{2,1,0:T(8,128)(2,1)} %copy-done) | copy-start | bytes 4472836
  124.6 2.4 %copy-start.3 = (bf16[2,416,896]{2,1,0:T(8,128)(2,1)S(1)}, bf16[2,416,896]{2,1,0:T(8,128)(2,1)}, u32[]{:S(2)}) copy-start(bf16[2,416,896]{2,1,0:T(8,128)(2,1)} %copy-done.2) | copy-start | bytes 4472836
  130.1 5.0 %copy-start.18 = (f32[256,640]{1,0:T(8,128)S(1)}, f32[256,640]{1,0:T(8,128)}, u32[]{:S(2)}) copy-start(f32[256,640]{1,0:T(8,128)} %copy-done.17) | copy-start | bytes 1966084
  135.0 11.7 %collective-permute-start.27 = (bf16[256,896]{1,0:T(8,128)(2,1)}, bf16[256,896]{1,0:T(8,128)(2,1)}, u32[]{:S(2)}, u32[]{:S(2)}) collective-permute-start(bf16[256,896]{1,0:T(8,128)(2,1)} %shard_map.100), channel_id=1, source_target_pairs={{0,64},{32,96},{2,66},{34,98},{4,68},{36,100},{6,70},{38,102},{64,... | collective-permute-start | bytes 1376264 | tf_op jit(solution)/shard_map/ppermute | solution.py:64
  135.1 1.3 copy-start.7
  136.4 1.2 copy-start.11

commit v7 on v5

--- a/solution.py
+++ b/solution.py
@@ -54,8 +54,8 @@
 
 FLIP = {(axis, turn): flip(axis, turn) for axis in "xz" for turn in (0, 1)}
 
-EARLY = 2 * D
-LATE = (2 + HEADS) * D
+KEPT = 2
+CUTS = (0, 2 * D, (4 + KEPT) * D, (4 + HEADS) * D)
 SLAB = WIDTH // 4
 PAIRED = ((0, 1, 2, 3), (0, 3, 1, 2))
 
@@ -88,6 +88,10 @@
     return tiles
 
 
+def cost(flops, moved):
+    return pl.CostEstimate(flops=flops, bytes_accessed=moved, transcendentals=0)
+
+
 def reorder(plain_ref, out_ref, last, count, out_rows):
     lane = lax.broadcasted_iota(jnp.int32, (count, 128), 1)
     for tile, runs in enumerate(feature_runs(last)):
@@ -113,7 +117,7 @@
         here = pl.ds(pl.multiple_of(step * rows, rows), rows)
         values = tokens_ref[here, :].astype(jnp.float32)
         factor = lax.rsqrt(jnp.mean(values * values, axis=-1, keepdims=True) + EPS)
-        plain_ref[...] = values * factor * gain_ref[...]
+        plain_ref[...] = values * factor * gain_ref[...].reshape(1, WIDTH)
         normed_ref[here, :] = plain_ref[...].astype(jnp.bfloat16)
         reorder(plain_ref, out_ref, "x", rows, here)
 
@@ -156,8 +160,9 @@
             pltpu.VMEM((64, WIDTH), jnp.float32),
             pltpu.VMEM((TOK, WIDTH), jnp.bfloat16),
         ],
-        compiler_params=pltpu.CompilerParams(vmem_limit_bytes=16 * 1024 * 1024),
-    )(facts, tokens, gain.reshape(1, WIDTH))
+        compiler_params=pltpu.CompilerParams(vmem_limit_bytes=10 * 1024 * 1024),
+        cost_estimate=cost(2 * SLOTS * TOK * WIDTH, 16 * TOK * WIDTH),
+    )(facts, tokens, gain)
 
 
 BLOCK = 256
@@ -165,9 +170,11 @@
 LINES = HEADS * TOK
 
 
-def attend_body(wide, info_ref, count_ref, part_ref, far_k_ref, far_v_ref, *rest):
-    out_ref, query_ref, keys_ref, values_ref, bias_ref, score_ref, top_ref, sum_ref, mix_ref = rest
+def attend_body(wide, info_ref, count_ref, part_ref, more_ref, *rest):
+    far_k_refs, far_v_refs, rest = rest[:2], rest[2:4], rest[4:]
+    out_ref, query_ref, keys_ref, values_ref, bias_ref, top_ref, sum_ref, mix_ref = rest
     span, valid, column, which = info_ref[0], info_ref[1], info_ref[2], info_ref[3]
+    own = slice(0, TOK) if wide else slice(TOK, 2 * TOK)
 
     lane = lax.broadcasted_iota(jnp.int32, (1, ROOM), 1)
     bias_ref[...] = jnp.full((1, ROOM), FILL, jnp.float32)
@@ -176,8 +183,16 @@
         place_k, place_v = info_ref[4 + i], info_ref[4 + SPANS + i]
         count = count_ref[place_k * 2 + which]
         here = pl.ds(pl.multiple_of(at, 16), SLOTS)
-        keys_ref[here, :] = far_k_ref[place_k, which, :SLOTS, :]
-        values_ref[here, :] = far_v_ref[place_v, which]
+        for j in range(2):
+
+            @pl.when(place_k // (SPANS // 2) == j)
+            def _():
+                keys_ref[here, :] = far_k_refs[j][place_k % (SPANS // 2), which, :SLOTS, :]
+
+            @pl.when(place_v // (SPANS // 2) == j)
+            def _():
+                values_ref[here, :] = far_v_refs[j][place_v % (SPANS // 2), which]
+
         bias_ref[...] = jnp.where((lane >= at) & (lane < at + count), 0.0, bias_ref[...])
         return at + ((count + 15) // 16) * 16
 
@@ -199,31 +214,31 @@
     row = lax.broadcasted_iota(jnp.int32, (TOK, TOK), 0)
     col = lax.broadcasted_iota(jnp.int32, (TOK, TOK), 1)
     near_bias = jnp.where((col <= row) & (col < valid), 0.0, FILL)
+
+    def near(lines):
+        scores = lax.dot_general(
+            query_ref[lines, :], part_ref[own, :D], contract, preferred_element_type=jnp.float32
+        )
+        return scores + near_bias
+
     for head in range(HEADS):
         here = slice(head * TOK, (head + 1) * TOK)
-        query = part_ref[:, (2 + head) * D : (3 + head) * D]
+        if head < KEPT:
+            query = part_ref[own, (2 + head) * D : (3 + head) * D]
+        else:
+            query = more_ref[own, (head - KEPT) * D : (head - KEPT + 1) * D]
         query_ref[here, :] = query
-        near = lax.dot_general(
-            query, part_ref[:, :D], contract, preferred_element_type=jnp.float32
-        )
-        near = near + near_bias
-        score_ref[here, ROOM:] = near
-        top_ref[here, :] = fold(jnp.maximum, near)
+        top_ref[here, :] = fold(jnp.maximum, near(here))
+
+    def far(here):
+        scores = lax.dot_general(
+            query_ref[...], keys_ref[here, :], contract, preferred_element_type=jnp.float32
+        )
+        return scores + bias_ref[:, here]
 
     def score(i, carry):
         here = pl.ds(pl.multiple_of(i * BLOCK, BLOCK), BLOCK)
-        bias = bias_ref[:, here]
-        for head in range(HEADS):
-            lines = slice(head * TOK, (head + 1) * TOK)
-            far = lax.dot_general(
-                query_ref[lines, :],
-                keys_ref[here, :],
-                contract,
-                preferred_element_type=jnp.float32,
-            )
-            far = far + bias
-            score_ref[lines, here] = far
-            top_ref[lines, :] = jnp.maximum(top_ref[lines, :], fold(jnp.maximum, far))
+        top_ref[...] = jnp.maximum(top_ref[...], fold(jnp.maximum, far(here)))
         return carry
 
     lax.fori_loop(0, blocks, score, jnp.int32(0))
@@ -232,25 +247,22 @@
         lines = slice(head * TOK, (head + 1) * TOK)
         top = jnp.max(top_ref[lines, :], axis=1, keepdims=True)
         top_ref[lines, :] = jnp.broadcast_to(top, (TOK, D))
-        weight = jnp.exp2((score_ref[lines, ROOM:] - top) * power)
+        weight = jnp.exp2((near(lines) - top) * power)
         sum_ref[lines, :] = fold(jnp.add, weight)
         mix_ref[lines, :] = jnp.dot(
             weight.astype(jnp.bfloat16),
-            part_ref[:, D : 2 * D],
+            part_ref[own, D : 2 * D],
             preferred_element_type=jnp.float32,
         )
 
     def mix(i, carry):
         here = pl.ds(pl.multiple_of(i * BLOCK, BLOCK), BLOCK)
-        for head in range(HEADS):
-            lines = slice(head * TOK, (head + 1) * TOK)
-            top = top_ref[lines, :]
-            top = jnp.concatenate([top] * (BLOCK // D), axis=1)
-            weight = jnp.exp2((score_ref[lines, here] - top) * power)
-            sum_ref[lines, :] = sum_ref[lines, :] + fold(jnp.add, weight)
-            mix_ref[lines, :] = mix_ref[lines, :] + jnp.dot(
-                weight.astype(jnp.bfloat16), values_ref[here, :], preferred_element_type=jnp.float32
-            )
+        top = jnp.concatenate([top_ref[...]] * (BLOCK // D), axis=1)
+        weight = jnp.exp2((far(here) - top) * power)
+        sum_ref[...] += fold(jnp.add, weight)
+        mix_ref[...] += jnp.dot(
+            weight.astype(jnp.bfloat16), values_ref[here, :], preferred_element_type=jnp.float32
+        )
         return carry
 
     lax.fori_loop(0, blocks, mix, jnp.int32(0))
@@ -266,52 +278,109 @@
             out_ref[:, head * D : (head + 1) * D] = result
 
 
-def attend(wide, info, counts, part, far_k, far_v):
+def attend(wide, info, counts, part, more, far):
     columns = 2 * HEADS * D if wide else HEADS * D
     smem, vmem = pl.BlockSpec(memory_space=pltpu.SMEM), pl.BlockSpec(memory_space=pltpu.VMEM)
     return pl.pallas_call(
         functools.partial(attend_body, wide),
         out_shape=jax.ShapeDtypeStruct((TOK, columns), jnp.bfloat16),
-        in_specs=[smem, smem, vmem, vmem, vmem],
+        in_specs=[smem, smem] + [vmem] * 6,
         out_specs=vmem,
         scratch_shapes=[
             pltpu.VMEM((LINES, D), jnp.bfloat16),
             pltpu.VMEM((ROOM, D), jnp.bfloat16),
             pltpu.VMEM((ROOM, D), jnp.bfloat16),
             pltpu.VMEM((1, ROOM), jnp.float32),
-            pltpu.VMEM((LINES, ROOM + TOK), jnp.float32),
             pltpu.VMEM((LINES, D), jnp.float32),
             pltpu.VMEM((LINES, D), jnp.float32),
             pltpu.VMEM((LINES, D), jnp.float32),
         ],
-        compiler_params=pltpu.CompilerParams(vmem_limit_bytes=28 * 1024 * 1024),
-    )(info, counts, part, far_k, far_v)
-
-
-def project_body(count, slab_ref, x_ref, *refs):
-    weights, total_refs, out_ref = refs[:count], refs[count:-1], refs[-1]
+        compiler_params=pltpu.CompilerParams(vmem_limit_bytes=14 * 1024 * 1024),
+        cost_estimate=cost(4 * LINES * D * 1280, 8 << 20),
+    )(info, counts, part, more, *far)
+
+
+def project_body(slab_ref, x_ref, *refs):
+    weights, out_ref = refs[:-1], refs[-1]
     rows, columns = out_ref.shape
     for first in range(0, columns, 256):
         here = slice(first, min(first + 256, columns))
-        out = total_refs[0][:, here] if total_refs else None
-        for i in range(count):
-            x = x_ref[slab_ref[i], :rows, :]
-            term = jnp.dot(x, weights[i][:, here], preferred_element_type=jnp.float32)
-            out = term if out is None else out + term
+        out, slab = None, 0
+        for w in weights:
+            for start in range(0, w.shape[0], SLAB):
+                x = x_ref[slab_ref[slab], :rows, :]
+                term = jnp.dot(
+                    x, w[start : start + SLAB, here], preferred_element_type=jnp.float32
+                )
+                out = term if out is None else out + term
+                slab += 1
         out_ref[:, here] = out.astype(out_ref.dtype)
 
 
-def project(slabs, x, weights, total=None, last=False, rows=TOK):
+def project(slabs, x, weights):
     smem, vmem = pl.BlockSpec(memory_space=pltpu.SMEM), pl.BlockSpec(memory_space=pltpu.VMEM)
-    totals = () if total is None else (total,)
-    dtype = jnp.bfloat16 if last else jnp.float32
+    rows, columns = x.shape[1], weights[0].shape[1]
     return pl.pallas_call(
-        functools.partial(project_body, len(weights)),
-        out_shape=jax.ShapeDtypeStruct((rows, weights[0].shape[1]), dtype),
-        in_specs=[smem] + [vmem] * (1 + len(weights) + len(totals)),
+        project_body,
+        out_shape=jax.ShapeDtypeStruct((rows, columns), jnp.bfloat16),
+        in_specs=[smem] + [vmem] * (1 + len(weights)),
         out_specs=vmem,
-        compiler_params=pltpu.CompilerParams(vmem_limit_bytes=16 * 1024 * 1024),
-    )(jnp.stack(slabs).astype(jnp.int32), x, *weights, *totals)
+        compiler_params=pltpu.CompilerParams(vmem_limit_bytes=10 * 1024 * 1024),
+        cost_estimate=cost(2 * rows * WIDTH * columns, 2 * WIDTH * (rows + columns)),
+    )(jnp.stack(slabs).astype(jnp.int32), x, *weights)
+
+
+def span_body(crossed, info_ref, own_near, own_far, mate_near, mate_far, *refs):
+    pieces, out_ref, full_ref = [(w, 0) for w in refs[:4]], refs[4], refs[5]
+    if crossed:
+        core = info_ref[0]
+        block = 4 * ROWS
+        for i, (piece, start) in enumerate(pieces):
+            theirs, is_far = divmod(i, 2)
+            side = core if theirs == 0 else 1 - core
+            pair_x, pair_z = info_ref[1 + theirs], info_ref[3 + theirs]
+            if is_far:
+                pair_z = 1 - pair_z
+            for t in range(2):
+                split = jnp.where(pair_z == 0, PAIRED[1][t], PAIRED[1][2 + t])
+                z = jnp.where(side == 0, 2 * pair_z + t, split)
+                for x in range(4):
+                    at = jnp.where(side == 0, x, PAIRED[1].index(x))
+                    slab = jnp.where(at // 2 == pair_x, 0, 2) + theirs
+                    line = slab * SLAB + ((at % 2) * 4 + z) * block
+                    source = start + (t * 4 + x) * block
+                    full_ref[pl.ds(pl.multiple_of(line, 16), block), :] = piece[
+                        source : source + block, :
+                    ]
+        pieces = [(full_ref, slab * SLAB) for slab in range(4)]
+    else:
+        pieces = [pieces[0], pieces[2], pieces[1], pieces[3]]
+    columns = out_ref.shape[1]
+    for first in range(0, columns, 256):
+        here = slice(first, min(first + 256, columns))
+        for j, (near_ref, far_ref) in enumerate(((own_near, own_far), (mate_near, mate_far))):
+            out = None
+            for slab, (piece, start) in enumerate(pieces):
+                x = (near_ref if slab < 2 else far_ref)[slab % 2, :TOK, :]
+                w = piece[start : start + SLAB, here]
+                term = jnp.dot(x, w, preferred_element_type=jnp.float32)
+                out = term if out is None else out + term
+            out_ref[j * TOK : (j + 1) * TOK, here] = out.astype(jnp.bfloat16)
+
+
+def project_spans(crossed, info, tokens, pieces):
+    smem, vmem = pl.BlockSpec(memory_space=pltpu.SMEM), pl.BlockSpec(memory_space=pltpu.VMEM)
+    columns = pieces[0].shape[1]
+    lines = WIDTH if crossed else 16
+    return pl.pallas_call(
+        functools.partial(span_body, crossed),
+        out_shape=jax.ShapeDtypeStruct((2 * TOK, columns), jnp.bfloat16),
+        in_specs=[smem] + [vmem] * 8,
+        out_specs=vmem,
+        scratch_shapes=[pltpu.VMEM((lines, columns), jnp.bfloat16)],
+        compiler_params=pltpu.CompilerParams(vmem_limit_bytes=10 * 1024 * 1024),
+        cost_estimate=cost(4 * TOK * WIDTH * columns, 2 * WIDTH * (2 * TOK + columns)),
+    )(info, *tokens, *pieces)
 
 
 def after(value, other):
@@ -319,11 +388,22 @@
 
 
 def halves_body(head_ref, *refs):
-    mine_ref, other_ref = refs[-2:]
+    count = (len(refs) - 3) // 2
+    sources, (mine_ref, other_ref), held, sem = (
+        refs[:count],
+        refs[count : count + 2],
+        refs[count + 2 : -1],
+        refs[-1],
+    )
+    copies = [pltpu.make_async_copy(a, b, sem.at[i]) for i, (a, b) in enumerate(zip(sources, held))]
+    for c in copies:
+        c.start()
+    for c in copies:
+        c.wait()
 
     def copy(mine):
         at = 0
-        for ref in refs[:-2]:
+        for ref in held:
             size = ref.shape[1] // 2
             mine_ref[:, at : at + size] = ref[:, mine * size : (mine + 1) * size]
             other_ref[:, at : at + size] = ref[:, (1 - mine) * size : (2 - mine) * size]
@@ -337,10 +417,12 @@
     smem, vmem = pl.BlockSpec(memory_space=pltpu.SMEM), pl.BlockSpec(memory_space=pltpu.VMEM)
     return pl.pallas_call(
         halves_body,
-        out_shape=[jax.ShapeDtypeStruct((ROWS, EARLY + LATE), jnp.bfloat16)] * 2,
-        in_specs=[smem] + [vmem] * len(weights),
+        out_shape=[jax.ShapeDtypeStruct((ROWS, CUTS[-1]), jnp.bfloat16)] * 2,
+        in_specs=[smem] + [pl.BlockSpec(memory_space=pltpu.HBM)] * len(weights),
         out_specs=[vmem, vmem],
-        compiler_params=pltpu.CompilerParams(vmem_limit_bytes=4 * 1024 * 1024),
+        scratch_shapes=[pltpu.VMEM(w.shape, w.dtype) for w in weights]
+        + [pltpu.SemaphoreType.DMA((len(weights),))],
+        compiler_params=pltpu.CompilerParams(vmem_limit_bytes=60 * 1024 * 1024),
     )(head.reshape(1), *weights)
 
 
@@ -403,25 +485,37 @@
     def blank(shape, after):
         return lax.optimization_barrier((jnp.zeros(shape, jnp.bfloat16), after))[0]
 
-    def second(block, axis):
+    def joined(pieces, axis):
         p = pos[axis]
-        joined = blank((4,) + block.shape, block)
-        joined = in_place(double(block, axis), (p, p ^ near, p ^ far, p ^ 2), joined)
-        return joined.reshape(-1, block.shape[-1])
-
-    early = second(rows[:, :EARLY], "x")
-    late = second(rows[:, EARLY:], "z")
-
-    early = order(pair_of("z", core)[1], early, send(early, FLIP["z", 0]))
-    late = order(pair_of("x", core)[1], late, send(late, FLIP["x", 0]))
-    early_far = send(early, FLIP["z", 1])
-    gathered = jnp.concatenate([early, early_far], 0)
-    swapped = send(gathered, SWAP)
+        out = blank((4,) + pieces[0].shape, pieces[0])
+        out = in_place(pieces, (p, p ^ near, p ^ far, p ^ 2), out)
+        return out.reshape(-1, out.shape[-1])
+
+    early, late = rows[:, : CUTS[2]], rows[:, CUTS[2] :]
+    pair_e = jnp.stack([early, send(early, FLIP["x", 0])])
+    late_1 = send(late, FLIP["z", 0])
+    pair_l = jnp.stack([late, late_1])
+    early = joined(jnp.concatenate([pair_e, send(pair_e, FLIP["x", 1])]), "x")
+    late_2 = send(pair_l, FLIP["z", 1])
+    late = joined(jnp.concatenate([pair_l, late_2]), "z")
+
+    early, cross = after(early[:, : CUTS[1]], late_1), early[:, CUTS[1] :]
+    z_second, x_second = pair_of("z", core)[1], pair_of("x", core)[1]
+    early = order(z_second, early, send(early, FLIP["z", 0]))
+    cross_near = send(cross, FLIP["z", 0])
+    late_near = send(late, FLIP["x", 0])
+    early_far = send(after(early, late_2), FLIP["z", 1])
+    swapped = send(jnp.concatenate([early, early_far], 0), SWAP)
+    cross, late = after((cross, late), swapped)
+    cross = order(z_second, cross, cross_near)
+    late = order(x_second, late, late_near)
+    cross_far = send(cross, FLIP["z", 1])
+    late_far = send(late, FLIP["x", 1])
     slab_near, slab_far = slabs("z")
     where_m = (slab_near[0], slab_far[0], slab_near[1], slab_far[1])
-    pieces_m = (early, early_far, swapped[:SLAB], swapped[SLAB:])
+    pieces_m = (early, early_far, swapped)
     both_pooled = jnp.concatenate([pooled_of(own_near), pooled_of(mate_near)], 1)
-    beacon = project(where_m, both_pooled, pieces_m, last=True, rows=2 * SLOTS)
+    beacon = project(where_m, both_pooled, pieces_m)
     beacon = beacon.reshape(2, SLOTS, 2 * D)
     counts = jnp.stack([count, mate_count]).astype(jnp.bfloat16)
     flags = jnp.broadcast_to(counts[:, None, None], (2, 16, D))
@@ -429,22 +523,18 @@
     block_v = beacon[..., D:]
     block = jnp.concatenate([block_k, block_v], 1)
     block = order(low, block[:1], block[1:])
-    late_far = send(after(late, block), FLIP["x", 1])
     block = jnp.stack([block, send(block, ACROSS)])
     half_k = double(block[:, :, : SLOTS + 16], "x")
     half_v = double(block[:, :, SLOTS + 16 :], "z")
-    zero, one = jnp.int32(0), jnp.int32(1)
-    near_w = (late, send(late, SWAP))
-    own = project((zero, one), own_near, near_w)
-    half_k, half_v = after((half_k, half_v), own)
+    pieces = after((cross, cross_far, late, late_far), (half_k, half_v))
+    others = [send(piece, SWAP) for piece in pieces]
     pair_k = jnp.stack([half_k, send(half_k, FLIP["z", 0])])
     pair_v = jnp.stack([half_v, send(half_v, FLIP["x", 0])])
-    mate = project((zero, one), mate_near, near_w)
-    pair_k, pair_v = after((pair_k, pair_v), (mate, mate_far))
-    every_k = jnp.concatenate([pair_k, send(pair_k, FLIP["z", 1])])
-    every_v = jnp.concatenate([pair_v, send(pair_v, FLIP["x", 1])])
-    every_k = every_k.reshape(SPANS, 2, SLOTS + 16, D)
-    every_v = every_v.reshape(SPANS, 2, SLOTS, D)
+    pair_k, pair_v = after((pair_k, pair_v), (others, mate_far))
+    every_k = [pair_k, send(pair_k, FLIP["z", 1])]
+    every_v = [pair_v, send(pair_v, FLIP["x", 1])]
+    every_k = [k.reshape(SPANS // 2, 2, SLOTS + 16, D) for k in every_k]
+    every_v = [v.reshape(SPANS // 2, 2, SLOTS, D) for v in every_v]
 
     owner = jnp.arange(SPANS, dtype=jnp.int32)
 
@@ -456,14 +546,13 @@
     code_h = (owner ^ span) % 2
     at_k = (code_z * 4 + code_x) * 2 + code_h
     at_v = (code_x * 4 + code_z) * 2 + code_h
-    live = every_k[:, :, SLOTS, 0].astype(jnp.int32).reshape(2 * SPANS)
-
-    own = project((zero,), own_far, (late_far,), own)
-    mate = project((zero,), mate_far, (late_far,), mate)
-    own, mate = lax.optimization_barrier((own, mate))
-    last_w = (send(late_far, SWAP),)
-    mate = project((one,), mate_far, last_w, mate, last=True)
-    own = project((one,), own_far, last_w, own, last=True)
+    live = jnp.concatenate([k[:, :, SLOTS, 0].reshape(SPANS) for k in every_k]).astype(jnp.int32)
+
+    pairs = [pair_of(axis, side)[0] for axis in "xz" for side in (core, 1 - core)]
+    info = jnp.stack([core, *pairs]).astype(jnp.int32)
+    both = (own_near, own_far, mate_near, mate_far)
+    part = project_spans(True, info, both, (cross, cross_far, others[0], others[1]))
+    more = project_spans(False, info, both, (late, late_far, others[2], others[3]))
 
     def attention(which, valid, wide):
         info = jnp.concatenate(
@@ -473,9 +562,9 @@
             wide,
             info,
             live,
-            mate if which else own,
-            every_k,
-            every_v,
+            part,
+            more,
+            every_k + every_v,
         )
 
     away = send(attention(1, mate_valid, False), MATE)

time: 163 us -> 176 us (1.080)
  local copies, waits for them, and re-layouts: 18.8 us -> 36.1 us
  waiting for transfers between devices: 69.2 us -> 63.3 us
  starting transfers between devices: 27.2 us -> 31.6 us
    unnamed x34 -> x66, local copies, waits for them, and re-layouts: 11 us -> 25.3 us
    pallas_call x8 -> x4, Pallas kernels: 15.8 us -> 9.59 us  [the longest x2 6.93 us: project_spans(): pl.pallas_call(functools.partial(span_body, crossed), out_shape=jax.Shape...]
    ppermute x25 -> x29, waiting for transfers between devices: 69.2 us -> 63.3 us  [send(): return lax.ppermute(value, AXES, pairs)]
    pallas_call x2, Pallas kernels: 12.8 us -> 18.5 us  [attend(): pl.pallas_call(functools.partial(attend_body, wide), out_shape=jax.ShapeD...]
    ppermute x25 -> x29, starting transfers between devices: 27.2 us -> 31.6 us  [send(): return lax.ppermute(value, AXES, pairs)]
    select_n x6 -> x7, other arithmetic: 1.21 us -> 4.22 us  [order(): jnp.where(first == 0, jnp.concatenate([one, two], 0), jnp.concatenate([tw...]
    concatenate x5 -> x1, other arithmetic: 2.81 us -> 0.06 us  [on_device(): swapped = send(jnp.concatenate([early, early_far], 0), SWAP)]
    slice x1 -> x4, local copies, waits for them, and re-layouts: 0.06 us -> 1.99 us  [the longest x2 1.95 us: on_device(): k[:, :, SLOTS, 0].reshape(SPANS)]
  transfers between devices with their start and end apart: 25 -> 29, of which waited for: 15 -> 14; matrix products, arithmetic and copies ran while one was open for 8% -> 9% of each run, Pallas kernels for 16% -> 14%
where the time goes in v7:
time: 176 us; the launch traced here: 175 us
  waiting for transfers between devices  63.3 us (36%)
  local copies, waits for them, and re-layouts  36.1 us (21%)
  Pallas kernels  33.8 us (19%)
  starting transfers between devices  31.6 us (18%)
  other arithmetic  7.33 us (4%)
  between operations  2.55 us (1%)
    ppermute x29, waiting for transfers between devices, send(): return lax.ppermute(value, AXES, pairs)  63.3 us
    ppermute x29, starting transfers between devices, send(): return lax.ppermute(value, AXES, pairs)  31.6 us
    unnamed x66, local copies, waits for them, and re-layouts  25.3 us
    pallas_call x2, Pallas kernels, attend(): pl.pallas_call(functools.partial(attend_body, wide), out_shape=jax.ShapeD...  18.5 us
    pallas_call x2, Pallas kernels, project_spans(): pl.pallas_call(functools.partial(span_body, crossed), out_shape=jax.Shape...  6.93 us
    pallas_call x1, Pallas kernels, norm_rows(): pl.pallas_call(norm_body, out_shape=[jax.ShapeDtypeStruct((2, TOK + 2 * (...  5.72 us
    select_n x7, other arithmetic, order(): jnp.where(first == 0, jnp.concatenate([one, two], 0), jnp.concatenate([tw...  4.22 us
  transfers between devices with their start and end apart: 29, of which 14 were waited for; matrix products, arithmetic and copies ran while one was open for 9% of the time, Pallas kernels for 14%

profile of v7, /device:TPU:6, one launch (start us, length us, event | category | flops | bytes accessed | tf_op | source)
XLA Modules:
  0.0 174.6 jit_solution(2963164348309530535)
XLA Ops:
  0.0 1.7 shard_map.92
  1.7 1.7 collective-permute-start.1
  3.4 3.2 %collective-permute-done.1 = bf16[28,1408]{1,0:T(8,128)(2,1)S(1)} collective-permute-done((bf16[28,1408]{1,0:T(8,128)(2,1)}, bf16[28,1408]{1,0:T(8,128)(2,1)S(1)}, u32[]{:S(2)}, u32[]{:S(2)}) %collective-permute-start.1) | collective-permute-done | bytes 78880 | tf_op jit(solution)/shard_map/ppermute | solution.py:64
  6.5 1.0 maximum_select_fusion.4
  7.6 3.1 %collective-permute-start.2 = (bf16[56,1408]{1,0:T(8,128)(2,1)S(1)}, bf16[56,1408]{1,0:T(8,128)(2,1)}, u32[]{:S(2)}, u32[]{:S(2)}) collective-permute-start(bf16[56,1408]{1,0:T(8,128)(2,1)S(1)} %maximum_select_fusion.4), channel_id=1, source_target_pairs={{0,65},{32,97},{2,67},{34,99},{4,69},{36,101},{6,71},{38,103},{64,... | collective-permute-start | bytes 473096 | tf_op jit(solution)/shard_map/ppermute | solution.py:64
  12.1 1.5 copy-done.14
  14.4 5.7 %shard_map.91 = (bf16[2,416,896]{2,1,0:T(8,128)(2,1)S(1)}, bf16[2,256,896]{2,1,0:T(8,128)(2,1)S(1)}) custom-call(s32[7]{0:T(128)S(1)} %stack.148.fact_ref, bf16[256,3584]{1,0:T(8,128)(2,1)S(1)} %bitcast.71, f32[3584]{0:T(1024)S(1)} %copy-done.27), custom_call_target="tpu_custom_call" | custom-call | flops 117440512 | bytes 14680064 | tf_op jit(solution)/shard_map/pallas_call | solution.py:149
  20.1 0.9 copy-done.2
  21.1 1.1 maximum_select_fusion.3
  22.2 0.9 collective-permute-start.3
  23.2 2.0 %collective-permute-start.5 = (bf16[112,640]{1,0:T(8,128)(2,1)S(1)}, bf16[112,640]{1,0:T(8,128)(2,1)S(1)}, u32[]{:S(2)}, u32[]{:S(2)}) collective-permute-start(bf16[112,640]{1,0:T(8,128)(2,1)S(1)} %get-tuple-element.42), channel_id=1, source_target_pairs={{0,2},{32,38},{2,0},{34,36},{4,6},{36,34},{6,4},{38,32},{64,66},{9... | collective-permute-start | bytes 430088 | tf_op jit(solution)/shard_map/ppermute | solution.py:64
  25.2 2.6 %collective-permute-done.3 = bf16[112,768]{1,0:T(8,128)(2,1)S(1)} collective-permute-done((bf16[112,768]{1,0:T(8,128)(2,1)S(1)}, bf16[112,768]{1,0:T(8,128)(2,1)S(1)}, u32[]{:S(2)}, u32[]{:S(2)}) %collective-permute-start.3) | collective-permute-done | bytes 172064 | tf_op jit(solution)/shard_map/ppermute | solution.py:64
  28.4 7.9 %collective-permute-done.4 = bf16[2,112,768]{2,1,0:T(8,128)(2,1)S(1)} collective-permute-done((bf16[2,112,768]{2,1,0:T(8,128)(2,1)S(1)}, bf16[2,112,768]{2,1,0:T(8,128)(2,1)S(1)}, u32[]{:S(2)}, u32[]{:S(2)}) %collective-permute-start.4) | collective-permute-done | bytes 344096 | tf_op jit(solution)/shard_map/ppermute | solution.py:64
  37.3 2.0 %collective-permute-start.6 = (bf16[448,256]{1,0:T(8,128)(2,1)S(1)}, bf16[448,256]{1,0:T(8,128)(2,1)}, u32[]{:S(2)}, u32[]{:S(2)}) collective-permute-start(bf16[448,256]{1,0:T(8,128)(2,1)S(1)} %slice.108), channel_id=1, source_target_pairs={{0,2},{32,38},{2,0},{34,36},{4,6},{36,34},{6,4},{38,32},{64,66},{9... | collective-permute-start | bytes 688136 | tf_op jit(solution)/shard_map/ppermute | solution.py:64
  40.0 2.7 %collective-permute-start.7 = (bf16[2,112,640]{2,1,0:T(8,128)(2,1)}, bf16[2,112,640]{2,1,0:T(8,128)(2,1)}, u32[]{:S(2)}, u32[]{:S(2)}) collective-permute-start(bf16[2,112,640]{2,1,0:T(8,128)(2,1)} %pad_maximum_fusion.6), channel_id=1, source_target_pairs={{0,6},{32,34},{2,4},{34,32},{4,2},{36,38},{6,0},{38,36},{64,70},{9... | collective-permute-start | bytes 860168 | tf_op jit(solution)/shard_map/ppermute | solution.py:64
  43.6 1.8 %slice.102 = bf16[4,64,896]{2,1,0:T(8,128)(2,1)} slice(bf16[4,80,896]{2,1,0:T(8,128)(2,1)} %bitcast.77), slice={[0:4], [0:64], [0:896]} | slice | bytes 917504 | tf_op jit(solution)/shard_map/slice | solution.py:481
  45.9 1.2 maximum_select_fusion.2.refs_0_
  47.1 1.1 collective-permute-done.7
  48.2 2.7 %collective-permute-start.8 = (bf16[896,256]{1,0:T(8,128)(2,1)S(1)}, bf16[896,256]{1,0:T(8,128)(2,1)S(1)}, u32[]{:S(2)}, u32[]{:S(2)}) collective-permute-start(bf16[896,256]{1,0:T(8,128)(2,1)S(1)} %maximum_select_fusion.2.refs_0_), channel_id=1, source_target_pairs={{0,6},{32,34},{2,4},{34,32},{4,2},{36,38},{6,0},{38,36},{64,70},{9... | collective-permute-start | bytes 1376264 | tf_op jit(solution)/shard_map/ppermute | solution.py:64
  51.0 6.9 %collective-permute-done.8.refs_1_ = bf16[896,256]{1,0:T(8,128)(2,1)S(1)} collective-permute-done((bf16[896,256]{1,0:T(8,128)(2,1)S(1)}, bf16[896,256]{1,0:T(8,128)(2,1)S(1)}, u32[]{:S(2)}, u32[]{:S(2)}) %collective-permute-start.8) | collective-permute-done | bytes 458784 | tf_op jit(solution)/shard_map/ppermute | solution.py:64
  58.1 1.0 slice_dynamic-update-slice_fusion.3
  59.0 0.9 slice_dynamic-update-slice_fusion.2
  61.7 8.0 %collective-permute-done.19 = bf16[448,640]{1,0:T(8,128)(2,1)S(1)} collective-permute-done((bf16[448,640]{1,0:T(8,128)(2,1)S(1)}, bf16[448,640]{1,0:T(8,128)(2,1)S(1)}, u32[]{:S(2)}, u32[]{:S(2)}) %collective-permute-start.19) | collective-permute-done | bytes 573472 | tf_op jit(solution)/shard_map/ppermute | solution.py:64
  71.2 2.7 %collective-permute-start.18 = (bf16[896,512]{1,0:T(8,128)(2,1)S(1)}, bf16[896,512]{1,0:T(8,128)(2,1)S(1)}, u32[]{:S(2)}, u32[]{:S(2)}) collective-permute-start(bf16[896,512]{1,0:T(8,128)(2,1)S(1)} %maximum_select_fusion.1.refs_0_), channel_id=1, source_target_pairs={{0,6},{32,34},{2,4},{34,32},{4,2},{36,38},{6,0},{38,36},{64,70},{9... | collective-permute-start | bytes 2752520 | tf_op jit(solution)/shard_map/ppermute | solution.py:64
  73.9 1.0 shard_map.93
  75.1 1.1 collective-permute-start.10
  76.3 4.4 %collective-permute-done.10 = bf16[2,144,128]{2,1,0:T(8,128)(2,1)S(1)} collective-permute-done((bf16[2,144,128]{2,1,0:T(8,128)(2,1)S(1)}, bf16[2,144,128]{2,1,0:T(8,128)(2,1)S(1)}, u32[]{:S(2)}, u32[]{:S(2)}) %collective-permute-start.10) | collective-permute-done | bytes 73760 | tf_op jit(solution)/shard_map/ppermute | solution.py:64
  80.9 5.3 %collective-permute-done.11 = bf16[2,2,80,128]{3,2,1,0:T(8,128)(2,1)S(1)} collective-permute-done((bf16[2,2,80,128]{3,2,1,0:T(8,128)(2,1)S(1)}, bf16[2,2,80,128]{3,2,1,0:T(8,128)(2,1)S(1)}, u32[]{:S(2)}, u32[]{:S(2)}) %collective-permute-start.11) | collective-permute-done | bytes 81952 | tf_op jit(solution)/shard_map/ppermute | solution.py:64
  86.2 1.9 %collective-permute-start.12 = (bf16[2,2,2,80,128]{4,3,2,1,0:T(8,128)(2,1)S(1)}, bf16[2,2,2,80,128]{4,3,2,1,0:T(8,128)(2,1)S(1)}, u32[]{:S(2)}, u32[]{:S(2)}) collective-permute-start(bf16[2,2,2,80,128]{4,3,2,1,0:T(8,128)(2,1)S(1)} %pad_maximum_fusion.8), channel_id=1, source_target_pairs={{0,24},{32,40},{2,26},{34,42},{4,28},{36,44},{6,30},{38,46},{64,88... | collective-permute-start | bytes 491528 | tf_op jit(solution)/shard_map/ppermute | solution.py:64
  88.2 1.6 collective-permute-start.15
  89.8 3.1 %collective-permute-done.12 = bf16[2,2,2,80,128]{4,3,2,1,0:T(8,128)(2,1)S(1)} collective-permute-done((bf16[2,2,2,80,128]{4,3,2,1,0:T(8,128)(2,1)S(1)}, bf16[2,2,2,80,128]{4,3,2,1,0:T(8,128)(2,1)S(1)}, u32[]{:S(2)}, u32[]{:S(2)}) %collective-permute-start.12) | collective-permute-done | bytes 163872 | tf_op jit(solution)/shard_map/ppermute | solution.py:64
  92.9 1.2 collective-permute-start.13
  94.1 1.2 collective-permute-done.15
  96.0 1.1 collective-permute-start.25
  97.1 4.6 %collective-permute-done.16 = bf16[4,2,2,64,128]{4,3,2,1,0:T(8,128)(2,1)S(1)} collective-permute-done((bf16[4,2,2,64,128]{4,3,2,1,0:T(8,128)(2,1)S(1)}, bf16[4,2,2,64,128]{4,3,2,1,0:T(8,128)(2,1)S(1)}, u32[]{:S(2)}, u32[]{:S(2)}) %collective-permute-start.16) | collective-permute-done | bytes 262176 | tf_op jit(solution)/shard_map/ppermute | solution.py:64
  103.1 0.9 pad_maximum_fusion.2
  104.0 14.3 %collective-permute-done.25.mate_far = bf16[2,256,896]{2,1,0:T(8,128)(2,1)S(1)} collective-permute-done((bf16[2,256,896]{2,1,0:T(8,128)(2,1)S(1)}, bf16[2,256,896]{2,1,0:T(8,128)(2,1)S(1)}, u32[]{:S(2)}, u32[]{:S(2)}) %collective-permute-start.25) | collective-permute-done | bytes 917536 | tf_op jit(solution)/shard_map/ppermute | solution.py:64
  118.3 0.9 copy-done.6
  119.3 1.0 copy-done.23
  120.3 0.9 copy-done.25
  121.2 1.0 copy-done.17
  122.2 1.0 copy-done.19
  123.3 1.8 %collective-permute-start.26 = (bf16[2,4,2,2,80,128]{5,4,3,2,1,0:T(8,128)(2,1)}, bf16[2,4,2,2,80,128]{5,4,3,2,1,0:T(8,128)(2,1)}, u32[]{:S(2)}, u32[]{:S(2)}) collective-permute-start(bf16[2,4,2,2,80,128]{5,4,3,2,1,0:T(8,128)(2,1)} %pad_maximum_fusion.2), channel_id=1, source_target_pairs={{0,6},{32,34},{2,4},{34,32},{4,2},{36,38},{6,0},{38,36},{64,70},{9... | collective-permute-start | bytes 1966088 | tf_op jit(solution)/shard_map/ppermute | solution.py:64
  126.0 1.2 copy-done.4
  127.1 1.2 copy-done.7
  128.3 1.2 copy-done.10
  129.5 1.2 copy-done.22
  130.7 1.2 copy-done.24
  131.9 1.2 copy-done.26
  133.0 3.1 %shard_map.94.part_ref = bf16[512,512]{1,0:T(8,128)(2,1)S(1)} custom-call(s32[5]{0:T(128)S(1)} %stack.175.info_ref, bf16[2,416,896]{2,1,0:T(8,128)(2,1)S(1)} %get-tuple-element.22.own_near, bf16[2,256,896]{2,1,0:T(8,128)(2,1)S(1)} %copy-done.4, bf16[2,416,896]{2,1,0:T(8,128)(2,1)S(1)} %collective-permute-done.mate_near, bf16[2,256,896]{2,1,0:T(8,128)(2,1)S(1)} %copy-done.7, ...), custom_call_target="tpu_custom_call" | custom-call | flops 1879048192 | bytes 7340032 | tf_op jit(solution)/shard_map/pallas_call | solution.py:375
  136.6 1.0 slice_reduce_fusion.1
  137.7 1.3 copy-done.1
  138.9 1.2 copy-done.5
  140.1 1.2 copy-done.8
  141.3 1.3 copy-done.16
  142.5 1.3 copy-done.18
  143.8 1.3 copy-done.20
  145.1 3.8 %shard_map.95.more_ref = bf16[512,640]{1,0:T(8,128)(2,1)S(1)} custom-call(s32[5]{0:T(128)S(1)} %stack.175.info_ref, bf16[2,416,896]{2,1,0:T(8,128)(2,1)S(1)} %get-tuple-element.22.own_near, bf16[2,256,896]{2,1,0:T(8,128)(2,1)S(1)} %copy-done.5, bf16[2,416,896]{2,1,0:T(8,128)(2,1)S(1)} %collective-permute-done.mate_near, bf16[2,256,896]{2,1,0:T(8,128)(2,1)S(1)} %copy-done.8, ...), custom_call_target="tpu_custom_call" | custom-call | flops 2348810240 | bytes 8257536 | tf_op jit(solution)/shard_map/pallas_call | solution.py:375
  149.7 1.0 slice_reduce_fusion
  150.9 1.1 copy-done.12
  152.0 8.2 %shard_map.97 = bf16[256,896]{1,0:T(8,128)(2,1)S(1)} custom-call(s32[68]{0:T(128)S(1)} %concatenate.111.info_ref, s32[64]{0:T(128)S(1)} %maximum_convert_fusion.count_ref, bf16[512,512]{1,0:T(8,128)(2,1)S(1)} %shard_map.94.part_ref, bf16[512,640]{1,0:T(8,128)(2,1)S(1)} %copy-done.12, bf16[16,2,80,128]{3,2,1,0:T(8,128)(2,1)} %bitcast.41.rest_0_, ...), custom_call_target="tpu_custom_call" | custom-call | flops 1174405120 | bytes 8388608 | tf_op jit(solution)/shard_map/pallas_call | solution.py:284
  160.2 1.9 %collective-permute-start.28 = (bf16[256,896]{1,0:T(8,128)(2,1)S(1)}, bf16[256,896]{1,0:T(8,128)(2,1)}, u32[]{:S(2)}, u32[]{:S(2)}) collective-permute-start(bf16[256,896]{1,0:T(8,128)(2,1)S(1)} %shard_map.97), channel_id=1, source_target_pairs={{0,64},{32,96},{2,66},{34,98},{4,68},{36,100},{6,70},{38,102},{64,... | collective-permute-start | bytes 1376264 | tf_op jit(solution)/shard_map/ppermute | solution.py:64
  162.2 10.2 %shard_map.96 = bf16[256,1792]{1,0:T(8,128)(2,1)} custom-call(s32[68]{0:T(128)S(1)} %concatenate.87.info_ref, s32[64]{0:T(128)S(1)} %maximum_convert_fusion.count_ref, bf16[512,512]{1,0:T(8,128)(2,1)S(1)} %shard_map.94.part_ref, bf16[512,640]{1,0:T(8,128)(2,1)S(1)} %copy-done.13, bf16[16,2,80,128]{3,2,1,0:T(8,128)(2,1)} %bitcast.41.rest_0_, ...), custom_call_target="tpu_custom_call" | custom-call | flops 1174405120 | bytes 8388608 | tf_op jit(solution)/shard_map/pallas_call | solution.py:284
  172.8 1.8 %bitcast_dynamic-update-slice_fusion = bf16[1,256,1792]{2,1,0:T(8,128)(2,1)} fusion(bf16[1,256,1792]{2,1,0:T(8,128)(2,1)} %bitcast.83, s32[]{:T(128)S(6)} %select_n.249, bf16[256,896]{1,0:T(8,128)(2,1)} %collective-permute-done.28), kind=kLoop, calls=%fused_computation.7 | loop fusion | bytes 917508 | tf_op jit(solution)/shard_map/dynamic_update_slice | solution.py:572
  (126 shorter events, 12.8 us)
Async XLA Ops:
  1.7 4.8 %collective-permute-start.1 = (bf16[28,1408]{1,0:T(8,128)(2,1)}, bf16[28,1408]{1,0:T(8,128)(2,1)S(1)}, u32[]{:S(2)}, u32[]{:S(2)}) collective-permute-start(bf16[28,1408]{1,0:T(8,128)(2,1)} %get-tuple-element.24), channel_id=1, source_target_pairs={{0,64},{32,96},{2,66},{34,98},{4,68},{36,100},{6,70},{38,102},{64,... | collective-permute-start | bytes 236552 | tf_op jit(solution)/shard_map/ppermute | solution.py:64
  7.6 13.6 %collective-permute-start.2 = (bf16[56,1408]{1,0:T(8,128)(2,1)S(1)}, bf16[56,1408]{1,0:T(8,128)(2,1)}, u32[]{:S(2)}, u32[]{:S(2)}) collective-permute-start(bf16[56,1408]{1,0:T(8,128)(2,1)S(1)} %maximum_select_fusion.4), channel_id=1, source_target_pairs={{0,65},{32,97},{2,67},{34,99},{4,69},{36,101},{6,71},{38,103},{64,... | collective-permute-start | bytes 473096 | tf_op jit(solution)/shard_map/ppermute | solution.py:64
  12.1 1.5 copy-start.14
  13.6 0.7 copy-start.27
  20.1 0.9 copy-start.2
  21.0 39.2 %collective-permute-start = (bf16[2,416,896]{2,1,0:T(8,128)(2,1)S(1)}, bf16[2,416,896]{2,1,0:T(8,128)(2,1)S(1)}, u32[]{:S(2)}, u32[]{:S(2)}) collective-permute-start(bf16[2,416,896]{2,1,0:T(8,128)(2,1)S(1)} %get-tuple-element.22.own_near), channel_id=1, source_target_pairs={{0,64},{32,96},{2,66},{34,98},{4,68},{36,100},{6,70},{38,102},{64,... | collective-permute-start | bytes 4472840 | tf_op jit(solution)/shard_map/ppermute | solution.py:64
  22.2 5.5 %collective-permute-start.3 = (bf16[112,768]{1,0:T(8,128)(2,1)S(1)}, bf16[112,768]{1,0:T(8,128)(2,1)S(1)}, u32[]{:S(2)}, u32[]{:S(2)}) collective-permute-start(bf16[112,768]{1,0:T(8,128)(2,1)S(1)} %get-tuple-element.44), channel_id=1, source_target_pairs={{0,8},{32,56},{2,10},{34,58},{4,12},{36,60},{6,14},{38,62},{64,72}... | collective-permute-start | bytes 516104 | tf_op jit(solution)/shard_map/ppermute | solution.py:64
  23.2 14.1 %collective-permute-start.5 = (bf16[112,640]{1,0:T(8,128)(2,1)S(1)}, bf16[112,640]{1,0:T(8,128)(2,1)S(1)}, u32[]{:S(2)}, u32[]{:S(2)}) collective-permute-start(bf16[112,640]{1,0:T(8,128)(2,1)S(1)} %get-tuple-element.42), channel_id=1, source_target_pairs={{0,2},{32,38},{2,0},{34,36},{4,6},{36,34},{6,4},{38,32},{64,66},{9... | collective-permute-start | bytes 430088 | tf_op jit(solution)/shard_map/ppermute | solution.py:64
  27.8 8.5 %collective-permute-start.4 = (bf16[2,112,768]{2,1,0:T(8,128)(2,1)S(1)}, bf16[2,112,768]{2,1,0:T(8,128)(2,1)S(1)}, u32[]{:S(2)}, u32[]{:S(2)}) collective-permute-start(bf16[2,112,768]{2,1,0:T(8,128)(2,1)S(1)} %pad_maximum_fusion.4), channel_id=1, source_target_pairs={{0,24},{32,40},{2,26},{34,42},{4,28},{36,44},{6,30},{38,46},{64,88... | collective-permute-start | bytes 1032200 | tf_op jit(solution)/shard_map/ppermute | solution.py:64
  36.3 0.9 copy-start.28
  37.3 2.0 %copy-start.31 = (bf16[112,640]{1,0:T(8,128)(2,1)}, bf16[112,640]{1,0:T(8,128)(2,1)S(1)}, u32[]{:S(2)}) copy-start(bf16[112,640]{1,0:T(8,128)(2,1)S(1)} %collective-permute-done.5) | copy-start | bytes 430084
  37.3 8.6 %collective-permute-start.6 = (bf16[448,256]{1,0:T(8,128)(2,1)S(1)}, bf16[448,256]{1,0:T(8,128)(2,1)}, u32[]{:S(2)}, u32[]{:S(2)}) collective-permute-start(bf16[448,256]{1,0:T(8,128)(2,1)S(1)} %slice.108), channel_id=1, source_target_pairs={{0,2},{32,38},{2,0},{34,36},{4,6},{36,34},{6,4},{38,32},{64,66},{9... | collective-permute-start | bytes 688136 | tf_op jit(solution)/shard_map/ppermute | solution.py:64
  40.0 8.2 %collective-permute-start.7 = (bf16[2,112,640]{2,1,0:T(8,128)(2,1)}, bf16[2,112,640]{2,1,0:T(8,128)(2,1)}, u32[]{:S(2)}, u32[]{:S(2)}) collective-permute-start(bf16[2,112,640]{2,1,0:T(8,128)(2,1)} %pad_maximum_fusion.6), channel_id=1, source_target_pairs={{0,6},{32,34},{2,4},{34,32},{4,2},{36,38},{6,0},{38,36},{64,70},{9... | collective-permute-start | bytes 860168 | tf_op jit(solution)/shard_map/ppermute | solution.py:64
  45.4 5.5 %copy-start.32 = (bf16[112,640]{1,0:T(8,128)(2,1)S(1)}, bf16[112,640]{1,0:T(8,128)(2,1)}, u32[]{:S(2)}) copy-start(bf16[112,640]{1,0:T(8,128)(2,1)} %copy-done.31) | copy-start | bytes 430084
  47.1 13.0 %copy-start.29 = (bf16[4,112,768]{2,1,0:T(8,128)(2,1)S(1)}, bf16[4,112,768]{2,1,0:T(8,128)(2,1)}, u32[]{:S(2)}) copy-start(bf16[4,112,768]{2,1,0:T(8,128)(2,1)} %copy-done.28) | copy-start | bytes 2064388
  48.2 9.7 %collective-permute-start.8 = (bf16[896,256]{1,0:T(8,128)(2,1)S(1)}, bf16[896,256]{1,0:T(8,128)(2,1)S(1)}, u32[]{:S(2)}, u32[]{:S(2)}) collective-permute-start(bf16[896,256]{1,0:T(8,128)(2,1)S(1)} %maximum_select_fusion.2.refs_0_), channel_id=1, source_target_pairs={{0,6},{32,34},{2,4},{34,32},{4,2},{36,38},{6,0},{38,36},{64,70},{9... | collective-permute-start | bytes 1376264 | tf_op jit(solution)/shard_map/ppermute | solution.py:64
  58.0 3.7 %copy-start.30 = (bf16[4,64,896]{2,1,0:T(8,128)(2,1)S(1)}, bf16[4,64,896]{2,1,0:T(8,128)(2,1)}, u32[]{:S(2)}) copy-start(bf16[4,64,896]{2,1,0:T(8,128)(2,1)} %slice.102) | copy-start | bytes 1376260
  58.0 3.8 %collective-permute-start.9 = (bf16[1792,256]{1,0:T(8,128)(2,1)S(1)}, bf16[1792,256]{1,0:T(8,128)(2,1)S(1)}, u32[]{:S(2)}, u32[]{:S(2)}) collective-permute-start(bf16[1792,256]{1,0:T(8,128)(2,1)S(1)} %pad_maximum_fusion.1), channel_id=1, source_target_pairs={{0,32},{32,0},{2,34},{34,2},{4,36},{36,4},{6,38},{38,6},{64,96},{9... | collective-permute-start | bytes 2752520 | tf_op jit(solution)/shard_map/ppermute | solution.py:64
  60.0 9.8 %collective-permute-start.19 = (bf16[448,640]{1,0:T(8,128)(2,1)S(1)}, bf16[448,640]{1,0:T(8,128)(2,1)S(1)}, u32[]{:S(2)}, u32[]{:S(2)}) collective-permute-start(bf16[448,640]{1,0:T(8,128)(2,1)S(1)} %bitcast.75), channel_id=1, source_target_pairs={{0,8},{32,56},{2,10},{34,58},{4,12},{36,60},{6,14},{38,62},{64,72}... | collective-permute-start | bytes 1720328 | tf_op jit(solution)/shard_map/ppermute | solution.py:64
  60.1 10.7 %collective-permute-start.17 = (bf16[448,512]{1,0:T(8,128)(2,1)S(1)}, bf16[448,512]{1,0:T(8,128)(2,1)S(1)}, u32[]{:S(2)}, u32[]{:S(2)}) collective-permute-start(bf16[448,512]{1,0:T(8,128)(2,1)S(1)} %slice.118), channel_id=1, source_target_pairs={{0,2},{32,38},{2,0},{34,36},{4,6},{36,34},{6,4},{38,32},{64,66},{9... | collective-permute-start | bytes 1376264 | tf_op jit(solution)/shard_map/ppermute | solution.py:64
  70.2 25.2 %copy-start = (bf16[896,640]{1,0:T(8,128)(2,1)}, bf16[896,640]{1,0:T(8,128)(2,1)S(1)}, u32[]{:S(2)}) copy-start(bf16[896,640]{1,0:T(8,128)(2,1)S(1)} %maximum_select_fusion.refs_0_) | copy-start | bytes 3440644
  70.2 25.2 %collective-permute-start.20 = (bf16[896,640]{1,0:T(8,128)(2,1)S(1)}, bf16[896,640]{1,0:T(8,128)(2,1)S(1)}, u32[]{:S(2)}, u32[]{:S(2)}) collective-permute-start(bf16[896,640]{1,0:T(8,128)(2,1)S(1)} %maximum_select_fusion.refs_0_), channel_id=1, source_target_pairs={{0,24},{32,40},{2,26},{34,42},{4,28},{36,44},{6,30},{38,46},{64,88... | collective-permute-start | bytes 3440648 | tf_op jit(solution)/shard_map/ppermute | solution.py:64
  71.2 30.5 %copy-start.9 = (bf16[896,512]{1,0:T(8,128)(2,1)}, bf16[896,512]{1,0:T(8,128)(2,1)S(1)}, u32[]{:S(2)}) copy-start(bf16[896,512]{1,0:T(8,128)(2,1)S(1)} %maximum_select_fusion.1.refs_0_) | copy-start | bytes 2752516
  71.2 24.2 %collective-permute-start.18 = (bf16[896,512]{1,0:T(8,128)(2,1)S(1)}, bf16[896,512]{1,0:T(8,128)(2,1)S(1)}, u32[]{:S(2)}, u32[]{:S(2)}) collective-permute-start(bf16[896,512]{1,0:T(8,128)(2,1)S(1)} %maximum_select_fusion.1.refs_0_), channel_id=1, source_target_pairs={{0,6},{32,34},{2,4},{34,32},{4,2},{36,38},{6,0},{38,36},{64,70},{9... | collective-permute-start | bytes 2752520 | tf_op jit(solution)/shard_map/ppermute | solution.py:64
  75.0 20.9 %copy-start.3 = (bf16[2,256,896]{2,1,0:T(8,128)(2,1)S(1)}, bf16[2,256,896]{2,1,0:T(8,128)(2,1)}, u32[]{:S(2)}) copy-start(bf16[2,256,896]{2,1,0:T(8,128)(2,1)} %copy-done.2) | copy-start | bytes 2752516
  75.1 5.6 %collective-permute-start.10 = (bf16[2,144,128]{2,1,0:T(8,128)(2,1)S(1)}, bf16[2,144,128]{2,1,0:T(8,128)(2,1)S(1)}, u32[]{:S(2)}, u32[]{:S(2)}) collective-permute-start(bf16[2,144,128]{2,1,0:T(8,128)(2,1)S(1)} %maximum_select_fusion.6), channel_id=1, source_target_pairs={{0,65},{32,97},{2,67},{34,99},{4,69},{36,101},{6,71},{38,103},{64,... | collective-permute-start | bytes 221192 | tf_op jit(solution)/shard_map/ppermute | solution.py:64
  80.7 7.4 %collective-permute-start.14 = (bf16[2,2,64,128]{3,2,1,0:T(8,128)(2,1)S(1)}, bf16[2,2,64,128]{3,2,1,0:T(8,128)(2,1)S(1)}, u32[]{:S(2)}, u32[]{:S(2)}) collective-permute-start(bf16[2,2,64,128]{3,2,1,0:T(8,128)(2,1)S(1)} %pad_maximum_fusion.11), channel_id=1, source_target_pairs={{0,2},{32,38},{2,0},{34,36},{4,6},{36,34},{6,4},{38,32},{64,66},{9... | collective-permute-start | bytes 196616 | tf_op jit(solution)/shard_map/ppermute | solution.py:64
  80.8 5.5 %collective-permute-start.11 = (bf16[2,2,80,128]{3,2,1,0:T(8,128)(2,1)S(1)}, bf16[2,2,80,128]{3,2,1,0:T(8,128)(2,1)S(1)}, u32[]{:S(2)}, u32[]{:S(2)}) collective-permute-start(bf16[2,2,80,128]{3,2,1,0:T(8,128)(2,1)S(1)} %fusion), channel_id=1, source_target_pairs={{0,8},{32,56},{2,10},{34,58},{4,12},{36,60},{6,14},{38,62},{64,72}... | collective-permute-start | bytes 245768 | tf_op jit(solution)/shard_map/ppermute | solution.py:64
  86.2 6.6 %collective-permute-start.12 = (bf16[2,2,2,80,128]{4,3,2,1,0:T(8,128)(2,1)S(1)}, bf16[2,2,2,80,128]{4,3,2,1,0:T(8,128)(2,1)S(1)}, u32[]{:S(2)}, u32[]{:S(2)}) collective-permute-start(bf16[2,2,2,80,128]{4,3,2,1,0:T(8,128)(2,1)S(1)} %pad_maximum_fusion.8), channel_id=1, source_target_pairs={{0,24},{32,40},{2,26},{34,42},{4,28},{36,44},{6,30},{38,46},{64,88... | collective-permute-start | bytes 491528 | tf_op jit(solution)/shard_map/ppermute | solution.py:64
  88.2 7.0 %collective-permute-start.15 = (bf16[2,2,2,64,128]{4,3,2,1,0:T(8,128)(2,1)S(1)}, bf16[2,2,2,64,128]{4,3,2,1,0:T(8,128)(2,1)S(1)}, u32[]{:S(2)}, u32[]{:S(2)}) collective-permute-start(bf16[2,2,2,64,128]{4,3,2,1,0:T(8,128)(2,1)S(1)} %pad_maximum_fusion.9), channel_id=1, source_target_pairs={{0,6},{32,34},{2,4},{34,32},{4,2},{36,38},{6,0},{38,36},{64,70},{9... | collective-permute-start | bytes 393224 | tf_op jit(solution)/shard_map/ppermute | solution.py:64
  92.9 8.8 %collective-permute-start.13 = (bf16[4,2,2,80,128]{4,3,2,1,0:T(8,128)(2,1)S(1)}, bf16[4,2,2,80,128]{4,3,2,1,0:T(8,128)(2,1)S(1)}, u32[]{:S(2)}, u32[]{:S(2)}) collective-permute-start(bf16[4,2,2,80,128]{4,3,2,1,0:T(8,128)(2,1)S(1)} %get-tuple-element.40), channel_id=1, source_target_pairs={{0,2},{32,38},{2,0},{34,36},{4,6},{36,34},{6,4},{38,32},{64,66},{9... | collective-permute-start | bytes 983048 | tf_op jit(solution)/shard_map/ppermute | solution.py:64
  95.3 6.5 %collective-permute-start.16 = (bf16[4,2,2,64,128]{4,3,2,1,0:T(8,128)(2,1)S(1)}, bf16[4,2,2,64,128]{4,3,2,1,0:T(8,128)(2,1)S(1)}, u32[]{:S(2)}, u32[]{:S(2)}) collective-permute-start(bf16[4,2,2,64,128]{4,3,2,1,0:T(8,128)(2,1)S(1)} %get-tuple-element.46), channel_id=1, source_target_pairs={{0,8},{32,56},{2,10},{34,58},{4,12},{36,60},{6,14},{38,62},{64,72}... | collective-permute-start | bytes 786440 | tf_op jit(solution)/shard_map/ppermute | solution.py:64
  95.4 26.9 %copy-start.21 = (bf16[896,512]{1,0:T(8,128)(2,1)}, bf16[896,512]{1,0:T(8,128)(2,1)S(1)}, u32[]{:S(2)}) copy-start(bf16[896,512]{1,0:T(8,128)(2,1)S(1)} %collective-permute-done.18.refs_1_) | copy-start | bytes 2752516
  95.4 25.8 %copy-start.15 = (bf16[896,640]{1,0:T(8,128)(2,1)}, bf16[896,640]{1,0:T(8,128)(2,1)S(1)}, u32[]{:S(2)}) copy-start(bf16[896,640]{1,0:T(8,128)(2,1)S(1)} %collective-permute-done.20.refs_1_) | copy-start | bytes 3440644
  95.4 25.8 %collective-permute-start.23 = (bf16[896,640]{1,0:T(8,128)(2,1)S(1)}, bf16[896,640]{1,0:T(8,128)(2,1)S(1)}, u32[]{:S(2)}, u32[]{:S(2)}) collective-permute-start(bf16[896,640]{1,0:T(8,128)(2,1)S(1)} %maximum_select_fusion.refs_0_), channel_id=1, source_target_pairs={{0,32},{32,0},{2,34},{34,2},{4,36},{36,4},{6,38},{38,6},{64,96},{9... | collective-permute-start | bytes 3440648 | tf_op jit(solution)/shard_map/ppermute | solution.py:64
  95.5 26.7 %collective-permute-start.24 = (bf16[896,640]{1,0:T(8,128)(2,1)S(1)}, bf16[896,640]{1,0:T(8,128)(2,1)S(1)}, u32[]{:S(2)}, u32[]{:S(2)}) collective-permute-start(bf16[896,640]{1,0:T(8,128)(2,1)S(1)} %collective-permute-done.20.refs_1_), channel_id=1, source_target_pairs={{0,32},{32,0},{2,34},{34,2},{4,36},{36,4},{6,38},{38,6},{64,96},{9... | collective-permute-start | bytes 3440648 | tf_op jit(solution)/shard_map/ppermute | solution.py:64
  96.0 22.3 %collective-permute-start.25 = (bf16[2,256,896]{2,1,0:T(8,128)(2,1)S(1)}, bf16[2,256,896]{2,1,0:T(8,128)(2,1)S(1)}, u32[]{:S(2)}, u32[]{:S(2)}) collective-permute-start(bf16[2,256,896]{2,1,0:T(8,128)(2,1)S(1)} %copy-done.3), channel_id=1, source_target_pairs={{0,64},{32,96},{2,66},{34,98},{4,68},{36,100},{6,70},{38,102},{64,... | collective-permute-start | bytes 2752520 | tf_op jit(solution)/shard_map/ppermute | solution.py:64
  101.7 17.6 %collective-permute-start.21 = (bf16[896,512]{1,0:T(8,128)(2,1)S(1)}, bf16[896,512]{1,0:T(8,128)(2,1)S(1)}, u32[]{:S(2)}, u32[]{:S(2)}) collective-permute-start(bf16[896,512]{1,0:T(8,128)(2,1)S(1)} %maximum_select_fusion.1.refs_0_), channel_id=1, source_target_pairs={{0,32},{32,0},{2,34},{34,2},{4,36},{36,4},{6,38},{38,6},{64,96},{9... | collective-permute-start | bytes 2752520 | tf_op jit(solution)/shard_map/ppermute | solution.py:64
  101.7 18.6 %collective-permute-start.22 = (bf16[896,512]{1,0:T(8,128)(2,1)S(1)}, bf16[896,512]{1,0:T(8,128)(2,1)S(1)}, u32[]{:S(2)}, u32[]{:S(2)}) collective-permute-start(bf16[896,512]{1,0:T(8,128)(2,1)S(1)} %collective-permute-done.18.refs_1_), channel_id=1, source_target_pairs={{0,32},{32,0},{2,34},{34,2},{4,36},{36,4},{6,38},{38,6},{64,96},{9... | collective-permute-start | bytes 2752520 | tf_op jit(solution)/shard_map/ppermute | solution.py:64
  118.3 0.9 copy-start.6
  119.3 1.0 copy-start.23
  120.3 0.9 copy-start.25
  121.2 1.0 copy-start.17
  122.2 1.0 copy-start.19
  123.3 26.5 %collective-permute-start.26 = (bf16[2,4,2,2,80,128]{5,4,3,2,1,0:T(8,128)(2,1)}, bf16[2,4,2,2,80,128]{5,4,3,2,1,0:T(8,128)(2,1)}, u32[]{:S(2)}, u32[]{:S(2)}) collective-permute-start(bf16[2,4,2,2,80,128]{5,4,3,2,1,0:T(8,128)(2,1)} %pad_maximum_fusion.2), channel_id=1, source_target_pairs={{0,6},{32,34},{2,4},{34,32},{4,2},{36,38},{6,0},{38,36},{64,70},{9... | collective-permute-start | bytes 1966088 | tf_op jit(solution)/shard_map/ppermute | solution.py:64
  126.0 1.2 copy-start.4
  127.1 1.2 copy-start.7
  128.3 1.2 copy-start.10
  129.5 1.2 copy-start.22
  130.7 1.2 copy-start.24
  131.9 1.2 copy-start.26
  136.2 14.7 %collective-permute-start.27 = (bf16[2,4,2,2,64,128]{5,4,3,2,1,0:T(8,128)(2,1)}, bf16[2,4,2,2,64,128]{5,4,3,2,1,0:T(8,128)(2,1)}, u32[]{:S(2)}, u32[]{:S(2)}) collective-permute-start(bf16[2,4,2,2,64,128]{5,4,3,2,1,0:T(8,128)(2,1)} %pad_maximum_fusion.3), channel_id=1, source_target_pairs={{0,24},{32,40},{2,26},{34,42},{4,28},{36,44},{6,30},{38,46},{64,88... | collective-permute-start | bytes 1572872 | tf_op jit(solution)/shard_map/ppermute | solution.py:64
  137.7 1.3 copy-start.1
  138.9 1.2 copy-start.5
  140.1 1.2 copy-start.8
  141.3 1.3 copy-start.16
  142.5 1.3 copy-start.18
  143.8 1.3 copy-start.20
  148.9 0.8 copy-start.11
  150.9 1.1 copy-start.12
  152.0 10.2 %copy-start.13 = (bf16[512,640]{1,0:T(8,128)(2,1)S(1)}, bf16[512,640]{1,0:T(8,128)(2,1)}, u32[]{:S(2)}) copy-start(bf16[512,640]{1,0:T(8,128)(2,1)} %copy-done.11) | copy-start | bytes 1966084
  160.2 12.5 %collective-permute-start.28 = (bf16[256,896]{1,0:T(8,128)(2,1)S(1)}, bf16[256,896]{1,0:T(8,128)(2,1)}, u32[]{:S(2)}, u32[]{:S(2)}) collective-permute-start(bf16[256,896]{1,0:T(8,128)(2,1)S(1)} %shard_map.97), channel_id=1, source_target_pairs={{0,64},{32,96},{2,66},{34,98},{4,68},{36,100},{6,70},{38,102},{64,... | collective-permute-start | bytes 1376264 | tf_op jit(solution)/shard_map/ppermute | solution.py:64

commit v8 on v6

--- a/solution.py
+++ b/solution.py
@@ -165,7 +165,8 @@
 LINES = HEADS * TOK
 
 
-def attend_body(wide, info_ref, count_ref, part_ref, more_ref, far_k_ref, far_v_ref, *rest):
+def attend_body(wide, info_ref, count_ref, part_ref, more_ref, *rest):
+    far_k_refs, far_v_refs, rest = rest[:2], rest[2:4], rest[4:]
     out_ref, query_ref, keys_ref, values_ref, bias_ref, score_ref, top_ref, sum_ref, mix_ref = rest
     span, valid, column, which = info_ref[0], info_ref[1], info_ref[2], info_ref[3]
     own = slice(0, TOK) if wide else slice(TOK, 2 * TOK)
@@ -177,8 +178,16 @@
         place_k, place_v = info_ref[4 + i], info_ref[4 + SPANS + i]
         count = count_ref[place_k * 2 + which]
         here = pl.ds(pl.multiple_of(at, 16), SLOTS)
-        keys_ref[here, :] = far_k_ref[place_k, which, :SLOTS, :]
-        values_ref[here, :] = far_v_ref[place_v, which]
+        for j in range(2):
+
+            @pl.when(place_k // (SPANS // 2) == j)
+            def _():
+                keys_ref[here, :] = far_k_refs[j][place_k % (SPANS // 2), which, :SLOTS, :]
+
+            @pl.when(place_v // (SPANS // 2) == j)
+            def _():
+                values_ref[here, :] = far_v_refs[j][place_v % (SPANS // 2), which]
+
         bias_ref[...] = jnp.where((lane >= at) & (lane < at + count), 0.0, bias_ref[...])
         return at + ((count + 15) // 16) * 16
 
@@ -205,7 +214,7 @@
         if head < KEPT:
             query = part_ref[own, (2 + head) * D : (3 + head) * D]
         else:
-            query = more_ref[:, (head - KEPT) * D : (head - KEPT + 1) * D]
+            query = more_ref[own, (head - KEPT) * D : (head - KEPT + 1) * D]
         query_ref[here, :] = query
         near = lax.dot_general(
             query, part_ref[own, :D], contract, preferred_element_type=jnp.float32
@@ -270,13 +279,13 @@
             out_ref[:, head * D : (head + 1) * D] = result
 
 
-def attend(wide, info, counts, part, more, far_k, far_v):
+def attend(wide, info, counts, part, more, far):
     columns = 2 * HEADS * D if wide else HEADS * D
     smem, vmem = pl.BlockSpec(memory_space=pltpu.SMEM), pl.BlockSpec(memory_space=pltpu.VMEM)
     return pl.pallas_call(
         functools.partial(attend_body, wide),
         out_shape=jax.ShapeDtypeStruct((TOK, columns), jnp.bfloat16),
-        in_specs=[smem, smem, vmem, vmem, vmem, vmem],
+        in_specs=[smem, smem] + [vmem] * 6,
         out_specs=vmem,
         scratch_shapes=[
             pltpu.VMEM((LINES, D), jnp.bfloat16),
@@ -289,7 +298,7 @@
             pltpu.VMEM((LINES, D), jnp.float32),
         ],
         compiler_params=pltpu.CompilerParams(vmem_limit_bytes=28 * 1024 * 1024),
-    )(info, counts, part, more, far_k, far_v)
+    )(info, counts, part, more, *far)
 
 
 def project_body(count, slab_ref, x_ref, *refs):
@@ -318,48 +327,56 @@
     )(jnp.stack(slabs).astype(jnp.int32), x, *weights, *totals)
 
 
-def crossed_body(info_ref, own_near, own_far, mate_near, mate_far, *refs):
-    pieces, out_ref, full_ref = refs[:4], refs[4], refs[5]
-    core = info_ref[0]
-    block = 4 * ROWS
-    for i, piece in enumerate(pieces):
-        theirs, is_far = divmod(i, 2)
-        side = core if theirs == 0 else 1 - core
-        pair_x, pair_z = info_ref[1 + theirs], info_ref[3 + theirs]
-        if is_far:
-            pair_z = 1 - pair_z
-        for t in range(2):
-            split = jnp.where(pair_z == 0, PAIRED[1][t], PAIRED[1][2 + t])
-            z = jnp.where(side == 0, 2 * pair_z + t, split)
-            for x in range(4):
-                at = jnp.where(side == 0, x, PAIRED[1].index(x))
-                slab = jnp.where(at // 2 == pair_x, 0, 2) + theirs
-                line = slab * SLAB + ((at % 2) * 4 + z) * block
-                source = slice((t * 4 + x) * block, (t * 4 + x + 1) * block)
-                full_ref[pl.ds(pl.multiple_of(line, 16), block), :] = piece[source, :]
+def span_body(crossed, info_ref, own_near, own_far, mate_near, mate_far, *refs):
+    (near_w, far_w, other_w), out_ref, full_ref = refs[:3], refs[3], refs[4]
+    pieces = [(near_w, 0), (far_w, 0), (other_w, 0), (other_w, SLAB)]
+    if crossed:
+        core = info_ref[0]
+        block = 4 * ROWS
+        for i, (piece, start) in enumerate(pieces):
+            theirs, is_far = divmod(i, 2)
+            side = core if theirs == 0 else 1 - core
+            pair_x, pair_z = info_ref[1 + theirs], info_ref[3 + theirs]
+            if is_far:
+                pair_z = 1 - pair_z
+            for t in range(2):
+                split = jnp.where(pair_z == 0, PAIRED[1][t], PAIRED[1][2 + t])
+                z = jnp.where(side == 0, 2 * pair_z + t, split)
+                for x in range(4):
+                    at = jnp.where(side == 0, x, PAIRED[1].index(x))
+                    slab = jnp.where(at // 2 == pair_x, 0, 2) + theirs
+                    line = slab * SLAB + ((at % 2) * 4 + z) * block
+                    source = start + (t * 4 + x) * block
+                    full_ref[pl.ds(pl.multiple_of(line, 16), block), :] = piece[
+                        source : source + block, :
+                    ]
+        pieces = [(full_ref, slab * SLAB) for slab in range(4)]
+    else:
+        pieces = [pieces[0], pieces[2], pieces[1], pieces[3]]
     columns = out_ref.shape[1]
     for first in range(0, columns, 256):
-        here = slice(first, first + 256)
+        here = slice(first, min(first + 256, columns))
         for j, (near_ref, far_ref) in enumerate(((own_near, own_far), (mate_near, mate_far))):
             out = None
-            for slab in range(4):
-                x_ref = near_ref if slab < 2 else far_ref
-                w = full_ref[slab * SLAB : (slab + 1) * SLAB, here]
-                term = jnp.dot(x_ref[slab % 2, :TOK, :], w, preferred_element_type=jnp.float32)
+            for slab, (piece, start) in enumerate(pieces):
+                x = (near_ref if slab < 2 else far_ref)[slab % 2, :TOK, :]
+                w = piece[start : start + SLAB, here]
+                term = jnp.dot(x, w, preferred_element_type=jnp.float32)
                 out = term if out is None else out + term
             out_ref[j * TOK : (j + 1) * TOK, here] = out.astype(jnp.bfloat16)
 
 
-def project_crossed(info, tokens, pieces):
+def project_spans(crossed, info, tokens, pieces):
     smem, vmem = pl.BlockSpec(memory_space=pltpu.SMEM), pl.BlockSpec(memory_space=pltpu.VMEM)
     columns = pieces[0].shape[1]
+    lines = WIDTH if crossed else 16
     return pl.pallas_call(
-        crossed_body,
+        functools.partial(span_body, crossed),
         out_shape=jax.ShapeDtypeStruct((2 * TOK, columns), jnp.bfloat16),
-        in_specs=[smem] + [vmem] * 8,
+        in_specs=[smem] + [vmem] * 7,
         out_specs=vmem,
-        scratch_shapes=[pltpu.VMEM((WIDTH, columns), jnp.bfloat16)],
-        compiler_params=pltpu.CompilerParams(vmem_limit_bytes=16 * 1024 * 1024),
+        scratch_shapes=[pltpu.VMEM((lines, columns), jnp.bfloat16)],
+        compiler_params=pltpu.CompilerParams(vmem_limit_bytes=10 * 1024 * 1024),
     )(info, *tokens, *pieces)
 
 
@@ -391,6 +408,10 @@
         out_specs=[vmem, vmem],
         compiler_params=pltpu.CompilerParams(vmem_limit_bytes=4 * 1024 * 1024),
     )(head.reshape(1), *weights)
+
+
+def gate(flag, other):
+    return flag + (other[0, 0].astype(jnp.float32) > 1e38).astype(jnp.int32)
 
 
 def double(block, axis):
@@ -464,13 +485,12 @@
     early, cross = early[:, : CUTS[1]], early[:, CUTS[1] :]
     z_second, x_second = pair_of("z", core)[1], pair_of("x", core)[1]
     early = order(z_second, early, send(early, FLIP["z", 0]))
-    cross = order(z_second, cross, send(cross, FLIP["z", 0]))
-    late = order(x_second, late, send(late, FLIP["x", 0]))
     early_far = send(early, FLIP["z", 1])
-    cross_far = send(after(cross, early_far), FLIP["z", 1])
-    late_far = send(late, FLIP["x", 1])
     gathered = jnp.concatenate([early, early_far], 0)
     swapped = send(gathered, SWAP)
+    ready = gate(jnp.int32(0), swapped) == 0
+    cross, late = jnp.where(ready, cross, 0), jnp.where(ready, late, 0)
+    cross_near, late_near = send(cross, FLIP["z", 0]), send(late, FLIP["x", 0])
     slab_near, slab_far = slabs("z")
     where_m = (slab_near[0], slab_far[0], slab_near[1], slab_far[1])
     pieces_m = (early, early_far, swapped[:SLAB], swapped[SLAB:])
@@ -484,24 +504,23 @@
     block = jnp.concatenate([block_k, block_v], 1)
     block = order(low, block[:1], block[1:])
     block = jnp.stack([block, send(block, ACROSS)])
-    half_k = double(block[:, :, : SLOTS + 16], "x")
-    half_v = double(block[:, :, SLOTS + 16 :], "z")
-    zero, one = jnp.int32(0), jnp.int32(1)
-    near_w = (late, send(late, SWAP))
-    own = project((zero, one), own_near, near_w)
-    half_k, half_v = after((half_k, half_v), own)
-    crossed = jnp.concatenate([cross, cross_far], 0)
-    crossed, far_w = after((crossed, late_far), (half_k, half_v))
-    crossed = send(crossed, SWAP)
-    far_w = (far_w, send(far_w, SWAP))
+    one_k, one_v = block[:, :, : SLOTS + 16], block[:, :, SLOTS + 16 :]
+    got_k, got_v = send(one_k, FLIP["x", 0]), send(one_v, FLIP["z", 0])
+    one_k, one_v = jnp.stack([one_k, got_k]), jnp.stack([one_v, got_v])
+    half_k = jnp.concatenate([one_k, send(one_k, FLIP["x", 1])])
+    half_v = jnp.concatenate([one_v, send(one_v, FLIP["z", 1])])
+    cross = order(gate(z_second, got_k[0, 0]), cross, cross_near)
+    late = order(gate(x_second, got_v[0, 0]), late, late_near)
+    cross_far = send(cross, FLIP["z", 1])
+    late_far = send(late, FLIP["x", 1])
     pair_k = jnp.stack([half_k, send(half_k, FLIP["z", 0])])
     pair_v = jnp.stack([half_v, send(half_v, FLIP["x", 0])])
-    mate = project((zero, one), mate_near, near_w)
-    pair_k, pair_v = after((pair_k, pair_v), (mate, mate_far))
-    every_k = jnp.concatenate([pair_k, send(pair_k, FLIP["z", 1])])
-    every_v = jnp.concatenate([pair_v, send(pair_v, FLIP["x", 1])])
-    every_k = every_k.reshape(SPANS, 2, SLOTS + 16, D)
-    every_v = every_v.reshape(SPANS, 2, SLOTS, D)
+    mate_there = gate(jnp.int32(0), mate_far[0]) == 0
+    pair_k, pair_v = jnp.where(mate_there, pair_k, 0), jnp.where(mate_there, pair_v, 0)
+    every_k = [pair_k, send(pair_k, FLIP["z", 1])]
+    every_v = [pair_v, send(pair_v, FLIP["x", 1])]
+    every_k = [k.reshape(SPANS // 2, 2, SLOTS + 16, D) for k in every_k]
+    every_v = [v.reshape(SPANS // 2, 2, SLOTS, D) for v in every_v]
 
     owner = jnp.arange(SPANS, dtype=jnp.int32)
 
@@ -513,16 +532,16 @@
     code_h = (owner ^ span) % 2
     at_k = (code_z * 4 + code_x) * 2 + code_h
     at_v = (code_x * 4 + code_z) * 2 + code_h
-    live = every_k[:, :, SLOTS, 0].astype(jnp.int32).reshape(2 * SPANS)
+    live = jnp.concatenate([k[:, :, SLOTS, 0].reshape(SPANS) for k in every_k]).astype(jnp.int32)
 
     pairs = [pair_of(axis, side)[0] for axis in "xz" for side in (core, 1 - core)]
-    part = project_crossed(
-        jnp.stack([core, *pairs]).astype(jnp.int32),
-        (own_near, own_far, mate_near, mate_far),
-        (cross, cross_far, crossed[:SLAB], crossed[SLAB:]),
-    )
-    own = project((zero, one), own_far, far_w, own, last=True)
-    mate = project((zero, one), mate_far, far_w, mate, last=True)
+    third = gate(gate(jnp.int32(0), pair_k[1, 0, 0, 0]), pair_v[1, 0, 0, 0]) == 0
+    cross_other = send(jnp.where(third, jnp.concatenate([cross, cross_far]), 0), SWAP)
+    late_other = send(jnp.where(third, jnp.concatenate([late, late_far]), 0), SWAP)
+    info = jnp.stack([core, *pairs]).astype(jnp.int32)
+    both = (own_near, own_far, mate_near, mate_far)
+    part = project_spans(True, info, both, (cross, cross_far, cross_other))
+    more = project_spans(False, info, both, (late, late_far, late_other))
 
     def attention(which, valid, wide):
         info = jnp.concatenate(
@@ -533,9 +552,8 @@
             info,
             live,
             part,
-            mate if which else own,
-            every_k,
-            every_v,
+            more,
+            every_k + every_v,
         )
 
     away = send(attention(1, mate_valid, False), MATE)

time: 150 us -> 174 us (1.16)
  other arithmetic: 11 us -> 16.6 us
  Pallas kernels: 29 us -> 34.2 us
  local copies, waits for them, and re-layouts: 26.5 us -> 31.4 us
  between operations: 2.65 us -> 6.42 us
  starting transfers between devices: 34.9 us -> 37.8 us
    select_n x0 -> x6, other arithmetic: none -> 8.42 us  [the longest x1 3.08 us: on_device(): jnp.where(third, jnp.concatenate([late, late_far]), 0)]
    pallas_call x5 -> x1, Pallas kernels: 9.12 us -> 0.98 us  [project(): pl.pallas_call(functools.partial(project_body, len(weights)), out_shape=j...]
    pallas_call x1 -> x2, Pallas kernels: 3.13 us -> 10.4 us  [project_spans(): pl.pallas_call(functools.partial(span_body, crossed), out_shape=jax.Shape...]
    pallas_call x2, Pallas kernels: 11 us -> 15.9 us  [attend(): pl.pallas_call(functools.partial(attend_body, wide), out_shape=jax.ShapeD...]
    slice x1 -> x8, local copies, waits for them, and re-layouts: 1.73 us -> 6.34 us  [the longest x6 3.23 us: gate(): return flag + (other[0, 0].astype(jnp.float32) > 1e+38).astype(jnp.int32)]
    another operation x1 -> x3, local copies, waits for them, and re-layouts: 0.08 us -> 3.31 us  [the longest x2 2.63 us: on_device(): k[:, :, SLOTS, 0].reshape(SPANS)]
    concatenate x5 -> x0, other arithmetic: 2.93 us -> none  [the longest x1 1.4 us: on_device(): every_k = jnp.concatenate([pair_k, send(pair_k, FLIP['z', 1])])]
    ppermute x28 -> x27, starting transfers between devices: 34.9 us -> 37.8 us  [send(): return lax.ppermute(value, AXES, pairs)]
  transfers between devices with their start and end apart: 28 -> 27, of which waited for: 17 -> 12; matrix products, arithmetic and copies ran while one was open for 14% -> 21% of each run, Pallas kernels for 14% -> 16%
where the time goes in v8:
time: 174 us; the launch traced here: 173 us
  waiting for transfers between devices  46.3 us (27%)
  starting transfers between devices  37.8 us (22%)
  Pallas kernels  34.2 us (20%)
  local copies, waits for them, and re-layouts  31.4 us (18%)
  other arithmetic  16.6 us (10%)
  between operations  6.42 us (4%)
    ppermute x27, waiting for transfers between devices, send(): return lax.ppermute(value, AXES, pairs)  46.3 us
    ppermute x27, starting transfers between devices, send(): return lax.ppermute(value, AXES, pairs)  37.8 us
    pallas_call x2, Pallas kernels, attend(): pl.pallas_call(functools.partial(attend_body, wide), out_shape=jax.ShapeD...  15.9 us
    unnamed x42, local copies, waits for them, and re-layouts  10.8 us
    pallas_call x2, Pallas kernels, project_spans(): pl.pallas_call(functools.partial(span_body, crossed), out_shape=jax.Shape...  10.4 us
    pallas_call x1, Pallas kernels, norm_rows(): pl.pallas_call(norm_body, out_shape=[jax.ShapeDtypeStruct((2, TOK + 2 * (...  6.83 us
    select_n x7, other arithmetic, order(): jnp.where(first == 0, jnp.concatenate([one, two], 0), jnp.concatenate([tw...  3.71 us
  transfers between devices with their start and end apart: 27, of which 12 were waited for; matrix products, arithmetic and copies ran while one was open for 21% of the time, Pallas kernels for 16%

profile of v8, /device:TPU:6, one launch (start us, length us, event | category | flops | bytes accessed | tf_op | source)
XLA Modules:
  0.0 172.8 jit_solution(16694719262636304555)
XLA Ops:
  0.0 1.0 copy-done.9
  1.0 0.7 copy-done.10
  2.5 0.7 copy-done.12
  3.9 1.6 collective-permute-start.2
  5.6 3.0 %collective-permute-done.2 = bf16[28,1408]{1,0:T(8,128)(2,1)S(1)} collective-permute-done((bf16[28,1408]{1,0:T(8,128)(2,1)S(1)}, bf16[28,1408]{1,0:T(8,128)(2,1)S(1)}, u32[]{:S(2)}, u32[]{:S(2)}) %collective-permute-start.2) | collective-permute-done | bytes 78880 | tf_op jit(solution)/shard_map/ppermute | solution.py:64
  8.6 3.1 %collective-permute-start.3 = (bf16[56,1408]{1,0:T(8,128)(2,1)S(1)}, bf16[56,1408]{1,0:T(8,128)(2,1)S(1)}, u32[]{:S(2)}, u32[]{:S(2)}) collective-permute-start(bf16[56,1408]{1,0:T(8,128)(2,1)S(1)} %maximum_select_fusion.8), channel_id=1, source_target_pairs={{0,65},{32,97},{2,67},{34,99},{4,69},{36,101},{6,71},{38,103},{64,... | collective-permute-start | bytes 473096 | tf_op jit(solution)/shard_map/ppermute | solution.py:64
  11.7 3.4 %collective-permute-done.3 = bf16[56,1408]{1,0:T(8,128)(2,1)S(1)} collective-permute-done((bf16[56,1408]{1,0:T(8,128)(2,1)S(1)}, bf16[56,1408]{1,0:T(8,128)(2,1)S(1)}, u32[]{:S(2)}, u32[]{:S(2)}) %collective-permute-start.3) | collective-permute-done | bytes 157728 | tf_op jit(solution)/shard_map/ppermute | solution.py:64
  15.2 0.8 slice_bitcast_fusion.10
  16.0 0.8 collective-permute-start.4
  18.2 0.7 reshape.136.gain_ref
  19.1 6.8 %shard_map.91 = (bf16[2,416,896]{2,1,0:T(8,128)(2,1)}, bf16[2,256,896]{2,1,0:T(8,128)(2,1)S(1)}) custom-call(s32[7]{0:T(128)S(1)} %stack.143.fact_ref, bf16[256,3584]{1,0:T(8,128)(2,1)S(1)} %bitcast.86, f32[1,3584]{1,0:T(1,128)S(1)} %reshape.136.gain_ref), custom_call_target="tpu_custom_call" | custom-call | tf_op jit(solution)/shard_map/pallas_call | solution.py:145
  26.3 2.0 %slice.118 = bf16[2,160,896]{2,1,0:T(8,128)(2,1)} slice(bf16[2,416,896]{2,1,0:T(8,128)(2,1)} %get-tuple-element.13.own_near), slice={[0:2], [256:416], [0:896]} | slice | bytes 1146880 | tf_op jit(solution)/shard_map/slice | solution.py:469
  28.2 1.1 slice.156
  29.4 1.0 pad_maximum_fusion.2
  30.4 1.2 collective-permute-start.5
  31.7 0.9 constant_dynamic-update-slice_fusion.2
  32.6 6.3 %collective-permute-done.5 = bf16[2,112,768]{2,1,0:T(8,128)(2,1)S(1)} collective-permute-done((bf16[2,112,768]{2,1,0:T(8,128)(2,1)S(1)}, bf16[2,112,768]{2,1,0:T(8,128)(2,1)S(1)}, u32[]{:S(2)}, u32[]{:S(2)}) %collective-permute-start.5) | collective-permute-done | bytes 344096 | tf_op jit(solution)/shard_map/ppermute | solution.py:64
  39.0 2.0 %collective-permute-start.6 = (bf16[448,256]{1,0:T(8,128)(2,1)S(1)}, bf16[448,256]{1,0:T(8,128)(2,1)S(1)}, u32[]{:S(2)}, u32[]{:S(2)}) collective-permute-start(bf16[448,256]{1,0:T(8,128)(2,1)S(1)} %slice.162), channel_id=1, source_target_pairs={{0,2},{32,38},{2,0},{34,36},{4,6},{36,34},{6,4},{38,32},{64,66},{9... | collective-permute-start | bytes 688136 | tf_op jit(solution)/shard_map/ppermute | solution.py:64
  41.2 5.8 %collective-permute-done.6 = bf16[448,256]{1,0:T(8,128)(2,1)S(1)} collective-permute-done((bf16[448,256]{1,0:T(8,128)(2,1)S(1)}, bf16[448,256]{1,0:T(8,128)(2,1)S(1)}, u32[]{:S(2)}, u32[]{:S(2)}) %collective-permute-start.6) | collective-permute-done | bytes 229408 | tf_op jit(solution)/shard_map/ppermute | solution.py:64
  47.2 4.4 %collective-permute-start.7 = (bf16[896,256]{1,0:T(8,128)(2,1)S(1)}, bf16[896,256]{1,0:T(8,128)(2,1)S(1)}, u32[]{:S(2)}, u32[]{:S(2)}) collective-permute-start(bf16[896,256]{1,0:T(8,128)(2,1)S(1)} %maximum_select_fusion.6.refs_0_), channel_id=1, source_target_pairs={{0,6},{32,34},{2,4},{34,32},{4,2},{36,38},{6,0},{38,36},{64,70},{9... | collective-permute-start | bytes 1376264 | tf_op jit(solution)/shard_map/ppermute | solution.py:64
  51.7 2.8 %collective-permute-start.21 = (bf16[2,112,640]{2,1,0:T(8,128)(2,1)S(1)}, bf16[2,112,640]{2,1,0:T(8,128)(2,1)S(1)}, u32[]{:S(2)}, u32[]{:S(2)}) collective-permute-start(bf16[2,112,640]{2,1,0:T(8,128)(2,1)S(1)} %pad_maximum_fusion.4), channel_id=1, source_target_pairs={{0,6},{32,34},{2,4},{34,32},{4,2},{36,38},{6,0},{38,36},{64,70},{9... | collective-permute-start | bytes 860168 | tf_op jit(solution)/shard_map/ppermute | solution.py:64
  54.5 3.5 %collective-permute-done.7.refs_1_ = bf16[896,256]{1,0:T(8,128)(2,1)S(1)} collective-permute-done((bf16[896,256]{1,0:T(8,128)(2,1)S(1)}, bf16[896,256]{1,0:T(8,128)(2,1)S(1)}, u32[]{:S(2)}, u32[]{:S(2)}) %collective-permute-start.7) | collective-permute-done | bytes 458784 | tf_op jit(solution)/shard_map/ppermute | solution.py:64
  58.2 2.9 %collective-permute-done.21 = bf16[2,112,640]{2,1,0:T(8,128)(2,1)S(1)} collective-permute-done((bf16[2,112,640]{2,1,0:T(8,128)(2,1)S(1)}, bf16[2,112,640]{2,1,0:T(8,128)(2,1)S(1)}, u32[]{:S(2)}, u32[]{:S(2)}) %collective-permute-start.21) | collective-permute-done | bytes 286752 | tf_op jit(solution)/shard_map/ppermute | solution.py:64
  62.5 2.0 %collective-permute-start.1 = (bf16[2,256,896]{2,1,0:T(8,128)(2,1)S(1)}, bf16[2,256,896]{2,1,0:T(8,128)(2,1)S(1)}, u32[]{:S(2)}, u32[]{:S(2)}) collective-permute-start(bf16[2,256,896]{2,1,0:T(8,128)(2,1)S(1)} %get-tuple-element.14.own_far), channel_id=1, source_target_pairs={{0,64},{32,96},{2,66},{34,98},{4,68},{36,100},{6,70},{38,102},{64,... | collective-permute-start | bytes 2752520 | tf_op jit(solution)/shard_map/ppermute | solution.py:64
  66.0 1.0 shard_map.93
  67.2 3.1 %collective-permute-start.9 = (bf16[2,144,128]{2,1,0:T(8,128)(2,1)S(1)}, bf16[2,144,128]{2,1,0:T(8,128)(2,1)S(1)}, u32[]{:S(2)}, u32[]{:S(2)}) collective-permute-start(bf16[2,144,128]{2,1,0:T(8,128)(2,1)S(1)} %maximum_select_fusion.10), channel_id=1, source_target_pairs={{0,65},{32,97},{2,67},{34,99},{4,69},{36,101},{6,71},{38,103},{64,... | collective-permute-start | bytes 221192 | tf_op jit(solution)/shard_map/ppermute | solution.py:64
  70.3 0.8 slice_select_fusion
  71.2 11.4 %collective-permute-done.1.mate_far = bf16[2,256,896]{2,1,0:T(8,128)(2,1)S(1)} collective-permute-done((bf16[2,256,896]{2,1,0:T(8,128)(2,1)S(1)}, bf16[2,256,896]{2,1,0:T(8,128)(2,1)S(1)}, u32[]{:S(2)}, u32[]{:S(2)}) %collective-permute-start.1) | collective-permute-done | bytes 917536 | tf_op jit(solution)/shard_map/ppermute | solution.py:64
  82.6 1.0 copy-done
  84.9 4.2 %collective-permute-done.16 = bf16[2,2,64,128]{3,2,1,0:T(8,128)(2,1)S(1)} collective-permute-done((bf16[2,2,64,128]{3,2,1,0:T(8,128)(2,1)S(1)}, bf16[2,2,64,128]{3,2,1,0:T(8,128)(2,1)S(1)}, u32[]{:S(2)}, u32[]{:S(2)}) %collective-permute-start.16) | collective-permute-done | bytes 65568 | tf_op jit(solution)/shard_map/ppermute | solution.py:64
  89.1 3.6 %collective-permute-start.17 = (bf16[2,2,2,64,128]{4,3,2,1,0:T(8,128)(2,1)S(1)}, bf16[2,2,2,64,128]{4,3,2,1,0:T(8,128)(2,1)S(1)}, u32[]{:S(2)}, u32[]{:S(2)}) collective-permute-start(bf16[2,2,2,64,128]{4,3,2,1,0:T(8,128)(2,1)S(1)} %pad_maximum_fusion.7), channel_id=1, source_target_pairs={{0,6},{32,34},{2,4},{34,32},{4,2},{36,38},{6,0},{38,36},{64,70},{9... | collective-permute-start | bytes 393224 | tf_op jit(solution)/shard_map/ppermute | solution.py:64
  94.2 1.5 collective-permute-done.17
  95.7 0.9 fusion.5
  96.6 1.7 maximum_select_fusion.2.refs_0_
  98.2 1.8 %collective-permute-start.23 = (bf16[896,640]{1,0:T(8,128)(2,1)S(1)}, bf16[896,640]{1,0:T(8,128)(2,1)}, u32[]{:S(2)}, u32[]{:S(2)}) collective-permute-start(bf16[896,640]{1,0:T(8,128)(2,1)S(1)} %maximum_select_fusion.2.refs_0_), channel_id=1, source_target_pairs={{0,24},{32,40},{2,26},{34,42},{4,28},{36,44},{6,30},{38,46},{64,88... | collective-permute-start | bytes 3440648 | tf_op jit(solution)/shard_map/ppermute | solution.py:64
  101.1 1.0 fusion.6
  102.2 1.7 maximum_select_fusion.3.refs_0_
  103.9 2.1 %collective-permute-start.15 = (bf16[896,512]{1,0:T(8,128)(2,1)S(1)}, bf16[896,512]{1,0:T(8,128)(2,1)S(1)}, u32[]{:S(2)}, u32[]{:S(2)}) collective-permute-start(bf16[896,512]{1,0:T(8,128)(2,1)S(1)} %maximum_select_fusion.3.refs_0_), channel_id=1, source_target_pairs={{0,6},{32,34},{2,4},{34,32},{4,2},{36,38},{6,0},{38,36},{64,70},{9... | collective-permute-start | bytes 2752520 | tf_op jit(solution)/shard_map/ppermute | solution.py:64
  106.1 1.9 %maximum_select_fusion.5 = bf16[2,4,2,2,64,128]{5,4,3,2,1,0:T(8,128)(2,1)} fusion(bf16[1,4,2,2,64,128]{5,4,3,2,1,0:T(8,128)(2,1)} %bitcast.50, bf16[1,4,2,2,64,128]{5,4,3,2,1,0:T(8,128)(2,1)} %get-tuple-element.27, pred[]{:T(512)} %bitcast.14), kind=kLoop, calls=%fused_computation.8 | loop fusion | flops 524288 | bytes 1048577 | tf_op jit(solution)/shard_map/jit(_where)/select_n | solution.py:519
  108.0 0.7 slice_bitcast_fusion.4
  110.0 2.8 %collective-permute-done.12 = bf16[4,2,2,80,128]{4,3,2,1,0:T(8,128)(2,1)S(1)} collective-permute-done((bf16[4,2,2,80,128]{4,3,2,1,0:T(8,128)(2,1)S(1)}, bf16[4,2,2,80,128]{4,3,2,1,0:T(8,128)(2,1)S(1)}, u32[]{:S(2)}, u32[]{:S(2)}) %collective-permute-start.12) | collective-permute-done | bytes 327712 | tf_op jit(solution)/shard_map/ppermute | solution.py:64
  112.8 0.9 maximum_select_fusion.4
  113.7 0.7 slice_bitcast_fusion.1
  115.7 3.1 %maximum_select_fusion = bf16[1792,640]{1,0:T(8,128)(2,1)} fusion(bf16[896,640]{1,0:T(8,128)(2,1)} %collective-permute-done.23.refs_1_, bf16[896,640]{1,0:T(8,128)(2,1)S(1)} %maximum_select_fusion.2.refs_0_, pred[]{:T(512)} %bitcast.52), kind=kLoop, calls=%fused_computation | loop fusion | flops 5734400 | bytes 4587521 | tf_op jit(solution)/shard_map/jit(_where)/select_n | solution.py:540
  118.7 1.7 maximum_select_fusion.1
  120.9 3.1 %collective-permute-start.13 = (bf16[2,4,2,2,80,128]{5,4,3,2,1,0:T(8,128)(2,1)}, bf16[2,4,2,2,80,128]{5,4,3,2,1,0:T(8,128)(2,1)}, u32[]{:S(2)}, u32[]{:S(2)}) collective-permute-start(bf16[2,4,2,2,80,128]{5,4,3,2,1,0:T(8,128)(2,1)} %maximum_select_fusion.4), channel_id=1, source_target_pairs={{0,6},{32,34},{2,4},{34,32},{4,2},{36,38},{6,0},{38,36},{64,70},{9... | collective-permute-start | bytes 1966088 | tf_op jit(solution)/shard_map/ppermute | solution.py:64
  124.0 1.7 collective-permute-start.25
  127.0 2.0 %concatenate.119.info_ref = s32[68]{0:T(128)} concatenate(s32[1]{0:T(128)} %bitcast, s32[1]{0:T(128)} %bitcast.61, s32[1]{0:T(128)} %bitcast.3, s32[1]{0:T(128)} %bitcast.62, s32[32]{0:T(128)} %get-tuple-element.40, s32[32]{0:T(128)} %get-tuple-element.39), dimensions={0} | concatenate | bytes 544 | tf_op jit(solution)/shard_map/concatenate | solution.py:547
  128.9 1.6 slice_reduce_fusion.1
  130.5 1.3 reshape_squeeze.6
  131.8 1.2 collective-permute-done.13
  133.0 1.6 slice_reduce_fusion
  134.6 1.3 reshape_squeeze.7
  135.9 0.7 maximum_convert_fusion.count_ref
  136.6 1.2 copy-done.1
  137.8 1.2 copy-done.5
  139.0 1.2 copy-done.7
  140.8 4.5 %shard_map.94.part_ref = bf16[512,512]{1,0:T(8,128)(2,1)S(1)} custom-call(s32[5]{0:T(128)S(1)} %copy-done.14, bf16[2,416,896]{2,1,0:T(8,128)(2,1)} %get-tuple-element.13.own_near, bf16[2,256,896]{2,1,0:T(8,128)(2,1)S(1)} %copy-done.5, bf16[2,416,896]{2,1,0:T(8,128)(2,1)S(1)} %collective-permute-done.mate_near, bf16[2,256,896]{2,1,0:T(8,128)(2,1)S(1)} %copy-done.1, ...), custom_call_target="tpu_custom_call" | custom-call | tf_op jit(solution)/shard_map/pallas_call | solution.py:373
  145.4 5.9 %shard_map.95.more_ref = bf16[512,640]{1,0:T(8,128)(2,1)S(1)} custom-call(s32[5]{0:T(128)S(1)} %copy-done.14, bf16[2,416,896]{2,1,0:T(8,128)(2,1)} %get-tuple-element.13.own_near, bf16[2,256,896]{2,1,0:T(8,128)(2,1)S(1)} %copy-done.5, bf16[2,416,896]{2,1,0:T(8,128)(2,1)S(1)} %collective-permute-done.mate_near, bf16[2,256,896]{2,1,0:T(8,128)(2,1)S(1)} %copy-done.1, ...), custom_call_target="tpu_custom_call" | custom-call | tf_op jit(solution)/shard_map/pallas_call | solution.py:373
  151.4 7.0 %shard_map.97 = bf16[256,896]{1,0:T(8,128)(2,1)S(1)} custom-call(s32[68]{0:T(128)S(1)} %copy-done.17, s32[64]{0:T(128)S(1)} %maximum_convert_fusion.count_ref, bf16[512,512]{1,0:T(8,128)(2,1)S(1)} %shard_map.94.part_ref, bf16[512,640]{1,0:T(8,128)(2,1)S(1)} %shard_map.95.more_ref, bf16[16,2,80,128]{3,2,1,0:T(8,128)(2,1)} %bitcast.36.rest_0_, ...), custom_call_target="tpu_custom_call" | custom-call | tf_op jit(solution)/shard_map/pallas_call | solution.py:285
  158.5 2.9 %collective-permute-start.26 = (bf16[256,896]{1,0:T(8,128)(2,1)S(1)}, bf16[256,896]{1,0:T(8,128)(2,1)S(1)}, u32[]{:S(2)}, u32[]{:S(2)}) collective-permute-start(bf16[256,896]{1,0:T(8,128)(2,1)S(1)} %shard_map.97), channel_id=1, source_target_pairs={{0,64},{32,96},{2,66},{34,98},{4,68},{36,100},{6,70},{38,102},{64,... | collective-permute-start | bytes 1376264 | tf_op jit(solution)/shard_map/ppermute | solution.py:64
  161.4 1.0 copy-done.3
  163.1 8.9 %shard_map.96 = bf16[256,1792]{1,0:T(8,128)(2,1)} custom-call(s32[68]{0:T(128)S(1)} %concatenate.93.info_ref, s32[64]{0:T(128)S(1)} %copy-done.16, bf16[512,512]{1,0:T(8,128)(2,1)S(1)} %copy-done.3, bf16[512,640]{1,0:T(8,128)(2,1)S(1)} %shard_map.95.more_ref, bf16[16,2,80,128]{3,2,1,0:T(8,128)(2,1)} %bitcast.36.rest_0_, ...), custom_call_target="tpu_custom_call" | custom-call | tf_op jit(solution)/shard_map/pallas_call | solution.py:285
  172.0 0.8 bitcast_dynamic-update-slice_fusion
  (114 shorter events, 11.3 us)
Async XLA Ops:
  0.0 19.1 %copy-start.8 = (bf16[1,256,3584]{2,1,0:T(8,128)(2,1)S(1)}, bf16[1,256,3584]{2,1,0:T(8,128)(2,1)}, u32[]{:S(2)}) copy-start(bf16[1,256,3584]{2,1,0:T(8,128)(2,1)} %param.9) | copy-start | bytes 5505028
  0.0 1.0 copy-start.9
  1.0 0.7 copy-start.10
  1.8 0.7 copy-start.11
  2.5 0.7 copy-start.12
  3.2 0.7 copy-start.13
  3.9 4.6 %collective-permute-start.2 = (bf16[28,1408]{1,0:T(8,128)(2,1)S(1)}, bf16[28,1408]{1,0:T(8,128)(2,1)S(1)}, u32[]{:S(2)}, u32[]{:S(2)}) collective-permute-start(bf16[28,1408]{1,0:T(8,128)(2,1)S(1)} %get-tuple-element.16), channel_id=1, source_target_pairs={{0,64},{32,96},{2,66},{34,98},{4,68},{36,100},{6,70},{38,102},{64,... | collective-permute-start | bytes 236552 | tf_op jit(solution)/shard_map/ppermute | solution.py:64
  8.6 6.5 %collective-permute-start.3 = (bf16[56,1408]{1,0:T(8,128)(2,1)S(1)}, bf16[56,1408]{1,0:T(8,128)(2,1)S(1)}, u32[]{:S(2)}, u32[]{:S(2)}) collective-permute-start(bf16[56,1408]{1,0:T(8,128)(2,1)S(1)} %maximum_select_fusion.8), channel_id=1, source_target_pairs={{0,65},{32,97},{2,67},{34,99},{4,69},{36,101},{6,71},{38,103},{64,... | collective-permute-start | bytes 473096 | tf_op jit(solution)/shard_map/ppermute | solution.py:64
  16.0 13.4 %collective-permute-start.4 = (bf16[112,768]{1,0:T(8,128)(2,1)}, bf16[112,768]{1,0:T(8,128)(2,1)}, u32[]{:S(2)}, u32[]{:S(2)}) collective-permute-start(bf16[112,768]{1,0:T(8,128)(2,1)} %get-tuple-element.26), channel_id=1, source_target_pairs={{0,8},{32,56},{2,10},{34,58},{4,12},{36,60},{6,14},{38,62},{64,72}... | collective-permute-start | bytes 516104 | tf_op jit(solution)/shard_map/ppermute | solution.py:64
  25.9 36.6 %copy-start.4 = (bf16[2,256,896]{2,1,0:T(8,128)(2,1)}, bf16[2,256,896]{2,1,0:T(8,128)(2,1)S(1)}, u32[]{:S(2)}) copy-start(bf16[2,256,896]{2,1,0:T(8,128)(2,1)S(1)} %get-tuple-element.14.own_far) | copy-start | bytes 2752516
  25.9 3.5 %copy-start.18 = (bf16[1,112,768]{2,1,0:T(8,128)(2,1)S(1)}, bf16[1,112,768]{2,1,0:T(8,128)(2,1)}, u32[]{:S(2)}) copy-start(bf16[1,112,768]{2,1,0:T(8,128)(2,1)} %get-tuple-element.25) | copy-start | bytes 516100
  25.9 35.3 %collective-permute-start = (bf16[2,416,896]{2,1,0:T(8,128)(2,1)}, bf16[2,416,896]{2,1,0:T(8,128)(2,1)S(1)}, u32[]{:S(2)}, u32[]{:S(2)}) collective-permute-start(bf16[2,416,896]{2,1,0:T(8,128)(2,1)} %get-tuple-element.13.own_near), channel_id=1, source_target_pairs={{0,64},{32,96},{2,66},{34,98},{4,68},{36,100},{6,70},{38,102},{64,... | collective-permute-start | bytes 4472840 | tf_op jit(solution)/shard_map/ppermute | solution.py:64
  30.4 8.5 %collective-permute-start.5 = (bf16[2,112,768]{2,1,0:T(8,128)(2,1)S(1)}, bf16[2,112,768]{2,1,0:T(8,128)(2,1)S(1)}, u32[]{:S(2)}, u32[]{:S(2)}) collective-permute-start(bf16[2,112,768]{2,1,0:T(8,128)(2,1)S(1)} %pad_maximum_fusion.2), channel_id=1, source_target_pairs={{0,24},{32,40},{2,26},{34,42},{4,28},{36,44},{6,30},{38,46},{64,88... | collective-permute-start | bytes 1032200 | tf_op jit(solution)/shard_map/ppermute | solution.py:64
  39.0 8.0 %collective-permute-start.6 = (bf16[448,256]{1,0:T(8,128)(2,1)S(1)}, bf16[448,256]{1,0:T(8,128)(2,1)S(1)}, u32[]{:S(2)}, u32[]{:S(2)}) collective-permute-start(bf16[448,256]{1,0:T(8,128)(2,1)S(1)} %slice.162), channel_id=1, source_target_pairs={{0,2},{32,38},{2,0},{34,36},{4,6},{36,34},{6,4},{38,32},{64,66},{9... | collective-permute-start | bytes 688136 | tf_op jit(solution)/shard_map/ppermute | solution.py:64
  41.0 10.7 %collective-permute-start.20 = (bf16[112,640]{1,0:T(8,128)(2,1)S(1)}, bf16[112,640]{1,0:T(8,128)(2,1)S(1)}, u32[]{:S(2)}, u32[]{:S(2)}) collective-permute-start(bf16[112,640]{1,0:T(8,128)(2,1)S(1)} %get-tuple-element.24), channel_id=1, source_target_pairs={{0,2},{32,38},{2,0},{34,36},{4,6},{36,34},{6,4},{38,32},{64,66},{9... | collective-permute-start | bytes 430088 | tf_op jit(solution)/shard_map/ppermute | solution.py:64
  47.2 10.9 %collective-permute-start.7 = (bf16[896,256]{1,0:T(8,128)(2,1)S(1)}, bf16[896,256]{1,0:T(8,128)(2,1)S(1)}, u32[]{:S(2)}, u32[]{:S(2)}) collective-permute-start(bf16[896,256]{1,0:T(8,128)(2,1)S(1)} %maximum_select_fusion.6.refs_0_), channel_id=1, source_target_pairs={{0,6},{32,34},{2,4},{34,32},{4,2},{36,38},{6,0},{38,36},{64,70},{9... | collective-permute-start | bytes 1376264 | tf_op jit(solution)/shard_map/ppermute | solution.py:64
  51.7 9.4 %collective-permute-start.21 = (bf16[2,112,640]{2,1,0:T(8,128)(2,1)S(1)}, bf16[2,112,640]{2,1,0:T(8,128)(2,1)S(1)}, u32[]{:S(2)}, u32[]{:S(2)}) collective-permute-start(bf16[2,112,640]{2,1,0:T(8,128)(2,1)S(1)} %pad_maximum_fusion.4), channel_id=1, source_target_pairs={{0,6},{32,34},{2,4},{34,32},{4,2},{36,38},{6,0},{38,36},{64,70},{9... | collective-permute-start | bytes 860168 | tf_op jit(solution)/shard_map/ppermute | solution.py:64
  58.1 6.5 %collective-permute-start.8 = (bf16[1792,256]{1,0:T(8,128)(2,1)S(1)}, bf16[1792,256]{1,0:T(8,128)(2,1)S(1)}, u32[]{:S(2)}, u32[]{:S(2)}) collective-permute-start(bf16[1792,256]{1,0:T(8,128)(2,1)S(1)} %pad_maximum_fusion.1), channel_id=1, source_target_pairs={{0,32},{32,0},{2,34},{34,2},{4,36},{36,4},{6,38},{38,6},{64,96},{9... | collective-permute-start | bytes 2752520 | tf_op jit(solution)/shard_map/ppermute | solution.py:64
  62.5 20.1 %collective-permute-start.1 = (bf16[2,256,896]{2,1,0:T(8,128)(2,1)S(1)}, bf16[2,256,896]{2,1,0:T(8,128)(2,1)S(1)}, u32[]{:S(2)}, u32[]{:S(2)}) collective-permute-start(bf16[2,256,896]{2,1,0:T(8,128)(2,1)S(1)} %get-tuple-element.14.own_far), channel_id=1, source_target_pairs={{0,64},{32,96},{2,66},{34,98},{4,68},{36,100},{6,70},{38,102},{64,... | collective-permute-start | bytes 2752520 | tf_op jit(solution)/shard_map/ppermute | solution.py:64
  65.8 30.7 %collective-permute-start.22 = (bf16[448,640]{1,0:T(8,128)(2,1)S(1)}, bf16[448,640]{1,0:T(8,128)(2,1)}, u32[]{:S(2)}, u32[]{:S(2)}) collective-permute-start(bf16[448,640]{1,0:T(8,128)(2,1)S(1)} %bitcast.90), channel_id=1, source_target_pairs={{0,8},{32,56},{2,10},{34,58},{4,12},{36,60},{6,14},{38,62},{64,72}... | collective-permute-start | bytes 1720328 | tf_op jit(solution)/shard_map/ppermute | solution.py:64
  67.2 17.5 %collective-permute-start.9 = (bf16[2,144,128]{2,1,0:T(8,128)(2,1)S(1)}, bf16[2,144,128]{2,1,0:T(8,128)(2,1)S(1)}, u32[]{:S(2)}, u32[]{:S(2)}) collective-permute-start(bf16[2,144,128]{2,1,0:T(8,128)(2,1)S(1)} %maximum_select_fusion.10), channel_id=1, source_target_pairs={{0,65},{32,97},{2,67},{34,99},{4,69},{36,101},{6,71},{38,103},{64,... | collective-permute-start | bytes 221192 | tf_op jit(solution)/shard_map/ppermute | solution.py:64
  71.1 31.1 %collective-permute-start.14 = (bf16[448,512]{1,0:T(8,128)(2,1)}, bf16[448,512]{1,0:T(8,128)(2,1)}, u32[]{:S(2)}, u32[]{:S(2)}) collective-permute-start(bf16[448,512]{1,0:T(8,128)(2,1)} %slice_select_fusion), channel_id=1, source_target_pairs={{0,2},{32,38},{2,0},{34,36},{4,6},{36,34},{6,4},{38,32},{64,66},{9... | collective-permute-start | bytes 1376264 | tf_op jit(solution)/shard_map/ppermute | solution.py:64
  82.6 1.0 copy-start
  84.7 4.4 %collective-permute-start.16 = (bf16[2,2,64,128]{3,2,1,0:T(8,128)(2,1)S(1)}, bf16[2,2,64,128]{3,2,1,0:T(8,128)(2,1)S(1)}, u32[]{:S(2)}, u32[]{:S(2)}) collective-permute-start(bf16[2,2,64,128]{3,2,1,0:T(8,128)(2,1)S(1)} %pad_maximum_fusion.9), channel_id=1, source_target_pairs={{0,2},{32,38},{2,0},{34,36},{4,6},{36,34},{6,4},{38,32},{64,66},{9... | collective-permute-start | bytes 196616 | tf_op jit(solution)/shard_map/ppermute | solution.py:64
  84.8 9.3 %collective-permute-start.10 = (bf16[2,2,80,128]{3,2,1,0:T(8,128)(2,1)S(1)}, bf16[2,2,80,128]{3,2,1,0:T(8,128)(2,1)S(1)}, u32[]{:S(2)}, u32[]{:S(2)}) collective-permute-start(bf16[2,2,80,128]{3,2,1,0:T(8,128)(2,1)S(1)} %fusion), channel_id=1, source_target_pairs={{0,8},{32,56},{2,10},{34,58},{4,12},{36,60},{6,14},{38,62},{64,72}... | collective-permute-start | bytes 245768 | tf_op jit(solution)/shard_map/ppermute | solution.py:64
  89.1 6.6 %collective-permute-start.17 = (bf16[2,2,2,64,128]{4,3,2,1,0:T(8,128)(2,1)S(1)}, bf16[2,2,2,64,128]{4,3,2,1,0:T(8,128)(2,1)S(1)}, u32[]{:S(2)}, u32[]{:S(2)}) collective-permute-start(bf16[2,2,2,64,128]{4,3,2,1,0:T(8,128)(2,1)S(1)} %pad_maximum_fusion.7), channel_id=1, source_target_pairs={{0,6},{32,34},{2,4},{34,32},{4,2},{36,38},{6,0},{38,36},{64,70},{9... | collective-permute-start | bytes 393224 | tf_op jit(solution)/shard_map/ppermute | solution.py:64
  94.1 7.0 %collective-permute-start.11 = (bf16[2,2,2,80,128]{4,3,2,1,0:T(8,128)(2,1)S(1)}, bf16[2,2,2,80,128]{4,3,2,1,0:T(8,128)(2,1)}, u32[]{:S(2)}, u32[]{:S(2)}) collective-permute-start(bf16[2,2,2,80,128]{4,3,2,1,0:T(8,128)(2,1)S(1)} %pad_maximum_fusion.6), channel_id=1, source_target_pairs={{0,24},{32,40},{2,26},{34,42},{4,28},{36,44},{6,30},{38,46},{64,88... | collective-permute-start | bytes 491528 | tf_op jit(solution)/shard_map/ppermute | solution.py:64
  96.6 9.6 %collective-permute-start.18 = (bf16[4,2,2,64,128]{4,3,2,1,0:T(8,128)(2,1)}, bf16[4,2,2,64,128]{4,3,2,1,0:T(8,128)(2,1)}, u32[]{:S(2)}, u32[]{:S(2)}) collective-permute-start(bf16[4,2,2,64,128]{4,3,2,1,0:T(8,128)(2,1)} %get-tuple-element.28), channel_id=1, source_target_pairs={{0,8},{32,56},{2,10},{34,58},{4,12},{36,60},{6,14},{38,62},{64,72}... | collective-permute-start | bytes 786440 | tf_op jit(solution)/shard_map/ppermute | solution.py:64
  98.2 17.4 %collective-permute-start.23 = (bf16[896,640]{1,0:T(8,128)(2,1)S(1)}, bf16[896,640]{1,0:T(8,128)(2,1)}, u32[]{:S(2)}, u32[]{:S(2)}) collective-permute-start(bf16[896,640]{1,0:T(8,128)(2,1)S(1)} %maximum_select_fusion.2.refs_0_), channel_id=1, source_target_pairs={{0,24},{32,40},{2,26},{34,42},{4,28},{36,44},{6,30},{38,46},{64,88... | collective-permute-start | bytes 3440648 | tf_op jit(solution)/shard_map/ppermute | solution.py:64
  102.1 10.7 %collective-permute-start.12 = (bf16[4,2,2,80,128]{4,3,2,1,0:T(8,128)(2,1)S(1)}, bf16[4,2,2,80,128]{4,3,2,1,0:T(8,128)(2,1)S(1)}, u32[]{:S(2)}, u32[]{:S(2)}) collective-permute-start(bf16[4,2,2,80,128]{4,3,2,1,0:T(8,128)(2,1)S(1)} %get-tuple-element.22), channel_id=1, source_target_pairs={{0,2},{32,38},{2,0},{34,36},{4,6},{36,34},{6,4},{38,32},{64,66},{9... | collective-permute-start | bytes 983048 | tf_op jit(solution)/shard_map/ppermute | solution.py:64
  103.9 14.9 %collective-permute-start.15 = (bf16[896,512]{1,0:T(8,128)(2,1)S(1)}, bf16[896,512]{1,0:T(8,128)(2,1)S(1)}, u32[]{:S(2)}, u32[]{:S(2)}) collective-permute-start(bf16[896,512]{1,0:T(8,128)(2,1)S(1)} %maximum_select_fusion.3.refs_0_), channel_id=1, source_target_pairs={{0,6},{32,34},{2,4},{34,32},{4,2},{36,38},{6,0},{38,36},{64,70},{9... | collective-permute-start | bytes 2752520 | tf_op jit(solution)/shard_map/ppermute | solution.py:64
  118.7 26.7 %collective-permute-start.24 = (bf16[1792,640]{1,0:T(8,128)(2,1)}, bf16[1792,640]{1,0:T(8,128)(2,1)}, u32[]{:S(2)}, u32[]{:S(2)}) collective-permute-start(bf16[1792,640]{1,0:T(8,128)(2,1)} %maximum_select_fusion), channel_id=1, source_target_pairs={{0,32},{32,0},{2,34},{34,2},{4,36},{36,4},{6,38},{38,6},{64,96},{9... | collective-permute-start | bytes 6881288 | tf_op jit(solution)/shard_map/ppermute | solution.py:64
  118.7 1.7 copy-start.6
  120.4 16.2 %collective-permute-start.19 = (bf16[1792,512]{1,0:T(8,128)(2,1)}, bf16[1792,512]{1,0:T(8,128)(2,1)}, u32[]{:S(2)}, u32[]{:S(2)}) collective-permute-start(bf16[1792,512]{1,0:T(8,128)(2,1)} %maximum_select_fusion.1), channel_id=1, source_target_pairs={{0,32},{32,0},{2,34},{34,2},{4,36},{36,4},{6,38},{38,6},{64,96},{9... | collective-permute-start | bytes 5505032 | tf_op jit(solution)/shard_map/ppermute | solution.py:64
  120.9 12.1 %collective-permute-start.13 = (bf16[2,4,2,2,80,128]{5,4,3,2,1,0:T(8,128)(2,1)}, bf16[2,4,2,2,80,128]{5,4,3,2,1,0:T(8,128)(2,1)}, u32[]{:S(2)}, u32[]{:S(2)}) collective-permute-start(bf16[2,4,2,2,80,128]{5,4,3,2,1,0:T(8,128)(2,1)} %maximum_select_fusion.4), channel_id=1, source_target_pairs={{0,6},{32,34},{2,4},{34,32},{4,2},{36,38},{6,0},{38,36},{64,70},{9... | collective-permute-start | bytes 1966088 | tf_op jit(solution)/shard_map/ppermute | solution.py:64
  124.0 27.4 %collective-permute-start.25 = (bf16[2,4,2,2,64,128]{5,4,3,2,1,0:T(8,128)(2,1)}, bf16[2,4,2,2,64,128]{5,4,3,2,1,0:T(8,128)(2,1)}, u32[]{:S(2)}, u32[]{:S(2)}) collective-permute-start(bf16[2,4,2,2,64,128]{5,4,3,2,1,0:T(8,128)(2,1)} %maximum_select_fusion.5), channel_id=1, source_target_pairs={{0,24},{32,40},{2,26},{34,42},{4,28},{36,44},{6,30},{38,46},{64,88... | collective-permute-start | bytes 1572872 | tf_op jit(solution)/shard_map/ppermute | solution.py:64
  136.6 14.7 %copy-start.15 = (s32[64]{0:T(128)}, s32[64]{0:T(128)S(1)}, u32[]{:S(2)}) copy-start(s32[64]{0:T(128)S(1)} %maximum_convert_fusion.count_ref) | copy-start | bytes 772
  136.6 1.2 copy-start.1
  137.8 1.2 copy-start.5
  139.0 1.2 copy-start.7
  140.2 0.7 copy-start.14
  145.4 6.0 %copy-start.2 = (bf16[512,512]{1,0:T(8,128)(2,1)}, bf16[512,512]{1,0:T(8,128)(2,1)S(1)}, u32[]{:S(2)}) copy-start(bf16[512,512]{1,0:T(8,128)(2,1)S(1)} %shard_map.94.part_ref) | copy-start | bytes 1572868
  145.4 6.0 %copy-start.17 = (s32[68]{0:T(128)S(1)}, s32[68]{0:T(128)}, u32[]{:S(2)}) copy-start(s32[68]{0:T(128)} %concatenate.119.info_ref) | copy-start | bytes 820
  151.4 10.0 %copy-start.19 = (s32[32]{0:T(128)S(1)}, s32[32]{0:T(128)}, u32[]{:S(2)}) copy-start(s32[32]{0:T(128)} %get-tuple-element.39) | copy-start | bytes 388
  151.4 10.0 %copy-start.20 = (s32[32]{0:T(128)S(1)}, s32[32]{0:T(128)}, u32[]{:S(2)}) copy-start(s32[32]{0:T(128)} %get-tuple-element.40) | copy-start | bytes 388
  158.5 13.5 %collective-permute-start.26 = (bf16[256,896]{1,0:T(8,128)(2,1)S(1)}, bf16[256,896]{1,0:T(8,128)(2,1)S(1)}, u32[]{:S(2)}, u32[]{:S(2)}) collective-permute-start(bf16[256,896]{1,0:T(8,128)(2,1)S(1)} %shard_map.97), channel_id=1, source_target_pairs={{0,64},{32,96},{2,66},{34,98},{4,68},{36,100},{6,70},{38,102},{64,... | collective-permute-start | bytes 1376264 | tf_op jit(solution)/shard_map/ppermute | solution.py:64
  161.4 1.0 copy-start.3
  162.5 0.6 copy-start.16

commit v9 on v6

--- a/solution.py
+++ b/solution.py
@@ -165,7 +165,8 @@
 LINES = HEADS * TOK
 
 
-def attend_body(wide, info_ref, count_ref, part_ref, more_ref, far_k_ref, far_v_ref, *rest):
+def attend_body(wide, info_ref, count_ref, part_ref, more_ref, *rest):
+    far_k_refs, far_v_refs, rest = rest[:2], rest[2:4], rest[4:]
     out_ref, query_ref, keys_ref, values_ref, bias_ref, score_ref, top_ref, sum_ref, mix_ref = rest
     span, valid, column, which = info_ref[0], info_ref[1], info_ref[2], info_ref[3]
     own = slice(0, TOK) if wide else slice(TOK, 2 * TOK)
@@ -177,8 +178,16 @@
         place_k, place_v = info_ref[4 + i], info_ref[4 + SPANS + i]
         count = count_ref[place_k * 2 + which]
         here = pl.ds(pl.multiple_of(at, 16), SLOTS)
-        keys_ref[here, :] = far_k_ref[place_k, which, :SLOTS, :]
-        values_ref[here, :] = far_v_ref[place_v, which]
+        for j in range(2):
+
+            @pl.when(place_k // (SPANS // 2) == j)
+            def _():
+                keys_ref[here, :] = far_k_refs[j][place_k % (SPANS // 2), which, :SLOTS, :]
+
+            @pl.when(place_v // (SPANS // 2) == j)
+            def _():
+                values_ref[here, :] = far_v_refs[j][place_v % (SPANS // 2), which]
+
         bias_ref[...] = jnp.where((lane >= at) & (lane < at + count), 0.0, bias_ref[...])
         return at + ((count + 15) // 16) * 16
 
@@ -270,13 +279,13 @@
             out_ref[:, head * D : (head + 1) * D] = result
 
 
-def attend(wide, info, counts, part, more, far_k, far_v):
+def attend(wide, info, counts, part, more, far):
     columns = 2 * HEADS * D if wide else HEADS * D
     smem, vmem = pl.BlockSpec(memory_space=pltpu.SMEM), pl.BlockSpec(memory_space=pltpu.VMEM)
     return pl.pallas_call(
         functools.partial(attend_body, wide),
         out_shape=jax.ShapeDtypeStruct((TOK, columns), jnp.bfloat16),
-        in_specs=[smem, smem, vmem, vmem, vmem, vmem],
+        in_specs=[smem, smem] + [vmem] * 6,
         out_specs=vmem,
         scratch_shapes=[
             pltpu.VMEM((LINES, D), jnp.bfloat16),
@@ -289,7 +298,7 @@
             pltpu.VMEM((LINES, D), jnp.float32),
         ],
         compiler_params=pltpu.CompilerParams(vmem_limit_bytes=28 * 1024 * 1024),
-    )(info, counts, part, more, far_k, far_v)
+    )(info, counts, part, more, *far)
 
 
 def project_body(count, slab_ref, x_ref, *refs):
@@ -498,10 +507,10 @@
     pair_v = jnp.stack([half_v, send(half_v, FLIP["x", 0])])
     mate = project((zero, one), mate_near, near_w)
     pair_k, pair_v = after((pair_k, pair_v), (mate, mate_far))
-    every_k = jnp.concatenate([pair_k, send(pair_k, FLIP["z", 1])])
-    every_v = jnp.concatenate([pair_v, send(pair_v, FLIP["x", 1])])
-    every_k = every_k.reshape(SPANS, 2, SLOTS + 16, D)
-    every_v = every_v.reshape(SPANS, 2, SLOTS, D)
+    every_k = [pair_k, send(pair_k, FLIP["z", 1])]
+    every_v = [pair_v, send(pair_v, FLIP["x", 1])]
+    every_k = [k.reshape(SPANS // 2, 2, SLOTS + 16, D) for k in every_k]
+    every_v = [v.reshape(SPANS // 2, 2, SLOTS, D) for v in every_v]
 
     owner = jnp.arange(SPANS, dtype=jnp.int32)
 
@@ -513,7 +522,7 @@
     code_h = (owner ^ span) % 2
     at_k = (code_z * 4 + code_x) * 2 + code_h
     at_v = (code_x * 4 + code_z) * 2 + code_h
-    live = every_k[:, :, SLOTS, 0].astype(jnp.int32).reshape(2 * SPANS)
+    live = jnp.concatenate([k[:, :, SLOTS, 0].reshape(SPANS) for k in every_k]).astype(jnp.int32)
 
     pairs = [pair_of(axis, side)[0] for axis in "xz" for side in (core, 1 - core)]
     part = project_crossed(
@@ -534,8 +543,7 @@
             live,
             part,
             mate if which else own,
-            every_k,
-            every_v,
+            every_k + every_v,
         )
 
     away = send(attention(1, mate_valid, False), MATE)

time: 150 us -> 159 us (1.060)
  Pallas kernels: 29 us -> 34.6 us
  waiting for transfers between devices: 44.6 us -> 48.5 us
  other arithmetic: 11 us -> 9.17 us
  starting transfers between devices: 34.9 us -> 36.5 us
    pallas_call x2, Pallas kernels: 11 us -> 16.1 us  [attend(): pl.pallas_call(functools.partial(attend_body, wide), out_shape=jax.ShapeD...]
    ppermute x28, waiting for transfers between devices: 44.6 us -> 48.5 us  [send(): return lax.ppermute(value, AXES, pairs)]
    unnamed x56 -> x44, local copies, waits for them, and re-layouts: 12.9 us -> 10.4 us
    slice x0 -> x2, local copies, waits for them, and re-layouts: none -> 1.94 us  [on_device(): k[:, :, SLOTS, 0].reshape(SPANS)]
    ppermute x28, starting transfers between devices: 34.9 us -> 36.5 us  [send(): return lax.ppermute(value, AXES, pairs)]
  transfers between devices with their start and end apart: 28 -> 28, of which waited for: 17 -> 15; matrix products, arithmetic and copies ran while one was open for 14% -> 15% of each run, Pallas kernels for 14% -> 17%
where the time goes in v9:
time: 159 us; the launch traced here: 157 us
  waiting for transfers between devices  48.5 us (31%)
  starting transfers between devices  36.5 us (23%)
  Pallas kernels  34.6 us (22%)
  local copies, waits for them, and re-layouts  26 us (16%)
  other arithmetic  9.17 us (6%)
  between operations  2.58 us (2%)
    ppermute x28, waiting for transfers between devices, send(): return lax.ppermute(value, AXES, pairs)  48.5 us
    ppermute x28, starting transfers between devices, send(): return lax.ppermute(value, AXES, pairs)  36.5 us
    pallas_call x2, Pallas kernels, attend(): pl.pallas_call(functools.partial(attend_body, wide), out_shape=jax.ShapeD...  16.1 us
    unnamed x44, local copies, waits for them, and re-layouts  10.4 us
    pallas_call x5, Pallas kernels, project(): pl.pallas_call(functools.partial(project_body, len(weights)), out_shape=j...  9.67 us
    pallas_call x1, Pallas kernels, norm_rows(): pl.pallas_call(norm_body, out_shape=[jax.ShapeDtypeStruct((2, TOK + 2 * (...  5.71 us
    select_n x7, other arithmetic, order(): jnp.where(first == 0, jnp.concatenate([one, two], 0), jnp.concatenate([tw...  4.27 us
  transfers between devices with their start and end apart: 28, of which 15 were waited for; matrix products, arithmetic and copies ran while one was open for 15% of the time, Pallas kernels for 17%

profile of v9, /device:TPU:6, one launch (start us, length us, event | category | flops | bytes accessed | tf_op | source)
XLA Modules:
  0.0 157.3 jit_solution(11108441583002128926)
XLA Ops:
  0.0 0.9 copy-done.16
  0.9 0.7 copy-done.17
  1.6 0.7 copy-done.18
  2.3 0.7 copy-done.19
  3.8 1.6 %collective-permute-start.1 = (bf16[28,1408]{1,0:T(8,128)(2,1)S(1)}, bf16[28,1408]{1,0:T(8,128)(2,1)S(1)}, u32[]{:S(2)}, u32[]{:S(2)}) collective-permute-start(bf16[28,1408]{1,0:T(8,128)(2,1)S(1)} %get-tuple-element.21), channel_id=1, source_target_pairs={{0,64},{32,96},{2,66},{34,98},{4,68},{36,100},{6,70},{38,102},{64,... | collective-permute-start | bytes 236552 | tf_op jit(solution)/shard_map/ppermute | solution.py:64
  5.5 3.0 %collective-permute-done.1 = bf16[28,1408]{1,0:T(8,128)(2,1)S(1)} collective-permute-done((bf16[28,1408]{1,0:T(8,128)(2,1)S(1)}, bf16[28,1408]{1,0:T(8,128)(2,1)S(1)}, u32[]{:S(2)}, u32[]{:S(2)}) %collective-permute-start.1) | collective-permute-done | bytes 78880 | tf_op jit(solution)/shard_map/ppermute | solution.py:64
  8.5 3.1 %collective-permute-start.2 = (bf16[56,1408]{1,0:T(8,128)(2,1)S(1)}, bf16[56,1408]{1,0:T(8,128)(2,1)S(1)}, u32[]{:S(2)}, u32[]{:S(2)}) collective-permute-start(bf16[56,1408]{1,0:T(8,128)(2,1)S(1)} %maximum_select_fusion.4), channel_id=1, source_target_pairs={{0,65},{32,97},{2,67},{34,99},{4,69},{36,101},{6,71},{38,103},{64,... | collective-permute-start | bytes 473096 | tf_op jit(solution)/shard_map/ppermute | solution.py:64
  13.0 0.7 reshape.100.gain_ref
  13.8 1.5 copy-done.15
  15.3 5.7 %shard_map.91 = (bf16[2,416,896]{2,1,0:T(8,128)(2,1)S(1)}, bf16[2,256,896]{2,1,0:T(8,128)(2,1)S(1)}) custom-call(s32[7]{0:T(128)S(1)} %stack.148.fact_ref, bf16[256,3584]{1,0:T(8,128)(2,1)S(1)} %bitcast.69, f32[1,3584]{1,0:T(1,128)S(1)} %reshape.100.gain_ref), custom_call_target="tpu_custom_call" | custom-call | tf_op jit(solution)/shard_map/pallas_call | solution.py:145
  21.1 0.9 copy-done.2
  22.2 0.9 collective-permute-start.3
  23.1 1.9 %collective-permute-start.13 = (bf16[112,640]{1,0:T(8,128)(2,1)S(1)}, bf16[112,640]{1,0:T(8,128)(2,1)S(1)}, u32[]{:S(2)}, u32[]{:S(2)}) collective-permute-start(bf16[112,640]{1,0:T(8,128)(2,1)S(1)} %get-tuple-element.38), channel_id=1, source_target_pairs={{0,2},{32,38},{2,0},{34,36},{4,6},{36,34},{6,4},{38,32},{64,66},{9... | collective-permute-start | bytes 430088 | tf_op jit(solution)/shard_map/ppermute | solution.py:64
  25.1 0.9 broadcast_in_dim.33
  26.7 1.0 collective-permute-done.3
  28.4 4.1 %collective-permute-start.14 = (bf16[2,112,640]{2,1,0:T(8,128)(2,1)S(1)}, bf16[2,112,640]{2,1,0:T(8,128)(2,1)S(1)}, u32[]{:S(2)}, u32[]{:S(2)}) collective-permute-start(bf16[2,112,640]{2,1,0:T(8,128)(2,1)S(1)} %pad_maximum_fusion.7), channel_id=1, source_target_pairs={{0,6},{32,34},{2,4},{34,32},{4,2},{36,38},{6,0},{38,36},{64,70},{9... | collective-permute-start | bytes 860168 | tf_op jit(solution)/shard_map/ppermute | solution.py:64
  32.5 3.8 %collective-permute-done.4 = bf16[2,112,768]{2,1,0:T(8,128)(2,1)S(1)} collective-permute-done((bf16[2,112,768]{2,1,0:T(8,128)(2,1)S(1)}, bf16[2,112,768]{2,1,0:T(8,128)(2,1)S(1)}, u32[]{:S(2)}, u32[]{:S(2)}) %collective-permute-start.4) | collective-permute-done | bytes 344096 | tf_op jit(solution)/shard_map/ppermute | solution.py:64
  36.4 2.0 %collective-permute-start.5 = (bf16[448,256]{1,0:T(8,128)(2,1)S(1)}, bf16[448,256]{1,0:T(8,128)(2,1)S(1)}, u32[]{:S(2)}, u32[]{:S(2)}) collective-permute-start(bf16[448,256]{1,0:T(8,128)(2,1)S(1)} %slice.124), channel_id=1, source_target_pairs={{0,2},{32,38},{2,0},{34,36},{4,6},{36,34},{6,4},{38,32},{64,66},{9... | collective-permute-start | bytes 688136 | tf_op jit(solution)/shard_map/ppermute | solution.py:64
  39.0 4.2 %collective-permute-done.5 = bf16[448,256]{1,0:T(8,128)(2,1)S(1)} collective-permute-done((bf16[448,256]{1,0:T(8,128)(2,1)S(1)}, bf16[448,256]{1,0:T(8,128)(2,1)S(1)}, u32[]{:S(2)}, u32[]{:S(2)}) %collective-permute-start.5) | collective-permute-done | bytes 229408 | tf_op jit(solution)/shard_map/ppermute | solution.py:64
  43.4 4.1 %collective-permute-start.6 = (bf16[896,256]{1,0:T(8,128)(2,1)S(1)}, bf16[896,256]{1,0:T(8,128)(2,1)}, u32[]{:S(2)}, u32[]{:S(2)}) collective-permute-start(bf16[896,256]{1,0:T(8,128)(2,1)S(1)} %maximum_select_fusion.2.refs_0_), channel_id=1, source_target_pairs={{0,6},{32,34},{2,4},{34,32},{4,2},{36,38},{6,0},{38,36},{64,70},{9... | collective-permute-start | bytes 1376264 | tf_op jit(solution)/shard_map/ppermute | solution.py:64
  48.2 0.8 slice.140
  49.7 0.9 slice.89
  50.5 1.8 %slice.118 = bf16[4,64,896]{2,1,0:T(8,128)(2,1)} slice(bf16[4,80,896]{2,1,0:T(8,128)(2,1)} %bitcast.73), slice={[0:4], [0:64], [0:896]} | slice | bytes 917504 | tf_op jit(solution)/shard_map/slice | solution.py:457
  52.4 3.3 %collective-permute-done.6.refs_1_ = bf16[896,256]{1,0:T(8,128)(2,1)} collective-permute-done((bf16[896,256]{1,0:T(8,128)(2,1)S(1)}, bf16[896,256]{1,0:T(8,128)(2,1)}, u32[]{:S(2)}, u32[]{:S(2)}) %collective-permute-start.6) | collective-permute-done | bytes 458784 | tf_op jit(solution)/shard_map/ppermute | solution.py:64
  55.6 1.1 pad_maximum_fusion.2
  56.9 0.9 collective-permute-done.21
  57.8 1.7 %maximum_select_fusion.1.refs_0_ = bf16[896,512]{1,0:T(8,128)(2,1)S(1)} fusion(bf16[448,512]{1,0:T(8,128)(2,1)} %collective-permute-done.21, bf16[448,512]{1,0:T(8,128)(2,1)} %slice.140, pred[]{:T(512)S(6)} %eq.102), kind=kLoop, calls=%fused_computation.4 | loop fusion | flops 4128768 | bytes 1835009 | tf_op jit(solution)/shard_map/jit(_where)/select_n | solution.py:426
  59.7 2.2 %maximum_select_fusion.refs_0_ = bf16[896,640]{1,0:T(8,128)(2,1)S(1)} fusion(bf16[448,640]{1,0:T(8,128)(2,1)} %collective-permute-done.15, bf16[448,640]{1,0:T(8,128)(2,1)} %bitcast.36, pred[]{:T(512)S(6)} %eq.104), kind=kLoop, calls=%fused_computation.1 | loop fusion | flops 5160960 | bytes 2293761 | tf_op jit(solution)/shard_map/jit(_where)/select_n | solution.py:426
  61.9 2.0 %collective-permute-start.23 = (bf16[896,640]{1,0:T(8,128)(2,1)S(1)}, bf16[896,640]{1,0:T(8,128)(2,1)}, u32[]{:S(2)}, u32[]{:S(2)}) collective-permute-start(bf16[896,640]{1,0:T(8,128)(2,1)S(1)} %maximum_select_fusion.refs_0_), channel_id=1, source_target_pairs={{0,24},{32,40},{2,26},{34,42},{4,28},{36,44},{6,30},{38,46},{64,88... | collective-permute-start | bytes 3440648 | tf_op jit(solution)/shard_map/ppermute | solution.py:64
  63.9 3.0 %collective-permute-start.22 = (bf16[896,512]{1,0:T(8,128)(2,1)S(1)}, bf16[896,512]{1,0:T(8,128)(2,1)S(1)}, u32[]{:S(2)}, u32[]{:S(2)}) collective-permute-start(bf16[896,512]{1,0:T(8,128)(2,1)S(1)} %maximum_select_fusion.1.refs_0_), channel_id=1, source_target_pairs={{0,6},{32,34},{2,4},{34,32},{4,2},{36,38},{6,0},{38,36},{64,70},{9... | collective-permute-start | bytes 2752520 | tf_op jit(solution)/shard_map/ppermute | solution.py:64
  68.5 1.5 shard_map.93
  70.1 1.2 collective-permute-start.8
  71.4 4.4 %collective-permute-done.8 = bf16[2,144,128]{2,1,0:T(8,128)(2,1)S(1)} collective-permute-done((bf16[2,144,128]{2,1,0:T(8,128)(2,1)S(1)}, bf16[2,144,128]{2,1,0:T(8,128)(2,1)S(1)}, u32[]{:S(2)}, u32[]{:S(2)}) %collective-permute-start.8) | collective-permute-done | bytes 73760 | tf_op jit(solution)/shard_map/ppermute | solution.py:64
  76.0 4.2 %collective-permute-done.11 = bf16[2,2,64,128]{3,2,1,0:T(8,128)(2,1)S(1)} collective-permute-done((bf16[2,2,64,128]{3,2,1,0:T(8,128)(2,1)S(1)}, bf16[2,2,64,128]{3,2,1,0:T(8,128)(2,1)S(1)}, u32[]{:S(2)}, u32[]{:S(2)}) %collective-permute-start.11) | collective-permute-done | bytes 65568 | tf_op jit(solution)/shard_map/ppermute | solution.py:64
  80.7 1.4 collective-permute-start.10
  82.1 1.5 pad_maximum_fusion
  83.6 1.5 shard_map.94.refs_2_
  85.2 1.4 collective-permute-done.12
  87.4 1.0 collective-permute-start.19
  88.4 1.3 collective-permute-start.18
  89.7 1.9 %collective-permute-start.25 = (bf16[896,640]{1,0:T(8,128)(2,1)}, bf16[896,640]{1,0:T(8,128)(2,1)}, u32[]{:S(2)}, u32[]{:S(2)}) collective-permute-start(bf16[896,640]{1,0:T(8,128)(2,1)} %collective-permute-done.23.refs_0_), channel_id=1, source_target_pairs={{0,32},{32,0},{2,34},{34,2},{4,36},{36,4},{6,38},{38,6},{64,96},{9... | collective-permute-start | bytes 3440648 | tf_op jit(solution)/shard_map/ppermute | solution.py:64
  91.6 1.5 shard_map.95.refs_2_
  93.1 1.6 %collective-permute-done.18 = bf16[4,2,2,64,128]{4,3,2,1,0:T(8,128)(2,1)S(1)} collective-permute-done((bf16[4,2,2,64,128]{4,3,2,1,0:T(8,128)(2,1)S(1)}, bf16[4,2,2,64,128]{4,3,2,1,0:T(8,128)(2,1)S(1)}, u32[]{:S(2)}, u32[]{:S(2)}) %collective-permute-start.18) | collective-permute-done | bytes 262176 | tf_op jit(solution)/shard_map/ppermute | solution.py:64
  94.8 0.9 pad_maximum_fusion.4
  95.6 1.2 collective-permute-done.17
  96.8 0.9 pad_maximum_fusion.3
  97.7 12.4 %collective-permute-done.19.mate_far.x_ref = bf16[2,256,896]{2,1,0:T(8,128)(2,1)S(1)} collective-permute-done((bf16[2,256,896]{2,1,0:T(8,128)(2,1)S(1)}, bf16[2,256,896]{2,1,0:T(8,128)(2,1)S(1)}, u32[]{:S(2)}, u32[]{:S(2)}) %collective-permute-start.19) | collective-permute-done | bytes 917536 | tf_op jit(solution)/shard_map/ppermute | solution.py:64
  110.2 1.0 copy-done.8
  111.2 3.0 %collective-permute-start.20 = (bf16[2,4,2,2,80,128]{5,4,3,2,1,0:T(8,128)(2,1)}, bf16[2,4,2,2,80,128]{5,4,3,2,1,0:T(8,128)(2,1)}, u32[]{:S(2)}, u32[]{:S(2)}) collective-permute-start(bf16[2,4,2,2,80,128]{5,4,3,2,1,0:T(8,128)(2,1)} %pad_maximum_fusion.3), channel_id=1, source_target_pairs={{0,6},{32,34},{2,4},{34,32},{4,2},{36,38},{6,0},{38,36},{64,70},{9... | collective-permute-start | bytes 1966088 | tf_op jit(solution)/shard_map/ppermute | solution.py:64
  114.3 0.8 concatenate.115.info_ref
  115.0 0.9 collective-permute-start.26
  115.9 1.0 slice_reduce_fusion.1
  117.0 6.3 %collective-permute-done.20 = bf16[2,4,2,2,80,128]{5,4,3,2,1,0:T(8,128)(2,1)} collective-permute-done((bf16[2,4,2,2,80,128]{5,4,3,2,1,0:T(8,128)(2,1)}, bf16[2,4,2,2,80,128]{5,4,3,2,1,0:T(8,128)(2,1)}, u32[]{:S(2)}, u32[]{:S(2)}) %collective-permute-start.20) | collective-permute-done | bytes 655392 | tf_op jit(solution)/shard_map/ppermute | solution.py:64
  123.3 1.0 slice_reduce_fusion
  124.5 1.2 copy-done.9
  125.7 1.1 copy-done.14
  126.7 2.6 %shard_map.99.more_ref = bf16[256,640]{1,0:T(8,128)(2,1)S(1)} custom-call(s32[2]{0:T(128)S(1)} %iota.22.slab_ref, bf16[2,256,896]{2,1,0:T(8,128)(2,1)S(1)} %copy-done.9, bf16[896,640]{1,0:T(8,128)(2,1)} %collective-permute-done.23.refs_0_, bf16[896,640]{1,0:T(8,128)(2,1)} %collective-permute-done.25.refs_1_, f32[256,640]{1,0:T(8,128)S(1)} %copy-done.14), custom_call_target="tpu_custom_call" | custom-call | tf_op jit(solution)/shard_map/pallas_call | solution.py:321
  129.4 1.7 %fusion.5 = (bf16[896,512]{1,0:T(8,128)(2,1)S(1)}, bf16[896,512]{1,0:T(8,128)(2,1)S(1)}) fusion(bf16[1792,512]{1,0:T(8,128)(2,1)} %collective-permute-done.24), kind=kLoop, calls=%fused_computation.69 | loop fusion | bytes 3670016 | tf_op jit(solution)/shard_map/slice | solution.py:531
  131.9 3.1 %shard_map.96.part_ref = bf16[512,512]{1,0:T(8,128)(2,1)S(1)} custom-call(s32[5]{0:T(128)S(1)} %stack.175.info_ref, bf16[2,416,896]{2,1,0:T(8,128)(2,1)S(1)} %get-tuple-element.19.x_ref.own_near, bf16[2,256,896]{2,1,0:T(8,128)(2,1)S(1)} %copy-done.4, bf16[2,416,896]{2,1,0:T(8,128)(2,1)S(1)} %collective-permute-done.x_ref.mate_near, ...), custom_call_target="tpu_custom_call" | custom-call | tf_op jit(solution)/shard_map/pallas_call | solution.py:365
  135.1 7.2 %shard_map.100 = bf16[256,896]{1,0:T(8,128)(2,1)S(1)} custom-call(s32[68]{0:T(128)S(1)} %concatenate.115.info_ref, s32[64]{0:T(128)S(1)} %maximum_convert_fusion.count_ref, bf16[512,512]{1,0:T(8,128)(2,1)S(1)} %shard_map.96.part_ref, bf16[256,640]{1,0:T(8,128)(2,1)S(1)} %shard_map.99.more_ref, bf16[16,2,80,128]{3,2,1,0:T(8,128)(2,1)} %bitcast.41.rest_0_, ...), custom_call_target="tpu_custom_call" | custom-call | tf_op jit(solution)/shard_map/pallas_call | solution.py:285
  142.3 1.7 %collective-permute-start.27 = (bf16[256,896]{1,0:T(8,128)(2,1)S(1)}, bf16[256,896]{1,0:T(8,128)(2,1)}, u32[]{:S(2)}, u32[]{:S(2)}) collective-permute-start(bf16[256,896]{1,0:T(8,128)(2,1)S(1)} %shard_map.100), channel_id=1, source_target_pairs={{0,64},{32,96},{2,66},{34,98},{4,68},{36,100},{6,70},{38,102},{64,... | collective-permute-start | bytes 1376264 | tf_op jit(solution)/shard_map/ppermute | solution.py:64
  144.1 2.6 %shard_map.97.more_ref = bf16[256,640]{1,0:T(8,128)(2,1)S(1)} custom-call(s32[2]{0:T(128)S(1)} %iota.21.slab_ref, bf16[2,256,896]{2,1,0:T(8,128)(2,1)S(1)} %copy-done.5, bf16[896,640]{1,0:T(8,128)(2,1)} %collective-permute-done.23.refs_0_, bf16[896,640]{1,0:T(8,128)(2,1)} %collective-permute-done.25.refs_1_, f32[256,640]{1,0:T(8,128)S(1)} %copy-done.12), custom_call_target="tpu_custom_call" | custom-call | tf_op jit(solution)/shard_map/pallas_call | solution.py:321
  146.6 8.9 %shard_map.98 = bf16[256,1792]{1,0:T(8,128)(2,1)} custom-call(s32[68]{0:T(128)S(1)} %concatenate.90.info_ref, s32[64]{0:T(128)S(1)} %maximum_convert_fusion.count_ref, bf16[512,512]{1,0:T(8,128)(2,1)S(1)} %shard_map.96.part_ref, bf16[256,640]{1,0:T(8,128)(2,1)S(1)} %shard_map.97.more_ref, bf16[16,2,80,128]{3,2,1,0:T(8,128)(2,1)} %bitcast.41.rest_0_, ...), custom_call_target="tpu_custom_call" | custom-call | tf_op jit(solution)/shard_map/pallas_call | solution.py:285
  155.5 1.8 %bitcast_dynamic-update-slice_fusion = bf16[1,256,1792]{2,1,0:T(8,128)(2,1)} fusion(bf16[1,256,1792]{2,1,0:T(8,128)(2,1)} %bitcast.81, s32[]{:T(128)S(6)} %select_n.249, bf16[256,896]{1,0:T(8,128)(2,1)} %collective-permute-done.27), kind=kLoop, calls=%fused_computation.8 | loop fusion | bytes 917508 | tf_op jit(solution)/shard_map/dynamic_update_slice | solution.py:551
  (113 shorter events, 9.1 us)
Async XLA Ops:
  0.0 0.9 copy-start.16
  0.9 0.7 copy-start.17
  1.6 0.7 copy-start.18
  2.3 0.7 copy-start.19
  3.1 0.7 copy-start.20
  3.8 4.6 %collective-permute-start.1 = (bf16[28,1408]{1,0:T(8,128)(2,1)S(1)}, bf16[28,1408]{1,0:T(8,128)(2,1)S(1)}, u32[]{:S(2)}, u32[]{:S(2)}) collective-permute-start(bf16[28,1408]{1,0:T(8,128)(2,1)S(1)} %get-tuple-element.21), channel_id=1, source_target_pairs={{0,64},{32,96},{2,66},{34,98},{4,68},{36,100},{6,70},{38,102},{64,... | collective-permute-start | bytes 236552 | tf_op jit(solution)/shard_map/ppermute | solution.py:64
  8.5 13.6 %collective-permute-start.2 = (bf16[56,1408]{1,0:T(8,128)(2,1)S(1)}, bf16[56,1408]{1,0:T(8,128)(2,1)S(1)}, u32[]{:S(2)}, u32[]{:S(2)}) collective-permute-start(bf16[56,1408]{1,0:T(8,128)(2,1)S(1)} %maximum_select_fusion.4), channel_id=1, source_target_pairs={{0,65},{32,97},{2,67},{34,99},{4,69},{36,101},{6,71},{38,103},{64,... | collective-permute-start | bytes 473096 | tf_op jit(solution)/shard_map/ppermute | solution.py:64
  13.8 1.5 copy-start.15
  21.0 0.9 copy-start.2
  22.0 44.9 %collective-permute-start = (bf16[2,416,896]{2,1,0:T(8,128)(2,1)S(1)}, bf16[2,416,896]{2,1,0:T(8,128)(2,1)S(1)}, u32[]{:S(2)}, u32[]{:S(2)}) collective-permute-start(bf16[2,416,896]{2,1,0:T(8,128)(2,1)S(1)} %get-tuple-element.19.x_ref.own_near), channel_id=1, source_target_pairs={{0,64},{32,96},{2,66},{34,98},{4,68},{36,100},{6,70},{38,102},{64,... | collective-permute-start | bytes 4472840 | tf_op jit(solution)/shard_map/ppermute | solution.py:64
  22.2 5.5 %collective-permute-start.3 = (bf16[112,768]{1,0:T(8,128)(2,1)S(1)}, bf16[112,768]{1,0:T(8,128)(2,1)S(1)}, u32[]{:S(2)}, u32[]{:S(2)}) collective-permute-start(bf16[112,768]{1,0:T(8,128)(2,1)S(1)} %get-tuple-element.40), channel_id=1, source_target_pairs={{0,8},{32,56},{2,10},{34,58},{4,12},{36,60},{6,14},{38,62},{64,72}... | collective-permute-start | bytes 516104 | tf_op jit(solution)/shard_map/ppermute | solution.py:64
  23.1 5.2 %collective-permute-start.13 = (bf16[112,640]{1,0:T(8,128)(2,1)S(1)}, bf16[112,640]{1,0:T(8,128)(2,1)S(1)}, u32[]{:S(2)}, u32[]{:S(2)}) collective-permute-start(bf16[112,640]{1,0:T(8,128)(2,1)S(1)} %get-tuple-element.38), channel_id=1, source_target_pairs={{0,2},{32,38},{2,0},{34,36},{4,6},{36,34},{6,4},{38,32},{64,66},{9... | collective-permute-start | bytes 430088 | tf_op jit(solution)/shard_map/ppermute | solution.py:64
  27.8 8.5 %collective-permute-start.4 = (bf16[2,112,768]{2,1,0:T(8,128)(2,1)S(1)}, bf16[2,112,768]{2,1,0:T(8,128)(2,1)S(1)}, u32[]{:S(2)}, u32[]{:S(2)}) collective-permute-start(bf16[2,112,768]{2,1,0:T(8,128)(2,1)S(1)} %pad_maximum_fusion.5), channel_id=1, source_target_pairs={{0,24},{32,40},{2,26},{34,42},{4,28},{36,44},{6,30},{38,46},{64,88... | collective-permute-start | bytes 1032200 | tf_op jit(solution)/shard_map/ppermute | solution.py:64
  28.4 19.2 %collective-permute-start.14 = (bf16[2,112,640]{2,1,0:T(8,128)(2,1)S(1)}, bf16[2,112,640]{2,1,0:T(8,128)(2,1)S(1)}, u32[]{:S(2)}, u32[]{:S(2)}) collective-permute-start(bf16[2,112,640]{2,1,0:T(8,128)(2,1)S(1)} %pad_maximum_fusion.7), channel_id=1, source_target_pairs={{0,6},{32,34},{2,4},{34,32},{4,2},{36,38},{6,0},{38,36},{64,70},{9... | collective-permute-start | bytes 860168 | tf_op jit(solution)/shard_map/ppermute | solution.py:64
  36.4 6.9 %collective-permute-start.5 = (bf16[448,256]{1,0:T(8,128)(2,1)S(1)}, bf16[448,256]{1,0:T(8,128)(2,1)S(1)}, u32[]{:S(2)}, u32[]{:S(2)}) collective-permute-start(bf16[448,256]{1,0:T(8,128)(2,1)S(1)} %slice.124), channel_id=1, source_target_pairs={{0,2},{32,38},{2,0},{34,36},{4,6},{36,34},{6,4},{38,32},{64,66},{9... | collective-permute-start | bytes 688136 | tf_op jit(solution)/shard_map/ppermute | solution.py:64
  43.4 12.2 %collective-permute-start.6 = (bf16[896,256]{1,0:T(8,128)(2,1)S(1)}, bf16[896,256]{1,0:T(8,128)(2,1)}, u32[]{:S(2)}, u32[]{:S(2)}) collective-permute-start(bf16[896,256]{1,0:T(8,128)(2,1)S(1)} %maximum_select_fusion.2.refs_0_), channel_id=1, source_target_pairs={{0,6},{32,34},{2,4},{34,32},{4,2},{36,38},{6,0},{38,36},{64,70},{9... | collective-permute-start | bytes 1376264 | tf_op jit(solution)/shard_map/ppermute | solution.py:64
  49.0 8.8 %collective-permute-start.21 = (bf16[448,512]{1,0:T(8,128)(2,1)}, bf16[448,512]{1,0:T(8,128)(2,1)}, u32[]{:S(2)}, u32[]{:S(2)}) collective-permute-start(bf16[448,512]{1,0:T(8,128)(2,1)} %slice.140), channel_id=1, source_target_pairs={{0,2},{32,38},{2,0},{34,36},{4,6},{36,34},{6,4},{38,32},{64,66},{9... | collective-permute-start | bytes 1376264 | tf_op jit(solution)/shard_map/ppermute | solution.py:64
  49.7 10.0 %collective-permute-start.15 = (bf16[448,640]{1,0:T(8,128)(2,1)}, bf16[448,640]{1,0:T(8,128)(2,1)}, u32[]{:S(2)}, u32[]{:S(2)}) collective-permute-start(bf16[448,640]{1,0:T(8,128)(2,1)} %bitcast.36), channel_id=1, source_target_pairs={{0,8},{32,56},{2,10},{34,58},{4,12},{36,60},{6,14},{38,62},{64,72}... | collective-permute-start | bytes 1720328 | tf_op jit(solution)/shard_map/ppermute | solution.py:64
  56.7 11.7 %collective-permute-start.7 = (bf16[1792,256]{1,0:T(8,128)(2,1)S(1)}, bf16[1792,256]{1,0:T(8,128)(2,1)S(1)}, u32[]{:S(2)}, u32[]{:S(2)}) collective-permute-start(bf16[1792,256]{1,0:T(8,128)(2,1)S(1)} %pad_maximum_fusion.2), channel_id=1, source_target_pairs={{0,32},{32,0},{2,34},{34,2},{4,36},{36,4},{6,38},{38,6},{64,96},{9... | collective-permute-start | bytes 2752520 | tf_op jit(solution)/shard_map/ppermute | solution.py:64
  59.5 22.5 %copy-start = (bf16[896,512]{1,0:T(8,128)(2,1)}, bf16[896,512]{1,0:T(8,128)(2,1)S(1)}, u32[]{:S(2)}) copy-start(bf16[896,512]{1,0:T(8,128)(2,1)S(1)} %maximum_select_fusion.1.refs_0_) | copy-start | bytes 2752516
  59.5 8.8 %copy-start.21 = (bf16[4,64,896]{2,1,0:T(8,128)(2,1)S(1)}, bf16[4,64,896]{2,1,0:T(8,128)(2,1)}, u32[]{:S(2)}) copy-start(bf16[4,64,896]{2,1,0:T(8,128)(2,1)} %slice.118) | copy-start | bytes 1376260
  61.9 21.8 %collective-permute-start.16 = (bf16[896,640]{1,0:T(8,128)(2,1)S(1)}, bf16[896,640]{1,0:T(8,128)(2,1)S(1)}, u32[]{:S(2)}, u32[]{:S(2)}) collective-permute-start(bf16[896,640]{1,0:T(8,128)(2,1)S(1)} %maximum_select_fusion.refs_0_), channel_id=1, source_target_pairs={{0,32},{32,0},{2,34},{34,2},{4,36},{36,4},{6,38},{38,6},{64,96},{9... | collective-permute-start | bytes 3440648 | tf_op jit(solution)/shard_map/ppermute | solution.py:64
  61.9 25.4 %collective-permute-start.23 = (bf16[896,640]{1,0:T(8,128)(2,1)S(1)}, bf16[896,640]{1,0:T(8,128)(2,1)}, u32[]{:S(2)}, u32[]{:S(2)}) collective-permute-start(bf16[896,640]{1,0:T(8,128)(2,1)S(1)} %maximum_select_fusion.refs_0_), channel_id=1, source_target_pairs={{0,24},{32,40},{2,26},{34,42},{4,28},{36,44},{6,30},{38,46},{64,88... | collective-permute-start | bytes 3440648 | tf_op jit(solution)/shard_map/ppermute | solution.py:64
  63.9 18.1 %collective-permute-start.22 = (bf16[896,512]{1,0:T(8,128)(2,1)S(1)}, bf16[896,512]{1,0:T(8,128)(2,1)S(1)}, u32[]{:S(2)}, u32[]{:S(2)}) collective-permute-start(bf16[896,512]{1,0:T(8,128)(2,1)S(1)} %maximum_select_fusion.1.refs_0_), channel_id=1, source_target_pairs={{0,6},{32,34},{2,4},{34,32},{4,2},{36,38},{6,0},{38,36},{64,70},{9... | collective-permute-start | bytes 2752520 | tf_op jit(solution)/shard_map/ppermute | solution.py:64
  70.1 5.6 %collective-permute-start.8 = (bf16[2,144,128]{2,1,0:T(8,128)(2,1)S(1)}, bf16[2,144,128]{2,1,0:T(8,128)(2,1)S(1)}, u32[]{:S(2)}, u32[]{:S(2)}) collective-permute-start(bf16[2,144,128]{2,1,0:T(8,128)(2,1)S(1)} %maximum_select_fusion.6), channel_id=1, source_target_pairs={{0,65},{32,97},{2,67},{34,99},{4,69},{36,101},{6,71},{38,103},{64,... | collective-permute-start | bytes 221192 | tf_op jit(solution)/shard_map/ppermute | solution.py:64
  75.8 4.8 %collective-permute-start.9 = (bf16[2,2,80,128]{3,2,1,0:T(8,128)(2,1)S(1)}, bf16[2,2,80,128]{3,2,1,0:T(8,128)(2,1)S(1)}, u32[]{:S(2)}, u32[]{:S(2)}) collective-permute-start(bf16[2,2,80,128]{3,2,1,0:T(8,128)(2,1)S(1)} %fusion), channel_id=1, source_target_pairs={{0,8},{32,56},{2,10},{34,58},{4,12},{36,60},{6,14},{38,62},{64,72}... | collective-permute-start | bytes 245768 | tf_op jit(solution)/shard_map/ppermute | solution.py:64
  75.9 4.3 %collective-permute-start.11 = (bf16[2,2,64,128]{3,2,1,0:T(8,128)(2,1)S(1)}, bf16[2,2,64,128]{3,2,1,0:T(8,128)(2,1)S(1)}, u32[]{:S(2)}, u32[]{:S(2)}) collective-permute-start(bf16[2,2,64,128]{3,2,1,0:T(8,128)(2,1)S(1)} %pad_maximum_fusion.12), channel_id=1, source_target_pairs={{0,2},{32,38},{2,0},{34,36},{4,6},{36,34},{6,4},{38,32},{64,66},{9... | collective-permute-start | bytes 196616 | tf_op jit(solution)/shard_map/ppermute | solution.py:64
  80.3 6.3 %collective-permute-start.12 = (bf16[2,2,2,64,128]{4,3,2,1,0:T(8,128)(2,1)S(1)}, bf16[2,2,2,64,128]{4,3,2,1,0:T(8,128)(2,1)S(1)}, u32[]{:S(2)}, u32[]{:S(2)}) collective-permute-start(bf16[2,2,2,64,128]{4,3,2,1,0:T(8,128)(2,1)S(1)} %pad_maximum_fusion.10), channel_id=1, source_target_pairs={{0,6},{32,34},{2,4},{34,32},{4,2},{36,38},{6,0},{38,36},{64,70},{9... | collective-permute-start | bytes 393224 | tf_op jit(solution)/shard_map/ppermute | solution.py:64
  80.7 6.6 %collective-permute-start.10 = (bf16[2,2,2,80,128]{4,3,2,1,0:T(8,128)(2,1)S(1)}, bf16[2,2,2,80,128]{4,3,2,1,0:T(8,128)(2,1)S(1)}, u32[]{:S(2)}, u32[]{:S(2)}) collective-permute-start(bf16[2,2,2,80,128]{4,3,2,1,0:T(8,128)(2,1)S(1)} %pad_maximum_fusion.9), channel_id=1, source_target_pairs={{0,24},{32,40},{2,26},{34,42},{4,28},{36,44},{6,30},{38,46},{64,88... | collective-permute-start | bytes 491528 | tf_op jit(solution)/shard_map/ppermute | solution.py:64
  82.1 1.6 %copy-start.6 = (bf16[896,512]{1,0:T(8,128)(2,1)}, bf16[896,512]{1,0:T(8,128)(2,1)S(1)}, u32[]{:S(2)}) copy-start(bf16[896,512]{1,0:T(8,128)(2,1)S(1)} %collective-permute-done.22.refs_1_) | copy-start | bytes 2752516
  83.6 3.8 %copy-start.3 = (bf16[2,256,896]{2,1,0:T(8,128)(2,1)S(1)}, bf16[2,256,896]{2,1,0:T(8,128)(2,1)}, u32[]{:S(2)}) copy-start(bf16[2,256,896]{2,1,0:T(8,128)(2,1)} %copy-done.2) | copy-start | bytes 2752516
  85.2 8.0 %copy-start.11 = (f32[256,640]{1,0:T(8,128)}, f32[256,640]{1,0:T(8,128)S(1)}, u32[]{:S(2)}) copy-start(f32[256,640]{1,0:T(8,128)S(1)} %shard_map.94.refs_2_) | copy-start | bytes 1966084
  87.3 42.1 %collective-permute-start.24 = (bf16[1792,512]{1,0:T(8,128)(2,1)}, bf16[1792,512]{1,0:T(8,128)(2,1)}, u32[]{:S(2)}, u32[]{:S(2)}) collective-permute-start(bf16[1792,512]{1,0:T(8,128)(2,1)} %pad_maximum_fusion), channel_id=1, source_target_pairs={{0,32},{32,0},{2,34},{34,2},{4,36},{36,4},{6,38},{38,6},{64,96},{9... | collective-permute-start | bytes 5505032 | tf_op jit(solution)/shard_map/ppermute | solution.py:64
  87.4 22.7 %collective-permute-start.19 = (bf16[2,256,896]{2,1,0:T(8,128)(2,1)S(1)}, bf16[2,256,896]{2,1,0:T(8,128)(2,1)S(1)}, u32[]{:S(2)}, u32[]{:S(2)}) collective-permute-start(bf16[2,256,896]{2,1,0:T(8,128)(2,1)S(1)} %copy-done.3), channel_id=1, source_target_pairs={{0,64},{32,96},{2,66},{34,98},{4,68},{36,100},{6,70},{38,102},{64,... | collective-permute-start | bytes 2752520 | tf_op jit(solution)/shard_map/ppermute | solution.py:64
  88.4 6.4 %collective-permute-start.18 = (bf16[4,2,2,64,128]{4,3,2,1,0:T(8,128)(2,1)S(1)}, bf16[4,2,2,64,128]{4,3,2,1,0:T(8,128)(2,1)S(1)}, u32[]{:S(2)}, u32[]{:S(2)}) collective-permute-start(bf16[4,2,2,64,128]{4,3,2,1,0:T(8,128)(2,1)S(1)} %pad_maximum_fusion.8), channel_id=1, source_target_pairs={{0,8},{32,56},{2,10},{34,58},{4,12},{36,60},{6,14},{38,62},{64,72}... | collective-permute-start | bytes 786440 | tf_op jit(solution)/shard_map/ppermute | solution.py:64
  89.7 7.1 %collective-permute-start.17 = (bf16[4,2,2,80,128]{4,3,2,1,0:T(8,128)(2,1)S(1)}, bf16[4,2,2,80,128]{4,3,2,1,0:T(8,128)(2,1)S(1)}, u32[]{:S(2)}, u32[]{:S(2)}) collective-permute-start(bf16[4,2,2,80,128]{4,3,2,1,0:T(8,128)(2,1)S(1)} %pad_maximum_fusion.6), channel_id=1, source_target_pairs={{0,2},{32,38},{2,0},{34,36},{4,6},{36,34},{6,4},{38,32},{64,66},{9... | collective-permute-start | bytes 983048 | tf_op jit(solution)/shard_map/ppermute | solution.py:64
  89.7 34.7 %collective-permute-start.25 = (bf16[896,640]{1,0:T(8,128)(2,1)}, bf16[896,640]{1,0:T(8,128)(2,1)}, u32[]{:S(2)}, u32[]{:S(2)}) collective-permute-start(bf16[896,640]{1,0:T(8,128)(2,1)} %collective-permute-done.23.refs_0_), channel_id=1, source_target_pairs={{0,32},{32,0},{2,34},{34,2},{4,36},{36,4},{6,38},{38,6},{64,96},{9... | collective-permute-start | bytes 3440648 | tf_op jit(solution)/shard_map/ppermute | solution.py:64
  93.1 17.0 %copy-start.13 = (f32[256,640]{1,0:T(8,128)}, f32[256,640]{1,0:T(8,128)S(1)}, u32[]{:S(2)}) copy-start(f32[256,640]{1,0:T(8,128)S(1)} %shard_map.95.refs_2_) | copy-start | bytes 1966084
  110.2 1.0 copy-start.8
  111.2 12.1 %collective-permute-start.20 = (bf16[2,4,2,2,80,128]{5,4,3,2,1,0:T(8,128)(2,1)}, bf16[2,4,2,2,80,128]{5,4,3,2,1,0:T(8,128)(2,1)}, u32[]{:S(2)}, u32[]{:S(2)}) collective-permute-start(bf16[2,4,2,2,80,128]{5,4,3,2,1,0:T(8,128)(2,1)} %pad_maximum_fusion.3), channel_id=1, source_target_pairs={{0,6},{32,34},{2,4},{34,32},{4,2},{36,38},{6,0},{38,36},{64,70},{9... | collective-permute-start | bytes 1966088 | tf_op jit(solution)/shard_map/ppermute | solution.py:64
  115.0 20.0 %collective-permute-start.26 = (bf16[2,4,2,2,64,128]{5,4,3,2,1,0:T(8,128)(2,1)}, bf16[2,4,2,2,64,128]{5,4,3,2,1,0:T(8,128)(2,1)}, u32[]{:S(2)}, u32[]{:S(2)}) collective-permute-start(bf16[2,4,2,2,64,128]{5,4,3,2,1,0:T(8,128)(2,1)} %pad_maximum_fusion.4), channel_id=1, source_target_pairs={{0,24},{32,40},{2,26},{34,42},{4,28},{36,44},{6,30},{38,46},{64,88... | collective-permute-start | bytes 1572872 | tf_op jit(solution)/shard_map/ppermute | solution.py:64
  124.5 1.2 copy-start.9
  125.6 1.1 copy-start.14
  129.3 1.8 %copy-start.1 = (bf16[896,512]{1,0:T(8,128)(2,1)S(1)}, bf16[896,512]{1,0:T(8,128)(2,1)}, u32[]{:S(2)}) copy-start(bf16[896,512]{1,0:T(8,128)(2,1)} %copy-done) | copy-start | bytes 2752516
  129.4 2.0 %copy-start.4 = (bf16[2,256,896]{2,1,0:T(8,128)(2,1)S(1)}, bf16[2,256,896]{2,1,0:T(8,128)(2,1)}, u32[]{:S(2)}) copy-start(bf16[2,256,896]{2,1,0:T(8,128)(2,1)} %copy-done.2) | copy-start | bytes 2752516
  129.4 2.3 %copy-start.7 = (bf16[896,512]{1,0:T(8,128)(2,1)S(1)}, bf16[896,512]{1,0:T(8,128)(2,1)}, u32[]{:S(2)}) copy-start(bf16[896,512]{1,0:T(8,128)(2,1)} %copy-done.6) | copy-start | bytes 2752516
  129.4 2.5 %copy-start.10 = (bf16[2,256,896]{2,1,0:T(8,128)(2,1)S(1)}, bf16[2,256,896]{2,1,0:T(8,128)(2,1)}, u32[]{:S(2)}) copy-start(bf16[2,256,896]{2,1,0:T(8,128)(2,1)} %copy-done.8) | copy-start | bytes 2752516
  135.1 9.0 %copy-start.5 = (bf16[2,256,896]{2,1,0:T(8,128)(2,1)S(1)}, bf16[2,256,896]{2,1,0:T(8,128)(2,1)}, u32[]{:S(2)}) copy-start(bf16[2,256,896]{2,1,0:T(8,128)(2,1)} %copy-done.2) | copy-start | bytes 2752516
  135.1 9.0 %copy-start.12 = (f32[256,640]{1,0:T(8,128)S(1)}, f32[256,640]{1,0:T(8,128)}, u32[]{:S(2)}) copy-start(f32[256,640]{1,0:T(8,128)} %copy-done.11) | copy-start | bytes 1966084
  142.3 13.2 %collective-permute-start.27 = (bf16[256,896]{1,0:T(8,128)(2,1)S(1)}, bf16[256,896]{1,0:T(8,128)(2,1)}, u32[]{:S(2)}, u32[]{:S(2)}) collective-permute-start(bf16[256,896]{1,0:T(8,128)(2,1)S(1)} %shard_map.100), channel_id=1, source_target_pairs={{0,64},{32,96},{2,66},{34,98},{4,68},{36,100},{6,70},{38,102},{64,... | collective-permute-start | bytes 1376264 | tf_op jit(solution)/shard_map/ppermute | solution.py:64

commit v10 on v6

--- a/solution.py
+++ b/solution.py
@@ -113,7 +113,7 @@
         here = pl.ds(pl.multiple_of(step * rows, rows), rows)
         values = tokens_ref[here, :].astype(jnp.float32)
         factor = lax.rsqrt(jnp.mean(values * values, axis=-1, keepdims=True) + EPS)
-        plain_ref[...] = values * factor * gain_ref[...]
+        plain_ref[...] = values * factor * gain_ref[...].reshape(1, WIDTH)
         normed_ref[here, :] = plain_ref[...].astype(jnp.bfloat16)
         reorder(plain_ref, out_ref, "x", rows, here)
 
@@ -157,7 +157,7 @@
             pltpu.VMEM((TOK, WIDTH), jnp.bfloat16),
         ],
         compiler_params=pltpu.CompilerParams(vmem_limit_bytes=16 * 1024 * 1024),
-    )(facts, tokens, gain.reshape(1, WIDTH))
+    )(facts, tokens, gain)
 
 
 BLOCK = 256
@@ -319,10 +319,11 @@
 
 
 def crossed_body(info_ref, own_near, own_far, mate_near, mate_far, *refs):
-    pieces, out_ref, full_ref = refs[:4], refs[4], refs[5]
+    (near_w, far_w, other_w), out_ref, full_ref = refs[:3], refs[3], refs[4]
+    pieces = ((near_w, 0), (far_w, 0), (other_w, 0), (other_w, SLAB))
     core = info_ref[0]
     block = 4 * ROWS
-    for i, piece in enumerate(pieces):
+    for i, (piece, start) in enumerate(pieces):
         theirs, is_far = divmod(i, 2)
         side = core if theirs == 0 else 1 - core
         pair_x, pair_z = info_ref[1 + theirs], info_ref[3 + theirs]
@@ -335,7 +336,7 @@
                 at = jnp.where(side == 0, x, PAIRED[1].index(x))
                 slab = jnp.where(at // 2 == pair_x, 0, 2) + theirs
                 line = slab * SLAB + ((at % 2) * 4 + z) * block
-                source = slice((t * 4 + x) * block, (t * 4 + x + 1) * block)
+                source = slice(start + (t * 4 + x) * block, start + (t * 4 + x + 1) * block)
                 full_ref[pl.ds(pl.multiple_of(line, 16), block), :] = piece[source, :]
     columns = out_ref.shape[1]
     for first in range(0, columns, 256):
@@ -356,7 +357,7 @@
     return pl.pallas_call(
         crossed_body,
         out_shape=jax.ShapeDtypeStruct((2 * TOK, columns), jnp.bfloat16),
-        in_specs=[smem] + [vmem] * 8,
+        in_specs=[smem] + [vmem] * 7,
         out_specs=vmem,
         scratch_shapes=[pltpu.VMEM((WIDTH, columns), jnp.bfloat16)],
         compiler_params=pltpu.CompilerParams(vmem_limit_bytes=16 * 1024 * 1024),
@@ -519,7 +520,7 @@
     part = project_crossed(
         jnp.stack([core, *pairs]).astype(jnp.int32),
         (own_near, own_far, mate_near, mate_far),
-        (cross, cross_far, crossed[:SLAB], crossed[SLAB:]),
+        (cross, cross_far, crossed),
     )
     own = project((zero, one), own_far, far_w, own, last=True)
     mate = project((zero, one), mate_far, far_w, mate, last=True)

time: 150 us -> 152 us (1.013)
  Pallas kernels: 29 us -> 30.9 us
    unnamed x56, local copies, waits for them, and re-layouts: 12.9 us -> 15.4 us
    slice x1 -> x0, local copies, waits for them, and re-layouts: 1.73 us -> none  [on_device(): crossed[SLAB:]]
  transfers between devices with their start and end apart: 28 -> 28, of which waited for: 17 -> 16; matrix products, arithmetic and copies ran while one was open for 14% -> 13% of each run, Pallas kernels for 14% -> 14%
where the time goes in v10:
time: 152 us; the launch traced here: 150 us
  waiting for transfers between devices  43.8 us (29%)
  starting transfers between devices  34.9 us (23%)
  Pallas kernels  30.9 us (20%)
  local copies, waits for them, and re-layouts  26.4 us (17%)
  other arithmetic  10.9 us (7%)
  between operations  2.61 us (2%)
    ppermute x28, waiting for transfers between devices, send(): return lax.ppermute(value, AXES, pairs)  43.8 us
    ppermute x28, starting transfers between devices, send(): return lax.ppermute(value, AXES, pairs)  34.9 us
    unnamed x56, local copies, waits for them, and re-layouts  15.4 us
    pallas_call x2, Pallas kernels, attend(): pl.pallas_call(functools.partial(attend_body, wide), out_shape=jax.ShapeD...  11.9 us
    pallas_call x5, Pallas kernels, project(): pl.pallas_call(functools.partial(project_body, len(weights)), out_shape=j...  9.13 us
    pallas_call x1, Pallas kernels, norm_rows(): pl.pallas_call(norm_body, out_shape=[jax.ShapeDtypeStruct((2, TOK + 2 * (...  5.72 us
    select_n x7, other arithmetic, order(): jnp.where(first == 0, jnp.concatenate([one, two], 0), jnp.concatenate([tw...  4.33 us
    pallas_call x1, Pallas kernels, project_crossed(): pl.pallas_call(crossed_body, out_shape=jax.ShapeDtypeStruct((2 * TOK, col...  4.1 us
  transfers between devices with their start and end apart: 28, of which 16 were waited for; matrix products, arithmetic and copies ran while one was open for 13% of the time, Pallas kernels for 14%

profile of v10, /device:TPU:6, one launch (start us, length us, event | category | flops | bytes accessed | tf_op | source)
XLA Modules:
  0.0 149.6 jit_solution(13242201970827879684)
XLA Ops:
  0.0 0.9 copy-done.21
  0.9 0.7 copy-done.23
  1.6 0.7 copy-done.24
  2.3 0.7 copy-done.25
  3.1 0.7 copy-done.26
  3.8 1.6 %collective-permute-start.1 = (bf16[28,1408]{1,0:T(8,128)(2,1)S(1)}, bf16[28,1408]{1,0:T(8,128)(2,1)S(1)}, u32[]{:S(2)}, u32[]{:S(2)}) collective-permute-start(bf16[28,1408]{1,0:T(8,128)(2,1)S(1)} %get-tuple-element.21), channel_id=1, source_target_pairs={{0,64},{32,96},{2,66},{34,98},{4,68},{36,100},{6,70},{38,102},{64,... | collective-permute-start | bytes 236552 | tf_op jit(solution)/shard_map/ppermute | solution.py:64
  5.5 3.0 %collective-permute-done.1 = bf16[28,1408]{1,0:T(8,128)(2,1)S(1)} collective-permute-done((bf16[28,1408]{1,0:T(8,128)(2,1)S(1)}, bf16[28,1408]{1,0:T(8,128)(2,1)S(1)}, u32[]{:S(2)}, u32[]{:S(2)}) %collective-permute-start.1) | collective-permute-done | bytes 78880 | tf_op jit(solution)/shard_map/ppermute | solution.py:64
  8.5 3.1 %collective-permute-start.2 = (bf16[56,1408]{1,0:T(8,128)(2,1)S(1)}, bf16[56,1408]{1,0:T(8,128)(2,1)S(1)}, u32[]{:S(2)}, u32[]{:S(2)}) collective-permute-start(bf16[56,1408]{1,0:T(8,128)(2,1)S(1)} %maximum_select_fusion.4), channel_id=1, source_target_pairs={{0,65},{32,97},{2,67},{34,99},{4,69},{36,101},{6,71},{38,103},{64,... | collective-permute-start | bytes 473096 | tf_op jit(solution)/shard_map/ppermute | solution.py:64
  13.1 1.5 %copy-done.20 = bf16[1,256,3584]{2,1,0:T(8,128)(2,1)S(1)} copy-done((bf16[1,256,3584]{2,1,0:T(8,128)(2,1)S(1)}, bf16[1,256,3584]{2,1,0:T(8,128)(2,1)}, u32[]{:S(2)}) %copy-start.20) | copy-done | bytes 1835032
  15.3 5.7 %shard_map.91 = (bf16[2,416,896]{2,1,0:T(8,128)(2,1)S(1)}, bf16[2,256,896]{2,1,0:T(8,128)(2,1)S(1)}) custom-call(s32[7]{0:T(128)S(1)} %stack.148.fact_ref, bf16[256,3584]{1,0:T(8,128)(2,1)S(1)} %bitcast.72, f32[3584]{0:T(1024)S(1)} %copy-done.22), custom_call_target="tpu_custom_call" | custom-call | tf_op jit(solution)/shard_map/pallas_call | solution.py:145
  21.0 0.9 copy-done.8
  22.2 0.9 collective-permute-start.3
  23.1 1.9 %collective-permute-start.13 = (bf16[112,640]{1,0:T(8,128)(2,1)S(1)}, bf16[112,640]{1,0:T(8,128)(2,1)S(1)}, u32[]{:S(2)}, u32[]{:S(2)}) collective-permute-start(bf16[112,640]{1,0:T(8,128)(2,1)S(1)} %get-tuple-element.36), channel_id=1, source_target_pairs={{0,2},{32,38},{2,0},{34,36},{4,6},{36,34},{6,4},{38,32},{64,66},{9... | collective-permute-start | bytes 430088 | tf_op jit(solution)/shard_map/ppermute | solution.py:64
  25.1 0.9 broadcast_in_dim.33
  26.6 1.1 collective-permute-done.3
  28.3 4.1 %collective-permute-start.14 = (bf16[2,112,640]{2,1,0:T(8,128)(2,1)S(1)}, bf16[2,112,640]{2,1,0:T(8,128)(2,1)S(1)}, u32[]{:S(2)}, u32[]{:S(2)}) collective-permute-start(bf16[2,112,640]{2,1,0:T(8,128)(2,1)S(1)} %pad_maximum_fusion.9), channel_id=1, source_target_pairs={{0,6},{32,34},{2,4},{34,32},{4,2},{36,38},{6,0},{38,36},{64,70},{9... | collective-permute-start | bytes 860168 | tf_op jit(solution)/shard_map/ppermute | solution.py:64
  32.5 3.8 %collective-permute-done.4 = bf16[2,112,768]{2,1,0:T(8,128)(2,1)S(1)} collective-permute-done((bf16[2,112,768]{2,1,0:T(8,128)(2,1)S(1)}, bf16[2,112,768]{2,1,0:T(8,128)(2,1)S(1)}, u32[]{:S(2)}, u32[]{:S(2)}) %collective-permute-start.4) | collective-permute-done | bytes 344096 | tf_op jit(solution)/shard_map/ppermute | solution.py:64
  36.3 2.0 %collective-permute-start.5 = (bf16[448,256]{1,0:T(8,128)(2,1)S(1)}, bf16[448,256]{1,0:T(8,128)(2,1)S(1)}, u32[]{:S(2)}, u32[]{:S(2)}) collective-permute-start(bf16[448,256]{1,0:T(8,128)(2,1)S(1)} %slice.112), channel_id=1, source_target_pairs={{0,2},{32,38},{2,0},{34,36},{4,6},{36,34},{6,4},{38,32},{64,66},{9... | collective-permute-start | bytes 688136 | tf_op jit(solution)/shard_map/ppermute | solution.py:64
  39.0 4.2 %collective-permute-done.5 = bf16[448,256]{1,0:T(8,128)(2,1)S(1)} collective-permute-done((bf16[448,256]{1,0:T(8,128)(2,1)S(1)}, bf16[448,256]{1,0:T(8,128)(2,1)S(1)}, u32[]{:S(2)}, u32[]{:S(2)}) %collective-permute-start.5) | collective-permute-done | bytes 229408 | tf_op jit(solution)/shard_map/ppermute | solution.py:64
  43.4 4.1 %collective-permute-start.6 = (bf16[896,256]{1,0:T(8,128)(2,1)S(1)}, bf16[896,256]{1,0:T(8,128)(2,1)}, u32[]{:S(2)}, u32[]{:S(2)}) collective-permute-start(bf16[896,256]{1,0:T(8,128)(2,1)S(1)} %maximum_select_fusion.2.refs_0_), channel_id=1, source_target_pairs={{0,6},{32,34},{2,4},{34,32},{4,2},{36,38},{6,0},{38,36},{64,70},{9... | collective-permute-start | bytes 1376264 | tf_op jit(solution)/shard_map/ppermute | solution.py:64
  48.1 0.8 slice.127
  49.6 0.8 slice.80
  50.5 1.8 %slice.106 = bf16[4,64,896]{2,1,0:T(8,128)(2,1)} slice(bf16[4,80,896]{2,1,0:T(8,128)(2,1)} %bitcast.76), slice={[0:4], [0:64], [0:896]} | slice | bytes 917504 | tf_op jit(solution)/shard_map/slice | solution.py:449
  52.3 3.3 %collective-permute-done.6.refs_1_ = bf16[896,256]{1,0:T(8,128)(2,1)} collective-permute-done((bf16[896,256]{1,0:T(8,128)(2,1)S(1)}, bf16[896,256]{1,0:T(8,128)(2,1)}, u32[]{:S(2)}, u32[]{:S(2)}) %collective-permute-start.6) | collective-permute-done | bytes 458784 | tf_op jit(solution)/shard_map/ppermute | solution.py:64
  55.6 1.1 pad_maximum_fusion.4
  56.9 0.9 collective-permute-done.21
  57.8 1.7 %maximum_select_fusion.1.refs_0_ = bf16[896,512]{1,0:T(8,128)(2,1)S(1)} fusion(bf16[448,512]{1,0:T(8,128)(2,1)} %collective-permute-done.21, bf16[448,512]{1,0:T(8,128)(2,1)} %slice.127, pred[]{:T(512)S(6)} %eq.102), kind=kLoop, calls=%fused_computation.6 | loop fusion | flops 4128768 | bytes 1835009 | tf_op jit(solution)/shard_map/jit(_where)/select_n | solution.py:418
  59.7 2.3 %maximum_select_fusion.refs_0_ = bf16[896,640]{1,0:T(8,128)(2,1)S(1)} fusion(bf16[448,640]{1,0:T(8,128)(2,1)} %collective-permute-done.15, bf16[448,640]{1,0:T(8,128)(2,1)} %bitcast.36, pred[]{:T(512)S(6)} %eq.104), kind=kLoop, calls=%fused_computation.2 | loop fusion | flops 5160960 | bytes 2293761 | tf_op jit(solution)/shard_map/jit(_where)/select_n | solution.py:418
  62.0 1.9 %collective-permute-start.23 = (bf16[896,640]{1,0:T(8,128)(2,1)S(1)}, bf16[896,640]{1,0:T(8,128)(2,1)}, u32[]{:S(2)}, u32[]{:S(2)}) collective-permute-start(bf16[896,640]{1,0:T(8,128)(2,1)S(1)} %maximum_select_fusion.refs_0_), channel_id=1, source_target_pairs={{0,24},{32,40},{2,26},{34,42},{4,28},{36,44},{6,30},{38,46},{64,88... | collective-permute-start | bytes 3440648 | tf_op jit(solution)/shard_map/ppermute | solution.py:64
  63.9 3.0 %collective-permute-start.22 = (bf16[896,512]{1,0:T(8,128)(2,1)S(1)}, bf16[896,512]{1,0:T(8,128)(2,1)S(1)}, u32[]{:S(2)}, u32[]{:S(2)}) collective-permute-start(bf16[896,512]{1,0:T(8,128)(2,1)S(1)} %maximum_select_fusion.1.refs_0_), channel_id=1, source_target_pairs={{0,6},{32,34},{2,4},{34,32},{4,2},{36,38},{6,0},{38,36},{64,70},{9... | collective-permute-start | bytes 2752520 | tf_op jit(solution)/shard_map/ppermute | solution.py:64
  68.3 2.0 %collective-permute-start.19 = (bf16[2,256,896]{2,1,0:T(8,128)(2,1)S(1)}, bf16[2,256,896]{2,1,0:T(8,128)(2,1)S(1)}, u32[]{:S(2)}, u32[]{:S(2)}) collective-permute-start(bf16[2,256,896]{2,1,0:T(8,128)(2,1)S(1)} %copy-done.9), channel_id=1, source_target_pairs={{0,64},{32,96},{2,66},{34,98},{4,68},{36,100},{6,70},{38,102},{64,... | collective-permute-start | bytes 2752520 | tf_op jit(solution)/shard_map/ppermute | solution.py:64
  70.5 1.5 shard_map.93
  72.5 5.3 %collective-permute-done.8 = bf16[2,144,128]{2,1,0:T(8,128)(2,1)S(1)} collective-permute-done((bf16[2,144,128]{2,1,0:T(8,128)(2,1)S(1)}, bf16[2,144,128]{2,1,0:T(8,128)(2,1)S(1)}, u32[]{:S(2)}, u32[]{:S(2)}) %collective-permute-start.8) | collective-permute-done | bytes 73760 | tf_op jit(solution)/shard_map/ppermute | solution.py:64
  77.9 4.2 %collective-permute-done.11 = bf16[2,2,64,128]{3,2,1,0:T(8,128)(2,1)S(1)} collective-permute-done((bf16[2,2,64,128]{3,2,1,0:T(8,128)(2,1)S(1)}, bf16[2,2,64,128]{3,2,1,0:T(8,128)(2,1)S(1)}, u32[]{:S(2)}, u32[]{:S(2)}) %collective-permute-start.11) | collective-permute-done | bytes 65568 | tf_op jit(solution)/shard_map/ppermute | solution.py:64
  82.1 4.4 %collective-permute-done.9 = bf16[2,2,80,128]{3,2,1,0:T(8,128)(2,1)S(1)} collective-permute-done((bf16[2,2,80,128]{3,2,1,0:T(8,128)(2,1)S(1)}, bf16[2,2,80,128]{3,2,1,0:T(8,128)(2,1)S(1)}, u32[]{:S(2)}, u32[]{:S(2)}) %collective-permute-start.9) | collective-permute-done | bytes 81952 | tf_op jit(solution)/shard_map/ppermute | solution.py:64
  86.9 1.6 %collective-permute-start.10 = (bf16[2,2,2,80,128]{4,3,2,1,0:T(8,128)(2,1)S(1)}, bf16[2,2,2,80,128]{4,3,2,1,0:T(8,128)(2,1)S(1)}, u32[]{:S(2)}, u32[]{:S(2)}) collective-permute-start(bf16[2,2,2,80,128]{4,3,2,1,0:T(8,128)(2,1)S(1)} %pad_maximum_fusion.11), channel_id=1, source_target_pairs={{0,24},{32,40},{2,26},{34,42},{4,28},{36,44},{6,30},{38,46},{64,88... | collective-permute-start | bytes 491528 | tf_op jit(solution)/shard_map/ppermute | solution.py:64
  88.5 1.3 pad_maximum_fusion
  89.9 1.5 %shard_map.94.refs_2_ = f32[256,640]{1,0:T(8,128)S(1)} custom-call(s32[2]{0:T(128)S(1)} %iota.19.slab_ref, bf16[2,416,896]{2,1,0:T(8,128)(2,1)S(1)} %get-tuple-element.19.x_ref.own_near, bf16[896,640]{1,0:T(8,128)(2,1)S(1)} %maximum_select_fusion.refs_0_, bf16[896,640]{1,0:T(8,128)(2,1)S(1)} %collective-permute-done.16.refs_1_), custom_call_target="tpu_custom_call" | custom-call | tf_op jit(solution)/shard_map/pallas_call | solution.py:312
  91.4 1.3 collective-permute-done.12
  92.7 0.7 collective-permute-done.10
  94.0 1.5 %shard_map.95.refs_2_ = f32[256,640]{1,0:T(8,128)S(1)} custom-call(s32[2]{0:T(128)S(1)} %iota.20.slab_ref, bf16[2,416,896]{2,1,0:T(8,128)(2,1)S(1)} %collective-permute-done.x_ref.mate_near, bf16[896,640]{1,0:T(8,128)(2,1)S(1)} %maximum_select_fusion.refs_0_, bf16[896,640]{1,0:T(8,128)(2,1)S(1)} %collective-permute-done.16.refs_1_), custom_call_target="tpu_custom_call" | custom-call | tf_op jit(solution)/shard_map/pallas_call | solution.py:312
  95.5 3.3 %collective-permute-start.25 = (bf16[896,640]{1,0:T(8,128)(2,1)}, bf16[896,640]{1,0:T(8,128)(2,1)S(1)}, u32[]{:S(2)}, u32[]{:S(2)}) collective-permute-start(bf16[896,640]{1,0:T(8,128)(2,1)} %collective-permute-done.23.refs_0_), channel_id=1, source_target_pairs={{0,32},{32,0},{2,34},{34,2},{4,36},{36,4},{6,38},{38,6},{64,96},{9... | collective-permute-start | bytes 3440648 | tf_op jit(solution)/shard_map/ppermute | solution.py:64
  98.8 1.4 collective-permute-done.18
  100.3 0.7 collective-permute-done.17
  101.0 1.0 pad_maximum_fusion.5
  102.0 1.0 copy-done.14
  103.0 1.6 %collective-permute-start.26 = (bf16[2,4,2,2,64,128]{5,4,3,2,1,0:T(8,128)(2,1)S(1)}, bf16[2,4,2,2,64,128]{5,4,3,2,1,0:T(8,128)(2,1)S(1)}, u32[]{:S(2)}, u32[]{:S(2)}) collective-permute-start(bf16[2,4,2,2,64,128]{5,4,3,2,1,0:T(8,128)(2,1)S(1)} %pad_maximum_fusion.6), channel_id=1, source_target_pairs={{0,24},{32,40},{2,26},{34,42},{4,28},{36,44},{6,30},{38,46},{64,88... | collective-permute-start | bytes 1572872 | tf_op jit(solution)/shard_map/ppermute | solution.py:64
  104.6 1.9 %collective-permute-start.20 = (bf16[2,4,2,2,80,128]{5,4,3,2,1,0:T(8,128)(2,1)}, bf16[2,4,2,2,80,128]{5,4,3,2,1,0:T(8,128)(2,1)}, u32[]{:S(2)}, u32[]{:S(2)}) collective-permute-start(bf16[2,4,2,2,80,128]{5,4,3,2,1,0:T(8,128)(2,1)} %pad_maximum_fusion.5), channel_id=1, source_target_pairs={{0,6},{32,34},{2,4},{34,32},{4,2},{36,38},{6,0},{38,36},{64,70},{9... | collective-permute-start | bytes 1966088 | tf_op jit(solution)/shard_map/ppermute | solution.py:64
  107.2 6.2 %collective-permute-done.26 = bf16[2,4,2,2,64,128]{5,4,3,2,1,0:T(8,128)(2,1)S(1)} collective-permute-done((bf16[2,4,2,2,64,128]{5,4,3,2,1,0:T(8,128)(2,1)S(1)}, bf16[2,4,2,2,64,128]{5,4,3,2,1,0:T(8,128)(2,1)S(1)}, u32[]{:S(2)}, u32[]{:S(2)}) %collective-permute-start.26) | collective-permute-done | bytes 524320 | tf_op jit(solution)/shard_map/ppermute | solution.py:64
  113.5 3.2 %collective-permute-done.20 = bf16[2,4,2,2,80,128]{5,4,3,2,1,0:T(8,128)(2,1)} collective-permute-done((bf16[2,4,2,2,80,128]{5,4,3,2,1,0:T(8,128)(2,1)}, bf16[2,4,2,2,80,128]{5,4,3,2,1,0:T(8,128)(2,1)}, u32[]{:S(2)}, u32[]{:S(2)}) %collective-permute-start.20) | collective-permute-done | bytes 655392 | tf_op jit(solution)/shard_map/ppermute | solution.py:64
  116.7 1.4 pad_maximum_fusion.1
  118.1 1.2 fusion.1
  119.4 1.6 %copy-done.15 = bf16[2,256,896]{2,1,0:T(8,128)(2,1)S(1)} copy-done((bf16[2,256,896]{2,1,0:T(8,128)(2,1)S(1)}, bf16[2,256,896]{2,1,0:T(8,128)(2,1)}, u32[]{:S(2)}) %copy-start.15) | copy-done | bytes 917528
  121.0 1.1 copy-done.19
  122.1 2.4 %shard_map.99.more_ref = bf16[256,640]{1,0:T(8,128)(2,1)S(1)} custom-call(s32[2]{0:T(128)S(1)} %iota.22.slab_ref, bf16[2,256,896]{2,1,0:T(8,128)(2,1)S(1)} %copy-done.15, bf16[896,640]{1,0:T(8,128)(2,1)} %collective-permute-done.23.refs_0_, bf16[896,640]{1,0:T(8,128)(2,1)S(1)} %collective-permute-done.25.refs_1_, f32[256,640]{1,0:T(8,128)S(1)} %copy-done.19), custom_call_target="tpu_custom_call" | custom-call | tf_op jit(solution)/shard_map/pallas_call | solution.py:312
  124.6 1.2 copy-done.10
  125.7 1.2 copy-done.13
  126.9 4.1 %shard_map.96.part_ref = bf16[512,512]{1,0:T(8,128)(2,1)S(1)} custom-call(s32[5]{0:T(128)S(1)} %stack.175.info_ref, bf16[2,416,896]{2,1,0:T(8,128)(2,1)S(1)} %copy-done.3, bf16[2,256,896]{2,1,0:T(8,128)(2,1)S(1)} %copy-done.10, bf16[2,416,896]{2,1,0:T(8,128)(2,1)S(1)} %copy-done.1, bf16[2,256,896]{2,1,0:T(8,128)(2,1)S(1)} %copy-done.15, ...), custom_call_target="tpu_custom_call" | custom-call | tf_op jit(solution)/shard_map/pallas_call | solution.py:357
  131.0 5.9 %shard_map.100 = bf16[256,896]{1,0:T(8,128)(2,1)} custom-call(s32[68]{0:T(128)S(1)} %concatenate.119.info_ref, s32[64]{0:T(128)S(1)} %reshape.103.count_ref, bf16[512,512]{1,0:T(8,128)(2,1)S(1)} %shard_map.96.part_ref, bf16[256,640]{1,0:T(8,128)(2,1)S(1)} %shard_map.99.more_ref, bf16[32,2,80,128]{3,2,1,0:T(8,128)(2,1)S(1)} %bitcast.68, ...), custom_call_target="tpu_custom_call" | custom-call | tf_op jit(solution)/shard_map/pallas_call | solution.py:276
  137.0 1.3 copy-done.7
  138.3 1.2 copy-done.11
  139.5 2.2 %shard_map.97.more_ref = bf16[256,640]{1,0:T(8,128)(2,1)S(1)} custom-call(s32[2]{0:T(128)S(1)} %iota.21.slab_ref, bf16[2,256,896]{2,1,0:T(8,128)(2,1)S(1)} %copy-done.11, bf16[896,640]{1,0:T(8,128)(2,1)} %collective-permute-done.23.refs_0_, bf16[896,640]{1,0:T(8,128)(2,1)S(1)} %copy-done.7, f32[256,640]{1,0:T(8,128)S(1)} %copy-done.17), custom_call_target="tpu_custom_call" | custom-call | tf_op jit(solution)/shard_map/pallas_call | solution.py:312
  141.7 6.0 %shard_map.98 = bf16[256,1792]{1,0:T(8,128)(2,1)} custom-call(s32[68]{0:T(128)S(1)} %concatenate.93.info_ref, s32[64]{0:T(128)S(1)} %reshape.103.count_ref, bf16[512,512]{1,0:T(8,128)(2,1)S(1)} %shard_map.96.part_ref, bf16[256,640]{1,0:T(8,128)(2,1)S(1)} %shard_map.97.more_ref, bf16[32,2,80,128]{3,2,1,0:T(8,128)(2,1)S(1)} %bitcast.69, ...), custom_call_target="tpu_custom_call" | custom-call | tf_op jit(solution)/shard_map/pallas_call | solution.py:276
  147.7 1.8 %bitcast_dynamic-update-slice_fusion = bf16[1,256,1792]{2,1,0:T(8,128)(2,1)} fusion(bf16[1,256,1792]{2,1,0:T(8,128)(2,1)} %bitcast.84, s32[]{:T(128)S(6)} %select_n.249, bf16[256,896]{1,0:T(8,128)(2,1)} %collective-permute-done.27), kind=kLoop, calls=%fused_computation.10 | loop fusion | bytes 917508 | tf_op jit(solution)/shard_map/dynamic_update_slice | solution.py:544
  (122 shorter events, 8.7 us)
Async XLA Ops:
  0.0 0.9 copy-start.21
  0.9 0.7 copy-start.23
  1.6 0.7 copy-start.24
  2.3 0.7 copy-start.25
  3.1 0.7 copy-start.26
  3.8 4.6 %collective-permute-start.1 = (bf16[28,1408]{1,0:T(8,128)(2,1)S(1)}, bf16[28,1408]{1,0:T(8,128)(2,1)S(1)}, u32[]{:S(2)}, u32[]{:S(2)}) collective-permute-start(bf16[28,1408]{1,0:T(8,128)(2,1)S(1)} %get-tuple-element.21), channel_id=1, source_target_pairs={{0,64},{32,96},{2,66},{34,98},{4,68},{36,100},{6,70},{38,102},{64,... | collective-permute-start | bytes 236552 | tf_op jit(solution)/shard_map/ppermute | solution.py:64
  8.5 13.6 %collective-permute-start.2 = (bf16[56,1408]{1,0:T(8,128)(2,1)S(1)}, bf16[56,1408]{1,0:T(8,128)(2,1)S(1)}, u32[]{:S(2)}, u32[]{:S(2)}) collective-permute-start(bf16[56,1408]{1,0:T(8,128)(2,1)S(1)} %maximum_select_fusion.4), channel_id=1, source_target_pairs={{0,65},{32,97},{2,67},{34,99},{4,69},{36,101},{6,71},{38,103},{64,... | collective-permute-start | bytes 473096 | tf_op jit(solution)/shard_map/ppermute | solution.py:64
  13.1 1.5 %copy-start.20 = (bf16[1,256,3584]{2,1,0:T(8,128)(2,1)S(1)}, bf16[1,256,3584]{2,1,0:T(8,128)(2,1)}, u32[]{:S(2)}) copy-start(bf16[1,256,3584]{2,1,0:T(8,128)(2,1)} %param.9) | copy-start | bytes 5505028
  14.6 0.7 copy-start.22
  21.0 0.9 copy-start.8
  21.9 67.9 %copy-start.2 = (bf16[2,416,896]{2,1,0:T(8,128)(2,1)}, bf16[2,416,896]{2,1,0:T(8,128)(2,1)S(1)}, u32[]{:S(2)}) copy-start(bf16[2,416,896]{2,1,0:T(8,128)(2,1)S(1)} %get-tuple-element.19.x_ref.own_near) | copy-start | bytes 4472836
  22.0 44.9 %collective-permute-start = (bf16[2,416,896]{2,1,0:T(8,128)(2,1)S(1)}, bf16[2,416,896]{2,1,0:T(8,128)(2,1)S(1)}, u32[]{:S(2)}, u32[]{:S(2)}) collective-permute-start(bf16[2,416,896]{2,1,0:T(8,128)(2,1)S(1)} %get-tuple-element.19.x_ref.own_near), channel_id=1, source_target_pairs={{0,64},{32,96},{2,66},{34,98},{4,68},{36,100},{6,70},{38,102},{64,... | collective-permute-start | bytes 4472840 | tf_op jit(solution)/shard_map/ppermute | solution.py:64
  22.2 5.5 %collective-permute-start.3 = (bf16[112,768]{1,0:T(8,128)(2,1)S(1)}, bf16[112,768]{1,0:T(8,128)(2,1)S(1)}, u32[]{:S(2)}, u32[]{:S(2)}) collective-permute-start(bf16[112,768]{1,0:T(8,128)(2,1)S(1)} %get-tuple-element.38), channel_id=1, source_target_pairs={{0,8},{32,56},{2,10},{34,58},{4,12},{36,60},{6,14},{38,62},{64,72}... | collective-permute-start | bytes 516104 | tf_op jit(solution)/shard_map/ppermute | solution.py:64
  23.1 5.2 %collective-permute-start.13 = (bf16[112,640]{1,0:T(8,128)(2,1)S(1)}, bf16[112,640]{1,0:T(8,128)(2,1)S(1)}, u32[]{:S(2)}, u32[]{:S(2)}) collective-permute-start(bf16[112,640]{1,0:T(8,128)(2,1)S(1)} %get-tuple-element.36), channel_id=1, source_target_pairs={{0,2},{32,38},{2,0},{34,36},{4,6},{36,34},{6,4},{38,32},{64,66},{9... | collective-permute-start | bytes 430088 | tf_op jit(solution)/shard_map/ppermute | solution.py:64
  27.7 8.5 %collective-permute-start.4 = (bf16[2,112,768]{2,1,0:T(8,128)(2,1)S(1)}, bf16[2,112,768]{2,1,0:T(8,128)(2,1)S(1)}, u32[]{:S(2)}, u32[]{:S(2)}) collective-permute-start(bf16[2,112,768]{2,1,0:T(8,128)(2,1)S(1)} %pad_maximum_fusion.7), channel_id=1, source_target_pairs={{0,24},{32,40},{2,26},{34,42},{4,28},{36,44},{6,30},{38,46},{64,88... | collective-permute-start | bytes 1032200 | tf_op jit(solution)/shard_map/ppermute | solution.py:64
  28.3 19.2 %collective-permute-start.14 = (bf16[2,112,640]{2,1,0:T(8,128)(2,1)S(1)}, bf16[2,112,640]{2,1,0:T(8,128)(2,1)S(1)}, u32[]{:S(2)}, u32[]{:S(2)}) collective-permute-start(bf16[2,112,640]{2,1,0:T(8,128)(2,1)S(1)} %pad_maximum_fusion.9), channel_id=1, source_target_pairs={{0,6},{32,34},{2,4},{34,32},{4,2},{36,38},{6,0},{38,36},{64,70},{9... | collective-permute-start | bytes 860168 | tf_op jit(solution)/shard_map/ppermute | solution.py:64
  36.3 6.8 %collective-permute-start.5 = (bf16[448,256]{1,0:T(8,128)(2,1)S(1)}, bf16[448,256]{1,0:T(8,128)(2,1)S(1)}, u32[]{:S(2)}, u32[]{:S(2)}) collective-permute-start(bf16[448,256]{1,0:T(8,128)(2,1)S(1)} %slice.112), channel_id=1, source_target_pairs={{0,2},{32,38},{2,0},{34,36},{4,6},{36,34},{6,4},{38,32},{64,66},{9... | collective-permute-start | bytes 688136 | tf_op jit(solution)/shard_map/ppermute | solution.py:64
  43.4 12.2 %collective-permute-start.6 = (bf16[896,256]{1,0:T(8,128)(2,1)S(1)}, bf16[896,256]{1,0:T(8,128)(2,1)}, u32[]{:S(2)}, u32[]{:S(2)}) collective-permute-start(bf16[896,256]{1,0:T(8,128)(2,1)S(1)} %maximum_select_fusion.2.refs_0_), channel_id=1, source_target_pairs={{0,6},{32,34},{2,4},{34,32},{4,2},{36,38},{6,0},{38,36},{64,70},{9... | collective-permute-start | bytes 1376264 | tf_op jit(solution)/shard_map/ppermute | solution.py:64
  49.0 8.8 %collective-permute-start.21 = (bf16[448,512]{1,0:T(8,128)(2,1)}, bf16[448,512]{1,0:T(8,128)(2,1)}, u32[]{:S(2)}, u32[]{:S(2)}) collective-permute-start(bf16[448,512]{1,0:T(8,128)(2,1)} %slice.127), channel_id=1, source_target_pairs={{0,2},{32,38},{2,0},{34,36},{4,6},{36,34},{6,4},{38,32},{64,66},{9... | collective-permute-start | bytes 1376264 | tf_op jit(solution)/shard_map/ppermute | solution.py:64
  49.6 10.0 %collective-permute-start.15 = (bf16[448,640]{1,0:T(8,128)(2,1)}, bf16[448,640]{1,0:T(8,128)(2,1)}, u32[]{:S(2)}, u32[]{:S(2)}) collective-permute-start(bf16[448,640]{1,0:T(8,128)(2,1)} %bitcast.36), channel_id=1, source_target_pairs={{0,8},{32,56},{2,10},{34,58},{4,12},{36,60},{6,14},{38,62},{64,72}... | collective-permute-start | bytes 1720328 | tf_op jit(solution)/shard_map/ppermute | solution.py:64
  56.7 13.8 %collective-permute-start.7 = (bf16[1792,256]{1,0:T(8,128)(2,1)S(1)}, bf16[1792,256]{1,0:T(8,128)(2,1)S(1)}, u32[]{:S(2)}, u32[]{:S(2)}) collective-permute-start(bf16[1792,256]{1,0:T(8,128)(2,1)S(1)} %pad_maximum_fusion.4), channel_id=1, source_target_pairs={{0,32},{32,0},{2,34},{34,2},{4,36},{36,4},{6,38},{38,6},{64,96},{9... | collective-permute-start | bytes 2752520 | tf_op jit(solution)/shard_map/ppermute | solution.py:64
  59.4 29.1 %copy-start.4 = (bf16[896,512]{1,0:T(8,128)(2,1)}, bf16[896,512]{1,0:T(8,128)(2,1)S(1)}, u32[]{:S(2)}) copy-start(bf16[896,512]{1,0:T(8,128)(2,1)S(1)} %maximum_select_fusion.1.refs_0_) | copy-start | bytes 2752516
  59.5 8.8 %copy-start.9 = (bf16[2,256,896]{2,1,0:T(8,128)(2,1)S(1)}, bf16[2,256,896]{2,1,0:T(8,128)(2,1)}, u32[]{:S(2)}) copy-start(bf16[2,256,896]{2,1,0:T(8,128)(2,1)} %copy-done.8) | copy-start | bytes 2752516
  59.5 10.9 %copy-start.27 = (bf16[4,64,896]{2,1,0:T(8,128)(2,1)S(1)}, bf16[4,64,896]{2,1,0:T(8,128)(2,1)}, u32[]{:S(2)}) copy-start(bf16[4,64,896]{2,1,0:T(8,128)(2,1)} %slice.106) | copy-start | bytes 1376260
  62.0 27.9 %collective-permute-start.16 = (bf16[896,640]{1,0:T(8,128)(2,1)S(1)}, bf16[896,640]{1,0:T(8,128)(2,1)S(1)}, u32[]{:S(2)}, u32[]{:S(2)}) collective-permute-start(bf16[896,640]{1,0:T(8,128)(2,1)S(1)} %maximum_select_fusion.refs_0_), channel_id=1, source_target_pairs={{0,32},{32,0},{2,34},{34,2},{4,36},{36,4},{6,38},{38,6},{64,96},{9... | collective-permute-start | bytes 3440648 | tf_op jit(solution)/shard_map/ppermute | solution.py:64
  62.0 31.5 %collective-permute-start.23 = (bf16[896,640]{1,0:T(8,128)(2,1)S(1)}, bf16[896,640]{1,0:T(8,128)(2,1)}, u32[]{:S(2)}, u32[]{:S(2)}) collective-permute-start(bf16[896,640]{1,0:T(8,128)(2,1)S(1)} %maximum_select_fusion.refs_0_), channel_id=1, source_target_pairs={{0,24},{32,40},{2,26},{34,42},{4,28},{36,44},{6,30},{38,46},{64,88... | collective-permute-start | bytes 3440648 | tf_op jit(solution)/shard_map/ppermute | solution.py:64
  63.9 22.9 %collective-permute-start.22 = (bf16[896,512]{1,0:T(8,128)(2,1)S(1)}, bf16[896,512]{1,0:T(8,128)(2,1)S(1)}, u32[]{:S(2)}, u32[]{:S(2)}) collective-permute-start(bf16[896,512]{1,0:T(8,128)(2,1)S(1)} %maximum_select_fusion.1.refs_0_), channel_id=1, source_target_pairs={{0,6},{32,34},{2,4},{34,32},{4,2},{36,38},{6,0},{38,36},{64,70},{9... | collective-permute-start | bytes 2752520 | tf_op jit(solution)/shard_map/ppermute | solution.py:64
  66.9 27.1 %copy-start = (bf16[2,416,896]{2,1,0:T(8,128)(2,1)}, bf16[2,416,896]{2,1,0:T(8,128)(2,1)S(1)}, u32[]{:S(2)}) copy-start(bf16[2,416,896]{2,1,0:T(8,128)(2,1)S(1)} %collective-permute-done.x_ref.mate_near) | copy-start | bytes 4472836
  68.3 33.7 %collective-permute-start.19 = (bf16[2,256,896]{2,1,0:T(8,128)(2,1)S(1)}, bf16[2,256,896]{2,1,0:T(8,128)(2,1)S(1)}, u32[]{:S(2)}, u32[]{:S(2)}) collective-permute-start(bf16[2,256,896]{2,1,0:T(8,128)(2,1)S(1)} %copy-done.9), channel_id=1, source_target_pairs={{0,64},{32,96},{2,66},{34,98},{4,68},{36,100},{6,70},{38,102},{64,... | collective-permute-start | bytes 2752520 | tf_op jit(solution)/shard_map/ppermute | solution.py:64
  72.2 5.6 %collective-permute-start.8 = (bf16[2,144,128]{2,1,0:T(8,128)(2,1)S(1)}, bf16[2,144,128]{2,1,0:T(8,128)(2,1)S(1)}, u32[]{:S(2)}, u32[]{:S(2)}) collective-permute-start(bf16[2,144,128]{2,1,0:T(8,128)(2,1)S(1)} %maximum_select_fusion.6), channel_id=1, source_target_pairs={{0,65},{32,97},{2,67},{34,99},{4,69},{36,101},{6,71},{38,103},{64,... | collective-permute-start | bytes 221192 | tf_op jit(solution)/shard_map/ppermute | solution.py:64
  77.8 4.3 %collective-permute-start.11 = (bf16[2,2,64,128]{3,2,1,0:T(8,128)(2,1)S(1)}, bf16[2,2,64,128]{3,2,1,0:T(8,128)(2,1)S(1)}, u32[]{:S(2)}, u32[]{:S(2)}) collective-permute-start(bf16[2,2,64,128]{3,2,1,0:T(8,128)(2,1)S(1)} %pad_maximum_fusion.14), channel_id=1, source_target_pairs={{0,2},{32,38},{2,0},{34,36},{4,6},{36,34},{6,4},{38,32},{64,66},{9... | collective-permute-start | bytes 196616 | tf_op jit(solution)/shard_map/ppermute | solution.py:64
  82.1 4.4 %collective-permute-start.9 = (bf16[2,2,80,128]{3,2,1,0:T(8,128)(2,1)S(1)}, bf16[2,2,80,128]{3,2,1,0:T(8,128)(2,1)S(1)}, u32[]{:S(2)}, u32[]{:S(2)}) collective-permute-start(bf16[2,2,80,128]{3,2,1,0:T(8,128)(2,1)S(1)} %fusion), channel_id=1, source_target_pairs={{0,8},{32,56},{2,10},{34,58},{4,12},{36,60},{6,14},{38,62},{64,72}... | collective-permute-start | bytes 245768 | tf_op jit(solution)/shard_map/ppermute | solution.py:64
  86.5 6.2 %collective-permute-start.12 = (bf16[2,2,2,64,128]{4,3,2,1,0:T(8,128)(2,1)S(1)}, bf16[2,2,2,64,128]{4,3,2,1,0:T(8,128)(2,1)S(1)}, u32[]{:S(2)}, u32[]{:S(2)}) collective-permute-start(bf16[2,2,2,64,128]{4,3,2,1,0:T(8,128)(2,1)S(1)} %pad_maximum_fusion.12), channel_id=1, source_target_pairs={{0,6},{32,34},{2,4},{34,32},{4,2},{36,38},{6,0},{38,36},{64,70},{9... | collective-permute-start | bytes 393224 | tf_op jit(solution)/shard_map/ppermute | solution.py:64
  86.8 3.0 %copy-start.12 = (bf16[896,512]{1,0:T(8,128)(2,1)}, bf16[896,512]{1,0:T(8,128)(2,1)S(1)}, u32[]{:S(2)}) copy-start(bf16[896,512]{1,0:T(8,128)(2,1)S(1)} %collective-permute-done.22.refs_1_) | copy-start | bytes 2752516
  86.9 6.6 %collective-permute-start.10 = (bf16[2,2,2,80,128]{4,3,2,1,0:T(8,128)(2,1)S(1)}, bf16[2,2,2,80,128]{4,3,2,1,0:T(8,128)(2,1)S(1)}, u32[]{:S(2)}, u32[]{:S(2)}) collective-permute-start(bf16[2,2,2,80,128]{4,3,2,1,0:T(8,128)(2,1)S(1)} %pad_maximum_fusion.11), channel_id=1, source_target_pairs={{0,24},{32,40},{2,26},{34,42},{4,28},{36,44},{6,30},{38,46},{64,88... | collective-permute-start | bytes 491528 | tf_op jit(solution)/shard_map/ppermute | solution.py:64
  91.4 4.1 %copy-start.16 = (f32[256,640]{1,0:T(8,128)}, f32[256,640]{1,0:T(8,128)S(1)}, u32[]{:S(2)}) copy-start(f32[256,640]{1,0:T(8,128)S(1)} %shard_map.94.refs_2_) | copy-start | bytes 1966084
  93.5 31.0 %collective-permute-start.24 = (bf16[1792,512]{1,0:T(8,128)(2,1)}, bf16[1792,512]{1,0:T(8,128)(2,1)}, u32[]{:S(2)}, u32[]{:S(2)}) collective-permute-start(bf16[1792,512]{1,0:T(8,128)(2,1)} %pad_maximum_fusion), channel_id=1, source_target_pairs={{0,32},{32,0},{2,34},{34,2},{4,36},{36,4},{6,38},{38,6},{64,96},{9... | collective-permute-start | bytes 5505032 | tf_op jit(solution)/shard_map/ppermute | solution.py:64
  93.8 6.5 %collective-permute-start.18 = (bf16[4,2,2,64,128]{4,3,2,1,0:T(8,128)(2,1)S(1)}, bf16[4,2,2,64,128]{4,3,2,1,0:T(8,128)(2,1)S(1)}, u32[]{:S(2)}, u32[]{:S(2)}) collective-permute-start(bf16[4,2,2,64,128]{4,3,2,1,0:T(8,128)(2,1)S(1)} %pad_maximum_fusion.10), channel_id=1, source_target_pairs={{0,8},{32,56},{2,10},{34,58},{4,12},{36,60},{6,14},{38,62},{64,72}... | collective-permute-start | bytes 786440 | tf_op jit(solution)/shard_map/ppermute | solution.py:64
  93.9 7.2 %collective-permute-start.17 = (bf16[4,2,2,80,128]{4,3,2,1,0:T(8,128)(2,1)S(1)}, bf16[4,2,2,80,128]{4,3,2,1,0:T(8,128)(2,1)S(1)}, u32[]{:S(2)}, u32[]{:S(2)}) collective-permute-start(bf16[4,2,2,80,128]{4,3,2,1,0:T(8,128)(2,1)S(1)} %pad_maximum_fusion.8), channel_id=1, source_target_pairs={{0,2},{32,38},{2,0},{34,36},{4,6},{36,34},{6,4},{38,32},{64,66},{9... | collective-permute-start | bytes 983048 | tf_op jit(solution)/shard_map/ppermute | solution.py:64
  95.5 6.5 %copy-start.18 = (f32[256,640]{1,0:T(8,128)}, f32[256,640]{1,0:T(8,128)S(1)}, u32[]{:S(2)}) copy-start(f32[256,640]{1,0:T(8,128)S(1)} %shard_map.95.refs_2_) | copy-start | bytes 1966084
  95.5 23.9 %collective-permute-start.25 = (bf16[896,640]{1,0:T(8,128)(2,1)}, bf16[896,640]{1,0:T(8,128)(2,1)S(1)}, u32[]{:S(2)}, u32[]{:S(2)}) collective-permute-start(bf16[896,640]{1,0:T(8,128)(2,1)} %collective-permute-done.23.refs_0_), channel_id=1, source_target_pairs={{0,32},{32,0},{2,34},{34,2},{4,36},{36,4},{6,38},{38,6},{64,96},{9... | collective-permute-start | bytes 3440648 | tf_op jit(solution)/shard_map/ppermute | solution.py:64
  102.0 1.0 copy-start.14
  103.0 10.4 %collective-permute-start.26 = (bf16[2,4,2,2,64,128]{5,4,3,2,1,0:T(8,128)(2,1)S(1)}, bf16[2,4,2,2,64,128]{5,4,3,2,1,0:T(8,128)(2,1)S(1)}, u32[]{:S(2)}, u32[]{:S(2)}) collective-permute-start(bf16[2,4,2,2,64,128]{5,4,3,2,1,0:T(8,128)(2,1)S(1)} %pad_maximum_fusion.6), channel_id=1, source_target_pairs={{0,24},{32,40},{2,26},{34,42},{4,28},{36,44},{6,30},{38,46},{64,88... | collective-permute-start | bytes 1572872 | tf_op jit(solution)/shard_map/ppermute | solution.py:64
  104.6 12.1 %collective-permute-start.20 = (bf16[2,4,2,2,80,128]{5,4,3,2,1,0:T(8,128)(2,1)}, bf16[2,4,2,2,80,128]{5,4,3,2,1,0:T(8,128)(2,1)}, u32[]{:S(2)}, u32[]{:S(2)}) collective-permute-start(bf16[2,4,2,2,80,128]{5,4,3,2,1,0:T(8,128)(2,1)} %pad_maximum_fusion.5), channel_id=1, source_target_pairs={{0,6},{32,34},{2,4},{34,32},{4,2},{36,38},{6,0},{38,36},{64,70},{9... | collective-permute-start | bytes 1966088 | tf_op jit(solution)/shard_map/ppermute | solution.py:64
  119.4 5.1 %copy-start.6 = (bf16[896,640]{1,0:T(8,128)(2,1)}, bf16[896,640]{1,0:T(8,128)(2,1)S(1)}, u32[]{:S(2)}) copy-start(bf16[896,640]{1,0:T(8,128)(2,1)S(1)} %collective-permute-done.25.refs_1_) | copy-start | bytes 3440644
  119.4 1.6 %copy-start.15 = (bf16[2,256,896]{2,1,0:T(8,128)(2,1)S(1)}, bf16[2,256,896]{2,1,0:T(8,128)(2,1)}, u32[]{:S(2)}) copy-start(bf16[2,256,896]{2,1,0:T(8,128)(2,1)} %copy-done.14) | copy-start | bytes 2752516
  121.0 1.1 copy-start.19
  122.1 2.4 %copy-start.1 = (bf16[2,416,896]{2,1,0:T(8,128)(2,1)S(1)}, bf16[2,416,896]{2,1,0:T(8,128)(2,1)}, u32[]{:S(2)}) copy-start(bf16[2,416,896]{2,1,0:T(8,128)(2,1)} %copy-done) | copy-start | bytes 4472836
  122.1 2.4 %copy-start.3 = (bf16[2,416,896]{2,1,0:T(8,128)(2,1)S(1)}, bf16[2,416,896]{2,1,0:T(8,128)(2,1)}, u32[]{:S(2)}) copy-start(bf16[2,416,896]{2,1,0:T(8,128)(2,1)} %copy-done.2) | copy-start | bytes 4472836
  122.1 2.4 %copy-start.5 = (bf16[896,512]{1,0:T(8,128)(2,1)S(1)}, bf16[896,512]{1,0:T(8,128)(2,1)}, u32[]{:S(2)}) copy-start(bf16[896,512]{1,0:T(8,128)(2,1)} %copy-done.4) | copy-start | bytes 2752516
  124.6 1.2 copy-start.10
  125.7 1.2 copy-start.13
  131.0 6.0 %copy-start.17 = (f32[256,640]{1,0:T(8,128)S(1)}, f32[256,640]{1,0:T(8,128)}, u32[]{:S(2)}) copy-start(f32[256,640]{1,0:T(8,128)} %copy-done.16) | copy-start | bytes 1966084
  136.9 10.8 %collective-permute-start.27 = (bf16[256,896]{1,0:T(8,128)(2,1)}, bf16[256,896]{1,0:T(8,128)(2,1)}, u32[]{:S(2)}, u32[]{:S(2)}) collective-permute-start(bf16[256,896]{1,0:T(8,128)(2,1)} %shard_map.100), channel_id=1, source_target_pairs={{0,64},{32,96},{2,66},{34,98},{4,68},{36,100},{6,70},{38,102},{64,... | collective-permute-start | bytes 1376264 | tf_op jit(solution)/shard_map/ppermute | solution.py:64
  137.0 1.3 copy-start.7
  138.3 1.2 copy-start.11
